TPU v7x, 32 devices: a whole 2x2x4 slice. The times are simulated.
32 devices in a mesh: mem: 8 (over y, x, core), tile: 4 (over z).
Axes of the slice: x: 2, y: 2, z: 4, core: 2. Of those that a mesh axis runs over, the one named last changes fastest.
Arguments:
- background: float32 [256, 128, 256], P('mem', 'tile'), may hold values from -6 to 6
- diffusion: float32 [256], replicated, may hold values from 0.05 to 0.2
- advection: float32 [256], replicated, may hold values from -0.25 to 0.25
- obs_where: int32 [4, 32, 512], P('tile'), may hold values from 0 to 255
- obs_count: int32 [4, 32], P('tile'), may hold values from 256 to 512
- obs_value: float32 [4, 32, 512], P('tile'), may hold values from -6 to 6
- obs_rinv: float32 [4, 32, 512], P('tile'), may hold values from 1 to 1000
Outputs:
- analysis: float32 [256, 128, 256], P('mem', 'tile')
Inputs may be any that keep to these rules, and one draw needn't show every extreme that they name: `obs_where`: each slot reads one entry of its column's 4 * 64 state entries. A column uses its first obs_count slots.
All inputs are finite; a program needn't handle non-finite values.
Results may differ from a plain program's by a relative error of at most 0.0003.
Values sent between devices are 32-bit elements; how exact they have to be, the bound alone decides.
No kernel may reach another device: no remote copies, remote signals or barrier semaphores. Data moves between devices by JAX's collectives and lax.ppermute only.
A program may use at most 64 MiB of HBM per device.

v0:
```python
import jax
import jax.numpy as jnp
from jax import lax
from jax.experimental import pallas as pl
from jax.experimental.pallas import tpu as pltpu
from jax.sharding import PartitionSpec as P

PAIRS = 6
MIB = 1024 * 1024
SMEM = pl.BlockSpec(memory_space=pltpu.SMEM)
VMEM = pl.BlockSpec(memory_space=pltpu.VMEM)
HBM = pl.BlockSpec(memory_space=pltpu.HBM)


def call(kernel, out_shape, flops, moved, vmem=48 * MIB, **options):
    return pl.pallas_call(
        kernel,
        out_shape=out_shape,
        compiler_params=pltpu.CompilerParams(vmem_limit_bytes=vmem),
        cost_estimate=pl.CostEstimate(flops=flops, bytes_accessed=moved, transcendentals=0),
        **options,
    )


def target(me, k, groups):
    if groups & (groups - 1) == 0:
        return me ^ k
    return lax.rem(me + k, groups)


def source(me, k, groups):
    if groups & (groups - 1) == 0:
        return me ^ k
    return lax.rem(me + groups - k, groups)


def exchange(blocks):
    groups = len(blocks)
    out = [blocks[0]]
    for k in range(1, groups):
        pairs = [(i, i ^ k if groups & (groups - 1) == 0 else (i + k) % groups) for i in range(groups)]
        out.append(lax.ppermute(blocks[k], "mem", pairs))
    return out


def split(x, parts):
    out = []
    for _ in range(parts):
        part = x.astype(jnp.bfloat16)
        out.append(part)
        x = x - part.astype(jnp.float32)
    return out


def dot(a, b):
    return jnp.dot(a, b, precision=lax.Precision.HIGH, preferred_element_type=jnp.float32)


def square_by_rows(parts):
    p0, p1, p2 = parts
    lhs = jnp.concatenate([p2, p0, p1, p1, p0, p0], axis=1)
    rhs = jnp.concatenate([p0, p2, p1, p0, p1, p0], axis=1)
    return lax.dot_general(lhs, rhs, (((1,), (1,)), ((), ())), preferred_element_type=jnp.float32)


def stencil(padded, diffusion, advection):
    middle = padded[1:-1]
    left = padded[:-2]
    right = padded[2:]
    return middle + diffusion * (left - 2.0 * middle + right) + advection * (0.5 * (left - right))


def inner_start(place, quarter):
    return place + quarter


def outer_start(place, quarter):
    return jnp.where(place < quarter, place, place + 2 * quarter)


def pieces_of(members):
    rows = 8 if members % 8 == 0 else members
    return [pl.ds(first, rows) for first in range(0, members, rows)]


def inner_kernel(state_ref, diff_ref, adv_ref, out_ref, low_ref, high_ref, held_ref, num_ref, edge_ref, made_ref, sems):
    members, columns, entries = state_ref.shape
    groups, half, _, _ = out_ref.shape
    quarter = columns // 4
    pieces = pieces_of(members)
    count = len(pieces)
    reads = [pltpu.make_async_copy(state_ref.at[part], held_ref.at[part], sems.at[i]) for i, part in enumerate(pieces)]
    reads.append(pltpu.make_async_copy(diff_ref, num_ref.at[0], sems.at[count]))
    reads.append(pltpu.make_async_copy(adv_ref, num_ref.at[1], sems.at[count + 1]))
    for copy in reads[count:] + reads[:count]:
        copy.start()
    reads[count].wait()
    reads[count + 1].wait()
    diffusion = num_ref[0:1][None]
    advection = num_ref[1:2][None]
    writes = []
    for i, part in enumerate(pieces):
        reads[i].wait()
        x = jnp.swapaxes(held_ref[part], 0, 1)
        edge_ref[0, :, part] = x[:2]
        edge_ref[1, :, part] = x[columns - 2 :]
        x = x[quarter - 2 : columns - quarter + 2]
        x = stencil(stencil(x, diffusion, advection), diffusion, advection)
        made_ref[:, :, part] = x.reshape(groups, half, part.size, entries)
        copy = pltpu.make_async_copy(made_ref.at[:, :, part], out_ref.at[:, :, part], sems.at[count + 2 + i])
        copy.start()
        writes.append(copy)
    for i, ref in enumerate((low_ref, high_ref)):
        copy = pltpu.make_async_copy(edge_ref.at[i], ref, sems.at[2 * count + 2 + i])
        copy.start()
        writes.append(copy)
    for copy in writes:
        copy.wait()


def outer_kernel(obs_ref, state_ref, before_ref, after_ref, diff_ref, adv_ref, out_ref, turned_ref):
    del obs_ref
    columns = state_ref.shape[1]
    quarter = columns // 4
    turned_ref[2 : columns + 2] = jnp.swapaxes(state_ref[...], 0, 1)
    turned_ref[:2] = before_ref[...]
    turned_ref[columns + 2 :] = after_ref[...]
    diffusion = diff_ref[...][None]
    advection = adv_ref[...][None]
    low = turned_ref[: quarter + 4]
    high = turned_ref[columns - quarter :]
    low = stencil(stencil(low, diffusion, advection), diffusion, advection)
    high = stencil(stencil(high, diffusion, advection), diffusion, advection)
    out_ref[...] = jnp.concatenate([low, high], axis=0).reshape(out_ref.shape)


def join_kernel(me_ref, inner_ref, *refs):
    *outer, out_ref, turned_ref, made_ref, sems = refs
    members, columns, entries = out_ref.shape
    groups, half, _, _ = inner_ref.shape
    quarter = columns // 4
    writes = []
    for i, part in enumerate(pieces_of(members)):
        for k in range(groups):
            place = source(me_ref[0], k, groups) * half
            turned_ref[pl.ds(outer_start(place, quarter), half), part] = outer[k][:, part]
        turned_ref[quarter : columns - quarter, part] = inner_ref[:, :, part].reshape(groups * half, part.size, entries)
        made_ref[part] = jnp.swapaxes(turned_ref[:, part], 0, 1)
        copy = pltpu.make_async_copy(made_ref.at[part], out_ref.at[part], sems.at[i])
        copy.start()
        writes.append(copy)
    for copy in writes:
        copy.wait()


def observe_kernel(me_ref, count_ref, where_ref, value_ref, rinv_ref, out_ref):
    columns, _, entries = out_ref.shape
    half = columns // 2
    quarter = where_ref.shape[0] // 4
    slots = where_ref.shape[1]
    place = me_ref[0] * half
    slot = lax.broadcasted_iota(jnp.int32, (1, slots), 1)
    row = lax.broadcasted_iota(jnp.int32, (16, slots), 0)
    entry = lax.broadcasted_iota(jnp.int32, (entries, slots), 0)
    for c in range(columns):
        at = inner_start(place, quarter) + c if c < half else outer_start(place, quarter) + c - half
        weight = jnp.where(slot < count_ref[0, at], rinv_ref[pl.ds(at, 1), :], 0.0)
        lhs = jnp.zeros((16, slots), jnp.float32)
        for first, source in ((0, weight), (3, weight * value_ref[pl.ds(at, 1), :])):
            for k, part in enumerate(split(source, 3)):
                lhs = jnp.where(row == first + k, part.astype(jnp.float32), lhs)
        onehot = (entry == where_ref[pl.ds(at, 1), :]).astype(jnp.float32).astype(jnp.bfloat16)
        sums = lax.dot_general(
            lhs.astype(jnp.bfloat16), onehot, (((1,), (1,)), ((), ())), preferred_element_type=jnp.float32
        )
        out_ref[c, 0:1] = sums[0:1] + (sums[1:2] + sums[2:3])
        out_ref[c, 1:2] = sums[3:4] + (sums[4:5] + sums[5:6])


def analyse_kernel(first, me_ref, after_ref, obs_ref, states_ref, *refs):
    del after_ref
    *outs, done_ref, root_ref, ahead_ref = refs
    done_ref[...] = jnp.zeros_like(done_ref)
    groups = states_ref.shape[0]
    if len(outs) == 1:
        states = [states_ref.at[k] for k in range(groups)]
        outs = [outs[0].at[k] for k in range(groups)]
    else:
        states = [states_ref.at[target(me_ref[0], k, groups)] for k in range(groups)]
    columns, local, entries = states[0].shape
    members = groups * local
    spread = members - 1.0
    every = range(columns)
    rows = lax.broadcasted_iota(jnp.int32, (members, members), 0)
    cols = lax.broadcasted_iota(jnp.int32, (members, members), 1)
    means, forces, scales, grams = [], [], [], []
    for c in every:
        x = jnp.concatenate([ref[c] for ref in states], axis=0)
        mean = jnp.sum(x, axis=0, keepdims=True) * (1.0 / members)
        anomaly = x - mean
        total = obs_ref[first + c, 0:1]
        forces.append(obs_ref[first + c, 1:2] - total * mean)
        means.append(mean)
        ahead_ref[c] = anomaly
        grams.append(square_by_rows(split(anomaly * jnp.sqrt(total), 3)))
    for c in every:
        gram = grams[c] + jnp.where(rows == cols, spread, 0.0)
        norm = jnp.sum(jnp.sum(gram * gram, axis=0, keepdims=True), axis=1, keepdims=True)
        scales.append(jnp.sqrt(norm))
        root_ref[c] = gram * (1.0 / scales[c])

    def factors():
        p = [dot(root_ref[c], root_ref[c]) for c in every]
        cubic = [dot(0.0625 * p[c] - 0.5625 * root_ref[c], p[c]) for c in every]
        return [1.6875 * p[c] - 2.4375 * root_ref[c] + cubic[c] for c in every]

    def pair(step, carry):
        r = factors()
        t = [2.25 * root_ref[c] + dot(r[c], root_ref[c]) for c in every]
        for c in every:
            ahead_ref[c] = 2.25 * ahead_ref[c] + dot(r[c], ahead_ref[c])
        for c in every:
            root_ref[c] = 2.25 * t[c] + dot(t[c], r[c])
        return carry

    lax.fori_loop(0, PAIRS - 1, pair, 0)
    r = factors()
    ahead = [2.25 * ahead_ref[c] + dot(r[c], ahead_ref[c]) for c in every]
    for c in every:
        w = ahead[c]
        inner = jnp.sum(w * forces[c], axis=1, keepdims=True)
        shift = jnp.sum(w * inner, axis=0, keepdims=True) / scales[c]
        result = means[c] + shift + w * jnp.sqrt(spread / scales[c])
        for k in range(groups):
            outs[k][c] = result[k * local : (k + 1) * local]


def analyse(states, obs, first, me, after, apart):
    groups, columns, local, entries = states.shape
    members = groups * local
    whole = jax.ShapeDtypeStruct(states.shape, jnp.float32)
    token = jax.ShapeDtypeStruct(after.shape, jnp.float32)

    def kernel(*refs):
        analyse_kernel(first, *refs)

    return call(
        kernel,
        ([jax.ShapeDtypeStruct(states.shape[1:], jnp.float32)] * groups if apart else [whole]) + [token],
        columns * 90 * 2 * members * members * entries,
        8 * columns * members * entries,
        in_specs=[SMEM, VMEM, VMEM, VMEM],
        scratch_shapes=[
            pltpu.VMEM((columns, members, members), jnp.float32),
            pltpu.VMEM((columns, members, entries), jnp.float32),
        ],
    )(me, after, obs, states)


def body(background, diffusion, advection, obs_where, obs_count, obs_value, obs_rinv):
    local, columns, entries = background.shape
    groups = lax.axis_size("mem")
    tiles = lax.axis_size("tile")
    half = columns // groups // 2
    size = background.size
    block = (half, local, entries)
    edge = jax.ShapeDtypeStruct((2, local, entries), jnp.float32)
    me = lax.axis_index("mem")[None].astype(jnp.int32)
    pieces = len(pieces_of(local))

    inner, low, high = call(
        inner_kernel,
        [jax.ShapeDtypeStruct((groups, *block), jnp.float32), edge, edge],
        20 * size,
        8 * size,
        vmem=60 * MIB,
        in_specs=[HBM, HBM, HBM],
        out_specs=[HBM, HBM, HBM],
        scratch_shapes=[
            pltpu.VMEM(background.shape, jnp.float32),
            pltpu.VMEM((8, entries), jnp.float32),
            pltpu.VMEM((2, 2, local, entries), jnp.float32),
            pltpu.VMEM((groups, *block), jnp.float32),
            pltpu.SemaphoreType.DMA((2 * pieces + 4,)),
        ],
    )(background, diffusion, advection)
    inner = lax.all_to_all(inner, "mem", split_axis=0, concat_axis=0, tiled=True)
    before = lax.ppermute(high, "tile", [(i, (i + 1) % tiles) for i in range(tiles)])
    after = lax.ppermute(low, "tile", [((i + 1) % tiles, i) for i in range(tiles)])
    obs = call(
        observe_kernel,
        jax.ShapeDtypeStruct((2 * half, 8, entries), jnp.float32),
        2 * half * 2 * 16 * obs_where.shape[2] * entries,
        12 * obs_where.size,
        in_specs=[SMEM, SMEM] + [VMEM] * 3,
    )(me, obs_count, obs_where[0], obs_value[0], obs_rinv[0])
    outer = call(
        outer_kernel,
        jax.ShapeDtypeStruct((groups, *block), jnp.float32),
        20 * size,
        8 * size,
        in_specs=[VMEM] * 6,
        scratch_shapes=[pltpu.VMEM((columns + 4, local, entries), jnp.float32)],
    )(obs, background, before, after, diffusion[None], advection[None])
    outer = lax.all_to_all(outer, "mem", split_axis=0, concat_axis=0, tiled=True)

    inner, done = analyse(inner, obs, 0, me, obs[0], False)
    inner = lax.all_to_all(inner, "mem", split_axis=0, concat_axis=0, tiled=True)
    *outer, _ = analyse(outer, obs, half, me, done, True)
    outer = exchange(outer)
    return call(
        join_kernel,
        jax.ShapeDtypeStruct(background.shape, jnp.float32),
        size,
        8 * size,
        in_specs=[SMEM] + [VMEM] * (groups + 1),
        out_specs=HBM,
        scratch_shapes=[
            pltpu.VMEM((columns, local, entries), jnp.float32),
            pltpu.VMEM(background.shape, jnp.float32),
            pltpu.SemaphoreType.DMA((pieces,)),
        ],
    )(me, inner, *outer)


def solution(mesh):
    return jax.shard_map(
        body,
        mesh=mesh,
        in_specs=(
            P("mem", "tile", None),
            P(),
            P(),
            P("tile", None, None),
            P("tile", None),
            P("tile", None, None),
            P("tile", None, None),
        ),
        out_specs=P("mem", "tile", None),
        check_vma=False,
    )
```

profile of v0, /device:TPU:0, one launch (start us, length us, event | category | flops | bytes accessed | tf_op | source)
XLA Modules:
  0.0 57.7 jit_solution(16030664361843720252)
XLA Ops:
  0.0 0.0 copy-start
  0.0 2.4 %shard_map.74 = (f32[8,2,32,256]{3,2,1,0:T(8,128)}, f32[2,32,256]{2,1,0:T(8,128)}, f32[2,32,256]{2,1,0:T(8,128)}) custom-call(f32[32,32,256]{2,1,0:T(8,128)} %state_ref.3, f32[256]{0:T(256)} %diff_ref.1, f32[256]{0:T(256)} %adv_ref.1), custom_call_target="tpu_custom_call" | custom-call | flops 5242880 | bytes 2097152 | tf_op jit(solution)/shard_map/pallas_call | solution.py:271
  2.4 0.0 copy-start.8
  2.4 0.0 copy-start.7
  2.4 0.0 copy-start.1
  2.4 0.0 copy-start.2
  2.4 0.0 copy-start.3
  2.4 5.3 %all-to-all-start = ((f32[8,2,32,256]{3,2,1,0:T(8,128)}), f32[8,2,32,256]{3,2,1,0:T(8,128)S(1)}, u32[]{:S(2)}, u32[]{:S(2)}) async-start(f32[8,2,32,256]{3,2,1,0:T(8,128)} %get-tuple-element.18), calls=%async_computation | async-start | bytes 1048576 | tf_op jit(solution)/shard_map/all_to_all | solution.py:287
  7.7 0.0 copy-done.8
  7.7 1.6 %collective-permute-start = (f32[2,32,256]{2,1,0:T(8,128)S(1)}, f32[2,32,256]{2,1,0:T(8,128)S(1)}, u32[]{:S(2)}, u32[]{:S(2)}) collective-permute-start(f32[2,32,256]{2,1,0:T(8,128)S(1)} %copy-done.8), channel_id=1, source_target_pairs={{0,1},{1,2},{2,3},{3,0},{4,5},{5,6},{6,7},{7,4},{8,9},{9,10},{10,1... | collective-permute-start | bytes 196616 | tf_op jit(solution)/shard_map/ppermute | solution.py:288
  9.4 0.0 copy-done.7
  9.4 2.2 %collective-permute-start.1 = (f32[2,32,256]{2,1,0:T(8,128)S(1)}, f32[2,32,256]{2,1,0:T(8,128)S(1)}, u32[]{:S(2)}, u32[]{:S(2)}) collective-permute-start(f32[2,32,256]{2,1,0:T(8,128)S(1)} %copy-done.7), channel_id=1, source_target_pairs={{1,0},{2,1},{3,2},{0,3},{5,4},{6,5},{7,6},{4,7},{9,8},{10,9},{11,1... | collective-permute-start | bytes 196616 | tf_op jit(solution)/shard_map/ppermute | solution.py:289
  11.6 0.0 copy-start.6
  11.6 0.0 copy-done.1
  11.6 0.0 copy-done.2
  11.6 0.0 copy-done.3
  11.6 0.6 %copy-done.6 = s32[1,32]{1,0:T(1,128)S(1)} copy-done((s32[1,32]{1,0:T(1,128)S(1)}, s32[1,32]{1,0:T(1,128)}, u32[]{:S(2)}) %copy-start.6) | copy-done | bytes 152
  12.3 0.0 copy-start.5
  12.3 0.9 %shard_map.73.refs_2_.obs_ref = f32[4,8,256]{2,1,0:T(8,128)S(1)} custom-call(s32[1]{0:T(128)} %bitcast.me_ref.refs_0_, s32[1,32]{1,0:T(1,128)S(1)} %copy-done.6, s32[32,512]{1,0:T(8,128)S(1)} %bitcast.8, f32[32,512]{1,0:T(8,128)S(1)} %bitcast.9, f32[32,512]{1,0:T(8,128)S(1)} %bitcast.10), custom_call_target="tpu_custom_call" | custom-call | flops 16777216 | bytes 196608 | tf_op jit(solution)/shard_map/pallas_call | solution.py:290
  13.2 1.0 %collective-permute-done.before_ref = f32[2,32,256]{2,1,0:T(8,128)S(1)} collective-permute-done((f32[2,32,256]{2,1,0:T(8,128)S(1)}, f32[2,32,256]{2,1,0:T(8,128)S(1)}, u32[]{:S(2)}, u32[]{:S(2)}) %collective-permute-start) | collective-permute-done | bytes 65568 | tf_op jit(solution)/shard_map/ppermute | solution.py:288
  14.3 0.7 %collective-permute-done.1.after_ref = f32[2,32,256]{2,1,0:T(8,128)S(1)} collective-permute-done((f32[2,32,256]{2,1,0:T(8,128)S(1)}, f32[2,32,256]{2,1,0:T(8,128)S(1)}, u32[]{:S(2)}, u32[]{:S(2)}) %collective-permute-start.1) | collective-permute-done | bytes 65568 | tf_op jit(solution)/shard_map/ppermute | solution.py:289
  14.9 0.0 copy-start.4
  14.9 0.0 copy-done
  14.9 0.0 copy-done.5
  14.9 0.7 %copy-done.4 = f32[256]{0:T(256)S(1)} copy-done((f32[256]{0:T(256)S(1)}, f32[256]{0:T(256)}, u32[]{:S(2)}) %copy-start.4) | copy-done | bytes 1048
  15.6 1.3 %shard_map.76 = f32[8,2,32,256]{3,2,1,0:T(8,128)} custom-call(f32[4,8,256]{2,1,0:T(8,128)S(1)} %shard_map.73.refs_2_.obs_ref, f32[32,32,256]{2,1,0:T(8,128)S(1)} %copy-done, f32[2,32,256]{2,1,0:T(8,128)S(1)} %collective-permute-done.before_ref, f32[2,32,256]{2,1,0:T(8,128)S(1)} %collective-permute-done.1.after_ref, f32[1,256]{1,0:T(1,128)S(1)} %bitcast.11, ...), custom_call_target="tpu_custom_call" | custom-call | flops 5242880 | bytes 2097152 | tf_op jit(solution)/shard_map/pallas_call | solution.py:297
  16.9 0.6 %all-to-all-done.refs_3_ = f32[8,2,32,256]{3,2,1,0:T(8,128)S(1)} async-done(((f32[8,2,32,256]{3,2,1,0:T(8,128)}), f32[8,2,32,256]{3,2,1,0:T(8,128)S(1)}, u32[]{:S(2)}, u32[]{:S(2)}) %all-to-all-start) | async-done | bytes 524320 | tf_op jit(solution)/shard_map/all_to_all | solution.py:287
  17.5 3.5 %all-to-all-start.2 = ((f32[8,2,32,256]{3,2,1,0:T(8,128)}), f32[8,2,32,256]{3,2,1,0:T(8,128)S(1)}, u32[]{:S(2)}, u32[]{:S(2)}) async-start(f32[8,2,32,256]{3,2,1,0:T(8,128)} %shard_map.76), calls=%async_computation.2 | async-start | bytes 1048576 | tf_op jit(solution)/shard_map/all_to_all | solution.py:305
  21.0 10.3 %shard_map.75 = (f32[8,2,32,256]{3,2,1,0:T(8,128)}, f32[8,256]{1,0:T(8,128)S(1)}) custom-call(s32[1]{0:T(128)} %bitcast.me_ref.refs_0_, f32[8,256]{1,0:T(8,128)S(1)} %slice_bitcast_fusion.refs_1_, f32[4,8,256]{2,1,0:T(8,128)S(1)} %shard_map.73.refs_2_.obs_ref, f32[8,2,32,256]{3,2,1,0:T(8,128)S(1)} %all-to-all-done.refs_3_), custom_call_target="tpu_custom_call" | custom-call | flops 6039797760 | bytes 1048576 | tf_op jit(solution)/shard_map/pallas_call | solution.py:247
  31.3 0.0 all-to-all-done.2.refs_3_
  31.3 4.1 %all-to-all-start.1 = ((f32[8,2,32,256]{3,2,1,0:T(8,128)}), f32[8,2,32,256]{3,2,1,0:T(8,128)S(1)}, u32[]{:S(2)}, u32[]{:S(2)}) async-start(f32[8,2,32,256]{3,2,1,0:T(8,128)} %get-tuple-element.19), calls=%async_computation.1 | async-start | bytes 1048576 | tf_op jit(solution)/shard_map/all_to_all | solution.py:308
  35.4 9.5 %shard_map.77 = (f32[2,32,256]{2,1,0:T(8,128)S(1)}, f32[2,32,256]{2,1,0:T(8,128)S(1)}, f32[2,32,256]{2,1,0:T(8,128)S(1)}, f32[2,32,256]{2,1,0:T(8,128)S(1)}, f32...) custom-call(s32[1]{0:T(128)} %bitcast.me_ref.refs_0_, ...), custom_call_target="tpu_custom_call" | custom-call | flops 6039797760 | bytes 1048576 | tf_op jit(solution)/shard_map/pallas_call | solution.py:247
  44.9 0.6 collective-permute-start.2
  45.5 1.7 %collective-permute-start.3 = (f32[2,32,256]{2,1,0:T(8,128)S(1)}, f32[2,32,256]{2,1,0:T(8,128)S(1)}, u32[]{:S(2)}, u32[]{:S(2)}) collective-permute-start(f32[2,32,256]{2,1,0:T(8,128)S(1)} %get-tuple-element.25), channel_id=1, source_target_pairs={{0,8},{4,12},{8,0},{12,4},{16,24},{20,28},{24,16},{28,20},{1,9},{5... | collective-permute-start | bytes 196616 | tf_op jit(solution)/shard_map/ppermute | solution.py:42
  47.2 0.0 collective-permute-start.4
  47.2 1.7 %collective-permute-start.5 = (f32[2,32,256]{2,1,0:T(8,128)S(1)}, f32[2,32,256]{2,1,0:T(8,128)S(1)}, u32[]{:S(2)}, u32[]{:S(2)}) collective-permute-start(f32[2,32,256]{2,1,0:T(8,128)S(1)} %get-tuple-element.27), channel_id=1, source_target_pairs={{0,16},{4,20},{8,24},{12,28},{16,0},{20,4},{24,8},{28,12},{1,17},{... | collective-permute-start | bytes 196616 | tf_op jit(solution)/shard_map/ppermute | solution.py:42
  48.9 0.1 collective-permute-start.6
  49.0 0.0 collective-permute-done.2.refs_1_
  49.0 2.6 %collective-permute-start.7 = (f32[2,32,256]{2,1,0:T(8,128)S(1)}, f32[2,32,256]{2,1,0:T(8,128)S(1)}, u32[]{:S(2)}, u32[]{:S(2)}) collective-permute-start(f32[2,32,256]{2,1,0:T(8,128)S(1)} %get-tuple-element.29), channel_id=1, source_target_pairs={{0,24},{4,28},{8,16},{12,20},{16,8},{20,12},{24,0},{28,4},{1,25},{... | collective-permute-start | bytes 196616 | tf_op jit(solution)/shard_map/ppermute | solution.py:42
  51.6 0.0 collective-permute-done.3.refs_2_
  51.6 0.0 collective-permute-start.8
  51.6 0.0 collective-permute-done.4.refs_3_
  51.6 0.0 collective-permute-done.5.refs_4_
  51.7 2.7 %collective-permute-done.6.refs_5_ = f32[2,32,256]{2,1,0:T(8,128)S(1)} collective-permute-done((f32[2,32,256]{2,1,0:T(8,128)S(1)}, f32[2,32,256]{2,1,0:T(8,128)S(1)}, u32[]{:S(2)}, u32[]{:S(2)}) %collective-permute-start.6) | collective-permute-done | bytes 65568 | tf_op jit(solution)/shard_map/ppermute | solution.py:42
  54.3 0.0 collective-permute-done.7.refs_6_
  54.4 2.3 %collective-permute-done.8.refs_7_ = f32[2,32,256]{2,1,0:T(8,128)S(1)} collective-permute-done((f32[2,32,256]{2,1,0:T(8,128)S(1)}, f32[2,32,256]{2,1,0:T(8,128)S(1)}, u32[]{:S(2)}, u32[]{:S(2)}) %collective-permute-start.8) | collective-permute-done | bytes 65568 | tf_op jit(solution)/shard_map/ppermute | solution.py:42
  56.6 0.0 all-to-all-done.1.inner_ref
  56.6 1.1 %shard_map.78 = f32[32,32,256]{2,1,0:T(8,128)} custom-call(s32[1]{0:T(128)} %bitcast.me_ref.refs_0_, f32[8,2,32,256]{3,2,1,0:T(8,128)S(1)} %all-to-all-done.1.inner_ref, f32[2,32,256]{2,1,0:T(8,128)S(1)} %get-tuple-element.23.refs_0_, f32[2,32,256]{2,1,0:T(8,128)S(1)} %collective-permute-done.2.refs_1_, f32[2,32,256]{2,1,0:T(8,128)S(1)} %collective-permute-done.3.refs_2_, ...), custom_call_target="tpu_custom_call" | custom-call | flops 262144 | bytes 2097152 | tf_op jit(solution)/shard_map/pallas_call | solution.py:311
  (1 shorter events, 0.0 us)
Async XLA Ops:
  0.0 14.9 %copy-start = (f32[32,32,256]{2,1,0:T(8,128)S(1)}, f32[32,32,256]{2,1,0:T(8,128)}, u32[]{:S(2)}) copy-start(f32[32,32,256]{2,1,0:T(8,128)} %state_ref.3) | copy-start | bytes 3145732
  2.4 5.4 %copy-start.8 = (f32[2,32,256]{2,1,0:T(8,128)S(1)}, f32[2,32,256]{2,1,0:T(8,128)}, u32[]{:S(2)}) copy-start(f32[2,32,256]{2,1,0:T(8,128)} %get-tuple-element.21) | copy-start | bytes 196612
  2.4 7.0 %copy-start.7 = (f32[2,32,256]{2,1,0:T(8,128)S(1)}, f32[2,32,256]{2,1,0:T(8,128)}, u32[]{:S(2)}) copy-start(f32[2,32,256]{2,1,0:T(8,128)} %get-tuple-element.22) | copy-start | bytes 196612
  2.4 9.2 %copy-start.1 = (s32[1,32,512]{2,1,0:T(8,128)S(1)}, s32[1,32,512]{2,1,0:T(8,128)}, u32[]{:S(2)}) copy-start(s32[1,32,512]{2,1,0:T(8,128)} %param.10) | copy-start | bytes 196612
  2.4 9.2 %copy-start.2 = (f32[1,32,512]{2,1,0:T(8,128)S(1)}, f32[1,32,512]{2,1,0:T(8,128)}, u32[]{:S(2)}) copy-start(f32[1,32,512]{2,1,0:T(8,128)} %param.12) | copy-start | bytes 196612
  2.4 9.2 %copy-start.3 = (f32[1,32,512]{2,1,0:T(8,128)S(1)}, f32[1,32,512]{2,1,0:T(8,128)}, u32[]{:S(2)}) copy-start(f32[1,32,512]{2,1,0:T(8,128)} %param.13) | copy-start | bytes 196612
  2.4 15.1 %all-to-all-start = ((f32[8,2,32,256]{3,2,1,0:T(8,128)}), f32[8,2,32,256]{3,2,1,0:T(8,128)S(1)}, u32[]{:S(2)}, u32[]{:S(2)}) async-start(f32[8,2,32,256]{3,2,1,0:T(8,128)} %get-tuple-element.18), calls=%async_computation | async-start | bytes 1048576 | tf_op jit(solution)/shard_map/all_to_all | solution.py:287
  7.7 6.5 %collective-permute-start = (f32[2,32,256]{2,1,0:T(8,128)S(1)}, f32[2,32,256]{2,1,0:T(8,128)S(1)}, u32[]{:S(2)}, u32[]{:S(2)}) collective-permute-start(f32[2,32,256]{2,1,0:T(8,128)S(1)} %copy-done.8), channel_id=1, source_target_pairs={{0,1},{1,2},{2,3},{3,0},{4,5},{5,6},{6,7},{7,4},{8,9},{9,10},{10,1... | collective-permute-start | bytes 196616 | tf_op jit(solution)/shard_map/ppermute | solution.py:288
  9.4 5.6 %collective-permute-start.1 = (f32[2,32,256]{2,1,0:T(8,128)S(1)}, f32[2,32,256]{2,1,0:T(8,128)S(1)}, u32[]{:S(2)}, u32[]{:S(2)}) collective-permute-start(f32[2,32,256]{2,1,0:T(8,128)S(1)} %copy-done.7), channel_id=1, source_target_pairs={{1,0},{2,1},{3,2},{0,3},{5,4},{6,5},{7,6},{4,7},{9,8},{10,9},{11,1... | collective-permute-start | bytes 196616 | tf_op jit(solution)/shard_map/ppermute | solution.py:289
  11.6 0.7 %copy-start.6 = (s32[1,32]{1,0:T(1,128)S(1)}, s32[1,32]{1,0:T(1,128)}, u32[]{:S(2)}) copy-start(s32[1,32]{1,0:T(1,128)} %count_ref.1) | copy-start | bytes 388
  12.3 2.7 %copy-start.5 = (f32[256]{0:T(256)S(1)}, f32[256]{0:T(256)}, u32[]{:S(2)}) copy-start(f32[256]{0:T(256)} %adv_ref.1) | copy-start | bytes 3076
  14.9 0.7 %copy-start.4 = (f32[256]{0:T(256)S(1)}, f32[256]{0:T(256)}, u32[]{:S(2)}) copy-start(f32[256]{0:T(256)} %diff_ref.1) | copy-start | bytes 3076
  17.5 13.8 %all-to-all-start.2 = ((f32[8,2,32,256]{3,2,1,0:T(8,128)}), f32[8,2,32,256]{3,2,1,0:T(8,128)S(1)}, u32[]{:S(2)}, u32[]{:S(2)}) async-start(f32[8,2,32,256]{3,2,1,0:T(8,128)} %shard_map.76), calls=%async_computation.2 | async-start | bytes 1048576 | tf_op jit(solution)/shard_map/all_to_all | solution.py:305
  31.3 25.4 %all-to-all-start.1 = ((f32[8,2,32,256]{3,2,1,0:T(8,128)}), f32[8,2,32,256]{3,2,1,0:T(8,128)S(1)}, u32[]{:S(2)}, u32[]{:S(2)}) async-start(f32[8,2,32,256]{3,2,1,0:T(8,128)} %get-tuple-element.19), calls=%async_computation.1 | async-start | bytes 1048576 | tf_op jit(solution)/shard_map/all_to_all | solution.py:308
  44.9 4.1 %collective-permute-start.2 = (f32[2,32,256]{2,1,0:T(8,128)S(1)}, f32[2,32,256]{2,1,0:T(8,128)S(1)}, u32[]{:S(2)}, u32[]{:S(2)}) collective-permute-start(f32[2,32,256]{2,1,0:T(8,128)S(1)} %get-tuple-element.24), channel_id=1, source_target_pairs={{0,4},{4,0},{8,12},{12,8},{16,20},{20,16},{24,28},{28,24},{1,5},{5... | collective-permute-start | bytes 196616 | tf_op jit(solution)/shard_map/ppermute | solution.py:42
  45.5 6.1 %collective-permute-start.3 = (f32[2,32,256]{2,1,0:T(8,128)S(1)}, f32[2,32,256]{2,1,0:T(8,128)S(1)}, u32[]{:S(2)}, u32[]{:S(2)}) collective-permute-start(f32[2,32,256]{2,1,0:T(8,128)S(1)} %get-tuple-element.25), channel_id=1, source_target_pairs={{0,8},{4,12},{8,0},{12,4},{16,24},{20,28},{24,16},{28,20},{1,9},{5... | collective-permute-start | bytes 196616 | tf_op jit(solution)/shard_map/ppermute | solution.py:42
  47.2 4.4 %collective-permute-start.4 = (f32[2,32,256]{2,1,0:T(8,128)S(1)}, f32[2,32,256]{2,1,0:T(8,128)S(1)}, u32[]{:S(2)}, u32[]{:S(2)}) collective-permute-start(f32[2,32,256]{2,1,0:T(8,128)S(1)} %get-tuple-element.26), channel_id=1, source_target_pairs={{0,12},{4,8},{8,4},{12,0},{16,28},{20,24},{24,20},{28,16},{1,13},{... | collective-permute-start | bytes 196616 | tf_op jit(solution)/shard_map/ppermute | solution.py:42
  47.2 4.5 %collective-permute-start.5 = (f32[2,32,256]{2,1,0:T(8,128)S(1)}, f32[2,32,256]{2,1,0:T(8,128)S(1)}, u32[]{:S(2)}, u32[]{:S(2)}) collective-permute-start(f32[2,32,256]{2,1,0:T(8,128)S(1)} %get-tuple-element.27), channel_id=1, source_target_pairs={{0,16},{4,20},{8,24},{12,28},{16,0},{20,4},{24,8},{28,12},{1,17},{... | collective-permute-start | bytes 196616 | tf_op jit(solution)/shard_map/ppermute | solution.py:42
  48.9 5.5 %collective-permute-start.6 = (f32[2,32,256]{2,1,0:T(8,128)S(1)}, f32[2,32,256]{2,1,0:T(8,128)S(1)}, u32[]{:S(2)}, u32[]{:S(2)}) collective-permute-start(f32[2,32,256]{2,1,0:T(8,128)S(1)} %get-tuple-element.28), channel_id=1, source_target_pairs={{0,20},{4,16},{8,28},{12,24},{16,4},{20,0},{24,12},{28,8},{1,21},{... | collective-permute-start | bytes 196616 | tf_op jit(solution)/shard_map/ppermute | solution.py:42
  49.0 5.3 %collective-permute-start.7 = (f32[2,32,256]{2,1,0:T(8,128)S(1)}, f32[2,32,256]{2,1,0:T(8,128)S(1)}, u32[]{:S(2)}, u32[]{:S(2)}) collective-permute-start(f32[2,32,256]{2,1,0:T(8,128)S(1)} %get-tuple-element.29), channel_id=1, source_target_pairs={{0,24},{4,28},{8,16},{12,20},{16,8},{20,12},{24,0},{28,4},{1,25},{... | collective-permute-start | bytes 196616 | tf_op jit(solution)/shard_map/ppermute | solution.py:42
  51.6 5.0 %collective-permute-start.8 = (f32[2,32,256]{2,1,0:T(8,128)S(1)}, f32[2,32,256]{2,1,0:T(8,128)S(1)}, u32[]{:S(2)}, u32[]{:S(2)}) collective-permute-start(f32[2,32,256]{2,1,0:T(8,128)S(1)} %get-tuple-element.30), channel_id=1, source_target_pairs={{0,28},{4,24},{8,20},{12,16},{16,12},{20,8},{24,4},{28,0},{1,29},{... | collective-permute-start | bytes 196616 | tf_op jit(solution)/shard_map/ppermute | solution.py:42
where the time goes:
time: 58.2 us; the launch traced here: 57.7 us
  Pallas kernels  25.5 us (44%)
  starting transfers between devices  23.5 us (40%)
  waiting for transfers between devices  7.31 us (13%)
  local copies, waits for them, and re-layouts  1.36 us (2%)
    pallas_call x2, Pallas kernels, analyse(): call(kernel, ([jax.ShapeDtypeStruct(states.shape[1:], jnp.float32)] * gro...  19.8 us
    all_to_all x2, starting transfers between devices, body(): lax.all_to_all(inner, 'mem', split_axis=0, concat_axis=0, tiled=True)  9.45 us
    ppermute x7, starting transfers between devices, exchange(): out.append(lax.ppermute(blocks[k], 'mem', pairs))  6.68 us
    ppermute x7, waiting for transfers between devices, exchange(): out.append(lax.ppermute(blocks[k], 'mem', pairs))  5 us
    all_to_all x1, starting transfers between devices, body(): lax.all_to_all(outer, 'mem', split_axis=0, concat_axis=0, tiled=True)  3.49 us
    pallas_call x1, Pallas kernels, body(): call(inner_kernel, [jax.ShapeDtypeStruct((groups, *block), jnp.float32),...  2.35 us
    ppermute x1, starting transfers between devices, body(): lax.ppermute(low, 'tile', [((i + 1) % tiles, i) for i in range(tiles)])  2.25 us
    ppermute x1, starting transfers between devices, body(): lax.ppermute(high, 'tile', [(i, (i + 1) % tiles) for i in range(tiles)])  1.63 us
  transfers between devices with their start and end apart: 12, of which 5 were waited for; matrix products, arithmetic and copies ran while one was open for 0% of the time, Pallas kernels for 38%

commit v1 on v0

--- a/solution.py
+++ b/solution.py
@@ -36,10 +36,10 @@
 
 def exchange(blocks):
     groups = len(blocks)
-    out = [blocks[0]]
-    for k in range(1, groups):
+    out = list(blocks)
+    for k in sorted(range(1, groups), key=lambda k: (-(k // 2).bit_count(), k == 1, k)):
         pairs = [(i, i ^ k if groups & (groups - 1) == 0 else (i + k) % groups) for i in range(groups)]
-        out.append(lax.ppermute(blocks[k], "mem", pairs))
+        out[k] = lax.ppermute(blocks[k], "mem", pairs)
     return out
 
 
@@ -52,8 +52,13 @@
     return out
 
 
-def dot(a, b):
-    return jnp.dot(a, b, precision=lax.Precision.HIGH, preferred_element_type=jnp.float32)
+def dot3(a, b):
+    lhs = jnp.concatenate([a[0], a[1], a[0]], axis=1)
+    rhs = jnp.concatenate([b[0], b[0], b[1]], axis=0)
+    middle = lhs.shape[0] // 2
+    upper = jnp.dot(lhs[:middle], rhs, preferred_element_type=jnp.float32)
+    lower = jnp.dot(lhs[middle:], rhs, preferred_element_type=jnp.float32)
+    return jnp.concatenate([upper, lower], axis=0)
 
 
 def square_by_rows(parts):
@@ -83,9 +88,11 @@
     return [pl.ds(first, rows) for first in range(0, members, rows)]
 
 
-def inner_kernel(state_ref, diff_ref, adv_ref, out_ref, low_ref, high_ref, held_ref, num_ref, edge_ref, made_ref, sems):
-    members, columns, entries = state_ref.shape
-    groups, half, _, _ = out_ref.shape
+def inner_kernel(me_ref, state_ref, diff_ref, adv_ref, *refs):
+    *outs, low_ref, high_ref, held_ref, num_ref, edge_ref, made_ref, sems = refs
+    members, columns, _ = state_ref.shape
+    groups = len(outs)
+    half = outs[0].shape[0]
     quarter = columns // 4
     pieces = pieces_of(members)
     count = len(pieces)
@@ -98,22 +105,21 @@
     reads[count + 1].wait()
     diffusion = num_ref[0:1][None]
     advection = num_ref[1:2][None]
-    writes = []
     for i, part in enumerate(pieces):
         reads[i].wait()
         x = jnp.swapaxes(held_ref[part], 0, 1)
         edge_ref[0, :, part] = x[:2]
         edge_ref[1, :, part] = x[columns - 2 :]
         x = x[quarter - 2 : columns - quarter + 2]
-        x = stencil(stencil(x, diffusion, advection), diffusion, advection)
-        made_ref[:, :, part] = x.reshape(groups, half, part.size, entries)
-        copy = pltpu.make_async_copy(made_ref.at[:, :, part], out_ref.at[:, :, part], sems.at[count + 2 + i])
+        made_ref[:, part] = stencil(stencil(x, diffusion, advection), diffusion, advection)
+    writes = []
+    for k in range(groups):
+        block = made_ref.at[pl.ds(target(me_ref[0], k, groups) * half, half)]
+        writes.append(pltpu.make_async_copy(block, outs[k], sems.at[count + 2 + k]))
+    for i, ref in enumerate((low_ref, high_ref)):
+        writes.append(pltpu.make_async_copy(edge_ref.at[i], ref, sems.at[count + 2 + groups + i]))
+    for copy in writes:
         copy.start()
-        writes.append(copy)
-    for i, ref in enumerate((low_ref, high_ref)):
-        copy = pltpu.make_async_copy(edge_ref.at[i], ref, sems.at[2 * count + 2 + i])
-        copy.start()
-        writes.append(copy)
     for copy in writes:
         copy.wait()
 
@@ -177,23 +183,17 @@
         out_ref[c, 1:2] = sums[3:4] + (sums[4:5] + sums[5:6])
 
 
-def analyse_kernel(first, me_ref, after_ref, obs_ref, states_ref, *refs):
+def analyse_kernel(first, me_ref, after_ref, obs_ref, states, outs, done_ref):
     del after_ref
-    *outs, done_ref, root_ref, ahead_ref = refs
     done_ref[...] = jnp.zeros_like(done_ref)
-    groups = states_ref.shape[0]
-    if len(outs) == 1:
-        states = [states_ref.at[k] for k in range(groups)]
-        outs = [outs[0].at[k] for k in range(groups)]
-    else:
-        states = [states_ref.at[target(me_ref[0], k, groups)] for k in range(groups)]
-    columns, local, entries = states[0].shape
+    groups = len(outs)
+    columns, local, entries = outs[0].shape
     members = groups * local
     spread = members - 1.0
     every = range(columns)
     rows = lax.broadcasted_iota(jnp.int32, (members, members), 0)
     cols = lax.broadcasted_iota(jnp.int32, (members, members), 1)
-    means, forces, scales, grams = [], [], [], []
+    means, forces, scales, grams, ahead, root = [], [], [], [], [], []
     for c in every:
         x = jnp.concatenate([ref[c] for ref in states], axis=0)
         mean = jnp.sum(x, axis=0, keepdims=True) * (1.0 / members)
@@ -201,31 +201,26 @@
         total = obs_ref[first + c, 0:1]
         forces.append(obs_ref[first + c, 1:2] - total * mean)
         means.append(mean)
-        ahead_ref[c] = anomaly
+        ahead.append(anomaly)
         grams.append(square_by_rows(split(anomaly * jnp.sqrt(total), 3)))
     for c in every:
         gram = grams[c] + jnp.where(rows == cols, spread, 0.0)
         norm = jnp.sum(jnp.sum(gram * gram, axis=0, keepdims=True), axis=1, keepdims=True)
         scales.append(jnp.sqrt(norm))
-        root_ref[c] = gram * (1.0 / scales[c])
-
-    def factors():
-        p = [dot(root_ref[c], root_ref[c]) for c in every]
-        cubic = [dot(0.0625 * p[c] - 0.5625 * root_ref[c], p[c]) for c in every]
-        return [1.6875 * p[c] - 2.4375 * root_ref[c] + cubic[c] for c in every]
-
-    def pair(step, carry):
-        r = factors()
-        t = [2.25 * root_ref[c] + dot(r[c], root_ref[c]) for c in every]
-        for c in every:
-            ahead_ref[c] = 2.25 * ahead_ref[c] + dot(r[c], ahead_ref[c])
-        for c in every:
-            root_ref[c] = 2.25 * t[c] + dot(t[c], r[c])
-        return carry
-
-    lax.fori_loop(0, PAIRS - 1, pair, 0)
-    r = factors()
-    ahead = [2.25 * ahead_ref[c] + dot(r[c], ahead_ref[c]) for c in every]
+        root.append(gram * (1.0 / scales[c]))
+
+    r = None
+    for step in range(PAIRS):
+        s = [split(root[c], 2) for c in every]
+        p = [dot3(s[c], s[c]) for c in every]
+        if r is not None:
+            ahead = [2.25 * ahead[c] + dot3(r[c], split(ahead[c], 2)) for c in every]
+        cubic = [dot3(split(0.0625 * p[c] - 0.5625 * root[c], 2), split(p[c], 2)) for c in every]
+        r = [split(1.6875 * p[c] - 2.4375 * root[c] + cubic[c], 2) for c in every]
+        if step < PAIRS - 1:
+            t = [2.25 * root[c] + dot3(r[c], s[c]) for c in every]
+            root = [2.25 * t[c] + dot3(split(t[c], 2), r[c]) for c in every]
+    ahead = [2.25 * ahead[c] + dot3(r[c], split(ahead[c], 2)) for c in every]
     for c in every:
         w = ahead[c]
         inner = jnp.sum(w * forces[c], axis=1, keepdims=True)
@@ -236,25 +231,30 @@
 
 
 def analyse(states, obs, first, me, after, apart):
-    groups, columns, local, entries = states.shape
+    groups = len(states)
+    columns, local, entries = states[0].shape
     members = groups * local
-    whole = jax.ShapeDtypeStruct(states.shape, jnp.float32)
+    block = jax.ShapeDtypeStruct((columns, local, entries), jnp.float32)
+    whole = jax.ShapeDtypeStruct((groups, columns, local, entries), jnp.float32)
     token = jax.ShapeDtypeStruct(after.shape, jnp.float32)
 
-    def kernel(*refs):
-        analyse_kernel(first, *refs)
-
+    def kernel(me_ref, after_ref, obs_ref, *refs):
+        if apart:
+            states_ref, *outs, done_ref = refs
+            ins = [states_ref.at[target(me_ref[0], k, groups)] for k in range(groups)]
+        else:
+            *ins, out_ref, done_ref = refs
+            outs = [out_ref.at[source(me_ref[0], k, groups)] for k in range(groups)]
+        analyse_kernel(first, me_ref, after_ref, obs_ref, ins, outs, done_ref)
+
+    operands = [states] if apart else states
     return call(
         kernel,
-        ([jax.ShapeDtypeStruct(states.shape[1:], jnp.float32)] * groups if apart else [whole]) + [token],
+        [block] * groups + [token] if apart else [whole, token],
         columns * 90 * 2 * members * members * entries,
         8 * columns * members * entries,
-        in_specs=[SMEM, VMEM, VMEM, VMEM],
-        scratch_shapes=[
-            pltpu.VMEM((columns, members, members), jnp.float32),
-            pltpu.VMEM((columns, members, entries), jnp.float32),
-        ],
-    )(me, after, obs, states)
+        in_specs=[SMEM] + [VMEM] * (len(operands) + 2),
+    )(me, after, obs, *operands)
 
 
 def body(background, diffusion, advection, obs_where, obs_count, obs_value, obs_rinv):
@@ -268,23 +268,23 @@
     me = lax.axis_index("mem")[None].astype(jnp.int32)
     pieces = len(pieces_of(local))
 
-    inner, low, high = call(
+    *inner, low, high = call(
         inner_kernel,
-        [jax.ShapeDtypeStruct((groups, *block), jnp.float32), edge, edge],
+        [jax.ShapeDtypeStruct(block, jnp.float32)] * groups + [edge, edge],
         20 * size,
         8 * size,
         vmem=60 * MIB,
-        in_specs=[HBM, HBM, HBM],
-        out_specs=[HBM, HBM, HBM],
+        in_specs=[SMEM, HBM, HBM, HBM],
+        out_specs=[HBM] * (groups + 2),
         scratch_shapes=[
             pltpu.VMEM(background.shape, jnp.float32),
             pltpu.VMEM((8, entries), jnp.float32),
             pltpu.VMEM((2, 2, local, entries), jnp.float32),
-            pltpu.VMEM((groups, *block), jnp.float32),
-            pltpu.SemaphoreType.DMA((2 * pieces + 4,)),
+            pltpu.VMEM((groups * half, local, entries), jnp.float32),
+            pltpu.SemaphoreType.DMA((pieces + groups + 4,)),
         ],
-    )(background, diffusion, advection)
-    inner = lax.all_to_all(inner, "mem", split_axis=0, concat_axis=0, tiled=True)
+    )(me, background, diffusion, advection)
+    inner = exchange(inner)
     before = lax.ppermute(high, "tile", [(i, (i + 1) % tiles) for i in range(tiles)])
     after = lax.ppermute(low, "tile", [((i + 1) % tiles, i) for i in range(tiles)])
     obs = call(

time: 58.2 us -> 58.7 us (level)
  Pallas kernels: 25.5 us -> 22.4 us
  local copies, waits for them, and re-layouts: 1.36 us -> 3.86 us
  starting transfers between devices: 23.5 us -> 25.5 us
  waiting for transfers between devices: 7.31 us -> 6.2 us
    ppermute x7 -> x14, starting transfers between devices: 6.68 us -> 14 us  [exchange(): out[k] = lax.ppermute(blocks[k], 'mem', pairs)]
    all_to_all x2 -> x1, starting transfers between devices: 9.45 us -> 3.68 us  [body(): lax.all_to_all(inner, 'mem', split_axis=0, concat_axis=0, tiled=True)]
    pallas_call x3, Pallas kernels: 22.2 us -> 19.1 us  [the longest x2 16.6 us: analyse(): call(kernel, [block] * groups + [token] if apart else [whole, token], col...]
    unnamed x18 -> x22, local copies, waits for them, and re-layouts: 1.35 us -> 3.86 us
    all_to_all x1, waiting for transfers between devices: 0.01 us -> 1.17 us  [body(): lax.all_to_all(outer, 'mem', split_axis=0, concat_axis=0, tiled=True)]
    ppermute x1, waiting for transfers between devices: 1.02 us -> 0.01 us  [body(): lax.ppermute(high, 'tile', [(i, (i + 1) % tiles) for i in range(tiles)])]
    ppermute x1, waiting for transfers between devices: 0.69 us -> 0.01 us  [body(): lax.ppermute(low, 'tile', [((i + 1) % tiles, i) for i in range(tiles)])]
    all_to_all x2 -> x1, waiting for transfers between devices: 0.59 us -> 0.01 us  [body(): lax.all_to_all(inner, 'mem', split_axis=0, concat_axis=0, tiled=True)]
  transfers between devices with their start and end apart: 12 -> 18, of which waited for: 5 -> 3; matrix products, arithmetic and copies ran while one was open for 0% -> 0% of each run, Pallas kernels for 38% -> 32%
where the time goes in v1:
time: 58.7 us; the launch traced here: 58.2 us
  starting transfers between devices  25.5 us (43%)
  Pallas kernels  22.4 us (38%)
  waiting for transfers between devices  6.2 us (11%)
  local copies, waits for them, and re-layouts  3.86 us (7%)
    pallas_call x2, Pallas kernels, analyse(): call(kernel, [block] * groups + [token] if apart else [whole, token], col...  16.6 us
    ppermute x14, starting transfers between devices, exchange(): out[k] = lax.ppermute(blocks[k], 'mem', pairs)  14 us
    ppermute x14, waiting for transfers between devices, exchange(): out[k] = lax.ppermute(blocks[k], 'mem', pairs)  5.03 us
    all_to_all x1, starting transfers between devices, body(): lax.all_to_all(outer, 'mem', split_axis=0, concat_axis=0, tiled=True)  4.04 us
    unnamed x22, local copies, waits for them, and re-layouts  3.86 us
    all_to_all x1, starting transfers between devices, body(): lax.all_to_all(inner, 'mem', split_axis=0, concat_axis=0, tiled=True)  3.68 us
    pallas_call x1, Pallas kernels, body(): call(inner_kernel, [jax.ShapeDtypeStruct(block, jnp.float32)] * groups +...  2.53 us
    ppermute x1, starting transfers between devices, body(): lax.ppermute(low, 'tile', [((i + 1) % tiles, i) for i in range(tiles)])  2.25 us
  transfers between devices with their start and end apart: 18, of which 3 were waited for; matrix products, arithmetic and copies ran while one was open for 0% of the time, Pallas kernels for 32%

profile of v1, /device:TPU:0, one launch (start us, length us, event | category | flops | bytes accessed | tf_op | source)
XLA Modules:
  0.0 58.2 jit_solution(15898878793825896165)
XLA Ops:
  0.0 2.5 %shard_map.74 = (f32[2,32,256]{2,1,0:T(8,128)}, f32[2,32,256]{2,1,0:T(8,128)}, f32[2,32,256]{2,1,0:T(8,128)}, f32[2,32,256]{2,1,0:T(8,128)}, f32[2,32,256]{2,1,0...) custom-call(s32[1]{0:T(128)} %bitcast.me_ref, ...), custom_call_target="tpu_custom_call" | custom-call | flops 5242880 | bytes 2097152 | tf_op jit(solution)/shard_map/pallas_call | solution.py:271
  2.5 0.5 collective-permute-start
  3.1 2.6 %collective-permute-start.1 = (f32[2,32,256]{2,1,0:T(8,128)}, f32[2,32,256]{2,1,0:T(8,128)S(1)}, u32[]{:S(2)}, u32[]{:S(2)}) collective-permute-start(f32[2,32,256]{2,1,0:T(8,128)} %get-tuple-element.27), channel_id=1, source_target_pairs={{0,8},{4,12},{8,0},{12,4},{16,24},{20,28},{24,16},{28,20},{1,9},{5... | collective-permute-start | bytes 196616 | tf_op jit(solution)/shard_map/ppermute | solution.py:42
  5.6 1.6 %collective-permute-start.7 = (f32[2,32,256]{2,1,0:T(8,128)}, f32[2,32,256]{2,1,0:T(8,128)S(1)}, u32[]{:S(2)}, u32[]{:S(2)}) collective-permute-start(f32[2,32,256]{2,1,0:T(8,128)} %get-tuple-element.35), channel_id=1, source_target_pairs={{0,1},{1,2},{2,3},{3,0},{4,5},{5,6},{6,7},{7,4},{8,9},{9,10},{10,1... | collective-permute-start | bytes 196616 | tf_op jit(solution)/shard_map/ppermute | solution.py:288
  7.2 2.2 %collective-permute-start.8 = (f32[2,32,256]{2,1,0:T(8,128)}, f32[2,32,256]{2,1,0:T(8,128)S(1)}, u32[]{:S(2)}, u32[]{:S(2)}) collective-permute-start(f32[2,32,256]{2,1,0:T(8,128)} %get-tuple-element.36), channel_id=1, source_target_pairs={{1,0},{2,1},{3,2},{0,3},{5,4},{6,5},{7,6},{4,7},{9,8},{10,9},{11,1... | collective-permute-start | bytes 196616 | tf_op jit(solution)/shard_map/ppermute | solution.py:289
  9.4 0.0 collective-permute-start.2
  9.5 0.7 %copy-done.6 = s32[1,32]{1,0:T(1,128)S(1)} copy-done((s32[1,32]{1,0:T(1,128)S(1)}, s32[1,32]{1,0:T(1,128)}, u32[]{:S(2)}) %copy-start.6) | copy-done | bytes 152
  10.1 0.8 %copy-done.1 = s32[1,32,512]{2,1,0:T(8,128)S(1)} copy-done((s32[1,32,512]{2,1,0:T(8,128)S(1)}, s32[1,32,512]{2,1,0:T(8,128)}, u32[]{:S(2)}) %copy-start.1) | copy-done | bytes 65560
  10.9 0.8 %copy-done.2 = f32[1,32,512]{2,1,0:T(8,128)S(1)} copy-done((f32[1,32,512]{2,1,0:T(8,128)S(1)}, f32[1,32,512]{2,1,0:T(8,128)}, u32[]{:S(2)}) %copy-start.2) | copy-done | bytes 65560
  11.8 0.8 %copy-done.3 = f32[1,32,512]{2,1,0:T(8,128)S(1)} copy-done((f32[1,32,512]{2,1,0:T(8,128)S(1)}, f32[1,32,512]{2,1,0:T(8,128)}, u32[]{:S(2)}) %copy-start.3) | copy-done | bytes 65560
  12.6 0.9 %shard_map.73.obs_ref = f32[4,8,256]{2,1,0:T(8,128)S(1)} custom-call(s32[1]{0:T(128)} %bitcast.me_ref, s32[1,32]{1,0:T(1,128)S(1)} %copy-done.6, s32[32,512]{1,0:T(8,128)S(1)} %bitcast.8, f32[32,512]{1,0:T(8,128)S(1)} %bitcast.9, f32[32,512]{1,0:T(8,128)S(1)} %bitcast.10), custom_call_target="tpu_custom_call" | custom-call | flops 16777216 | bytes 196608 | tf_op jit(solution)/shard_map/pallas_call | solution.py:290
  13.6 0.0 collective-permute-done.refs_1_
  13.6 1.6 %collective-permute-start.3 = (f32[2,32,256]{2,1,0:T(8,128)}, f32[2,32,256]{2,1,0:T(8,128)S(1)}, u32[]{:S(2)}, u32[]{:S(2)}) collective-permute-start(f32[2,32,256]{2,1,0:T(8,128)} %get-tuple-element.29), channel_id=1, source_target_pairs={{0,16},{4,20},{8,24},{12,28},{16,0},{20,4},{24,8},{28,12},{1,17},{... | collective-permute-start | bytes 196616 | tf_op jit(solution)/shard_map/ppermute | solution.py:42
  15.2 0.0 collective-permute-done.1.refs_2_
  15.2 0.3 collective-permute-start.4
  15.5 0.0 collective-permute-done.7.before_ref
  15.5 2.6 %collective-permute-start.5 = (f32[2,32,256]{2,1,0:T(8,128)S(1)}, f32[2,32,256]{2,1,0:T(8,128)S(1)}, u32[]{:S(2)}, u32[]{:S(2)}) collective-permute-start(f32[2,32,256]{2,1,0:T(8,128)S(1)} %copy-done.9), channel_id=1, source_target_pairs={{0,24},{4,28},{8,16},{12,20},{16,8},{20,12},{24,0},{28,4},{1,25},{... | collective-permute-start | bytes 196616 | tf_op jit(solution)/shard_map/ppermute | solution.py:42
  18.1 0.0 collective-permute-done.8.after_ref
  18.1 0.0 collective-permute-start.6
  18.1 0.0 copy-start.5
  18.1 0.0 copy-start.4
  18.2 0.6 %copy-done.5 = f32[256]{0:T(256)S(1)} copy-done((f32[256]{0:T(256)S(1)}, f32[256]{0:T(256)}, u32[]{:S(2)}) %copy-start.5) | copy-done | bytes 1048
  18.8 0.0 copy-done.4
  18.8 1.3 %shard_map.76 = f32[8,2,32,256]{3,2,1,0:T(8,128)} custom-call(f32[4,8,256]{2,1,0:T(8,128)S(1)} %shard_map.73.obs_ref, f32[32,32,256]{2,1,0:T(8,128)S(1)} %copy-done, f32[2,32,256]{2,1,0:T(8,128)S(1)} %collective-permute-done.7.before_ref, f32[2,32,256]{2,1,0:T(8,128)S(1)} %collective-permute-done.8.after_ref, f32[1,256]{1,0:T(1,128)S(1)} %bitcast.11, ...), custom_call_target="tpu_custom_call" | custom-call | flops 5242880 | bytes 2097152 | tf_op jit(solution)/shard_map/pallas_call | solution.py:297
  20.1 4.0 %all-to-all-start.1 = ((f32[8,2,32,256]{3,2,1,0:T(8,128)}), f32[8,2,32,256]{3,2,1,0:T(8,128)S(1)}, u32[]{:S(2)}, u32[]{:S(2)}) async-start(f32[8,2,32,256]{3,2,1,0:T(8,128)} %shard_map.76), calls=%async_computation.1 | async-start | bytes 1048576 | tf_op jit(solution)/shard_map/all_to_all | solution.py:305
  24.1 0.0 collective-permute-done.2.refs_3_
  24.1 0.0 collective-permute-done.3.refs_4_
  24.1 0.0 collective-permute-done.4.refs_5_
  24.2 0.0 collective-permute-done.5.refs_6_
  24.2 0.0 collective-permute-done.6.refs_7_
  24.2 8.5 %shard_map.75 = (f32[8,2,32,256]{3,2,1,0:T(8,128)}, f32[8,256]{1,0:T(8,128)S(1)}) custom-call(s32[1]{0:T(128)} %bitcast.me_ref, f32[8,256]{1,0:T(8,128)S(1)} %slice_bitcast_fusion.after_ref, f32[4,8,256]{2,1,0:T(8,128)S(1)} %shard_map.73.obs_ref, f32[2,32,256]{2,1,0:T(8,128)S(1)} %copy-done.7, f32[2,32,256]{2,1,0:T(8,128)S(1)} %collective-permute-done.refs_1_, ...), custom_call_target="tpu_custom_call" | custom-call | flops 6039797760 | bytes 1048576 | tf_op jit(solution)/shard_map/pallas_call | solution.py:251
  32.7 1.2 %all-to-all-done.1.refs_0_ = f32[8,2,32,256]{3,2,1,0:T(8,128)S(1)} async-done(((f32[8,2,32,256]{3,2,1,0:T(8,128)}), f32[8,2,32,256]{3,2,1,0:T(8,128)S(1)}, u32[]{:S(2)}, u32[]{:S(2)}) %all-to-all-start.1) | async-done | bytes 524320 | tf_op jit(solution)/shard_map/all_to_all | solution.py:305
  33.9 3.7 %all-to-all-start = ((f32[8,2,32,256]{3,2,1,0:T(8,128)}), f32[8,2,32,256]{3,2,1,0:T(8,128)S(1)}, u32[]{:S(2)}, u32[]{:S(2)}) async-start(f32[8,2,32,256]{3,2,1,0:T(8,128)} %get-tuple-element.33), calls=%async_computation | async-start | bytes 1048576 | tf_op jit(solution)/shard_map/all_to_all | solution.py:308
  37.6 8.1 %shard_map.77 = (f32[2,32,256]{2,1,0:T(8,128)S(1)}, f32[2,32,256]{2,1,0:T(8,128)S(1)}, f32[2,32,256]{2,1,0:T(8,128)S(1)}, f32[2,32,256]{2,1,0:T(8,128)S(1)}, f32...) custom-call(s32[1]{0:T(128)} %bitcast.me_ref, ...), custom_call_target="tpu_custom_call" | custom-call | flops 6039797760 | bytes 1048576 | tf_op jit(solution)/shard_map/pallas_call | solution.py:251
  45.6 0.2 collective-permute-start.9
  45.8 1.7 %collective-permute-start.10 = (f32[2,32,256]{2,1,0:T(8,128)S(1)}, f32[2,32,256]{2,1,0:T(8,128)S(1)}, u32[]{:S(2)}, u32[]{:S(2)}) collective-permute-start(f32[2,32,256]{2,1,0:T(8,128)S(1)} %get-tuple-element.39), channel_id=1, source_target_pairs={{0,8},{4,12},{8,0},{12,4},{16,24},{20,28},{24,16},{28,20},{1,9},{5... | collective-permute-start | bytes 196616 | tf_op jit(solution)/shard_map/ppermute | solution.py:42
  47.5 0.0 collective-permute-start.11
  47.5 1.7 %collective-permute-start.12 = (f32[2,32,256]{2,1,0:T(8,128)S(1)}, f32[2,32,256]{2,1,0:T(8,128)S(1)}, u32[]{:S(2)}, u32[]{:S(2)}) collective-permute-start(f32[2,32,256]{2,1,0:T(8,128)S(1)} %get-tuple-element.41), channel_id=1, source_target_pairs={{0,16},{4,20},{8,24},{12,28},{16,0},{20,4},{24,8},{28,12},{1,17},{... | collective-permute-start | bytes 196616 | tf_op jit(solution)/shard_map/ppermute | solution.py:42
  49.2 0.1 collective-permute-start.13
  49.3 0.0 collective-permute-done.9.refs_1_
  49.3 2.6 %collective-permute-start.14 = (f32[2,32,256]{2,1,0:T(8,128)S(1)}, f32[2,32,256]{2,1,0:T(8,128)S(1)}, u32[]{:S(2)}, u32[]{:S(2)}) collective-permute-start(f32[2,32,256]{2,1,0:T(8,128)S(1)} %get-tuple-element.43), channel_id=1, source_target_pairs={{0,24},{4,28},{8,16},{12,20},{16,8},{20,12},{24,0},{28,4},{1,25},{... | collective-permute-start | bytes 196616 | tf_op jit(solution)/shard_map/ppermute | solution.py:42
  51.9 0.0 collective-permute-done.10.refs_2_
  51.9 0.0 collective-permute-start.15
  52.0 0.0 collective-permute-done.12.refs_4_
  52.0 2.7 %collective-permute-done.13.refs_5_ = f32[2,32,256]{2,1,0:T(8,128)S(1)} collective-permute-done((f32[2,32,256]{2,1,0:T(8,128)S(1)}, f32[2,32,256]{2,1,0:T(8,128)S(1)}, u32[]{:S(2)}, u32[]{:S(2)}) %collective-permute-start.13) | collective-permute-done | bytes 65568 | tf_op jit(solution)/shard_map/ppermute | solution.py:42
  54.7 0.0 collective-permute-done.14.refs_6_
  54.7 2.3 %collective-permute-done.15.refs_7_ = f32[2,32,256]{2,1,0:T(8,128)S(1)} collective-permute-done((f32[2,32,256]{2,1,0:T(8,128)S(1)}, f32[2,32,256]{2,1,0:T(8,128)S(1)}, u32[]{:S(2)}, u32[]{:S(2)}) %collective-permute-start.15) | collective-permute-done | bytes 65568 | tf_op jit(solution)/shard_map/ppermute | solution.py:42
  57.0 1.1 %shard_map.78 = f32[32,32,256]{2,1,0:T(8,128)} custom-call(s32[1]{0:T(128)} %bitcast.me_ref, f32[8,2,32,256]{3,2,1,0:T(8,128)S(1)} %all-to-all-done.inner_ref, f32[2,32,256]{2,1,0:T(8,128)S(1)} %get-tuple-element.37.refs_0_, f32[2,32,256]{2,1,0:T(8,128)S(1)} %collective-permute-done.9.refs_1_, f32[2,32,256]{2,1,0:T(8,128)S(1)} %collective-permute-done.10.refs_2_, ...), custom_call_target="tpu_custom_call" | custom-call | flops 262144 | bytes 2097152 | tf_op jit(solution)/shard_map/pallas_call | solution.py:311
  (17 shorter events, 0.0 us)
Async XLA Ops:
  0.0 18.2 %copy-start = (f32[32,32,256]{2,1,0:T(8,128)S(1)}, f32[32,32,256]{2,1,0:T(8,128)}, u32[]{:S(2)}) copy-start(f32[32,32,256]{2,1,0:T(8,128)} %state_ref.3) | copy-start | bytes 3145732
  2.5 11.0 %collective-permute-start = (f32[2,32,256]{2,1,0:T(8,128)}, f32[2,32,256]{2,1,0:T(8,128)S(1)}, u32[]{:S(2)}, u32[]{:S(2)}) collective-permute-start(f32[2,32,256]{2,1,0:T(8,128)} %get-tuple-element.26), channel_id=1, source_target_pairs={{0,4},{4,0},{8,12},{12,8},{16,20},{20,16},{24,28},{28,24},{1,5},{5... | collective-permute-start | bytes 196616 | tf_op jit(solution)/shard_map/ppermute | solution.py:42
  3.1 12.1 %collective-permute-start.1 = (f32[2,32,256]{2,1,0:T(8,128)}, f32[2,32,256]{2,1,0:T(8,128)S(1)}, u32[]{:S(2)}, u32[]{:S(2)}) collective-permute-start(f32[2,32,256]{2,1,0:T(8,128)} %get-tuple-element.27), channel_id=1, source_target_pairs={{0,8},{4,12},{8,0},{12,4},{16,24},{20,28},{24,16},{28,20},{1,9},{5... | collective-permute-start | bytes 196616 | tf_op jit(solution)/shard_map/ppermute | solution.py:42
  5.6 9.9 %collective-permute-start.7 = (f32[2,32,256]{2,1,0:T(8,128)}, f32[2,32,256]{2,1,0:T(8,128)S(1)}, u32[]{:S(2)}, u32[]{:S(2)}) collective-permute-start(f32[2,32,256]{2,1,0:T(8,128)} %get-tuple-element.35), channel_id=1, source_target_pairs={{0,1},{1,2},{2,3},{3,0},{4,5},{5,6},{6,7},{7,4},{8,9},{9,10},{10,1... | collective-permute-start | bytes 196616 | tf_op jit(solution)/shard_map/ppermute | solution.py:288
  7.2 10.9 %collective-permute-start.8 = (f32[2,32,256]{2,1,0:T(8,128)}, f32[2,32,256]{2,1,0:T(8,128)S(1)}, u32[]{:S(2)}, u32[]{:S(2)}) collective-permute-start(f32[2,32,256]{2,1,0:T(8,128)} %get-tuple-element.36), channel_id=1, source_target_pairs={{1,0},{2,1},{3,2},{0,3},{5,4},{6,5},{7,6},{4,7},{9,8},{10,9},{11,1... | collective-permute-start | bytes 196616 | tf_op jit(solution)/shard_map/ppermute | solution.py:289
  9.4 14.7 %collective-permute-start.2 = (f32[2,32,256]{2,1,0:T(8,128)}, f32[2,32,256]{2,1,0:T(8,128)S(1)}, u32[]{:S(2)}, u32[]{:S(2)}) collective-permute-start(f32[2,32,256]{2,1,0:T(8,128)} %get-tuple-element.28), channel_id=1, source_target_pairs={{0,12},{4,8},{8,4},{12,0},{16,28},{20,24},{24,20},{28,16},{1,13},{... | collective-permute-start | bytes 196616 | tf_op jit(solution)/shard_map/ppermute | solution.py:42
  9.5 0.7 %copy-start.6 = (s32[1,32]{1,0:T(1,128)S(1)}, s32[1,32]{1,0:T(1,128)}, u32[]{:S(2)}) copy-start(s32[1,32]{1,0:T(1,128)} %count_ref.1) | copy-start | bytes 388
  10.1 0.8 %copy-start.1 = (s32[1,32,512]{2,1,0:T(8,128)S(1)}, s32[1,32,512]{2,1,0:T(8,128)}, u32[]{:S(2)}) copy-start(s32[1,32,512]{2,1,0:T(8,128)} %param.10) | copy-start | bytes 196612
  10.9 0.8 %copy-start.2 = (f32[1,32,512]{2,1,0:T(8,128)S(1)}, f32[1,32,512]{2,1,0:T(8,128)}, u32[]{:S(2)}) copy-start(f32[1,32,512]{2,1,0:T(8,128)} %param.12) | copy-start | bytes 196612
  11.8 0.8 %copy-start.3 = (f32[1,32,512]{2,1,0:T(8,128)S(1)}, f32[1,32,512]{2,1,0:T(8,128)}, u32[]{:S(2)}) copy-start(f32[1,32,512]{2,1,0:T(8,128)} %param.13) | copy-start | bytes 196612
  12.6 2.6 %copy-start.10 = (f32[2,32,256]{2,1,0:T(8,128)S(1)}, f32[2,32,256]{2,1,0:T(8,128)}, u32[]{:S(2)}) copy-start(f32[2,32,256]{2,1,0:T(8,128)} %get-tuple-element.30) | copy-start | bytes 196612
  12.6 2.9 %copy-start.9 = (f32[2,32,256]{2,1,0:T(8,128)S(1)}, f32[2,32,256]{2,1,0:T(8,128)}, u32[]{:S(2)}) copy-start(f32[2,32,256]{2,1,0:T(8,128)} %get-tuple-element.31) | copy-start | bytes 196612
  12.6 5.5 %copy-start.8 = (f32[2,32,256]{2,1,0:T(8,128)S(1)}, f32[2,32,256]{2,1,0:T(8,128)}, u32[]{:S(2)}) copy-start(f32[2,32,256]{2,1,0:T(8,128)} %get-tuple-element.32) | copy-start | bytes 196612
  13.6 10.5 %collective-permute-start.3 = (f32[2,32,256]{2,1,0:T(8,128)}, f32[2,32,256]{2,1,0:T(8,128)S(1)}, u32[]{:S(2)}, u32[]{:S(2)}) collective-permute-start(f32[2,32,256]{2,1,0:T(8,128)} %get-tuple-element.29), channel_id=1, source_target_pairs={{0,16},{4,20},{8,24},{12,28},{16,0},{20,4},{24,8},{28,12},{1,17},{... | collective-permute-start | bytes 196616 | tf_op jit(solution)/shard_map/ppermute | solution.py:42
  15.2 9.0 %collective-permute-start.4 = (f32[2,32,256]{2,1,0:T(8,128)S(1)}, f32[2,32,256]{2,1,0:T(8,128)S(1)}, u32[]{:S(2)}, u32[]{:S(2)}) collective-permute-start(f32[2,32,256]{2,1,0:T(8,128)S(1)} %copy-done.10), channel_id=1, source_target_pairs={{0,20},{4,16},{8,28},{12,24},{16,4},{20,0},{24,12},{28,8},{1,21},{... | collective-permute-start | bytes 196616 | tf_op jit(solution)/shard_map/ppermute | solution.py:42
  15.5 8.6 %collective-permute-start.5 = (f32[2,32,256]{2,1,0:T(8,128)S(1)}, f32[2,32,256]{2,1,0:T(8,128)S(1)}, u32[]{:S(2)}, u32[]{:S(2)}) collective-permute-start(f32[2,32,256]{2,1,0:T(8,128)S(1)} %copy-done.9), channel_id=1, source_target_pairs={{0,24},{4,28},{8,16},{12,20},{16,8},{20,12},{24,0},{28,4},{1,25},{... | collective-permute-start | bytes 196616 | tf_op jit(solution)/shard_map/ppermute | solution.py:42
  18.1 6.0 %collective-permute-start.6 = (f32[2,32,256]{2,1,0:T(8,128)S(1)}, f32[2,32,256]{2,1,0:T(8,128)S(1)}, u32[]{:S(2)}, u32[]{:S(2)}) collective-permute-start(f32[2,32,256]{2,1,0:T(8,128)S(1)} %copy-done.8), channel_id=1, source_target_pairs={{0,28},{4,24},{8,20},{12,16},{16,12},{20,8},{24,4},{28,0},{1,29},{... | collective-permute-start | bytes 196616 | tf_op jit(solution)/shard_map/ppermute | solution.py:42
  18.1 0.7 %copy-start.5 = (f32[256]{0:T(256)S(1)}, f32[256]{0:T(256)}, u32[]{:S(2)}) copy-start(f32[256]{0:T(256)} %adv_ref.1) | copy-start | bytes 3076
  18.1 0.7 %copy-start.4 = (f32[256]{0:T(256)S(1)}, f32[256]{0:T(256)}, u32[]{:S(2)}) copy-start(f32[256]{0:T(256)} %diff_ref.1) | copy-start | bytes 3076
  20.1 4.1 %copy-start.7 = (f32[2,32,256]{2,1,0:T(8,128)S(1)}, f32[2,32,256]{2,1,0:T(8,128)}, u32[]{:S(2)}) copy-start(f32[2,32,256]{2,1,0:T(8,128)} %get-tuple-element.25.refs_0_) | copy-start | bytes 196612
  20.1 13.8 %all-to-all-start.1 = ((f32[8,2,32,256]{3,2,1,0:T(8,128)}), f32[8,2,32,256]{3,2,1,0:T(8,128)S(1)}, u32[]{:S(2)}, u32[]{:S(2)}) async-start(f32[8,2,32,256]{3,2,1,0:T(8,128)} %shard_map.76), calls=%async_computation.1 | async-start | bytes 1048576 | tf_op jit(solution)/shard_map/all_to_all | solution.py:305
  33.9 18.1 %all-to-all-start = ((f32[8,2,32,256]{3,2,1,0:T(8,128)}), f32[8,2,32,256]{3,2,1,0:T(8,128)S(1)}, u32[]{:S(2)}, u32[]{:S(2)}) async-start(f32[8,2,32,256]{3,2,1,0:T(8,128)} %get-tuple-element.33), calls=%async_computation | async-start | bytes 1048576 | tf_op jit(solution)/shard_map/all_to_all | solution.py:308
  45.6 3.7 %collective-permute-start.9 = (f32[2,32,256]{2,1,0:T(8,128)S(1)}, f32[2,32,256]{2,1,0:T(8,128)S(1)}, u32[]{:S(2)}, u32[]{:S(2)}) collective-permute-start(f32[2,32,256]{2,1,0:T(8,128)S(1)} %get-tuple-element.38), channel_id=1, source_target_pairs={{0,4},{4,0},{8,12},{12,8},{16,20},{20,16},{24,28},{28,24},{1,5},{5... | collective-permute-start | bytes 196616 | tf_op jit(solution)/shard_map/ppermute | solution.py:42
  45.8 6.1 %collective-permute-start.10 = (f32[2,32,256]{2,1,0:T(8,128)S(1)}, f32[2,32,256]{2,1,0:T(8,128)S(1)}, u32[]{:S(2)}, u32[]{:S(2)}) collective-permute-start(f32[2,32,256]{2,1,0:T(8,128)S(1)} %get-tuple-element.39), channel_id=1, source_target_pairs={{0,8},{4,12},{8,0},{12,4},{16,24},{20,28},{24,16},{28,20},{1,9},{5... | collective-permute-start | bytes 196616 | tf_op jit(solution)/shard_map/ppermute | solution.py:42
  47.5 4.5 %collective-permute-start.11 = (f32[2,32,256]{2,1,0:T(8,128)S(1)}, f32[2,32,256]{2,1,0:T(8,128)S(1)}, u32[]{:S(2)}, u32[]{:S(2)}) collective-permute-start(f32[2,32,256]{2,1,0:T(8,128)S(1)} %get-tuple-element.40), channel_id=1, source_target_pairs={{0,12},{4,8},{8,4},{12,0},{16,28},{20,24},{24,20},{28,16},{1,13},{... | collective-permute-start | bytes 196616 | tf_op jit(solution)/shard_map/ppermute | solution.py:42
  47.5 4.5 %collective-permute-start.12 = (f32[2,32,256]{2,1,0:T(8,128)S(1)}, f32[2,32,256]{2,1,0:T(8,128)S(1)}, u32[]{:S(2)}, u32[]{:S(2)}) collective-permute-start(f32[2,32,256]{2,1,0:T(8,128)S(1)} %get-tuple-element.41), channel_id=1, source_target_pairs={{0,16},{4,20},{8,24},{12,28},{16,0},{20,4},{24,8},{28,12},{1,17},{... | collective-permute-start | bytes 196616 | tf_op jit(solution)/shard_map/ppermute | solution.py:42
  49.2 5.5 %collective-permute-start.13 = (f32[2,32,256]{2,1,0:T(8,128)S(1)}, f32[2,32,256]{2,1,0:T(8,128)S(1)}, u32[]{:S(2)}, u32[]{:S(2)}) collective-permute-start(f32[2,32,256]{2,1,0:T(8,128)S(1)} %get-tuple-element.42), channel_id=1, source_target_pairs={{0,20},{4,16},{8,28},{12,24},{16,4},{20,0},{24,12},{28,8},{1,21},{... | collective-permute-start | bytes 196616 | tf_op jit(solution)/shard_map/ppermute | solution.py:42
  49.3 5.4 %collective-permute-start.14 = (f32[2,32,256]{2,1,0:T(8,128)S(1)}, f32[2,32,256]{2,1,0:T(8,128)S(1)}, u32[]{:S(2)}, u32[]{:S(2)}) collective-permute-start(f32[2,32,256]{2,1,0:T(8,128)S(1)} %get-tuple-element.43), channel_id=1, source_target_pairs={{0,24},{4,28},{8,16},{12,20},{16,8},{20,12},{24,0},{28,4},{1,25},{... | collective-permute-start | bytes 196616 | tf_op jit(solution)/shard_map/ppermute | solution.py:42
  51.9 5.0 %collective-permute-start.15 = (f32[2,32,256]{2,1,0:T(8,128)S(1)}, f32[2,32,256]{2,1,0:T(8,128)S(1)}, u32[]{:S(2)}, u32[]{:S(2)}) collective-permute-start(f32[2,32,256]{2,1,0:T(8,128)S(1)} %get-tuple-element.44), channel_id=1, source_target_pairs={{0,28},{4,24},{8,20},{12,16},{16,12},{20,8},{24,4},{28,0},{1,29},{... | collective-permute-start | bytes 196616 | tf_op jit(solution)/shard_map/ppermute | solution.py:42

commit v2 on v1

--- a/solution.py
+++ b/solution.py
@@ -34,12 +34,16 @@
     return lax.rem(me + groups - k, groups)
 
 
+def issue_order(groups):
+    return sorted(range(1, groups), key=lambda k: (-(k // 2).bit_count(), k == 1, k)) + [0]
+
+
 def exchange(blocks):
     groups = len(blocks)
-    out = list(blocks)
-    for k in sorted(range(1, groups), key=lambda k: (-(k // 2).bit_count(), k == 1, k)):
+    out = []
+    for k in issue_order(groups):
         pairs = [(i, i ^ k if groups & (groups - 1) == 0 else (i + k) % groups) for i in range(groups)]
-        out[k] = lax.ppermute(blocks[k], "mem", pairs)
+        out.append(lax.ppermute(blocks[k], "mem", pairs) if k else blocks[0])
     return out
 
 
@@ -55,10 +59,7 @@
 def dot3(a, b):
     lhs = jnp.concatenate([a[0], a[1], a[0]], axis=1)
     rhs = jnp.concatenate([b[0], b[0], b[1]], axis=0)
-    middle = lhs.shape[0] // 2
-    upper = jnp.dot(lhs[:middle], rhs, preferred_element_type=jnp.float32)
-    lower = jnp.dot(lhs[middle:], rhs, preferred_element_type=jnp.float32)
-    return jnp.concatenate([upper, lower], axis=0)
+    return jnp.dot(lhs, rhs, preferred_element_type=jnp.float32)
 
 
 def square_by_rows(parts):
@@ -88,11 +89,9 @@
     return [pl.ds(first, rows) for first in range(0, members, rows)]
 
 
-def inner_kernel(me_ref, state_ref, diff_ref, adv_ref, *refs):
-    *outs, low_ref, high_ref, held_ref, num_ref, edge_ref, made_ref, sems = refs
-    members, columns, _ = state_ref.shape
-    groups = len(outs)
-    half = outs[0].shape[0]
+def inner_kernel(state_ref, diff_ref, adv_ref, out_ref, low_ref, high_ref, held_ref, num_ref, edge_ref, made_ref, sems):
+    members, columns, entries = state_ref.shape
+    groups, half, _, _ = out_ref.shape
     quarter = columns // 4
     pieces = pieces_of(members)
     count = len(pieces)
@@ -105,21 +104,22 @@
     reads[count + 1].wait()
     diffusion = num_ref[0:1][None]
     advection = num_ref[1:2][None]
+    writes = []
     for i, part in enumerate(pieces):
         reads[i].wait()
         x = jnp.swapaxes(held_ref[part], 0, 1)
         edge_ref[0, :, part] = x[:2]
         edge_ref[1, :, part] = x[columns - 2 :]
         x = x[quarter - 2 : columns - quarter + 2]
-        made_ref[:, part] = stencil(stencil(x, diffusion, advection), diffusion, advection)
-    writes = []
-    for k in range(groups):
-        block = made_ref.at[pl.ds(target(me_ref[0], k, groups) * half, half)]
-        writes.append(pltpu.make_async_copy(block, outs[k], sems.at[count + 2 + k]))
+        x = stencil(stencil(x, diffusion, advection), diffusion, advection)
+        made_ref[:, :, part] = x.reshape(groups, half, part.size, entries)
+        copy = pltpu.make_async_copy(made_ref.at[:, :, part], out_ref.at[:, :, part], sems.at[count + 2 + i])
+        copy.start()
+        writes.append(copy)
     for i, ref in enumerate((low_ref, high_ref)):
-        writes.append(pltpu.make_async_copy(edge_ref.at[i], ref, sems.at[count + 2 + groups + i]))
-    for copy in writes:
+        copy = pltpu.make_async_copy(edge_ref.at[i], ref, sems.at[2 * count + 2 + i])
         copy.start()
+        writes.append(copy)
     for copy in writes:
         copy.wait()
 
@@ -140,16 +140,16 @@
     out_ref[...] = jnp.concatenate([low, high], axis=0).reshape(out_ref.shape)
 
 
-def join_kernel(me_ref, inner_ref, *refs):
-    *outer, out_ref, turned_ref, made_ref, sems = refs
+def join_kernel(me_ref, *refs):
+    *outer, inner_ref, out_ref, turned_ref, made_ref, sems = refs
     members, columns, entries = out_ref.shape
     groups, half, _, _ = inner_ref.shape
     quarter = columns // 4
     writes = []
     for i, part in enumerate(pieces_of(members)):
-        for k in range(groups):
+        for k, block in zip(issue_order(groups), outer):
             place = source(me_ref[0], k, groups) * half
-            turned_ref[pl.ds(outer_start(place, quarter), half), part] = outer[k][:, part]
+            turned_ref[pl.ds(outer_start(place, quarter), half), part] = block[:, part]
         turned_ref[quarter : columns - quarter, part] = inner_ref[:, :, part].reshape(groups * half, part.size, entries)
         made_ref[part] = jnp.swapaxes(turned_ref[:, part], 0, 1)
         copy = pltpu.make_async_copy(made_ref.at[part], out_ref.at[part], sems.at[i])
@@ -183,7 +183,7 @@
         out_ref[c, 1:2] = sums[3:4] + (sums[4:5] + sums[5:6])
 
 
-def analyse_kernel(first, me_ref, after_ref, obs_ref, states, outs, done_ref):
+def analyse_kernel(first, after_ref, obs_ref, states, outs, done_ref):
     del after_ref
     done_ref[...] = jnp.zeros_like(done_ref)
     groups = len(outs)
@@ -231,30 +231,28 @@
 
 
 def analyse(states, obs, first, me, after, apart):
-    groups = len(states)
-    columns, local, entries = states[0].shape
+    groups, columns, local, entries = states.shape
     members = groups * local
     block = jax.ShapeDtypeStruct((columns, local, entries), jnp.float32)
-    whole = jax.ShapeDtypeStruct((groups, columns, local, entries), jnp.float32)
+    whole = jax.ShapeDtypeStruct(states.shape, jnp.float32)
     token = jax.ShapeDtypeStruct(after.shape, jnp.float32)
 
-    def kernel(me_ref, after_ref, obs_ref, *refs):
+    def kernel(me_ref, after_ref, obs_ref, states_ref, *refs):
+        *outs, done_ref = refs
         if apart:
-            states_ref, *outs, done_ref = refs
             ins = [states_ref.at[target(me_ref[0], k, groups)] for k in range(groups)]
         else:
-            *ins, out_ref, done_ref = refs
-            outs = [out_ref.at[source(me_ref[0], k, groups)] for k in range(groups)]
-        analyse_kernel(first, me_ref, after_ref, obs_ref, ins, outs, done_ref)
-
-    operands = [states] if apart else states
+            ins = [states_ref.at[k] for k in range(groups)]
+            outs = [outs[0].at[k] for k in range(groups)]
+        analyse_kernel(first, after_ref, obs_ref, ins, outs, done_ref)
+
     return call(
         kernel,
         [block] * groups + [token] if apart else [whole, token],
         columns * 90 * 2 * members * members * entries,
         8 * columns * members * entries,
-        in_specs=[SMEM] + [VMEM] * (len(operands) + 2),
-    )(me, after, obs, *operands)
+        in_specs=[SMEM] + [VMEM] * 3,
+    )(me, after, obs, states)
 
 
 def body(background, diffusion, advection, obs_where, obs_count, obs_value, obs_rinv):
@@ -268,23 +266,23 @@
     me = lax.axis_index("mem")[None].astype(jnp.int32)
     pieces = len(pieces_of(local))
 
-    *inner, low, high = call(
+    inner, low, high = call(
         inner_kernel,
-        [jax.ShapeDtypeStruct(block, jnp.float32)] * groups + [edge, edge],
+        [jax.ShapeDtypeStruct((groups, *block), jnp.float32), edge, edge],
         20 * size,
         8 * size,
         vmem=60 * MIB,
-        in_specs=[SMEM, HBM, HBM, HBM],
-        out_specs=[HBM] * (groups + 2),
+        in_specs=[HBM, HBM, HBM],
+        out_specs=[HBM, HBM, HBM],
         scratch_shapes=[
             pltpu.VMEM(background.shape, jnp.float32),
             pltpu.VMEM((8, entries), jnp.float32),
             pltpu.VMEM((2, 2, local, entries), jnp.float32),
-            pltpu.VMEM((groups * half, local, entries), jnp.float32),
-            pltpu.SemaphoreType.DMA((pieces + groups + 4,)),
+            pltpu.VMEM((groups, *block), jnp.float32),
+            pltpu.SemaphoreType.DMA((2 * pieces + 4,)),
         ],
-    )(me, background, diffusion, advection)
-    inner = exchange(inner)
+    )(background, diffusion, advection)
+    inner = lax.all_to_all(inner, "mem", split_axis=0, concat_axis=0, tiled=True)
     before = lax.ppermute(high, "tile", [(i, (i + 1) % tiles) for i in range(tiles)])
     after = lax.ppermute(low, "tile", [((i + 1) % tiles, i) for i in range(tiles)])
     obs = call(
@@ -320,7 +318,7 @@
             pltpu.VMEM(background.shape, jnp.float32),
             pltpu.SemaphoreType.DMA((pieces,)),
         ],
-    )(me, inner, *outer)
+    )(me, *outer, inner)
 
 
 def solution(mesh):

time: 58.7 us -> 55.5 us (0.945)
  starting transfers between devices: 25.5 us -> 22.7 us
  local copies, waits for them, and re-layouts: 3.86 us -> 1.36 us
  waiting for transfers between devices: 6.2 us -> 7.31 us
  Pallas kernels: 22.4 us -> 23.4 us
    ppermute x14 -> x7, starting transfers between devices: 14 us -> 6.38 us  [exchange(): out.append(lax.ppermute(blocks[k], 'mem', pairs) if k else blocks[0])]
    all_to_all x1 -> x2, starting transfers between devices: 3.68 us -> 8.99 us  [body(): lax.all_to_all(inner, 'mem', split_axis=0, concat_axis=0, tiled=True)]
    unnamed x22 -> x18, local copies, waits for them, and re-layouts: 3.86 us -> 1.35 us
    pallas_call x2, Pallas kernels: 16.6 us -> 17.7 us  [analyse(): call(kernel, [block] * groups + [token] if apart else [whole, token], col...]
    ppermute x1, waiting for transfers between devices: 0.01 us -> 1.02 us  [body(): lax.ppermute(high, 'tile', [(i, (i + 1) % tiles) for i in range(tiles)])]
    ppermute x1, waiting for transfers between devices: 0.01 us -> 0.69 us  [body(): lax.ppermute(low, 'tile', [((i + 1) % tiles, i) for i in range(tiles)])]
    all_to_all x1, waiting for transfers between devices: 1.17 us -> 0.57 us  [body(): lax.all_to_all(outer, 'mem', split_axis=0, concat_axis=0, tiled=True)]
    ppermute x14 -> x7, waiting for transfers between devices: 5.03 us -> 4.44 us  [exchange(): out.append(lax.ppermute(blocks[k], 'mem', pairs) if k else blocks[0])]
  transfers between devices with their start and end apart: 18 -> 12, of which waited for: 3 -> 8; matrix products, arithmetic and copies ran while one was open for 0% -> 0% of each run, Pallas kernels for 32% -> 36%
where the time goes in v2:
time: 55.5 us; the launch traced here: 55.1 us
  Pallas kernels  23.4 us (42%)
  starting transfers between devices  22.7 us (41%)
  waiting for transfers between devices  7.31 us (13%)
  local copies, waits for them, and re-layouts  1.36 us (2%)
    pallas_call x2, Pallas kernels, analyse(): call(kernel, [block] * groups + [token] if apart else [whole, token], col...  17.7 us
    all_to_all x2, starting transfers between devices, body(): lax.all_to_all(inner, 'mem', split_axis=0, concat_axis=0, tiled=True)  8.99 us
    ppermute x7, starting transfers between devices, exchange(): out.append(lax.ppermute(blocks[k], 'mem', pairs) if k else blocks[0])  6.38 us
    ppermute x7, waiting for transfers between devices, exchange(): out.append(lax.ppermute(blocks[k], 'mem', pairs) if k else blocks[0])  4.44 us
    all_to_all x1, starting transfers between devices, body(): lax.all_to_all(outer, 'mem', split_axis=0, concat_axis=0, tiled=True)  3.49 us
    pallas_call x1, Pallas kernels, body(): call(inner_kernel, [jax.ShapeDtypeStruct((groups, *block), jnp.float32),...  2.35 us
    ppermute x1, starting transfers between devices, body(): lax.ppermute(low, 'tile', [((i + 1) % tiles, i) for i in range(tiles)])  2.25 us
    ppermute x1, starting transfers between devices, body(): lax.ppermute(high, 'tile', [(i, (i + 1) % tiles) for i in range(tiles)])  1.63 us
  transfers between devices with their start and end apart: 12, of which 8 were waited for; matrix products, arithmetic and copies ran while one was open for 0% of the time, Pallas kernels for 36%

profile of v2, /device:TPU:0, one launch (start us, length us, event | category | flops | bytes accessed | tf_op | source)
XLA Modules:
  0.0 55.1 jit_solution(250823317489535804)
XLA Ops:
  0.0 0.0 copy-start
  0.0 2.4 %shard_map.74 = (f32[8,2,32,256]{3,2,1,0:T(8,128)}, f32[2,32,256]{2,1,0:T(8,128)}, f32[2,32,256]{2,1,0:T(8,128)}) custom-call(f32[32,32,256]{2,1,0:T(8,128)} %state_ref.3, f32[256]{0:T(256)} %diff_ref.1, f32[256]{0:T(256)} %adv_ref.1), custom_call_target="tpu_custom_call" | custom-call | flops 5242880 | bytes 2097152 | tf_op jit(solution)/shard_map/pallas_call | solution.py:269
  2.4 0.0 copy-start.8
  2.4 0.0 copy-start.7
  2.4 0.0 copy-start.1
  2.4 0.0 copy-start.2
  2.4 0.0 copy-start.3
  2.4 5.3 %all-to-all-start = ((f32[8,2,32,256]{3,2,1,0:T(8,128)}), f32[8,2,32,256]{3,2,1,0:T(8,128)S(1)}, u32[]{:S(2)}, u32[]{:S(2)}) async-start(f32[8,2,32,256]{3,2,1,0:T(8,128)} %get-tuple-element.18), calls=%async_computation | async-start | bytes 1048576 | tf_op jit(solution)/shard_map/all_to_all | solution.py:285
  7.7 0.0 copy-done.8
  7.7 1.6 %collective-permute-start = (f32[2,32,256]{2,1,0:T(8,128)S(1)}, f32[2,32,256]{2,1,0:T(8,128)S(1)}, u32[]{:S(2)}, u32[]{:S(2)}) collective-permute-start(f32[2,32,256]{2,1,0:T(8,128)S(1)} %copy-done.8), channel_id=1, source_target_pairs={{0,1},{1,2},{2,3},{3,0},{4,5},{5,6},{6,7},{7,4},{8,9},{9,10},{10,1... | collective-permute-start | bytes 196616 | tf_op jit(solution)/shard_map/ppermute | solution.py:286
  9.4 0.0 copy-done.7
  9.4 2.2 %collective-permute-start.1 = (f32[2,32,256]{2,1,0:T(8,128)S(1)}, f32[2,32,256]{2,1,0:T(8,128)S(1)}, u32[]{:S(2)}, u32[]{:S(2)}) collective-permute-start(f32[2,32,256]{2,1,0:T(8,128)S(1)} %copy-done.7), channel_id=1, source_target_pairs={{1,0},{2,1},{3,2},{0,3},{5,4},{6,5},{7,6},{4,7},{9,8},{10,9},{11,1... | collective-permute-start | bytes 196616 | tf_op jit(solution)/shard_map/ppermute | solution.py:287
  11.6 0.0 copy-start.6
  11.6 0.0 copy-done.1
  11.6 0.0 copy-done.2
  11.6 0.0 copy-done.3
  11.6 0.6 %copy-done.6 = s32[1,32]{1,0:T(1,128)S(1)} copy-done((s32[1,32]{1,0:T(1,128)S(1)}, s32[1,32]{1,0:T(1,128)}, u32[]{:S(2)}) %copy-start.6) | copy-done | bytes 152
  12.3 0.0 copy-start.5
  12.3 0.9 %shard_map.73.obs_ref = f32[4,8,256]{2,1,0:T(8,128)S(1)} custom-call(s32[1]{0:T(128)} %bitcast.me_ref, s32[1,32]{1,0:T(1,128)S(1)} %copy-done.6, s32[32,512]{1,0:T(8,128)S(1)} %bitcast.8, f32[32,512]{1,0:T(8,128)S(1)} %bitcast.9, f32[32,512]{1,0:T(8,128)S(1)} %bitcast.10), custom_call_target="tpu_custom_call" | custom-call | flops 16777216 | bytes 196608 | tf_op jit(solution)/shard_map/pallas_call | solution.py:288
  13.2 1.0 %collective-permute-done.before_ref = f32[2,32,256]{2,1,0:T(8,128)S(1)} collective-permute-done((f32[2,32,256]{2,1,0:T(8,128)S(1)}, f32[2,32,256]{2,1,0:T(8,128)S(1)}, u32[]{:S(2)}, u32[]{:S(2)}) %collective-permute-start) | collective-permute-done | bytes 65568 | tf_op jit(solution)/shard_map/ppermute | solution.py:286
  14.3 0.7 %collective-permute-done.1.after_ref = f32[2,32,256]{2,1,0:T(8,128)S(1)} collective-permute-done((f32[2,32,256]{2,1,0:T(8,128)S(1)}, f32[2,32,256]{2,1,0:T(8,128)S(1)}, u32[]{:S(2)}, u32[]{:S(2)}) %collective-permute-start.1) | collective-permute-done | bytes 65568 | tf_op jit(solution)/shard_map/ppermute | solution.py:287
  14.9 0.0 copy-start.4
  14.9 0.0 copy-done
  14.9 0.0 copy-done.5
  14.9 0.7 %copy-done.4 = f32[256]{0:T(256)S(1)} copy-done((f32[256]{0:T(256)S(1)}, f32[256]{0:T(256)}, u32[]{:S(2)}) %copy-start.4) | copy-done | bytes 1048
  15.6 1.3 %shard_map.76 = f32[8,2,32,256]{3,2,1,0:T(8,128)} custom-call(f32[4,8,256]{2,1,0:T(8,128)S(1)} %shard_map.73.obs_ref, f32[32,32,256]{2,1,0:T(8,128)S(1)} %copy-done, f32[2,32,256]{2,1,0:T(8,128)S(1)} %collective-permute-done.before_ref, f32[2,32,256]{2,1,0:T(8,128)S(1)} %collective-permute-done.1.after_ref, f32[1,256]{1,0:T(1,128)S(1)} %bitcast.11, ...), custom_call_target="tpu_custom_call" | custom-call | flops 5242880 | bytes 2097152 | tf_op jit(solution)/shard_map/pallas_call | solution.py:295
  16.9 0.6 %all-to-all-done.states_ref = f32[8,2,32,256]{3,2,1,0:T(8,128)S(1)} async-done(((f32[8,2,32,256]{3,2,1,0:T(8,128)}), f32[8,2,32,256]{3,2,1,0:T(8,128)S(1)}, u32[]{:S(2)}, u32[]{:S(2)}) %all-to-all-start) | async-done | bytes 524320 | tf_op jit(solution)/shard_map/all_to_all | solution.py:285
  17.5 3.5 %all-to-all-start.1 = ((f32[8,2,32,256]{3,2,1,0:T(8,128)}), f32[8,2,32,256]{3,2,1,0:T(8,128)S(1)}, u32[]{:S(2)}, u32[]{:S(2)}) async-start(f32[8,2,32,256]{3,2,1,0:T(8,128)} %shard_map.76), calls=%async_computation.1 | async-start | bytes 1048576 | tf_op jit(solution)/shard_map/all_to_all | solution.py:303
  21.0 9.1 %shard_map.75 = (f32[8,2,32,256]{3,2,1,0:T(8,128)}, f32[8,256]{1,0:T(8,128)S(1)}) custom-call(s32[1]{0:T(128)} %bitcast.me_ref, f32[8,256]{1,0:T(8,128)S(1)} %slice_bitcast_fusion.after_ref, f32[4,8,256]{2,1,0:T(8,128)S(1)} %shard_map.73.obs_ref, f32[8,2,32,256]{3,2,1,0:T(8,128)S(1)} %all-to-all-done.states_ref), custom_call_target="tpu_custom_call" | custom-call | flops 6039797760 | bytes 1048576 | tf_op jit(solution)/shard_map/pallas_call | solution.py:249
  30.1 0.6 %all-to-all-done.1.states_ref = f32[8,2,32,256]{3,2,1,0:T(8,128)S(1)} async-done(((f32[8,2,32,256]{3,2,1,0:T(8,128)}), f32[8,2,32,256]{3,2,1,0:T(8,128)S(1)}, u32[]{:S(2)}, u32[]{:S(2)}) %all-to-all-start.1) | async-done | bytes 524320 | tf_op jit(solution)/shard_map/all_to_all | solution.py:303
  30.7 3.7 %all-to-all-start.2 = ((f32[8,2,32,256]{3,2,1,0:T(8,128)}), f32[8,2,32,256]{3,2,1,0:T(8,128)S(1)}, u32[]{:S(2)}, u32[]{:S(2)}) async-start(f32[8,2,32,256]{3,2,1,0:T(8,128)} %get-tuple-element.30), calls=%async_computation.2 | async-start | bytes 1048576 | tf_op jit(solution)/shard_map/all_to_all | solution.py:306
  34.3 8.6 %shard_map.77 = (f32[2,32,256]{2,1,0:T(8,128)S(1)}, f32[2,32,256]{2,1,0:T(8,128)S(1)}, f32[2,32,256]{2,1,0:T(8,128)S(1)}, f32[2,32,256]{2,1,0:T(8,128)S(1)}, f32...) custom-call(s32[1]{0:T(128)} %bitcast.me_ref, ...), custom_call_target="tpu_custom_call" | custom-call | flops 6039797760 | bytes 1048576 | tf_op jit(solution)/shard_map/pallas_call | solution.py:249
  43.0 2.8 %collective-permute-start.2 = (f32[2,32,256]{2,1,0:T(8,128)S(1)}, f32[2,32,256]{2,1,0:T(8,128)S(1)}, u32[]{:S(2)}, u32[]{:S(2)}) collective-permute-start(f32[2,32,256]{2,1,0:T(8,128)S(1)} %get-tuple-element.22), channel_id=1, source_target_pairs={{0,24},{4,28},{8,16},{12,20},{16,8},{20,12},{24,0},{28,4},{1,25},{... | collective-permute-start | bytes 196616 | tf_op jit(solution)/shard_map/ppermute | solution.py:46
  45.8 0.0 collective-permute-start.3
  45.8 1.5 %collective-permute-start.4 = (f32[2,32,256]{2,1,0:T(8,128)S(1)}, f32[2,32,256]{2,1,0:T(8,128)S(1)}, u32[]{:S(2)}, u32[]{:S(2)}) collective-permute-start(f32[2,32,256]{2,1,0:T(8,128)S(1)} %get-tuple-element.24), channel_id=1, source_target_pairs={{0,8},{4,12},{8,0},{12,4},{16,24},{20,28},{24,16},{28,20},{1,9},{5... | collective-permute-start | bytes 196616 | tf_op jit(solution)/shard_map/ppermute | solution.py:46
  47.3 0.3 collective-permute-start.5
  47.5 1.7 %collective-permute-start.6 = (f32[2,32,256]{2,1,0:T(8,128)S(1)}, f32[2,32,256]{2,1,0:T(8,128)S(1)}, u32[]{:S(2)}, u32[]{:S(2)}) collective-permute-start(f32[2,32,256]{2,1,0:T(8,128)S(1)} %get-tuple-element.26), channel_id=1, source_target_pairs={{0,16},{4,20},{8,24},{12,28},{16,0},{20,4},{24,8},{28,12},{1,17},{... | collective-permute-start | bytes 196616 | tf_op jit(solution)/shard_map/ppermute | solution.py:46
  49.3 0.0 collective-permute-done.2.refs_0_
  49.3 0.0 collective-permute-start.7
  49.3 1.8 %collective-permute-done.3.refs_1_ = f32[2,32,256]{2,1,0:T(8,128)S(1)} collective-permute-done((f32[2,32,256]{2,1,0:T(8,128)S(1)}, f32[2,32,256]{2,1,0:T(8,128)S(1)}, u32[]{:S(2)}, u32[]{:S(2)}) %collective-permute-start.3) | collective-permute-done | bytes 65568 | tf_op jit(solution)/shard_map/ppermute | solution.py:46
  51.1 0.1 collective-permute-start.8
  51.1 0.5 collective-permute-done.4.refs_2_
  51.6 1.3 %collective-permute-done.5.refs_3_ = f32[2,32,256]{2,1,0:T(8,128)S(1)} collective-permute-done((f32[2,32,256]{2,1,0:T(8,128)S(1)}, f32[2,32,256]{2,1,0:T(8,128)S(1)}, u32[]{:S(2)}, u32[]{:S(2)}) %collective-permute-start.5) | collective-permute-done | bytes 65568 | tf_op jit(solution)/shard_map/ppermute | solution.py:46
  52.9 0.0 collective-permute-done.6.refs_4_
  52.9 0.9 %collective-permute-done.7.refs_5_ = f32[2,32,256]{2,1,0:T(8,128)S(1)} collective-permute-done((f32[2,32,256]{2,1,0:T(8,128)S(1)}, f32[2,32,256]{2,1,0:T(8,128)S(1)}, u32[]{:S(2)}, u32[]{:S(2)}) %collective-permute-start.7) | collective-permute-done | bytes 65568 | tf_op jit(solution)/shard_map/ppermute | solution.py:46
  53.8 0.0 collective-permute-done.8.refs_6_
  53.8 0.0 all-to-all-done.2.refs_8_
  53.8 1.1 %shard_map.78 = f32[32,32,256]{2,1,0:T(8,128)} custom-call(s32[1]{0:T(128)} %bitcast.me_ref, f32[2,32,256]{2,1,0:T(8,128)S(1)} %collective-permute-done.2.refs_0_, f32[2,32,256]{2,1,0:T(8,128)S(1)} %collective-permute-done.3.refs_1_, f32[2,32,256]{2,1,0:T(8,128)S(1)} %collective-permute-done.4.refs_2_, f32[2,32,256]{2,1,0:T(8,128)S(1)} %collective-permute-done.5.refs_3_, ...), custom_call_target="tpu_custom_call" | custom-call | flops 262144 | bytes 2097152 | tf_op jit(solution)/shard_map/pallas_call | solution.py:309
  (1 shorter events, 0.0 us)
Async XLA Ops:
  0.0 14.9 %copy-start = (f32[32,32,256]{2,1,0:T(8,128)S(1)}, f32[32,32,256]{2,1,0:T(8,128)}, u32[]{:S(2)}) copy-start(f32[32,32,256]{2,1,0:T(8,128)} %state_ref.3) | copy-start | bytes 3145732
  2.4 5.4 %copy-start.8 = (f32[2,32,256]{2,1,0:T(8,128)S(1)}, f32[2,32,256]{2,1,0:T(8,128)}, u32[]{:S(2)}) copy-start(f32[2,32,256]{2,1,0:T(8,128)} %get-tuple-element.20) | copy-start | bytes 196612
  2.4 7.0 %copy-start.7 = (f32[2,32,256]{2,1,0:T(8,128)S(1)}, f32[2,32,256]{2,1,0:T(8,128)}, u32[]{:S(2)}) copy-start(f32[2,32,256]{2,1,0:T(8,128)} %get-tuple-element.21) | copy-start | bytes 196612
  2.4 9.2 %copy-start.1 = (s32[1,32,512]{2,1,0:T(8,128)S(1)}, s32[1,32,512]{2,1,0:T(8,128)}, u32[]{:S(2)}) copy-start(s32[1,32,512]{2,1,0:T(8,128)} %param.10) | copy-start | bytes 196612
  2.4 9.2 %copy-start.2 = (f32[1,32,512]{2,1,0:T(8,128)S(1)}, f32[1,32,512]{2,1,0:T(8,128)}, u32[]{:S(2)}) copy-start(f32[1,32,512]{2,1,0:T(8,128)} %param.12) | copy-start | bytes 196612
  2.4 9.2 %copy-start.3 = (f32[1,32,512]{2,1,0:T(8,128)S(1)}, f32[1,32,512]{2,1,0:T(8,128)}, u32[]{:S(2)}) copy-start(f32[1,32,512]{2,1,0:T(8,128)} %param.13) | copy-start | bytes 196612
  2.4 15.1 %all-to-all-start = ((f32[8,2,32,256]{3,2,1,0:T(8,128)}), f32[8,2,32,256]{3,2,1,0:T(8,128)S(1)}, u32[]{:S(2)}, u32[]{:S(2)}) async-start(f32[8,2,32,256]{3,2,1,0:T(8,128)} %get-tuple-element.18), calls=%async_computation | async-start | bytes 1048576 | tf_op jit(solution)/shard_map/all_to_all | solution.py:285
  7.7 6.5 %collective-permute-start = (f32[2,32,256]{2,1,0:T(8,128)S(1)}, f32[2,32,256]{2,1,0:T(8,128)S(1)}, u32[]{:S(2)}, u32[]{:S(2)}) collective-permute-start(f32[2,32,256]{2,1,0:T(8,128)S(1)} %copy-done.8), channel_id=1, source_target_pairs={{0,1},{1,2},{2,3},{3,0},{4,5},{5,6},{6,7},{7,4},{8,9},{9,10},{10,1... | collective-permute-start | bytes 196616 | tf_op jit(solution)/shard_map/ppermute | solution.py:286
  9.4 5.6 %collective-permute-start.1 = (f32[2,32,256]{2,1,0:T(8,128)S(1)}, f32[2,32,256]{2,1,0:T(8,128)S(1)}, u32[]{:S(2)}, u32[]{:S(2)}) collective-permute-start(f32[2,32,256]{2,1,0:T(8,128)S(1)} %copy-done.7), channel_id=1, source_target_pairs={{1,0},{2,1},{3,2},{0,3},{5,4},{6,5},{7,6},{4,7},{9,8},{10,9},{11,1... | collective-permute-start | bytes 196616 | tf_op jit(solution)/shard_map/ppermute | solution.py:287
  11.6 0.7 %copy-start.6 = (s32[1,32]{1,0:T(1,128)S(1)}, s32[1,32]{1,0:T(1,128)}, u32[]{:S(2)}) copy-start(s32[1,32]{1,0:T(1,128)} %count_ref.1) | copy-start | bytes 388
  12.3 2.7 %copy-start.5 = (f32[256]{0:T(256)S(1)}, f32[256]{0:T(256)}, u32[]{:S(2)}) copy-start(f32[256]{0:T(256)} %adv_ref.1) | copy-start | bytes 3076
  14.9 0.7 %copy-start.4 = (f32[256]{0:T(256)S(1)}, f32[256]{0:T(256)}, u32[]{:S(2)}) copy-start(f32[256]{0:T(256)} %diff_ref.1) | copy-start | bytes 3076
  17.5 13.2 %all-to-all-start.1 = ((f32[8,2,32,256]{3,2,1,0:T(8,128)}), f32[8,2,32,256]{3,2,1,0:T(8,128)S(1)}, u32[]{:S(2)}, u32[]{:S(2)}) async-start(f32[8,2,32,256]{3,2,1,0:T(8,128)} %shard_map.76), calls=%async_computation.1 | async-start | bytes 1048576 | tf_op jit(solution)/shard_map/all_to_all | solution.py:303
  30.7 23.1 %all-to-all-start.2 = ((f32[8,2,32,256]{3,2,1,0:T(8,128)}), f32[8,2,32,256]{3,2,1,0:T(8,128)S(1)}, u32[]{:S(2)}, u32[]{:S(2)}) async-start(f32[8,2,32,256]{3,2,1,0:T(8,128)} %get-tuple-element.30), calls=%async_computation.2 | async-start | bytes 1048576 | tf_op jit(solution)/shard_map/all_to_all | solution.py:306
  43.0 6.3 %collective-permute-start.2 = (f32[2,32,256]{2,1,0:T(8,128)S(1)}, f32[2,32,256]{2,1,0:T(8,128)S(1)}, u32[]{:S(2)}, u32[]{:S(2)}) collective-permute-start(f32[2,32,256]{2,1,0:T(8,128)S(1)} %get-tuple-element.22), channel_id=1, source_target_pairs={{0,24},{4,28},{8,16},{12,20},{16,8},{20,12},{24,0},{28,4},{1,25},{... | collective-permute-start | bytes 196616 | tf_op jit(solution)/shard_map/ppermute | solution.py:46
  45.8 5.3 %collective-permute-start.3 = (f32[2,32,256]{2,1,0:T(8,128)S(1)}, f32[2,32,256]{2,1,0:T(8,128)S(1)}, u32[]{:S(2)}, u32[]{:S(2)}) collective-permute-start(f32[2,32,256]{2,1,0:T(8,128)S(1)} %get-tuple-element.23), channel_id=1, source_target_pairs={{0,28},{4,24},{8,20},{12,16},{16,12},{20,8},{24,4},{28,0},{1,29},{... | collective-permute-start | bytes 196616 | tf_op jit(solution)/shard_map/ppermute | solution.py:46
  45.8 5.8 %collective-permute-start.4 = (f32[2,32,256]{2,1,0:T(8,128)S(1)}, f32[2,32,256]{2,1,0:T(8,128)S(1)}, u32[]{:S(2)}, u32[]{:S(2)}) collective-permute-start(f32[2,32,256]{2,1,0:T(8,128)S(1)} %get-tuple-element.24), channel_id=1, source_target_pairs={{0,8},{4,12},{8,0},{12,4},{16,24},{20,28},{24,16},{28,20},{1,9},{5... | collective-permute-start | bytes 196616 | tf_op jit(solution)/shard_map/ppermute | solution.py:46
  47.3 5.6 %collective-permute-start.5 = (f32[2,32,256]{2,1,0:T(8,128)S(1)}, f32[2,32,256]{2,1,0:T(8,128)S(1)}, u32[]{:S(2)}, u32[]{:S(2)}) collective-permute-start(f32[2,32,256]{2,1,0:T(8,128)S(1)} %get-tuple-element.25), channel_id=1, source_target_pairs={{0,12},{4,8},{8,4},{12,0},{16,28},{20,24},{24,20},{28,16},{1,13},{... | collective-permute-start | bytes 196616 | tf_op jit(solution)/shard_map/ppermute | solution.py:46
  47.5 5.4 %collective-permute-start.6 = (f32[2,32,256]{2,1,0:T(8,128)S(1)}, f32[2,32,256]{2,1,0:T(8,128)S(1)}, u32[]{:S(2)}, u32[]{:S(2)}) collective-permute-start(f32[2,32,256]{2,1,0:T(8,128)S(1)} %get-tuple-element.26), channel_id=1, source_target_pairs={{0,16},{4,20},{8,24},{12,28},{16,0},{20,4},{24,8},{28,12},{1,17},{... | collective-permute-start | bytes 196616 | tf_op jit(solution)/shard_map/ppermute | solution.py:46
  49.3 4.5 %collective-permute-start.7 = (f32[2,32,256]{2,1,0:T(8,128)S(1)}, f32[2,32,256]{2,1,0:T(8,128)S(1)}, u32[]{:S(2)}, u32[]{:S(2)}) collective-permute-start(f32[2,32,256]{2,1,0:T(8,128)S(1)} %get-tuple-element.27), channel_id=1, source_target_pairs={{0,20},{4,16},{8,28},{12,24},{16,4},{20,0},{24,12},{28,8},{1,21},{... | collective-permute-start | bytes 196616 | tf_op jit(solution)/shard_map/ppermute | solution.py:46
  51.1 2.7 %collective-permute-start.8 = (f32[2,32,256]{2,1,0:T(8,128)S(1)}, f32[2,32,256]{2,1,0:T(8,128)S(1)}, u32[]{:S(2)}, u32[]{:S(2)}) collective-permute-start(f32[2,32,256]{2,1,0:T(8,128)S(1)} %get-tuple-element.28), channel_id=1, source_target_pairs={{0,4},{4,0},{8,12},{12,8},{16,20},{20,16},{24,28},{28,24},{1,5},{5... | collective-permute-start | bytes 196616 | tf_op jit(solution)/shard_map/ppermute | solution.py:46

commit v3 on v2

--- a/solution.py
+++ b/solution.py
@@ -6,6 +6,7 @@
 from jax.sharding import PartitionSpec as P
 
 PAIRS = 6
+SCRATCH = 9
 MIB = 1024 * 1024
 SMEM = pl.BlockSpec(memory_space=pltpu.SMEM)
 VMEM = pl.BlockSpec(memory_space=pltpu.VMEM)
@@ -35,7 +36,7 @@
 
 
 def issue_order(groups):
-    return sorted(range(1, groups), key=lambda k: (-(k // 2).bit_count(), k == 1, k)) + [0]
+    return sorted(range(1, groups), key=lambda k: (k != 1, -(k // 2).bit_count(), k)) + [0]
 
 
 def exchange(blocks):
@@ -56,9 +57,14 @@
     return out
 
 
-def dot3(a, b):
-    lhs = jnp.concatenate([a[0], a[1], a[0]], axis=1)
-    rhs = jnp.concatenate([b[0], b[0], b[1]], axis=0)
+def store(ref, c, rows, x):
+    for i, part in enumerate(split(x, 2)):
+        ref[i, c, rows] = part
+
+
+def multiply(a_ref, b_ref, c, rows):
+    lhs = jnp.concatenate([a_ref[0, c, rows], a_ref[1, c, rows], a_ref[0, c, rows]], axis=1)
+    rhs = jnp.concatenate([b_ref[0, c], b_ref[0, c], b_ref[1, c]], axis=0)
     return jnp.dot(lhs, rhs, preferred_element_type=jnp.float32)
 
 
@@ -183,7 +189,7 @@
         out_ref[c, 1:2] = sums[3:4] + (sums[4:5] + sums[5:6])
 
 
-def analyse_kernel(first, after_ref, obs_ref, states, outs, done_ref):
+def analyse_kernel(first, after_ref, obs_ref, states, outs, done_ref, root, mixed, ahead, s, p, u, t, r, w):
     del after_ref
     done_ref[...] = jnp.zeros_like(done_ref)
     groups = len(outs)
@@ -191,9 +197,10 @@
     members = groups * local
     spread = members - 1.0
     every = range(columns)
+    parts = [(c, pl.ds(half, members // 2)) for c in every for half in (0, members // 2)]
     rows = lax.broadcasted_iota(jnp.int32, (members, members), 0)
     cols = lax.broadcasted_iota(jnp.int32, (members, members), 1)
-    means, forces, scales, grams, ahead, root = [], [], [], [], [], []
+    means, forces, scales, grams = [], [], [], []
     for c in every:
         x = jnp.concatenate([ref[c] for ref in states], axis=0)
         mean = jnp.sum(x, axis=0, keepdims=True) * (1.0 / members)
@@ -201,31 +208,50 @@
         total = obs_ref[first + c, 0:1]
         forces.append(obs_ref[first + c, 1:2] - total * mean)
         means.append(mean)
-        ahead.append(anomaly)
         grams.append(square_by_rows(split(anomaly * jnp.sqrt(total), 3)))
+        ahead[c] = anomaly
+        store(w.at[0], c, slice(None), anomaly)
     for c in every:
         gram = grams[c] + jnp.where(rows == cols, spread, 0.0)
         norm = jnp.sum(jnp.sum(gram * gram, axis=0, keepdims=True), axis=1, keepdims=True)
         scales.append(jnp.sqrt(norm))
-        root.append(gram * (1.0 / scales[c]))
-
-    r = None
+        gram = gram * (1.0 / scales[c])
+        root[c] = gram
+        store(s, c, slice(None), gram)
+
+    def advance(step):
+        for c, rows in parts:
+            x = 2.25 * ahead[c, rows] + multiply(r.at[step % 2], w.at[step % 2], c, rows)
+            ahead[c, rows] = x
+            if step < PAIRS - 1:
+                store(w.at[(step + 1) % 2], c, rows, x)
+
     for step in range(PAIRS):
-        s = [split(root[c], 2) for c in every]
-        p = [dot3(s[c], s[c]) for c in every]
-        if r is not None:
-            ahead = [2.25 * ahead[c] + dot3(r[c], split(ahead[c], 2)) for c in every]
-        cubic = [dot3(split(0.0625 * p[c] - 0.5625 * root[c], 2), split(p[c], 2)) for c in every]
-        r = [split(1.6875 * p[c] - 2.4375 * root[c] + cubic[c], 2) for c in every]
+        for c, rows in parts:
+            x = multiply(s, s, c, rows)
+            y = root[c, rows]
+            store(p, c, rows, x)
+            store(u, c, rows, 0.0625 * x - 0.5625 * y)
+            mixed[c, rows] = 1.6875 * x - 2.4375 * y
+        if step > 0:
+            advance(step - 1)
+        for c, rows in parts:
+            store(r.at[step % 2], c, rows, mixed[c, rows] + multiply(u, p, c, rows))
         if step < PAIRS - 1:
-            t = [2.25 * root[c] + dot3(r[c], s[c]) for c in every]
-            root = [2.25 * t[c] + dot3(split(t[c], 2), r[c]) for c in every]
-    ahead = [2.25 * ahead[c] + dot3(r[c], split(ahead[c], 2)) for c in every]
+            for c, rows in parts:
+                x = 2.25 * root[c, rows] + multiply(r.at[step % 2], s, c, rows)
+                store(t, c, rows, x)
+                mixed[c, rows] = 2.25 * x
+            for c, rows in parts:
+                x = mixed[c, rows] + multiply(t, r.at[step % 2], c, rows)
+                root[c, rows] = x
+                store(s, c, rows, x)
+    advance(PAIRS - 1)
     for c in every:
-        w = ahead[c]
-        inner = jnp.sum(w * forces[c], axis=1, keepdims=True)
-        shift = jnp.sum(w * inner, axis=0, keepdims=True) / scales[c]
-        result = means[c] + shift + w * jnp.sqrt(spread / scales[c])
+        x = ahead[c]
+        inner = jnp.sum(x * forces[c], axis=1, keepdims=True)
+        shift = jnp.sum(x * inner, axis=0, keepdims=True) / scales[c]
+        result = means[c] + shift + x * jnp.sqrt(spread / scales[c])
         for k in range(groups):
             outs[k][c] = result[k * local : (k + 1) * local]
 
@@ -236,15 +262,21 @@
     block = jax.ShapeDtypeStruct((columns, local, entries), jnp.float32)
     whole = jax.ShapeDtypeStruct(states.shape, jnp.float32)
     token = jax.ShapeDtypeStruct(after.shape, jnp.float32)
+    full = pltpu.VMEM((columns, members, members), jnp.float32)
+    pair = pltpu.VMEM((2, columns, members, members), jnp.bfloat16)
+    two = pltpu.VMEM((2, 2, columns, members, members), jnp.bfloat16)
+    ahead = pltpu.VMEM((columns, members, entries), jnp.float32)
+    factor = pltpu.VMEM((2, 2, columns, members, entries), jnp.bfloat16)
 
     def kernel(me_ref, after_ref, obs_ref, states_ref, *refs):
-        *outs, done_ref = refs
+        *outs, done_ref = refs[:-SCRATCH]
+        scratch = refs[-SCRATCH:]
         if apart:
             ins = [states_ref.at[target(me_ref[0], k, groups)] for k in range(groups)]
         else:
             ins = [states_ref.at[k] for k in range(groups)]
             outs = [outs[0].at[k] for k in range(groups)]
-        analyse_kernel(first, after_ref, obs_ref, ins, outs, done_ref)
+        analyse_kernel(first, after_ref, obs_ref, ins, outs, done_ref, *scratch)
 
     return call(
         kernel,
@@ -252,6 +284,7 @@
         columns * 90 * 2 * members * members * entries,
         8 * columns * members * entries,
         in_specs=[SMEM] + [VMEM] * 3,
+        scratch_shapes=[full, full, ahead, pair, pair, pair, pair, two, factor],
     )(me, after, obs, states)
 
 

time: 55.5 us -> 54.9 us (0.989)
  Pallas kernels: 23.4 us -> 22.2 us
  waiting for transfers between devices: 7.31 us -> 7.89 us
    pallas_call x2, Pallas kernels: 17.7 us -> 16.6 us  [analyse(): call(kernel, [block] * groups + [token] if apart else [whole, token], col...]
    all_to_all x1, waiting for transfers between devices: 0.57 us -> 1.16 us  [body(): lax.all_to_all(outer, 'mem', split_axis=0, concat_axis=0, tiled=True)]
  transfers between devices with their start and end apart: 12 -> 12, of which waited for: 8 -> 8; matrix products, arithmetic and copies ran while one was open for 0% -> 0% of each run, Pallas kernels for 36% -> 35%
where the time goes in v3:
time: 54.9 us; the launch traced here: 54.4 us
  starting transfers between devices  22.7 us (41%)
  Pallas kernels  22.2 us (40%)
  waiting for transfers between devices  7.89 us (14%)
  local copies, waits for them, and re-layouts  1.36 us (2%)
    pallas_call x2, Pallas kernels, analyse(): call(kernel, [block] * groups + [token] if apart else [whole, token], col...  16.6 us
    all_to_all x2, starting transfers between devices, body(): lax.all_to_all(inner, 'mem', split_axis=0, concat_axis=0, tiled=True)  8.99 us
    ppermute x7, starting transfers between devices, exchange(): out.append(lax.ppermute(blocks[k], 'mem', pairs) if k else blocks[0])  6.34 us
    ppermute x7, waiting for transfers between devices, exchange(): out.append(lax.ppermute(blocks[k], 'mem', pairs) if k else blocks[0])  4.43 us
    all_to_all x1, starting transfers between devices, body(): lax.all_to_all(outer, 'mem', split_axis=0, concat_axis=0, tiled=True)  3.49 us
    pallas_call x1, Pallas kernels, body(): call(inner_kernel, [jax.ShapeDtypeStruct((groups, *block), jnp.float32),...  2.35 us
    ppermute x1, starting transfers between devices, body(): lax.ppermute(low, 'tile', [((i + 1) % tiles, i) for i in range(tiles)])  2.25 us
    ppermute x1, starting transfers between devices, body(): lax.ppermute(high, 'tile', [(i, (i + 1) % tiles) for i in range(tiles)])  1.63 us
  transfers between devices with their start and end apart: 12, of which 8 were waited for; matrix products, arithmetic and copies ran while one was open for 0% of the time, Pallas kernels for 35%

profile of v3, /device:TPU:0, one launch (start us, length us, event | category | flops | bytes accessed | tf_op | source)
XLA Modules:
  0.0 54.4 jit_solution(12202954835149460502)
XLA Ops:
  0.0 0.0 copy-start
  0.0 2.4 %shard_map.74 = (f32[8,2,32,256]{3,2,1,0:T(8,128)}, f32[2,32,256]{2,1,0:T(8,128)}, f32[2,32,256]{2,1,0:T(8,128)}) custom-call(f32[32,32,256]{2,1,0:T(8,128)} %state_ref.3, f32[256]{0:T(256)} %diff_ref.1, f32[256]{0:T(256)} %adv_ref.1), custom_call_target="tpu_custom_call" | custom-call | flops 5242880 | bytes 2097152 | tf_op jit(solution)/shard_map/pallas_call | solution.py:302
  2.4 0.0 copy-start.8
  2.4 0.0 copy-start.7
  2.4 0.0 copy-start.1
  2.4 0.0 copy-start.2
  2.4 0.0 copy-start.3
  2.4 5.3 %all-to-all-start = ((f32[8,2,32,256]{3,2,1,0:T(8,128)}), f32[8,2,32,256]{3,2,1,0:T(8,128)S(1)}, u32[]{:S(2)}, u32[]{:S(2)}) async-start(f32[8,2,32,256]{3,2,1,0:T(8,128)} %get-tuple-element.18), calls=%async_computation | async-start | bytes 1048576 | tf_op jit(solution)/shard_map/all_to_all | solution.py:318
  7.7 0.0 copy-done.8
  7.7 1.6 %collective-permute-start = (f32[2,32,256]{2,1,0:T(8,128)S(1)}, f32[2,32,256]{2,1,0:T(8,128)S(1)}, u32[]{:S(2)}, u32[]{:S(2)}) collective-permute-start(f32[2,32,256]{2,1,0:T(8,128)S(1)} %copy-done.8), channel_id=1, source_target_pairs={{0,1},{1,2},{2,3},{3,0},{4,5},{5,6},{6,7},{7,4},{8,9},{9,10},{10,1... | collective-permute-start | bytes 196616 | tf_op jit(solution)/shard_map/ppermute | solution.py:319
  9.4 0.0 copy-done.7
  9.4 2.2 %collective-permute-start.1 = (f32[2,32,256]{2,1,0:T(8,128)S(1)}, f32[2,32,256]{2,1,0:T(8,128)S(1)}, u32[]{:S(2)}, u32[]{:S(2)}) collective-permute-start(f32[2,32,256]{2,1,0:T(8,128)S(1)} %copy-done.7), channel_id=1, source_target_pairs={{1,0},{2,1},{3,2},{0,3},{5,4},{6,5},{7,6},{4,7},{9,8},{10,9},{11,1... | collective-permute-start | bytes 196616 | tf_op jit(solution)/shard_map/ppermute | solution.py:320
  11.6 0.0 copy-start.6
  11.6 0.0 copy-done.1
  11.6 0.0 copy-done.2
  11.6 0.0 copy-done.3
  11.6 0.6 %copy-done.6 = s32[1,32]{1,0:T(1,128)S(1)} copy-done((s32[1,32]{1,0:T(1,128)S(1)}, s32[1,32]{1,0:T(1,128)}, u32[]{:S(2)}) %copy-start.6) | copy-done | bytes 152
  12.3 0.0 copy-start.5
  12.3 0.9 %shard_map.73.obs_ref = f32[4,8,256]{2,1,0:T(8,128)S(1)} custom-call(s32[1]{0:T(128)} %bitcast.me_ref, s32[1,32]{1,0:T(1,128)S(1)} %copy-done.6, s32[32,512]{1,0:T(8,128)S(1)} %bitcast.8, f32[32,512]{1,0:T(8,128)S(1)} %bitcast.9, f32[32,512]{1,0:T(8,128)S(1)} %bitcast.10), custom_call_target="tpu_custom_call" | custom-call | flops 16777216 | bytes 196608 | tf_op jit(solution)/shard_map/pallas_call | solution.py:321
  13.2 1.0 %collective-permute-done.before_ref = f32[2,32,256]{2,1,0:T(8,128)S(1)} collective-permute-done((f32[2,32,256]{2,1,0:T(8,128)S(1)}, f32[2,32,256]{2,1,0:T(8,128)S(1)}, u32[]{:S(2)}, u32[]{:S(2)}) %collective-permute-start) | collective-permute-done | bytes 65568 | tf_op jit(solution)/shard_map/ppermute | solution.py:319
  14.3 0.7 %collective-permute-done.1.after_ref = f32[2,32,256]{2,1,0:T(8,128)S(1)} collective-permute-done((f32[2,32,256]{2,1,0:T(8,128)S(1)}, f32[2,32,256]{2,1,0:T(8,128)S(1)}, u32[]{:S(2)}, u32[]{:S(2)}) %collective-permute-start.1) | collective-permute-done | bytes 65568 | tf_op jit(solution)/shard_map/ppermute | solution.py:320
  14.9 0.0 copy-start.4
  14.9 0.0 copy-done
  14.9 0.0 copy-done.5
  14.9 0.7 %copy-done.4 = f32[256]{0:T(256)S(1)} copy-done((f32[256]{0:T(256)S(1)}, f32[256]{0:T(256)}, u32[]{:S(2)}) %copy-start.4) | copy-done | bytes 1048
  15.6 1.3 %shard_map.76 = f32[8,2,32,256]{3,2,1,0:T(8,128)} custom-call(f32[4,8,256]{2,1,0:T(8,128)S(1)} %shard_map.73.obs_ref, f32[32,32,256]{2,1,0:T(8,128)S(1)} %copy-done, f32[2,32,256]{2,1,0:T(8,128)S(1)} %collective-permute-done.before_ref, f32[2,32,256]{2,1,0:T(8,128)S(1)} %collective-permute-done.1.after_ref, f32[1,256]{1,0:T(1,128)S(1)} %bitcast.11, ...), custom_call_target="tpu_custom_call" | custom-call | flops 5242880 | bytes 2097152 | tf_op jit(solution)/shard_map/pallas_call | solution.py:328
  16.9 0.6 %all-to-all-done.states_ref = f32[8,2,32,256]{3,2,1,0:T(8,128)S(1)} async-done(((f32[8,2,32,256]{3,2,1,0:T(8,128)}), f32[8,2,32,256]{3,2,1,0:T(8,128)S(1)}, u32[]{:S(2)}, u32[]{:S(2)}) %all-to-all-start) | async-done | bytes 524320 | tf_op jit(solution)/shard_map/all_to_all | solution.py:318
  17.5 3.5 %all-to-all-start.1 = ((f32[8,2,32,256]{3,2,1,0:T(8,128)}), f32[8,2,32,256]{3,2,1,0:T(8,128)S(1)}, u32[]{:S(2)}, u32[]{:S(2)}) async-start(f32[8,2,32,256]{3,2,1,0:T(8,128)} %shard_map.76), calls=%async_computation.1 | async-start | bytes 1048576 | tf_op jit(solution)/shard_map/all_to_all | solution.py:336
  21.0 8.5 %shard_map.75 = (f32[8,2,32,256]{3,2,1,0:T(8,128)}, f32[8,256]{1,0:T(8,128)S(1)}) custom-call(s32[1]{0:T(128)} %bitcast.me_ref, f32[8,256]{1,0:T(8,128)S(1)} %slice_bitcast_fusion.after_ref, f32[4,8,256]{2,1,0:T(8,128)S(1)} %shard_map.73.obs_ref, f32[8,2,32,256]{3,2,1,0:T(8,128)S(1)} %all-to-all-done.states_ref), custom_call_target="tpu_custom_call" | custom-call | flops 6039797760 | bytes 1048576 | tf_op jit(solution)/shard_map/pallas_call | solution.py:281
  29.5 1.2 %all-to-all-done.1.states_ref = f32[8,2,32,256]{3,2,1,0:T(8,128)S(1)} async-done(((f32[8,2,32,256]{3,2,1,0:T(8,128)}), f32[8,2,32,256]{3,2,1,0:T(8,128)S(1)}, u32[]{:S(2)}, u32[]{:S(2)}) %all-to-all-start.1) | async-done | bytes 524320 | tf_op jit(solution)/shard_map/all_to_all | solution.py:336
  30.7 3.7 %all-to-all-start.2 = ((f32[8,2,32,256]{3,2,1,0:T(8,128)}), f32[8,2,32,256]{3,2,1,0:T(8,128)S(1)}, u32[]{:S(2)}, u32[]{:S(2)}) async-start(f32[8,2,32,256]{3,2,1,0:T(8,128)} %get-tuple-element.30), calls=%async_computation.2 | async-start | bytes 1048576 | tf_op jit(solution)/shard_map/all_to_all | solution.py:339
  34.3 8.1 %shard_map.77 = (f32[2,32,256]{2,1,0:T(8,128)S(1)}, f32[2,32,256]{2,1,0:T(8,128)S(1)}, f32[2,32,256]{2,1,0:T(8,128)S(1)}, f32[2,32,256]{2,1,0:T(8,128)S(1)}, f32...) custom-call(s32[1]{0:T(128)} %bitcast.me_ref, ...), custom_call_target="tpu_custom_call" | custom-call | flops 6039797760 | bytes 1048576 | tf_op jit(solution)/shard_map/pallas_call | solution.py:281
  42.4 0.2 collective-permute-start.2
  42.6 2.6 %collective-permute-start.3 = (f32[2,32,256]{2,1,0:T(8,128)S(1)}, f32[2,32,256]{2,1,0:T(8,128)S(1)}, u32[]{:S(2)}, u32[]{:S(2)}) collective-permute-start(f32[2,32,256]{2,1,0:T(8,128)S(1)} %get-tuple-element.23), channel_id=1, source_target_pairs={{0,24},{4,28},{8,16},{12,20},{16,8},{20,12},{24,0},{28,4},{1,25},{... | collective-permute-start | bytes 196616 | tf_op jit(solution)/shard_map/ppermute | solution.py:47
  45.2 0.0 collective-permute-start.4
  45.2 1.7 %collective-permute-start.5 = (f32[2,32,256]{2,1,0:T(8,128)S(1)}, f32[2,32,256]{2,1,0:T(8,128)S(1)}, u32[]{:S(2)}, u32[]{:S(2)}) collective-permute-start(f32[2,32,256]{2,1,0:T(8,128)S(1)} %get-tuple-element.25), channel_id=1, source_target_pairs={{0,8},{4,12},{8,0},{12,4},{16,24},{20,28},{24,16},{28,20},{1,9},{5... | collective-permute-start | bytes 196616 | tf_op jit(solution)/shard_map/ppermute | solution.py:47
  46.9 0.1 collective-permute-start.6
  47.0 0.0 collective-permute-done.2.refs_0_
  47.0 1.7 %collective-permute-start.7 = (f32[2,32,256]{2,1,0:T(8,128)S(1)}, f32[2,32,256]{2,1,0:T(8,128)S(1)}, u32[]{:S(2)}, u32[]{:S(2)}) collective-permute-start(f32[2,32,256]{2,1,0:T(8,128)S(1)} %get-tuple-element.27), channel_id=1, source_target_pairs={{0,16},{4,20},{8,24},{12,28},{16,0},{20,4},{24,8},{28,12},{1,17},{... | collective-permute-start | bytes 196616 | tf_op jit(solution)/shard_map/ppermute | solution.py:47
  48.7 0.0 collective-permute-done.3.refs_1_
  48.7 0.0 collective-permute-start.8
  48.8 1.6 %collective-permute-done.4.refs_2_ = f32[2,32,256]{2,1,0:T(8,128)S(1)} collective-permute-done((f32[2,32,256]{2,1,0:T(8,128)S(1)}, f32[2,32,256]{2,1,0:T(8,128)S(1)}, u32[]{:S(2)}, u32[]{:S(2)}) %collective-permute-start.4) | collective-permute-done | bytes 65568 | tf_op jit(solution)/shard_map/ppermute | solution.py:47
  50.3 0.9 %collective-permute-done.5.refs_3_ = f32[2,32,256]{2,1,0:T(8,128)S(1)} collective-permute-done((f32[2,32,256]{2,1,0:T(8,128)S(1)}, f32[2,32,256]{2,1,0:T(8,128)S(1)}, u32[]{:S(2)}, u32[]{:S(2)}) %collective-permute-start.5) | collective-permute-done | bytes 65568 | tf_op jit(solution)/shard_map/ppermute | solution.py:47
  51.3 0.9 %collective-permute-done.6.refs_4_ = f32[2,32,256]{2,1,0:T(8,128)S(1)} collective-permute-done((f32[2,32,256]{2,1,0:T(8,128)S(1)}, f32[2,32,256]{2,1,0:T(8,128)S(1)}, u32[]{:S(2)}, u32[]{:S(2)}) %collective-permute-start.6) | collective-permute-done | bytes 65568 | tf_op jit(solution)/shard_map/ppermute | solution.py:47
  52.2 0.0 collective-permute-done.7.refs_5_
  52.2 1.0 %collective-permute-done.8.refs_6_ = f32[2,32,256]{2,1,0:T(8,128)S(1)} collective-permute-done((f32[2,32,256]{2,1,0:T(8,128)S(1)}, f32[2,32,256]{2,1,0:T(8,128)S(1)}, u32[]{:S(2)}, u32[]{:S(2)}) %collective-permute-start.8) | collective-permute-done | bytes 65568 | tf_op jit(solution)/shard_map/ppermute | solution.py:47
  53.2 0.0 all-to-all-done.2.refs_8_
  53.2 1.1 %shard_map.78 = f32[32,32,256]{2,1,0:T(8,128)} custom-call(s32[1]{0:T(128)} %bitcast.me_ref, f32[2,32,256]{2,1,0:T(8,128)S(1)} %collective-permute-done.2.refs_0_, f32[2,32,256]{2,1,0:T(8,128)S(1)} %collective-permute-done.3.refs_1_, f32[2,32,256]{2,1,0:T(8,128)S(1)} %collective-permute-done.4.refs_2_, f32[2,32,256]{2,1,0:T(8,128)S(1)} %collective-permute-done.5.refs_3_, ...), custom_call_target="tpu_custom_call" | custom-call | flops 262144 | bytes 2097152 | tf_op jit(solution)/shard_map/pallas_call | solution.py:342
  (1 shorter events, 0.0 us)
Async XLA Ops:
  0.0 14.9 %copy-start = (f32[32,32,256]{2,1,0:T(8,128)S(1)}, f32[32,32,256]{2,1,0:T(8,128)}, u32[]{:S(2)}) copy-start(f32[32,32,256]{2,1,0:T(8,128)} %state_ref.3) | copy-start | bytes 3145732
  2.4 5.4 %copy-start.8 = (f32[2,32,256]{2,1,0:T(8,128)S(1)}, f32[2,32,256]{2,1,0:T(8,128)}, u32[]{:S(2)}) copy-start(f32[2,32,256]{2,1,0:T(8,128)} %get-tuple-element.20) | copy-start | bytes 196612
  2.4 7.0 %copy-start.7 = (f32[2,32,256]{2,1,0:T(8,128)S(1)}, f32[2,32,256]{2,1,0:T(8,128)}, u32[]{:S(2)}) copy-start(f32[2,32,256]{2,1,0:T(8,128)} %get-tuple-element.21) | copy-start | bytes 196612
  2.4 9.2 %copy-start.1 = (s32[1,32,512]{2,1,0:T(8,128)S(1)}, s32[1,32,512]{2,1,0:T(8,128)}, u32[]{:S(2)}) copy-start(s32[1,32,512]{2,1,0:T(8,128)} %param.10) | copy-start | bytes 196612
  2.4 9.2 %copy-start.2 = (f32[1,32,512]{2,1,0:T(8,128)S(1)}, f32[1,32,512]{2,1,0:T(8,128)}, u32[]{:S(2)}) copy-start(f32[1,32,512]{2,1,0:T(8,128)} %param.12) | copy-start | bytes 196612
  2.4 9.2 %copy-start.3 = (f32[1,32,512]{2,1,0:T(8,128)S(1)}, f32[1,32,512]{2,1,0:T(8,128)}, u32[]{:S(2)}) copy-start(f32[1,32,512]{2,1,0:T(8,128)} %param.13) | copy-start | bytes 196612
  2.4 15.1 %all-to-all-start = ((f32[8,2,32,256]{3,2,1,0:T(8,128)}), f32[8,2,32,256]{3,2,1,0:T(8,128)S(1)}, u32[]{:S(2)}, u32[]{:S(2)}) async-start(f32[8,2,32,256]{3,2,1,0:T(8,128)} %get-tuple-element.18), calls=%async_computation | async-start | bytes 1048576 | tf_op jit(solution)/shard_map/all_to_all | solution.py:318
  7.7 6.5 %collective-permute-start = (f32[2,32,256]{2,1,0:T(8,128)S(1)}, f32[2,32,256]{2,1,0:T(8,128)S(1)}, u32[]{:S(2)}, u32[]{:S(2)}) collective-permute-start(f32[2,32,256]{2,1,0:T(8,128)S(1)} %copy-done.8), channel_id=1, source_target_pairs={{0,1},{1,2},{2,3},{3,0},{4,5},{5,6},{6,7},{7,4},{8,9},{9,10},{10,1... | collective-permute-start | bytes 196616 | tf_op jit(solution)/shard_map/ppermute | solution.py:319
  9.4 5.6 %collective-permute-start.1 = (f32[2,32,256]{2,1,0:T(8,128)S(1)}, f32[2,32,256]{2,1,0:T(8,128)S(1)}, u32[]{:S(2)}, u32[]{:S(2)}) collective-permute-start(f32[2,32,256]{2,1,0:T(8,128)S(1)} %copy-done.7), channel_id=1, source_target_pairs={{1,0},{2,1},{3,2},{0,3},{5,4},{6,5},{7,6},{4,7},{9,8},{10,9},{11,1... | collective-permute-start | bytes 196616 | tf_op jit(solution)/shard_map/ppermute | solution.py:320
  11.6 0.7 %copy-start.6 = (s32[1,32]{1,0:T(1,128)S(1)}, s32[1,32]{1,0:T(1,128)}, u32[]{:S(2)}) copy-start(s32[1,32]{1,0:T(1,128)} %count_ref.1) | copy-start | bytes 388
  12.3 2.7 %copy-start.5 = (f32[256]{0:T(256)S(1)}, f32[256]{0:T(256)}, u32[]{:S(2)}) copy-start(f32[256]{0:T(256)} %adv_ref.1) | copy-start | bytes 3076
  14.9 0.7 %copy-start.4 = (f32[256]{0:T(256)S(1)}, f32[256]{0:T(256)}, u32[]{:S(2)}) copy-start(f32[256]{0:T(256)} %diff_ref.1) | copy-start | bytes 3076
  17.5 13.2 %all-to-all-start.1 = ((f32[8,2,32,256]{3,2,1,0:T(8,128)}), f32[8,2,32,256]{3,2,1,0:T(8,128)S(1)}, u32[]{:S(2)}, u32[]{:S(2)}) async-start(f32[8,2,32,256]{3,2,1,0:T(8,128)} %shard_map.76), calls=%async_computation.1 | async-start | bytes 1048576 | tf_op jit(solution)/shard_map/all_to_all | solution.py:336
  30.7 22.5 %all-to-all-start.2 = ((f32[8,2,32,256]{3,2,1,0:T(8,128)}), f32[8,2,32,256]{3,2,1,0:T(8,128)S(1)}, u32[]{:S(2)}, u32[]{:S(2)}) async-start(f32[8,2,32,256]{3,2,1,0:T(8,128)} %get-tuple-element.30), calls=%async_computation.2 | async-start | bytes 1048576 | tf_op jit(solution)/shard_map/all_to_all | solution.py:339
  42.4 4.6 %collective-permute-start.2 = (f32[2,32,256]{2,1,0:T(8,128)S(1)}, f32[2,32,256]{2,1,0:T(8,128)S(1)}, u32[]{:S(2)}, u32[]{:S(2)}) collective-permute-start(f32[2,32,256]{2,1,0:T(8,128)S(1)} %get-tuple-element.22), channel_id=1, source_target_pairs={{0,4},{4,0},{8,12},{12,8},{16,20},{20,16},{24,28},{28,24},{1,5},{5... | collective-permute-start | bytes 196616 | tf_op jit(solution)/shard_map/ppermute | solution.py:47
  42.6 6.1 %collective-permute-start.3 = (f32[2,32,256]{2,1,0:T(8,128)S(1)}, f32[2,32,256]{2,1,0:T(8,128)S(1)}, u32[]{:S(2)}, u32[]{:S(2)}) collective-permute-start(f32[2,32,256]{2,1,0:T(8,128)S(1)} %get-tuple-element.23), channel_id=1, source_target_pairs={{0,24},{4,28},{8,16},{12,20},{16,8},{20,12},{24,0},{28,4},{1,25},{... | collective-permute-start | bytes 196616 | tf_op jit(solution)/shard_map/ppermute | solution.py:47
  45.2 5.1 %collective-permute-start.4 = (f32[2,32,256]{2,1,0:T(8,128)S(1)}, f32[2,32,256]{2,1,0:T(8,128)S(1)}, u32[]{:S(2)}, u32[]{:S(2)}) collective-permute-start(f32[2,32,256]{2,1,0:T(8,128)S(1)} %get-tuple-element.24), channel_id=1, source_target_pairs={{0,28},{4,24},{8,20},{12,16},{16,12},{20,8},{24,4},{28,0},{1,29},{... | collective-permute-start | bytes 196616 | tf_op jit(solution)/shard_map/ppermute | solution.py:47
  45.2 6.0 %collective-permute-start.5 = (f32[2,32,256]{2,1,0:T(8,128)S(1)}, f32[2,32,256]{2,1,0:T(8,128)S(1)}, u32[]{:S(2)}, u32[]{:S(2)}) collective-permute-start(f32[2,32,256]{2,1,0:T(8,128)S(1)} %get-tuple-element.25), channel_id=1, source_target_pairs={{0,8},{4,12},{8,0},{12,4},{16,24},{20,28},{24,16},{28,20},{1,9},{5... | collective-permute-start | bytes 196616 | tf_op jit(solution)/shard_map/ppermute | solution.py:47
  46.9 5.2 %collective-permute-start.6 = (f32[2,32,256]{2,1,0:T(8,128)S(1)}, f32[2,32,256]{2,1,0:T(8,128)S(1)}, u32[]{:S(2)}, u32[]{:S(2)}) collective-permute-start(f32[2,32,256]{2,1,0:T(8,128)S(1)} %get-tuple-element.26), channel_id=1, source_target_pairs={{0,12},{4,8},{8,4},{12,0},{16,28},{20,24},{24,20},{28,16},{1,13},{... | collective-permute-start | bytes 196616 | tf_op jit(solution)/shard_map/ppermute | solution.py:47
  47.0 5.1 %collective-permute-start.7 = (f32[2,32,256]{2,1,0:T(8,128)S(1)}, f32[2,32,256]{2,1,0:T(8,128)S(1)}, u32[]{:S(2)}, u32[]{:S(2)}) collective-permute-start(f32[2,32,256]{2,1,0:T(8,128)S(1)} %get-tuple-element.27), channel_id=1, source_target_pairs={{0,16},{4,20},{8,24},{12,28},{16,0},{20,4},{24,8},{28,12},{1,17},{... | collective-permute-start | bytes 196616 | tf_op jit(solution)/shard_map/ppermute | solution.py:47
  48.7 4.5 %collective-permute-start.8 = (f32[2,32,256]{2,1,0:T(8,128)S(1)}, f32[2,32,256]{2,1,0:T(8,128)S(1)}, u32[]{:S(2)}, u32[]{:S(2)}) collective-permute-start(f32[2,32,256]{2,1,0:T(8,128)S(1)} %get-tuple-element.28), channel_id=1, source_target_pairs={{0,20},{4,16},{8,28},{12,24},{16,4},{20,0},{24,12},{28,8},{1,21},{... | collective-permute-start | bytes 196616 | tf_op jit(solution)/shard_map/ppermute | solution.py:47

commit v4 on v3

--- a/solution.py
+++ b/solution.py
@@ -68,11 +68,14 @@
     return jnp.dot(lhs, rhs, preferred_element_type=jnp.float32)
 
 
-def square_by_rows(parts):
-    p0, p1, p2 = parts
-    lhs = jnp.concatenate([p2, p0, p1, p1, p0, p0], axis=1)
-    rhs = jnp.concatenate([p0, p2, p1, p0, p1, p0], axis=1)
-    return lax.dot_general(lhs, rhs, (((1,), (1,)), ((), ())), preferred_element_type=jnp.float32)
+def square_by_rows(x):
+    a, b = split(x, 3), split(x.T, 3)
+    lhs = jnp.concatenate([a[2], a[0], a[1], a[1], a[0], a[0]], axis=1)
+    rhs = jnp.concatenate([b[0], b[2], b[1], b[0], b[1], b[0]], axis=0)
+    middle = lhs.shape[0] // 2
+    upper = jnp.dot(lhs[:middle], rhs, preferred_element_type=jnp.float32)
+    lower = jnp.dot(lhs[middle:], rhs, preferred_element_type=jnp.float32)
+    return jnp.concatenate([upper, lower], axis=0)
 
 
 def stencil(padded, diffusion, advection):
@@ -95,7 +98,7 @@
     return [pl.ds(first, rows) for first in range(0, members, rows)]
 
 
-def inner_kernel(state_ref, diff_ref, adv_ref, out_ref, low_ref, high_ref, held_ref, num_ref, edge_ref, made_ref, sems):
+def inner_kernel(state_ref, diff_ref, adv_ref, out_ref, low_ref, high_ref, held_ref, num_ref, sems):
     members, columns, entries = state_ref.shape
     groups, half, _, _ = out_ref.shape
     quarter = columns // 4
@@ -110,24 +113,14 @@
     reads[count + 1].wait()
     diffusion = num_ref[0:1][None]
     advection = num_ref[1:2][None]
-    writes = []
     for i, part in enumerate(pieces):
         reads[i].wait()
         x = jnp.swapaxes(held_ref[part], 0, 1)
-        edge_ref[0, :, part] = x[:2]
-        edge_ref[1, :, part] = x[columns - 2 :]
+        low_ref[:, part] = x[:2]
+        high_ref[:, part] = x[columns - 2 :]
         x = x[quarter - 2 : columns - quarter + 2]
         x = stencil(stencil(x, diffusion, advection), diffusion, advection)
-        made_ref[:, :, part] = x.reshape(groups, half, part.size, entries)
-        copy = pltpu.make_async_copy(made_ref.at[:, :, part], out_ref.at[:, :, part], sems.at[count + 2 + i])
-        copy.start()
-        writes.append(copy)
-    for i, ref in enumerate((low_ref, high_ref)):
-        copy = pltpu.make_async_copy(edge_ref.at[i], ref, sems.at[2 * count + 2 + i])
-        copy.start()
-        writes.append(copy)
-    for copy in writes:
-        copy.wait()
+        out_ref[:, :, part] = x.reshape(groups, half, part.size, entries)
 
 
 def outer_kernel(obs_ref, state_ref, before_ref, after_ref, diff_ref, adv_ref, out_ref, turned_ref):
@@ -146,21 +139,44 @@
     out_ref[...] = jnp.concatenate([low, high], axis=0).reshape(out_ref.shape)
 
 
-def join_kernel(me_ref, *refs):
-    *outer, inner_ref, out_ref, turned_ref, made_ref, sems = refs
+def inner_join_kernel(after_ref, inner_ref, out_ref, made_ref, sems):
+    del after_ref
     members, columns, entries = out_ref.shape
     groups, half, _, _ = inner_ref.shape
     quarter = columns // 4
     writes = []
     for i, part in enumerate(pieces_of(members)):
-        for k, block in zip(issue_order(groups), outer):
-            place = source(me_ref[0], k, groups) * half
-            turned_ref[pl.ds(outer_start(place, quarter), half), part] = block[:, part]
-        turned_ref[quarter : columns - quarter, part] = inner_ref[:, :, part].reshape(groups * half, part.size, entries)
-        made_ref[part] = jnp.swapaxes(turned_ref[:, part], 0, 1)
-        copy = pltpu.make_async_copy(made_ref.at[part], out_ref.at[part], sems.at[i])
+        x = inner_ref[:, :, part].reshape(groups * half, part.size, entries)
+        made_ref[part] = jnp.swapaxes(x, 0, 1)
+        copy = pltpu.make_async_copy(
+            made_ref.at[part], out_ref.at[part, pl.ds(quarter, columns - 2 * quarter)], sems.at[i]
+        )
         copy.start()
         writes.append(copy)
+    for copy in writes:
+        copy.wait()
+
+
+def outer_join_kernel(me_ref, held_ref, *refs):
+    del held_ref
+    *outer, out_ref, turned_ref, made_ref, sems = refs
+    members, columns, _ = out_ref.shape
+    groups = len(outer)
+    half = outer[0].shape[0]
+    quarter = columns // 4
+    writes = []
+    for i, part in enumerate(pieces_of(members)):
+        for k, block in zip(issue_order(groups), outer):
+            turned_ref[pl.ds(source(me_ref[0], k, groups) * half, half), part] = block[:, part]
+        made_ref[part] = jnp.swapaxes(turned_ref[:, part], 0, 1)
+        for side in range(2):
+            copy = pltpu.make_async_copy(
+                made_ref.at[part, pl.ds(side * quarter, quarter)],
+                out_ref.at[part, pl.ds(side * (columns - quarter), quarter)],
+                sems.at[2 * i + side],
+            )
+            copy.start()
+            writes.append(copy)
     for copy in writes:
         copy.wait()
 
@@ -208,7 +224,7 @@
         total = obs_ref[first + c, 0:1]
         forces.append(obs_ref[first + c, 1:2] - total * mean)
         means.append(mean)
-        grams.append(square_by_rows(split(anomaly * jnp.sqrt(total), 3)))
+        grams.append(square_by_rows(anomaly * jnp.sqrt(total)))
         ahead[c] = anomaly
         store(w.at[0], c, slice(None), anomaly)
     for c in every:
@@ -304,17 +320,13 @@
         [jax.ShapeDtypeStruct((groups, *block), jnp.float32), edge, edge],
         20 * size,
         8 * size,
-        vmem=60 * MIB,
-        in_specs=[HBM, HBM, HBM],
-        out_specs=[HBM, HBM, HBM],
+        in_specs=[HBM] * 3,
         scratch_shapes=[
             pltpu.VMEM(background.shape, jnp.float32),
             pltpu.VMEM((8, entries), jnp.float32),
-            pltpu.VMEM((2, 2, local, entries), jnp.float32),
-            pltpu.VMEM((groups, *block), jnp.float32),
-            pltpu.SemaphoreType.DMA((2 * pieces + 4,)),
+            pltpu.SemaphoreType.DMA((pieces + 2,)),
         ],
-    )(background, diffusion, advection)
+    )(*(pltpu.with_memory_space_constraint(x, pltpu.HBM) for x in (background, diffusion, advection)))
     inner = lax.all_to_all(inner, "mem", split_axis=0, concat_axis=0, tiled=True)
     before = lax.ppermute(high, "tile", [(i, (i + 1) % tiles) for i in range(tiles)])
     after = lax.ppermute(low, "tile", [((i + 1) % tiles, i) for i in range(tiles)])
@@ -339,19 +351,33 @@
     inner = lax.all_to_all(inner, "mem", split_axis=0, concat_axis=0, tiled=True)
     *outer, _ = analyse(outer, obs, half, me, done, True)
     outer = exchange(outer)
-    return call(
-        join_kernel,
-        jax.ShapeDtypeStruct(background.shape, jnp.float32),
+    result = jax.ShapeDtypeStruct(background.shape, jnp.float32)
+    made = call(
+        inner_join_kernel,
+        result,
         size,
-        8 * size,
-        in_specs=[SMEM] + [VMEM] * (groups + 1),
+        4 * size,
+        in_specs=[VMEM, VMEM],
         out_specs=HBM,
         scratch_shapes=[
-            pltpu.VMEM((columns, local, entries), jnp.float32),
-            pltpu.VMEM(background.shape, jnp.float32),
+            pltpu.VMEM((local, groups * half, entries), jnp.float32),
             pltpu.SemaphoreType.DMA((pieces,)),
         ],
-    )(me, *outer, inner)
+    )(outer[2], inner)
+    return call(
+        outer_join_kernel,
+        result,
+        size,
+        4 * size,
+        in_specs=[SMEM, HBM] + [VMEM] * groups,
+        out_specs=HBM,
+        scratch_shapes=[
+            pltpu.VMEM((groups * half, local, entries), jnp.float32),
+            pltpu.VMEM((local, groups * half, entries), jnp.float32),
+            pltpu.SemaphoreType.DMA((2 * pieces,)),
+        ],
+        input_output_aliases={1: 0},
+    )(me, made, *outer)
 
 
 def solution(mesh):

time: 54.9 us -> 55 us (level)
  Pallas kernels: 22.2 us -> 23.1 us
  waiting for transfers between devices: 7.89 us -> 7.01 us
    ppermute x7, waiting for transfers between devices: 4.43 us -> 3.57 us  [exchange(): out.append(lax.ppermute(blocks[k], 'mem', pairs) if k else blocks[0])]
    pallas_call x1 -> x2, Pallas kernels: 1.09 us -> 1.75 us  [the longest x1 0.9 us: body(): call(outer_join_kernel, result, size, 4 * size, in_specs=[SMEM, HBM] + [V...]
    unnamed x18 -> x14, local copies, waits for them, and re-layouts: 1.35 us -> 1.34 us
  transfers between devices with their start and end apart: 12 -> 12, of which waited for: 8 -> 10; matrix products, arithmetic and copies ran while one was open for 0% -> 0% of each run, Pallas kernels for 35% -> 36%
where the time goes in v4:
time: 55 us; the launch traced here: 54.6 us
  Pallas kernels  23.1 us (42%)
  starting transfers between devices  22.9 us (42%)
  waiting for transfers between devices  7.01 us (13%)
  local copies, waits for them, and re-layouts  1.35 us (2%)
    pallas_call x2, Pallas kernels, analyse(): call(kernel, [block] * groups + [token] if apart else [whole, token], col...  16.7 us
    all_to_all x2, starting transfers between devices, body(): lax.all_to_all(inner, 'mem', split_axis=0, concat_axis=0, tiled=True)  8.99 us
    ppermute x7, starting transfers between devices, exchange(): out.append(lax.ppermute(blocks[k], 'mem', pairs) if k else blocks[0])  6.55 us
    ppermute x7, waiting for transfers between devices, exchange(): out.append(lax.ppermute(blocks[k], 'mem', pairs) if k else blocks[0])  3.57 us
    all_to_all x1, starting transfers between devices, body(): lax.all_to_all(outer, 'mem', split_axis=0, concat_axis=0, tiled=True)  3.49 us
    pallas_call x1, Pallas kernels, body(): call(inner_kernel, [jax.ShapeDtypeStruct((groups, *block), jnp.float32),...  2.41 us
    ppermute x1, starting transfers between devices, body(): lax.ppermute(low, 'tile', [((i + 1) % tiles, i) for i in range(tiles)])  2.25 us
    ppermute x1, starting transfers between devices, body(): lax.ppermute(high, 'tile', [(i, (i + 1) % tiles) for i in range(tiles)])  1.58 us
  transfers between devices with their start and end apart: 12, of which 10 were waited for; matrix products, arithmetic and copies ran while one was open for 0% of the time, Pallas kernels for 36%

profile of v4, /device:TPU:0, one launch (start us, length us, event | category | flops | bytes accessed | tf_op | source)
XLA Modules:
  0.0 54.6 jit_solution(14962251704270069307)
XLA Ops:
  0.0 0.0 copy-start
  0.0 2.4 %shard_map.74 = (f32[8,2,32,256]{3,2,1,0:T(8,128)}, f32[2,32,256]{2,1,0:T(8,128)S(1)}, f32[2,32,256]{2,1,0:T(8,128)S(1)}) custom-call(f32[32,32,256]{2,1,0:T(8,128)} %state_ref.3, f32[256]{0:T(256)} %diff_ref.1, f32[256]{0:T(256)} %adv_ref.1), custom_call_target="tpu_custom_call" | custom-call | flops 5242880 | bytes 2097152 | tf_op jit(solution)/shard_map/pallas_call | solution.py:318
  2.4 0.0 copy-start.1
  2.4 0.0 copy-start.2
  2.4 0.0 copy-start.3
  2.5 5.3 %all-to-all-start = ((f32[8,2,32,256]{3,2,1,0:T(8,128)}), f32[8,2,32,256]{3,2,1,0:T(8,128)S(1)}, u32[]{:S(2)}, u32[]{:S(2)}) async-start(f32[8,2,32,256]{3,2,1,0:T(8,128)} %get-tuple-element.18), calls=%async_computation | async-start | bytes 1048576 | tf_op jit(solution)/shard_map/all_to_all | solution.py:330
  7.8 1.6 %collective-permute-start = (f32[2,32,256]{2,1,0:T(8,128)S(1)}, f32[2,32,256]{2,1,0:T(8,128)S(1)}, u32[]{:S(2)}, u32[]{:S(2)}) collective-permute-start(f32[2,32,256]{2,1,0:T(8,128)S(1)} %get-tuple-element.20), channel_id=1, source_target_pairs={{0,1},{1,2},{2,3},{3,0},{4,5},{5,6},{6,7},{7,4},{8,9},{9,10},{10,1... | collective-permute-start | bytes 196616 | tf_op jit(solution)/shard_map/ppermute | solution.py:331
  9.3 2.2 %collective-permute-start.1 = (f32[2,32,256]{2,1,0:T(8,128)S(1)}, f32[2,32,256]{2,1,0:T(8,128)S(1)}, u32[]{:S(2)}, u32[]{:S(2)}) collective-permute-start(f32[2,32,256]{2,1,0:T(8,128)S(1)} %get-tuple-element.21), channel_id=1, source_target_pairs={{1,0},{2,1},{3,2},{0,3},{5,4},{6,5},{7,6},{4,7},{9,8},{10,9},{11,1... | collective-permute-start | bytes 196616 | tf_op jit(solution)/shard_map/ppermute | solution.py:332
  11.6 0.0 copy-start.6
  11.6 0.0 copy-done.1
  11.6 0.0 copy-done.2
  11.6 0.0 copy-done.3
  11.6 0.6 %copy-done.6 = s32[1,32]{1,0:T(1,128)S(1)} copy-done((s32[1,32]{1,0:T(1,128)S(1)}, s32[1,32]{1,0:T(1,128)}, u32[]{:S(2)}) %copy-start.6) | copy-done | bytes 152
  12.3 0.0 copy-start.5
  12.3 0.9 %shard_map.73.obs_ref = f32[4,8,256]{2,1,0:T(8,128)S(1)} custom-call(s32[1]{0:T(128)} %bitcast.me_ref, s32[1,32]{1,0:T(1,128)S(1)} %copy-done.6, s32[32,512]{1,0:T(8,128)S(1)} %bitcast.8, f32[32,512]{1,0:T(8,128)S(1)} %bitcast.9, f32[32,512]{1,0:T(8,128)S(1)} %bitcast.10), custom_call_target="tpu_custom_call" | custom-call | flops 16777216 | bytes 196608 | tf_op jit(solution)/shard_map/pallas_call | solution.py:333
  13.2 1.1 %collective-permute-done.before_ref = f32[2,32,256]{2,1,0:T(8,128)S(1)} collective-permute-done((f32[2,32,256]{2,1,0:T(8,128)S(1)}, f32[2,32,256]{2,1,0:T(8,128)S(1)}, u32[]{:S(2)}, u32[]{:S(2)}) %collective-permute-start) | collective-permute-done | bytes 65568 | tf_op jit(solution)/shard_map/ppermute | solution.py:331
  14.3 0.7 %collective-permute-done.1.after_ref = f32[2,32,256]{2,1,0:T(8,128)S(1)} collective-permute-done((f32[2,32,256]{2,1,0:T(8,128)S(1)}, f32[2,32,256]{2,1,0:T(8,128)S(1)}, u32[]{:S(2)}, u32[]{:S(2)}) %collective-permute-start.1) | collective-permute-done | bytes 65568 | tf_op jit(solution)/shard_map/ppermute | solution.py:332
  15.0 0.0 copy-start.4
  15.0 0.0 copy-done
  15.0 0.0 copy-done.5
  15.0 0.7 %copy-done.4 = f32[256]{0:T(256)S(1)} copy-done((f32[256]{0:T(256)S(1)}, f32[256]{0:T(256)}, u32[]{:S(2)}) %copy-start.4) | copy-done | bytes 1048
  15.7 1.3 %shard_map.76 = f32[8,2,32,256]{3,2,1,0:T(8,128)} custom-call(f32[4,8,256]{2,1,0:T(8,128)S(1)} %shard_map.73.obs_ref, f32[32,32,256]{2,1,0:T(8,128)S(1)} %copy-done, f32[2,32,256]{2,1,0:T(8,128)S(1)} %collective-permute-done.before_ref, f32[2,32,256]{2,1,0:T(8,128)S(1)} %collective-permute-done.1.after_ref, f32[1,256]{1,0:T(1,128)S(1)} %bitcast.11, ...), custom_call_target="tpu_custom_call" | custom-call | flops 5242880 | bytes 2097152 | tf_op jit(solution)/shard_map/pallas_call | solution.py:340
  16.9 0.6 %all-to-all-done.states_ref = f32[8,2,32,256]{3,2,1,0:T(8,128)S(1)} async-done(((f32[8,2,32,256]{3,2,1,0:T(8,128)}), f32[8,2,32,256]{3,2,1,0:T(8,128)S(1)}, u32[]{:S(2)}, u32[]{:S(2)}) %all-to-all-start) | async-done | bytes 524320 | tf_op jit(solution)/shard_map/all_to_all | solution.py:330
  17.5 3.5 %all-to-all-start.1 = ((f32[8,2,32,256]{3,2,1,0:T(8,128)}), f32[8,2,32,256]{3,2,1,0:T(8,128)S(1)}, u32[]{:S(2)}, u32[]{:S(2)}) async-start(f32[8,2,32,256]{3,2,1,0:T(8,128)} %shard_map.76), calls=%async_computation.1 | async-start | bytes 1048576 | tf_op jit(solution)/shard_map/all_to_all | solution.py:348
  21.0 8.6 %shard_map.75 = (f32[8,2,32,256]{3,2,1,0:T(8,128)}, f32[8,256]{1,0:T(8,128)S(1)}) custom-call(s32[1]{0:T(128)} %bitcast.me_ref, f32[8,256]{1,0:T(8,128)S(1)} %slice_bitcast_fusion.after_ref, f32[4,8,256]{2,1,0:T(8,128)S(1)} %shard_map.73.obs_ref, f32[8,2,32,256]{3,2,1,0:T(8,128)S(1)} %all-to-all-done.states_ref), custom_call_target="tpu_custom_call" | custom-call | flops 6039797760 | bytes 1048576 | tf_op jit(solution)/shard_map/pallas_call | solution.py:297
  29.6 1.1 %all-to-all-done.1.states_ref = f32[8,2,32,256]{3,2,1,0:T(8,128)S(1)} async-done(((f32[8,2,32,256]{3,2,1,0:T(8,128)}), f32[8,2,32,256]{3,2,1,0:T(8,128)S(1)}, u32[]{:S(2)}, u32[]{:S(2)}) %all-to-all-start.1) | async-done | bytes 524320 | tf_op jit(solution)/shard_map/all_to_all | solution.py:348
  30.7 3.7 %all-to-all-start.2 = ((f32[8,2,32,256]{3,2,1,0:T(8,128)}), f32[8,2,32,256]{3,2,1,0:T(8,128)S(1)}, u32[]{:S(2)}, u32[]{:S(2)}) async-start(f32[8,2,32,256]{3,2,1,0:T(8,128)} %get-tuple-element.23), calls=%async_computation.2 | async-start | bytes 1048576 | tf_op jit(solution)/shard_map/all_to_all | solution.py:351
  34.4 8.1 %shard_map.77 = (f32[2,32,256]{2,1,0:T(8,128)S(1)}, f32[2,32,256]{2,1,0:T(8,128)S(1)}, f32[2,32,256]{2,1,0:T(8,128)S(1)}, f32[2,32,256]{2,1,0:T(8,128)S(1)}, f32...) custom-call(s32[1]{0:T(128)} %bitcast.me_ref, ...), custom_call_target="tpu_custom_call" | custom-call | flops 6039797760 | bytes 1048576 | tf_op jit(solution)/shard_map/pallas_call | solution.py:297
  42.5 2.4 %collective-permute-start.2 = (f32[2,32,256]{2,1,0:T(8,128)S(1)}, f32[2,32,256]{2,1,0:T(8,128)S(1)}, u32[]{:S(2)}, u32[]{:S(2)}) collective-permute-start(f32[2,32,256]{2,1,0:T(8,128)S(1)} %get-tuple-element.22), channel_id=1, source_target_pairs={{0,28},{4,24},{8,20},{12,16},{16,12},{20,8},{24,4},{28,0},{1,29},{... | collective-permute-start | bytes 196616 | tf_op jit(solution)/shard_map/ppermute | solution.py:47
  44.9 0.4 collective-permute-start.3
  45.3 0.3 collective-permute-start.4
  45.6 1.7 %collective-permute-start.5 = (f32[2,32,256]{2,1,0:T(8,128)S(1)}, f32[2,32,256]{2,1,0:T(8,128)S(1)}, u32[]{:S(2)}, u32[]{:S(2)}) collective-permute-start(f32[2,32,256]{2,1,0:T(8,128)S(1)} %get-tuple-element.26), channel_id=1, source_target_pairs={{0,8},{4,12},{8,0},{12,4},{16,24},{20,28},{24,16},{28,20},{1,9},{5... | collective-permute-start | bytes 196616 | tf_op jit(solution)/shard_map/ppermute | solution.py:47
  47.3 0.0 collective-permute-start.6
  47.3 0.2 collective-permute-done.2.after_ref.refs_2_
  47.5 1.8 %collective-permute-start.7 = (f32[2,32,256]{2,1,0:T(8,128)S(1)}, f32[2,32,256]{2,1,0:T(8,128)S(1)}, u32[]{:S(2)}, u32[]{:S(2)}) collective-permute-start(f32[2,32,256]{2,1,0:T(8,128)S(1)} %get-tuple-element.28), channel_id=1, source_target_pairs={{0,16},{4,20},{8,24},{12,28},{16,0},{20,4},{24,8},{28,12},{1,17},{... | collective-permute-start | bytes 196616 | tf_op jit(solution)/shard_map/ppermute | solution.py:47
  49.3 0.0 collective-permute-done.3.refs_0_
  49.3 0.0 collective-permute-start.8
  49.3 0.0 all-to-all-done.2.inner_ref
  49.3 0.8 %shard_map.78.held_ref = f32[32,32,256]{2,1,0:T(8,128)} custom-call(f32[2,32,256]{2,1,0:T(8,128)S(1)} %collective-permute-done.2.after_ref.refs_2_, f32[8,2,32,256]{3,2,1,0:T(8,128)S(1)} %all-to-all-done.2.inner_ref), custom_call_target="tpu_custom_call" | custom-call | flops 262144 | bytes 1048576 | tf_op jit(solution)/shard_map/pallas_call | solution.py:355
  50.1 1.0 %collective-permute-done.4.refs_1_ = f32[2,32,256]{2,1,0:T(8,128)S(1)} collective-permute-done((f32[2,32,256]{2,1,0:T(8,128)S(1)}, f32[2,32,256]{2,1,0:T(8,128)S(1)}, u32[]{:S(2)}, u32[]{:S(2)}) %collective-permute-start.4) | collective-permute-done | bytes 65568 | tf_op jit(solution)/shard_map/ppermute | solution.py:47
  51.2 0.3 collective-permute-done.5.refs_3_
  51.5 0.2 collective-permute-done.6.refs_4_
  51.8 0.4 collective-permute-done.7.refs_5_
  52.2 1.4 %collective-permute-done.8.refs_6_ = f32[2,32,256]{2,1,0:T(8,128)S(1)} collective-permute-done((f32[2,32,256]{2,1,0:T(8,128)S(1)}, f32[2,32,256]{2,1,0:T(8,128)S(1)}, u32[]{:S(2)}, u32[]{:S(2)}) %collective-permute-start.8) | collective-permute-done | bytes 65568 | tf_op jit(solution)/shard_map/ppermute | solution.py:47
  53.5 0.9 %shard_map.79 = f32[32,32,256]{2,1,0:T(8,128)} custom-call(s32[1]{0:T(128)} %bitcast.me_ref, f32[32,32,256]{2,1,0:T(8,128)} %shard_map.78.held_ref, f32[2,32,256]{2,1,0:T(8,128)S(1)} %collective-permute-done.3.refs_0_, f32[2,32,256]{2,1,0:T(8,128)S(1)} %collective-permute-done.4.refs_1_, ...), custom_call_target="tpu_custom_call", output_to_operand_aliasing={{}: (1, {})} | custom-call | flops 262144 | bytes 1048576 | tf_op jit(solution)/shard_map/pallas_call | solution.py:367
  (1 shorter events, 0.0 us)
Async XLA Ops:
  0.0 15.0 %copy-start = (f32[32,32,256]{2,1,0:T(8,128)S(1)}, f32[32,32,256]{2,1,0:T(8,128)}, u32[]{:S(2)}) copy-start(f32[32,32,256]{2,1,0:T(8,128)} %state_ref.3) | copy-start | bytes 3145732
  2.4 9.2 %copy-start.1 = (s32[1,32,512]{2,1,0:T(8,128)S(1)}, s32[1,32,512]{2,1,0:T(8,128)}, u32[]{:S(2)}) copy-start(s32[1,32,512]{2,1,0:T(8,128)} %param.10) | copy-start | bytes 196612
  2.4 9.2 %copy-start.2 = (f32[1,32,512]{2,1,0:T(8,128)S(1)}, f32[1,32,512]{2,1,0:T(8,128)}, u32[]{:S(2)}) copy-start(f32[1,32,512]{2,1,0:T(8,128)} %param.12) | copy-start | bytes 196612
  2.4 9.2 %copy-start.3 = (f32[1,32,512]{2,1,0:T(8,128)S(1)}, f32[1,32,512]{2,1,0:T(8,128)}, u32[]{:S(2)}) copy-start(f32[1,32,512]{2,1,0:T(8,128)} %param.13) | copy-start | bytes 196612
  2.5 15.1 %all-to-all-start = ((f32[8,2,32,256]{3,2,1,0:T(8,128)}), f32[8,2,32,256]{3,2,1,0:T(8,128)S(1)}, u32[]{:S(2)}, u32[]{:S(2)}) async-start(f32[8,2,32,256]{3,2,1,0:T(8,128)} %get-tuple-element.18), calls=%async_computation | async-start | bytes 1048576 | tf_op jit(solution)/shard_map/all_to_all | solution.py:330
  7.8 6.5 %collective-permute-start = (f32[2,32,256]{2,1,0:T(8,128)S(1)}, f32[2,32,256]{2,1,0:T(8,128)S(1)}, u32[]{:S(2)}, u32[]{:S(2)}) collective-permute-start(f32[2,32,256]{2,1,0:T(8,128)S(1)} %get-tuple-element.20), channel_id=1, source_target_pairs={{0,1},{1,2},{2,3},{3,0},{4,5},{5,6},{6,7},{7,4},{8,9},{9,10},{10,1... | collective-permute-start | bytes 196616 | tf_op jit(solution)/shard_map/ppermute | solution.py:331
  9.3 5.6 %collective-permute-start.1 = (f32[2,32,256]{2,1,0:T(8,128)S(1)}, f32[2,32,256]{2,1,0:T(8,128)S(1)}, u32[]{:S(2)}, u32[]{:S(2)}) collective-permute-start(f32[2,32,256]{2,1,0:T(8,128)S(1)} %get-tuple-element.21), channel_id=1, source_target_pairs={{1,0},{2,1},{3,2},{0,3},{5,4},{6,5},{7,6},{4,7},{9,8},{10,9},{11,1... | collective-permute-start | bytes 196616 | tf_op jit(solution)/shard_map/ppermute | solution.py:332
  11.6 0.7 %copy-start.6 = (s32[1,32]{1,0:T(1,128)S(1)}, s32[1,32]{1,0:T(1,128)}, u32[]{:S(2)}) copy-start(s32[1,32]{1,0:T(1,128)} %count_ref.1) | copy-start | bytes 388
  12.3 2.7 %copy-start.5 = (f32[256]{0:T(256)S(1)}, f32[256]{0:T(256)}, u32[]{:S(2)}) copy-start(f32[256]{0:T(256)} %adv_ref.1) | copy-start | bytes 3076
  15.0 0.7 %copy-start.4 = (f32[256]{0:T(256)S(1)}, f32[256]{0:T(256)}, u32[]{:S(2)}) copy-start(f32[256]{0:T(256)} %diff_ref.1) | copy-start | bytes 3076
  17.5 13.2 %all-to-all-start.1 = ((f32[8,2,32,256]{3,2,1,0:T(8,128)}), f32[8,2,32,256]{3,2,1,0:T(8,128)S(1)}, u32[]{:S(2)}, u32[]{:S(2)}) async-start(f32[8,2,32,256]{3,2,1,0:T(8,128)} %shard_map.76), calls=%async_computation.1 | async-start | bytes 1048576 | tf_op jit(solution)/shard_map/all_to_all | solution.py:348
  30.7 18.6 %all-to-all-start.2 = ((f32[8,2,32,256]{3,2,1,0:T(8,128)}), f32[8,2,32,256]{3,2,1,0:T(8,128)S(1)}, u32[]{:S(2)}, u32[]{:S(2)}) async-start(f32[8,2,32,256]{3,2,1,0:T(8,128)} %get-tuple-element.23), calls=%async_computation.2 | async-start | bytes 1048576 | tf_op jit(solution)/shard_map/all_to_all | solution.py:351
  42.5 5.0 %collective-permute-start.2 = (f32[2,32,256]{2,1,0:T(8,128)S(1)}, f32[2,32,256]{2,1,0:T(8,128)S(1)}, u32[]{:S(2)}, u32[]{:S(2)}) collective-permute-start(f32[2,32,256]{2,1,0:T(8,128)S(1)} %get-tuple-element.22), channel_id=1, source_target_pairs={{0,28},{4,24},{8,20},{12,16},{16,12},{20,8},{24,4},{28,0},{1,29},{... | collective-permute-start | bytes 196616 | tf_op jit(solution)/shard_map/ppermute | solution.py:47
  44.9 4.3 %collective-permute-start.3 = (f32[2,32,256]{2,1,0:T(8,128)S(1)}, f32[2,32,256]{2,1,0:T(8,128)S(1)}, u32[]{:S(2)}, u32[]{:S(2)}) collective-permute-start(f32[2,32,256]{2,1,0:T(8,128)S(1)} %get-tuple-element.24), channel_id=1, source_target_pairs={{0,4},{4,0},{8,12},{12,8},{16,20},{20,16},{24,28},{28,24},{1,5},{5... | collective-permute-start | bytes 196616 | tf_op jit(solution)/shard_map/ppermute | solution.py:47
  45.3 5.9 %collective-permute-start.4 = (f32[2,32,256]{2,1,0:T(8,128)S(1)}, f32[2,32,256]{2,1,0:T(8,128)S(1)}, u32[]{:S(2)}, u32[]{:S(2)}) collective-permute-start(f32[2,32,256]{2,1,0:T(8,128)S(1)} %get-tuple-element.25), channel_id=1, source_target_pairs={{0,24},{4,28},{8,16},{12,20},{16,8},{20,12},{24,0},{28,4},{1,25},{... | collective-permute-start | bytes 196616 | tf_op jit(solution)/shard_map/ppermute | solution.py:47
  45.6 5.9 %collective-permute-start.5 = (f32[2,32,256]{2,1,0:T(8,128)S(1)}, f32[2,32,256]{2,1,0:T(8,128)S(1)}, u32[]{:S(2)}, u32[]{:S(2)}) collective-permute-start(f32[2,32,256]{2,1,0:T(8,128)S(1)} %get-tuple-element.26), channel_id=1, source_target_pairs={{0,8},{4,12},{8,0},{12,4},{16,24},{20,28},{24,16},{28,20},{1,9},{5... | collective-permute-start | bytes 196616 | tf_op jit(solution)/shard_map/ppermute | solution.py:47
  47.3 4.5 %collective-permute-start.6 = (f32[2,32,256]{2,1,0:T(8,128)S(1)}, f32[2,32,256]{2,1,0:T(8,128)S(1)}, u32[]{:S(2)}, u32[]{:S(2)}) collective-permute-start(f32[2,32,256]{2,1,0:T(8,128)S(1)} %get-tuple-element.27), channel_id=1, source_target_pairs={{0,12},{4,8},{8,4},{12,0},{16,28},{20,24},{24,20},{28,16},{1,13},{... | collective-permute-start | bytes 196616 | tf_op jit(solution)/shard_map/ppermute | solution.py:47
  47.5 4.7 %collective-permute-start.7 = (f32[2,32,256]{2,1,0:T(8,128)S(1)}, f32[2,32,256]{2,1,0:T(8,128)S(1)}, u32[]{:S(2)}, u32[]{:S(2)}) collective-permute-start(f32[2,32,256]{2,1,0:T(8,128)S(1)} %get-tuple-element.28), channel_id=1, source_target_pairs={{0,16},{4,20},{8,24},{12,28},{16,0},{20,4},{24,8},{28,12},{1,17},{... | collective-permute-start | bytes 196616 | tf_op jit(solution)/shard_map/ppermute | solution.py:47
  49.3 4.3 %collective-permute-start.8 = (f32[2,32,256]{2,1,0:T(8,128)S(1)}, f32[2,32,256]{2,1,0:T(8,128)S(1)}, u32[]{:S(2)}, u32[]{:S(2)}) collective-permute-start(f32[2,32,256]{2,1,0:T(8,128)S(1)} %get-tuple-element.29), channel_id=1, source_target_pairs={{0,20},{4,16},{8,28},{12,24},{16,4},{20,0},{24,12},{28,8},{1,21},{... | collective-permute-start | bytes 196616 | tf_op jit(solution)/shard_map/ppermute | solution.py:47

commit v5 on v4

--- a/solution.py
+++ b/solution.py
@@ -69,12 +69,13 @@
 
 
 def square_by_rows(x):
-    a, b = split(x, 3), split(x.T, 3)
-    lhs = jnp.concatenate([a[2], a[0], a[1], a[1], a[0], a[0]], axis=1)
-    rhs = jnp.concatenate([b[0], b[2], b[1], b[0], b[1], b[0]], axis=0)
+    p0, p1, p2 = split(x, 3)
+    lhs = jnp.concatenate([p2, p0, p1, p1, p0, p0], axis=1)
+    rhs = jnp.concatenate([p0, p2, p1, p0, p1, p0], axis=1)
     middle = lhs.shape[0] // 2
-    upper = jnp.dot(lhs[:middle], rhs, preferred_element_type=jnp.float32)
-    lower = jnp.dot(lhs[middle:], rhs, preferred_element_type=jnp.float32)
+    dims = (((1,), (1,)), ((), ()))
+    upper = lax.dot_general(lhs[:middle], rhs, dims, preferred_element_type=jnp.float32)
+    lower = lax.dot_general(lhs[middle:], rhs, dims, preferred_element_type=jnp.float32)
     return jnp.concatenate([upper, lower], axis=0)
 
 
@@ -98,7 +99,7 @@
     return [pl.ds(first, rows) for first in range(0, members, rows)]
 
 
-def inner_kernel(state_ref, diff_ref, adv_ref, out_ref, low_ref, high_ref, held_ref, num_ref, sems):
+def inner_kernel(state_ref, diff_ref, adv_ref, out_ref, rest_ref, low_ref, high_ref, held_ref, num_ref, sems):
     members, columns, entries = state_ref.shape
     groups, half, _, _ = out_ref.shape
     quarter = columns // 4
@@ -118,22 +119,19 @@
         x = jnp.swapaxes(held_ref[part], 0, 1)
         low_ref[:, part] = x[:2]
         high_ref[:, part] = x[columns - 2 :]
+        rest_ref[0, :, part] = x[: quarter + 2]
+        rest_ref[1, :, part] = x[columns - quarter - 2 :]
         x = x[quarter - 2 : columns - quarter + 2]
         x = stencil(stencil(x, diffusion, advection), diffusion, advection)
         out_ref[:, :, part] = x.reshape(groups, half, part.size, entries)
 
 
-def outer_kernel(obs_ref, state_ref, before_ref, after_ref, diff_ref, adv_ref, out_ref, turned_ref):
+def outer_kernel(obs_ref, rest_ref, before_ref, after_ref, diff_ref, adv_ref, out_ref):
     del obs_ref
-    columns = state_ref.shape[1]
-    quarter = columns // 4
-    turned_ref[2 : columns + 2] = jnp.swapaxes(state_ref[...], 0, 1)
-    turned_ref[:2] = before_ref[...]
-    turned_ref[columns + 2 :] = after_ref[...]
     diffusion = diff_ref[...][None]
     advection = adv_ref[...][None]
-    low = turned_ref[: quarter + 4]
-    high = turned_ref[columns - quarter :]
+    low = jnp.concatenate([before_ref[...], rest_ref[0]], axis=0)
+    high = jnp.concatenate([rest_ref[1], after_ref[...]], axis=0)
     low = stencil(stencil(low, diffusion, advection), diffusion, advection)
     high = stencil(stencil(high, diffusion, advection), diffusion, advection)
     out_ref[...] = jnp.concatenate([low, high], axis=0).reshape(out_ref.shape)
@@ -311,13 +309,14 @@
     half = columns // groups // 2
     size = background.size
     block = (half, local, entries)
+    rest = jax.ShapeDtypeStruct((2, columns // 4 + 2, local, entries), jnp.float32)
     edge = jax.ShapeDtypeStruct((2, local, entries), jnp.float32)
     me = lax.axis_index("mem")[None].astype(jnp.int32)
     pieces = len(pieces_of(local))
 
-    inner, low, high = call(
+    inner, rest, low, high = call(
         inner_kernel,
-        [jax.ShapeDtypeStruct((groups, *block), jnp.float32), edge, edge],
+        [jax.ShapeDtypeStruct((groups, *block), jnp.float32), rest, edge, edge],
         20 * size,
         8 * size,
         in_specs=[HBM] * 3,
@@ -343,8 +342,7 @@
         20 * size,
         8 * size,
         in_specs=[VMEM] * 6,
-        scratch_shapes=[pltpu.VMEM((columns + 4, local, entries), jnp.float32)],
-    )(obs, background, before, after, diffusion[None], advection[None])
+    )(obs, rest, before, after, diffusion[None], advection[None])
     outer = lax.all_to_all(outer, "mem", split_axis=0, concat_axis=0, tiled=True)
 
     inner, done = analyse(inner, obs, 0, me, obs[0], False)

time: 55 us -> 55.2 us (level)
    pallas_call x2, Pallas kernels: 16.7 us -> 17.3 us  [analyse(): call(kernel, [block] * groups + [token] if apart else [whole, token], col...]
    unnamed x14 -> x12, local copies, waits for them, and re-layouts: 1.34 us -> 1.34 us
  transfers between devices with their start and end apart: 12 -> 12, of which waited for: 10 -> 10; matrix products, arithmetic and copies ran while one was open for 0% -> 0% of each run, Pallas kernels for 36% -> 37%
where the time goes in v5:
time: 55.2 us; the launch traced here: 54.8 us
  Pallas kernels  23.5 us (43%)
  starting transfers between devices  22.8 us (41%)
  waiting for transfers between devices  6.87 us (12%)
  local copies, waits for them, and re-layouts  1.35 us (2%)
    pallas_call x2, Pallas kernels, analyse(): call(kernel, [block] * groups + [token] if apart else [whole, token], col...  17.3 us
    all_to_all x2, starting transfers between devices, body(): lax.all_to_all(inner, 'mem', split_axis=0, concat_axis=0, tiled=True)  8.99 us
    ppermute x7, starting transfers between devices, exchange(): out.append(lax.ppermute(blocks[k], 'mem', pairs) if k else blocks[0])  6.51 us
    ppermute x7, waiting for transfers between devices, exchange(): out.append(lax.ppermute(blocks[k], 'mem', pairs) if k else blocks[0])  3.6 us
    all_to_all x1, starting transfers between devices, body(): lax.all_to_all(outer, 'mem', split_axis=0, concat_axis=0, tiled=True)  3.49 us
    pallas_call x1, Pallas kernels, body(): call(inner_kernel, [jax.ShapeDtypeStruct((groups, *block), jnp.float32),...  2.34 us
    ppermute x1, starting transfers between devices, body(): lax.ppermute(low, 'tile', [((i + 1) % tiles, i) for i in range(tiles)])  2.25 us
    ppermute x1, starting transfers between devices, body(): lax.ppermute(high, 'tile', [(i, (i + 1) % tiles) for i in range(tiles)])  1.58 us
  transfers between devices with their start and end apart: 12, of which 10 were waited for; matrix products, arithmetic and copies ran while one was open for 0% of the time, Pallas kernels for 37%

profile of v5, /device:TPU:0, one launch (start us, length us, event | category | flops | bytes accessed | tf_op | source)
XLA Modules:
  0.0 54.8 jit_solution(10509506253962332613)
XLA Ops:
  0.0 2.3 %shard_map.74 = (f32[8,2,32,256]{3,2,1,0:T(8,128)}, f32[2,10,32,256]{3,2,1,0:T(8,128)S(1)}, f32[2,32,256]{2,1,0:T(8,128)S(1)}, f32[2,32,256]{2,1,0:T(8,128)S(1)}) custom-call(f32[32,32,256]{2,1,0:T(8,128)} %state_ref.1, f32[256]{0:T(256)} %diff_ref.1, f32[256]{0:T(256)} %adv_ref.1), custom_call_target="tpu_custom_call" | custom-call | flops 5242880 | bytes 2097152 | tf_op jit(solution)/shard_map/pallas_call | solution.py:317
  2.3 0.0 copy-start
  2.4 0.0 copy-start.1
  2.4 0.0 copy-start.2
  2.4 5.3 %all-to-all-start = ((f32[8,2,32,256]{3,2,1,0:T(8,128)}), f32[8,2,32,256]{3,2,1,0:T(8,128)S(1)}, u32[]{:S(2)}, u32[]{:S(2)}) async-start(f32[8,2,32,256]{3,2,1,0:T(8,128)} %get-tuple-element.19), calls=%async_computation | async-start | bytes 1048576 | tf_op jit(solution)/shard_map/all_to_all | solution.py:329
  7.7 1.6 %collective-permute-start = (f32[2,32,256]{2,1,0:T(8,128)S(1)}, f32[2,32,256]{2,1,0:T(8,128)S(1)}, u32[]{:S(2)}, u32[]{:S(2)}) collective-permute-start(f32[2,32,256]{2,1,0:T(8,128)S(1)} %get-tuple-element.22), channel_id=1, source_target_pairs={{0,1},{1,2},{2,3},{3,0},{4,5},{5,6},{6,7},{7,4},{8,9},{9,10},{10,1... | collective-permute-start | bytes 196616 | tf_op jit(solution)/shard_map/ppermute | solution.py:330
  9.3 2.2 %collective-permute-start.1 = (f32[2,32,256]{2,1,0:T(8,128)S(1)}, f32[2,32,256]{2,1,0:T(8,128)S(1)}, u32[]{:S(2)}, u32[]{:S(2)}) collective-permute-start(f32[2,32,256]{2,1,0:T(8,128)S(1)} %get-tuple-element.23), channel_id=1, source_target_pairs={{1,0},{2,1},{3,2},{0,3},{5,4},{6,5},{7,6},{4,7},{9,8},{10,9},{11,1... | collective-permute-start | bytes 196616 | tf_op jit(solution)/shard_map/ppermute | solution.py:331
  11.5 0.0 copy-start.5
  11.5 0.0 copy-done
  11.5 0.0 copy-done.1
  11.5 0.0 copy-done.2
  11.5 0.6 %copy-done.5 = s32[1,32]{1,0:T(1,128)S(1)} copy-done((s32[1,32]{1,0:T(1,128)S(1)}, s32[1,32]{1,0:T(1,128)}, u32[]{:S(2)}) %copy-start.5) | copy-done | bytes 152
  12.2 0.0 copy-start.4
  12.2 0.9 %shard_map.73.obs_ref = f32[4,8,256]{2,1,0:T(8,128)S(1)} custom-call(s32[1]{0:T(128)} %bitcast.me_ref, s32[1,32]{1,0:T(1,128)S(1)} %copy-done.5, s32[32,512]{1,0:T(8,128)S(1)} %bitcast.8, f32[32,512]{1,0:T(8,128)S(1)} %bitcast.9, f32[32,512]{1,0:T(8,128)S(1)} %bitcast.10), custom_call_target="tpu_custom_call" | custom-call | flops 16777216 | bytes 196608 | tf_op jit(solution)/shard_map/pallas_call | solution.py:332
  13.1 1.1 %collective-permute-done.before_ref = f32[2,32,256]{2,1,0:T(8,128)S(1)} collective-permute-done((f32[2,32,256]{2,1,0:T(8,128)S(1)}, f32[2,32,256]{2,1,0:T(8,128)S(1)}, u32[]{:S(2)}, u32[]{:S(2)}) %collective-permute-start) | collective-permute-done | bytes 65568 | tf_op jit(solution)/shard_map/ppermute | solution.py:330
  14.2 0.7 %collective-permute-done.1.after_ref = f32[2,32,256]{2,1,0:T(8,128)S(1)} collective-permute-done((f32[2,32,256]{2,1,0:T(8,128)S(1)}, f32[2,32,256]{2,1,0:T(8,128)S(1)}, u32[]{:S(2)}, u32[]{:S(2)}) %collective-permute-start.1) | collective-permute-done | bytes 65568 | tf_op jit(solution)/shard_map/ppermute | solution.py:331
  14.9 0.0 copy-start.3
  14.9 0.0 copy-done.4
  14.9 0.7 %copy-done.3 = f32[256]{0:T(256)S(1)} copy-done((f32[256]{0:T(256)S(1)}, f32[256]{0:T(256)}, u32[]{:S(2)}) %copy-start.3) | copy-done | bytes 1048
  15.6 1.1 %shard_map.76 = f32[8,2,32,256]{3,2,1,0:T(8,128)} custom-call(f32[4,8,256]{2,1,0:T(8,128)S(1)} %shard_map.73.obs_ref, f32[2,10,32,256]{3,2,1,0:T(8,128)S(1)} %get-tuple-element.21.rest_ref, f32[2,32,256]{2,1,0:T(8,128)S(1)} %collective-permute-done.before_ref, f32[2,32,256]{2,1,0:T(8,128)S(1)} %collective-permute-done.1.after_ref, f32[1,256]{1,0:T(1,128)S(1)} %bitcast.11, ...), custom_call_target="tpu_custom_call" | custom-call | flops 5242880 | bytes 2097152 | tf_op jit(solution)/shard_map/pallas_call | solution.py:339
  16.7 0.7 %all-to-all-done.states_ref = f32[8,2,32,256]{3,2,1,0:T(8,128)S(1)} async-done(((f32[8,2,32,256]{3,2,1,0:T(8,128)}), f32[8,2,32,256]{3,2,1,0:T(8,128)S(1)}, u32[]{:S(2)}, u32[]{:S(2)}) %all-to-all-start) | async-done | bytes 524320 | tf_op jit(solution)/shard_map/all_to_all | solution.py:329
  17.4 3.5 %all-to-all-start.1 = ((f32[8,2,32,256]{3,2,1,0:T(8,128)}), f32[8,2,32,256]{3,2,1,0:T(8,128)S(1)}, u32[]{:S(2)}, u32[]{:S(2)}) async-start(f32[8,2,32,256]{3,2,1,0:T(8,128)} %shard_map.76), calls=%async_computation.1 | async-start | bytes 1048576 | tf_op jit(solution)/shard_map/all_to_all | solution.py:346
  20.9 8.9 %shard_map.75 = (f32[8,2,32,256]{3,2,1,0:T(8,128)}, f32[8,256]{1,0:T(8,128)S(1)}) custom-call(s32[1]{0:T(128)} %bitcast.me_ref, f32[8,256]{1,0:T(8,128)S(1)} %slice_bitcast_fusion.after_ref, f32[4,8,256]{2,1,0:T(8,128)S(1)} %shard_map.73.obs_ref, f32[8,2,32,256]{3,2,1,0:T(8,128)S(1)} %all-to-all-done.states_ref), custom_call_target="tpu_custom_call" | custom-call | flops 6039797760 | bytes 1048576 | tf_op jit(solution)/shard_map/pallas_call | solution.py:295
  29.8 0.8 %all-to-all-done.1.states_ref = f32[8,2,32,256]{3,2,1,0:T(8,128)S(1)} async-done(((f32[8,2,32,256]{3,2,1,0:T(8,128)}), f32[8,2,32,256]{3,2,1,0:T(8,128)S(1)}, u32[]{:S(2)}, u32[]{:S(2)}) %all-to-all-start.1) | async-done | bytes 524320 | tf_op jit(solution)/shard_map/all_to_all | solution.py:346
  30.6 3.7 %all-to-all-start.2 = ((f32[8,2,32,256]{3,2,1,0:T(8,128)}), f32[8,2,32,256]{3,2,1,0:T(8,128)S(1)}, u32[]{:S(2)}, u32[]{:S(2)}) async-start(f32[8,2,32,256]{3,2,1,0:T(8,128)} %get-tuple-element.25), calls=%async_computation.2 | async-start | bytes 1048576 | tf_op jit(solution)/shard_map/all_to_all | solution.py:349
  34.3 8.5 %shard_map.77 = (f32[2,32,256]{2,1,0:T(8,128)S(1)}, f32[2,32,256]{2,1,0:T(8,128)S(1)}, f32[2,32,256]{2,1,0:T(8,128)S(1)}, f32[2,32,256]{2,1,0:T(8,128)S(1)}, f32...) custom-call(s32[1]{0:T(128)} %bitcast.me_ref, ...), custom_call_target="tpu_custom_call" | custom-call | flops 6039797760 | bytes 1048576 | tf_op jit(solution)/shard_map/pallas_call | solution.py:295
  42.8 2.4 %collective-permute-start.2 = (f32[2,32,256]{2,1,0:T(8,128)S(1)}, f32[2,32,256]{2,1,0:T(8,128)S(1)}, u32[]{:S(2)}, u32[]{:S(2)}) collective-permute-start(f32[2,32,256]{2,1,0:T(8,128)S(1)} %get-tuple-element.24), channel_id=1, source_target_pairs={{0,28},{4,24},{8,20},{12,16},{16,12},{20,8},{24,4},{28,0},{1,29},{... | collective-permute-start | bytes 196616 | tf_op jit(solution)/shard_map/ppermute | solution.py:47
  45.2 0.4 collective-permute-start.3
  45.5 0.3 collective-permute-start.4
  45.8 1.7 %collective-permute-start.5 = (f32[2,32,256]{2,1,0:T(8,128)S(1)}, f32[2,32,256]{2,1,0:T(8,128)S(1)}, u32[]{:S(2)}, u32[]{:S(2)}) collective-permute-start(f32[2,32,256]{2,1,0:T(8,128)S(1)} %get-tuple-element.28), channel_id=1, source_target_pairs={{0,8},{4,12},{8,0},{12,4},{16,24},{20,28},{24,16},{28,20},{1,9},{5... | collective-permute-start | bytes 196616 | tf_op jit(solution)/shard_map/ppermute | solution.py:47
  47.5 0.0 collective-permute-start.6
  47.5 0.2 collective-permute-done.2.after_ref.refs_2_
  47.7 1.7 %collective-permute-start.7 = (f32[2,32,256]{2,1,0:T(8,128)S(1)}, f32[2,32,256]{2,1,0:T(8,128)S(1)}, u32[]{:S(2)}, u32[]{:S(2)}) collective-permute-start(f32[2,32,256]{2,1,0:T(8,128)S(1)} %get-tuple-element.30), channel_id=1, source_target_pairs={{0,16},{4,20},{8,24},{12,28},{16,0},{20,4},{24,8},{28,12},{1,17},{... | collective-permute-start | bytes 196616 | tf_op jit(solution)/shard_map/ppermute | solution.py:47
  49.5 0.0 collective-permute-done.3.refs_0_
  49.5 0.0 collective-permute-start.8
  49.5 0.0 all-to-all-done.2.inner_ref
  49.5 0.8 %shard_map.78.held_ref = f32[32,32,256]{2,1,0:T(8,128)} custom-call(f32[2,32,256]{2,1,0:T(8,128)S(1)} %collective-permute-done.2.after_ref.refs_2_, f32[8,2,32,256]{3,2,1,0:T(8,128)S(1)} %all-to-all-done.2.inner_ref), custom_call_target="tpu_custom_call" | custom-call | flops 262144 | bytes 1048576 | tf_op jit(solution)/shard_map/pallas_call | solution.py:353
  50.3 1.0 %collective-permute-done.4.refs_1_ = f32[2,32,256]{2,1,0:T(8,128)S(1)} collective-permute-done((f32[2,32,256]{2,1,0:T(8,128)S(1)}, f32[2,32,256]{2,1,0:T(8,128)S(1)}, u32[]{:S(2)}, u32[]{:S(2)}) %collective-permute-start.4) | collective-permute-done | bytes 65568 | tf_op jit(solution)/shard_map/ppermute | solution.py:47
  51.4 0.3 collective-permute-done.5.refs_3_
  51.7 0.3 collective-permute-done.6.refs_4_
  52.0 0.4 collective-permute-done.7.refs_5_
  52.4 1.4 %collective-permute-done.8.refs_6_ = f32[2,32,256]{2,1,0:T(8,128)S(1)} collective-permute-done((f32[2,32,256]{2,1,0:T(8,128)S(1)}, f32[2,32,256]{2,1,0:T(8,128)S(1)}, u32[]{:S(2)}, u32[]{:S(2)}) %collective-permute-start.8) | collective-permute-done | bytes 65568 | tf_op jit(solution)/shard_map/ppermute | solution.py:47
  53.7 0.9 %shard_map.79 = f32[32,32,256]{2,1,0:T(8,128)} custom-call(s32[1]{0:T(128)} %bitcast.me_ref, f32[32,32,256]{2,1,0:T(8,128)} %shard_map.78.held_ref, f32[2,32,256]{2,1,0:T(8,128)S(1)} %collective-permute-done.3.refs_0_, f32[2,32,256]{2,1,0:T(8,128)S(1)} %collective-permute-done.4.refs_1_, ...), custom_call_target="tpu_custom_call", output_to_operand_aliasing={{}: (1, {})} | custom-call | flops 262144 | bytes 1048576 | tf_op jit(solution)/shard_map/pallas_call | solution.py:365
  (1 shorter events, 0.0 us)
Async XLA Ops:
  2.3 9.2 %copy-start = (s32[1,32,512]{2,1,0:T(8,128)S(1)}, s32[1,32,512]{2,1,0:T(8,128)}, u32[]{:S(2)}) copy-start(s32[1,32,512]{2,1,0:T(8,128)} %param.10) | copy-start | bytes 196612
  2.4 9.2 %copy-start.1 = (f32[1,32,512]{2,1,0:T(8,128)S(1)}, f32[1,32,512]{2,1,0:T(8,128)}, u32[]{:S(2)}) copy-start(f32[1,32,512]{2,1,0:T(8,128)} %param.12) | copy-start | bytes 196612
  2.4 9.2 %copy-start.2 = (f32[1,32,512]{2,1,0:T(8,128)S(1)}, f32[1,32,512]{2,1,0:T(8,128)}, u32[]{:S(2)}) copy-start(f32[1,32,512]{2,1,0:T(8,128)} %param.13) | copy-start | bytes 196612
  2.4 15.1 %all-to-all-start = ((f32[8,2,32,256]{3,2,1,0:T(8,128)}), f32[8,2,32,256]{3,2,1,0:T(8,128)S(1)}, u32[]{:S(2)}, u32[]{:S(2)}) async-start(f32[8,2,32,256]{3,2,1,0:T(8,128)} %get-tuple-element.19), calls=%async_computation | async-start | bytes 1048576 | tf_op jit(solution)/shard_map/all_to_all | solution.py:329
  7.7 6.5 %collective-permute-start = (f32[2,32,256]{2,1,0:T(8,128)S(1)}, f32[2,32,256]{2,1,0:T(8,128)S(1)}, u32[]{:S(2)}, u32[]{:S(2)}) collective-permute-start(f32[2,32,256]{2,1,0:T(8,128)S(1)} %get-tuple-element.22), channel_id=1, source_target_pairs={{0,1},{1,2},{2,3},{3,0},{4,5},{5,6},{6,7},{7,4},{8,9},{9,10},{10,1... | collective-permute-start | bytes 196616 | tf_op jit(solution)/shard_map/ppermute | solution.py:330
  9.3 5.6 %collective-permute-start.1 = (f32[2,32,256]{2,1,0:T(8,128)S(1)}, f32[2,32,256]{2,1,0:T(8,128)S(1)}, u32[]{:S(2)}, u32[]{:S(2)}) collective-permute-start(f32[2,32,256]{2,1,0:T(8,128)S(1)} %get-tuple-element.23), channel_id=1, source_target_pairs={{1,0},{2,1},{3,2},{0,3},{5,4},{6,5},{7,6},{4,7},{9,8},{10,9},{11,1... | collective-permute-start | bytes 196616 | tf_op jit(solution)/shard_map/ppermute | solution.py:331
  11.5 0.7 %copy-start.5 = (s32[1,32]{1,0:T(1,128)S(1)}, s32[1,32]{1,0:T(1,128)}, u32[]{:S(2)}) copy-start(s32[1,32]{1,0:T(1,128)} %count_ref.1) | copy-start | bytes 388
  12.2 2.7 %copy-start.4 = (f32[256]{0:T(256)S(1)}, f32[256]{0:T(256)}, u32[]{:S(2)}) copy-start(f32[256]{0:T(256)} %adv_ref.1) | copy-start | bytes 3076
  14.9 0.7 %copy-start.3 = (f32[256]{0:T(256)S(1)}, f32[256]{0:T(256)}, u32[]{:S(2)}) copy-start(f32[256]{0:T(256)} %diff_ref.1) | copy-start | bytes 3076
  17.4 13.2 %all-to-all-start.1 = ((f32[8,2,32,256]{3,2,1,0:T(8,128)}), f32[8,2,32,256]{3,2,1,0:T(8,128)S(1)}, u32[]{:S(2)}, u32[]{:S(2)}) async-start(f32[8,2,32,256]{3,2,1,0:T(8,128)} %shard_map.76), calls=%async_computation.1 | async-start | bytes 1048576 | tf_op jit(solution)/shard_map/all_to_all | solution.py:346
  30.6 18.9 %all-to-all-start.2 = ((f32[8,2,32,256]{3,2,1,0:T(8,128)}), f32[8,2,32,256]{3,2,1,0:T(8,128)S(1)}, u32[]{:S(2)}, u32[]{:S(2)}) async-start(f32[8,2,32,256]{3,2,1,0:T(8,128)} %get-tuple-element.25), calls=%async_computation.2 | async-start | bytes 1048576 | tf_op jit(solution)/shard_map/all_to_all | solution.py:349
  42.8 5.0 %collective-permute-start.2 = (f32[2,32,256]{2,1,0:T(8,128)S(1)}, f32[2,32,256]{2,1,0:T(8,128)S(1)}, u32[]{:S(2)}, u32[]{:S(2)}) collective-permute-start(f32[2,32,256]{2,1,0:T(8,128)S(1)} %get-tuple-element.24), channel_id=1, source_target_pairs={{0,28},{4,24},{8,20},{12,16},{16,12},{20,8},{24,4},{28,0},{1,29},{... | collective-permute-start | bytes 196616 | tf_op jit(solution)/shard_map/ppermute | solution.py:47
  45.2 4.3 %collective-permute-start.3 = (f32[2,32,256]{2,1,0:T(8,128)S(1)}, f32[2,32,256]{2,1,0:T(8,128)S(1)}, u32[]{:S(2)}, u32[]{:S(2)}) collective-permute-start(f32[2,32,256]{2,1,0:T(8,128)S(1)} %get-tuple-element.26), channel_id=1, source_target_pairs={{0,4},{4,0},{8,12},{12,8},{16,20},{20,16},{24,28},{28,24},{1,5},{5... | collective-permute-start | bytes 196616 | tf_op jit(solution)/shard_map/ppermute | solution.py:47
  45.5 5.9 %collective-permute-start.4 = (f32[2,32,256]{2,1,0:T(8,128)S(1)}, f32[2,32,256]{2,1,0:T(8,128)S(1)}, u32[]{:S(2)}, u32[]{:S(2)}) collective-permute-start(f32[2,32,256]{2,1,0:T(8,128)S(1)} %get-tuple-element.27), channel_id=1, source_target_pairs={{0,24},{4,28},{8,16},{12,20},{16,8},{20,12},{24,0},{28,4},{1,25},{... | collective-permute-start | bytes 196616 | tf_op jit(solution)/shard_map/ppermute | solution.py:47
  45.8 5.9 %collective-permute-start.5 = (f32[2,32,256]{2,1,0:T(8,128)S(1)}, f32[2,32,256]{2,1,0:T(8,128)S(1)}, u32[]{:S(2)}, u32[]{:S(2)}) collective-permute-start(f32[2,32,256]{2,1,0:T(8,128)S(1)} %get-tuple-element.28), channel_id=1, source_target_pairs={{0,8},{4,12},{8,0},{12,4},{16,24},{20,28},{24,16},{28,20},{1,9},{5... | collective-permute-start | bytes 196616 | tf_op jit(solution)/shard_map/ppermute | solution.py:47
  47.5 4.5 %collective-permute-start.6 = (f32[2,32,256]{2,1,0:T(8,128)S(1)}, f32[2,32,256]{2,1,0:T(8,128)S(1)}, u32[]{:S(2)}, u32[]{:S(2)}) collective-permute-start(f32[2,32,256]{2,1,0:T(8,128)S(1)} %get-tuple-element.29), channel_id=1, source_target_pairs={{0,12},{4,8},{8,4},{12,0},{16,28},{20,24},{24,20},{28,16},{1,13},{... | collective-permute-start | bytes 196616 | tf_op jit(solution)/shard_map/ppermute | solution.py:47
  47.7 4.6 %collective-permute-start.7 = (f32[2,32,256]{2,1,0:T(8,128)S(1)}, f32[2,32,256]{2,1,0:T(8,128)S(1)}, u32[]{:S(2)}, u32[]{:S(2)}) collective-permute-start(f32[2,32,256]{2,1,0:T(8,128)S(1)} %get-tuple-element.30), channel_id=1, source_target_pairs={{0,16},{4,20},{8,24},{12,28},{16,0},{20,4},{24,8},{28,12},{1,17},{... | collective-permute-start | bytes 196616 | tf_op jit(solution)/shard_map/ppermute | solution.py:47
  49.5 4.3 %collective-permute-start.8 = (f32[2,32,256]{2,1,0:T(8,128)S(1)}, f32[2,32,256]{2,1,0:T(8,128)S(1)}, u32[]{:S(2)}, u32[]{:S(2)}) collective-permute-start(f32[2,32,256]{2,1,0:T(8,128)S(1)} %get-tuple-element.31), channel_id=1, source_target_pairs={{0,20},{4,16},{8,28},{12,24},{16,4},{20,0},{24,12},{28,8},{1,21},{... | collective-permute-start | bytes 196616 | tf_op jit(solution)/shard_map/ppermute | solution.py:47

commit v6 on v5

--- a/solution.py
+++ b/solution.py
@@ -23,6 +23,10 @@
     )
 
 
+def in_hbm(x):
+    return pltpu.with_memory_space_constraint(x, pltpu.HBM)
+
+
 def target(me, k, groups):
     if groups & (groups - 1) == 0:
         return me ^ k
@@ -42,9 +46,9 @@
 def exchange(blocks):
     groups = len(blocks)
     out = []
-    for k in issue_order(groups):
+    for k, block in zip(issue_order(groups), blocks):
         pairs = [(i, i ^ k if groups & (groups - 1) == 0 else (i + k) % groups) for i in range(groups)]
-        out.append(lax.ppermute(blocks[k], "mem", pairs) if k else blocks[0])
+        out.append(lax.ppermute(block, "mem", pairs) if k else block)
     return out
 
 
@@ -68,15 +72,11 @@
     return jnp.dot(lhs, rhs, preferred_element_type=jnp.float32)
 
 
-def square_by_rows(x):
-    p0, p1, p2 = split(x, 3)
+def square_by_rows(parts):
+    p0, p1, p2 = parts
     lhs = jnp.concatenate([p2, p0, p1, p1, p0, p0], axis=1)
     rhs = jnp.concatenate([p0, p2, p1, p0, p1, p0], axis=1)
-    middle = lhs.shape[0] // 2
-    dims = (((1,), (1,)), ((), ()))
-    upper = lax.dot_general(lhs[:middle], rhs, dims, preferred_element_type=jnp.float32)
-    lower = lax.dot_general(lhs[middle:], rhs, dims, preferred_element_type=jnp.float32)
-    return jnp.concatenate([upper, lower], axis=0)
+    return lax.dot_general(lhs, rhs, (((1,), (1,)), ((), ())), preferred_element_type=jnp.float32)
 
 
 def stencil(padded, diffusion, advection):
@@ -99,35 +99,43 @@
     return [pl.ds(first, rows) for first in range(0, members, rows)]
 
 
-def inner_kernel(state_ref, diff_ref, adv_ref, out_ref, rest_ref, low_ref, high_ref, held_ref, num_ref, sems):
-    members, columns, entries = state_ref.shape
-    groups, half, _, _ = out_ref.shape
+def edge_kernel(state_ref, low_ref, high_ref, held_ref, sems):
+    columns = state_ref.shape[1]
+    width = held_ref.shape[2]
+    reads = [
+        pltpu.make_async_copy(state_ref.at[:, pl.ds(first, width)], held_ref.at[i], sems.at[i])
+        for i, first in enumerate((0, columns - width))
+    ]
+    for copy in reads:
+        copy.start()
+    reads[0].wait()
+    for i in range(2):
+        low_ref[i] = held_ref[0, :, i]
+    reads[1].wait()
+    for i in range(2):
+        high_ref[i] = held_ref[1, :, width - 2 + i]
+
+
+def inner_kernel(me_ref, after_ref, state_ref, diff_ref, adv_ref, *refs):
+    del after_ref
+    *outs, rest_ref, turned_ref = refs
+    groups = len(outs)
+    half = outs[0].shape[0]
+    columns = state_ref.shape[1]
     quarter = columns // 4
-    pieces = pieces_of(members)
-    count = len(pieces)
-    reads = [pltpu.make_async_copy(state_ref.at[part], held_ref.at[part], sems.at[i]) for i, part in enumerate(pieces)]
-    reads.append(pltpu.make_async_copy(diff_ref, num_ref.at[0], sems.at[count]))
-    reads.append(pltpu.make_async_copy(adv_ref, num_ref.at[1], sems.at[count + 1]))
-    for copy in reads[count:] + reads[:count]:
-        copy.start()
-    reads[count].wait()
-    reads[count + 1].wait()
-    diffusion = num_ref[0:1][None]
-    advection = num_ref[1:2][None]
-    for i, part in enumerate(pieces):
-        reads[i].wait()
-        x = jnp.swapaxes(held_ref[part], 0, 1)
-        low_ref[:, part] = x[:2]
-        high_ref[:, part] = x[columns - 2 :]
-        rest_ref[0, :, part] = x[: quarter + 2]
-        rest_ref[1, :, part] = x[columns - quarter - 2 :]
-        x = x[quarter - 2 : columns - quarter + 2]
-        x = stencil(stencil(x, diffusion, advection), diffusion, advection)
-        out_ref[:, :, part] = x.reshape(groups, half, part.size, entries)
-
-
-def outer_kernel(obs_ref, rest_ref, before_ref, after_ref, diff_ref, adv_ref, out_ref):
-    del obs_ref
+    turned_ref[...] = jnp.swapaxes(state_ref[...], 0, 1)
+    diffusion = diff_ref[...][None]
+    advection = adv_ref[...][None]
+    for k, out_ref in zip(issue_order(groups), outs):
+        x = turned_ref[pl.ds(target(me_ref[0], k, groups) * half + (quarter - 2), half + 4)]
+        out_ref[...] = stencil(stencil(x, diffusion, advection), diffusion, advection)
+    rest_ref[0] = turned_ref[: quarter + 2]
+    rest_ref[1] = turned_ref[columns - quarter - 2 :]
+
+
+def outer_kernel(
+    me_ref, rest_ref, before_ref, after_ref, diff_ref, adv_ref, count_ref, where_ref, value_ref, rinv_ref, out_ref, obs_ref
+):
     diffusion = diff_ref[...][None]
     advection = adv_ref[...][None]
     low = jnp.concatenate([before_ref[...], rest_ref[0]], axis=0)
@@ -135,6 +143,7 @@
     low = stencil(stencil(low, diffusion, advection), diffusion, advection)
     high = stencil(stencil(high, diffusion, advection), diffusion, advection)
     out_ref[...] = jnp.concatenate([low, high], axis=0).reshape(out_ref.shape)
+    observe(me_ref[0], count_ref, where_ref, value_ref, rinv_ref, obs_ref)
 
 
 def inner_join_kernel(after_ref, inner_ref, out_ref, made_ref, sems):
@@ -179,18 +188,20 @@
         copy.wait()
 
 
-def observe_kernel(me_ref, count_ref, where_ref, value_ref, rinv_ref, out_ref):
+def observe(me, count_ref, where_ref, value_ref, rinv_ref, out_ref):
     columns, _, entries = out_ref.shape
     half = columns // 2
     quarter = where_ref.shape[0] // 4
     slots = where_ref.shape[1]
-    place = me_ref[0] * half
+    place = me * half
+    column = lax.broadcasted_iota(jnp.int32, count_ref.shape, 1)
     slot = lax.broadcasted_iota(jnp.int32, (1, slots), 1)
     row = lax.broadcasted_iota(jnp.int32, (16, slots), 0)
     entry = lax.broadcasted_iota(jnp.int32, (entries, slots), 0)
     for c in range(columns):
         at = inner_start(place, quarter) + c if c < half else outer_start(place, quarter) + c - half
-        weight = jnp.where(slot < count_ref[0, at], rinv_ref[pl.ds(at, 1), :], 0.0)
+        count = jnp.sum(jnp.where(column == at, count_ref[...], 0), axis=1, keepdims=True)
+        weight = jnp.where(slot < count, rinv_ref[pl.ds(at, 1), :], 0.0)
         lhs = jnp.zeros((16, slots), jnp.float32)
         for first, source in ((0, weight), (3, weight * value_ref[pl.ds(at, 1), :])):
             for k, part in enumerate(split(source, 3)):
@@ -222,7 +233,7 @@
         total = obs_ref[first + c, 0:1]
         forces.append(obs_ref[first + c, 1:2] - total * mean)
         means.append(mean)
-        grams.append(square_by_rows(anomaly * jnp.sqrt(total)))
+        grams.append(square_by_rows(split(anomaly * jnp.sqrt(total), 3)))
         ahead[c] = anomaly
         store(w.at[0], c, slice(None), anomaly)
     for c in every:
@@ -270,11 +281,12 @@
             outs[k][c] = result[k * local : (k + 1) * local]
 
 
-def analyse(states, obs, first, me, after, apart):
-    groups, columns, local, entries = states.shape
+def analyse(states, obs, first, me, after, back):
+    groups = len(states)
+    columns, local, entries = states[0].shape
     members = groups * local
     block = jax.ShapeDtypeStruct((columns, local, entries), jnp.float32)
-    whole = jax.ShapeDtypeStruct(states.shape, jnp.float32)
+    whole = jax.ShapeDtypeStruct((groups, columns, local, entries), jnp.float32)
     token = jax.ShapeDtypeStruct(after.shape, jnp.float32)
     full = pltpu.VMEM((columns, members, members), jnp.float32)
     pair = pltpu.VMEM((2, columns, members, members), jnp.bfloat16)
@@ -282,24 +294,25 @@
     ahead = pltpu.VMEM((columns, members, entries), jnp.float32)
     factor = pltpu.VMEM((2, 2, columns, members, entries), jnp.bfloat16)
 
-    def kernel(me_ref, after_ref, obs_ref, states_ref, *refs):
-        *outs, done_ref = refs[:-SCRATCH]
-        scratch = refs[-SCRATCH:]
-        if apart:
-            ins = [states_ref.at[target(me_ref[0], k, groups)] for k in range(groups)]
+    def kernel(me_ref, after_ref, obs_ref, *refs):
+        *blocks, done_ref = refs[:-SCRATCH]
+        if back:
+            whole_ref, *outs = blocks
+            ins = [whole_ref.at[target(me_ref[0], k, groups)] for k in issue_order(groups)]
         else:
-            ins = [states_ref.at[k] for k in range(groups)]
-            outs = [outs[0].at[k] for k in range(groups)]
-        analyse_kernel(first, after_ref, obs_ref, ins, outs, done_ref, *scratch)
-
+            *ins, whole_ref = blocks
+            outs = [whole_ref.at[source(me_ref[0], k, groups)] for k in issue_order(groups)]
+        analyse_kernel(first, after_ref, obs_ref, ins, outs, done_ref, *refs[-SCRATCH:])
+
+    operands = [states] if back else states
     return call(
         kernel,
-        [block] * groups + [token] if apart else [whole, token],
+        [block] * groups + [token] if back else [whole, token],
         columns * 90 * 2 * members * members * entries,
         8 * columns * members * entries,
-        in_specs=[SMEM] + [VMEM] * 3,
+        in_specs=[SMEM] + [VMEM] * (len(operands) + 2),
         scratch_shapes=[full, full, ahead, pair, pair, pair, pair, two, factor],
-    )(me, after, obs, states)
+    )(me, after, obs, *operands)
 
 
 def body(background, diffusion, advection, obs_where, obs_count, obs_value, obs_rinv):
@@ -308,41 +321,44 @@
     tiles = lax.axis_size("tile")
     half = columns // groups // 2
     size = background.size
-    block = (half, local, entries)
+    block = jax.ShapeDtypeStruct((half, local, entries), jnp.float32)
+    whole = jax.ShapeDtypeStruct((groups, half, local, entries), jnp.float32)
     rest = jax.ShapeDtypeStruct((2, columns // 4 + 2, local, entries), jnp.float32)
     edge = jax.ShapeDtypeStruct((2, local, entries), jnp.float32)
     me = lax.axis_index("mem")[None].astype(jnp.int32)
     pieces = len(pieces_of(local))
-
-    inner, rest, low, high = call(
+    width = min(columns, 8)
+    diffusion, advection = diffusion[None], advection[None]
+
+    low, high = call(
+        edge_kernel,
+        [edge, edge],
+        0,
+        16 * local * width * entries,
+        in_specs=[HBM],
+        scratch_shapes=[
+            pltpu.VMEM((2, local, width, entries), jnp.float32),
+            pltpu.SemaphoreType.DMA((2,)),
+        ],
+    )(in_hbm(background))
+    before = lax.ppermute(high, "tile", [(i, (i + 1) % tiles) for i in range(tiles)])
+    after = lax.ppermute(low, "tile", [((i + 1) % tiles, i) for i in range(tiles)])
+    *inner, rest = call(
         inner_kernel,
-        [jax.ShapeDtypeStruct((groups, *block), jnp.float32), rest, edge, edge],
+        [block] * groups + [rest],
         20 * size,
         8 * size,
-        in_specs=[HBM] * 3,
-        scratch_shapes=[
-            pltpu.VMEM(background.shape, jnp.float32),
-            pltpu.VMEM((8, entries), jnp.float32),
-            pltpu.SemaphoreType.DMA((pieces + 2,)),
-        ],
-    )(*(pltpu.with_memory_space_constraint(x, pltpu.HBM) for x in (background, diffusion, advection)))
-    inner = lax.all_to_all(inner, "mem", split_axis=0, concat_axis=0, tiled=True)
-    before = lax.ppermute(high, "tile", [(i, (i + 1) % tiles) for i in range(tiles)])
-    after = lax.ppermute(low, "tile", [((i + 1) % tiles, i) for i in range(tiles)])
-    obs = call(
-        observe_kernel,
-        jax.ShapeDtypeStruct((2 * half, 8, entries), jnp.float32),
-        2 * half * 2 * 16 * obs_where.shape[2] * entries,
-        12 * obs_where.size,
-        in_specs=[SMEM, SMEM] + [VMEM] * 3,
-    )(me, obs_count, obs_where[0], obs_value[0], obs_rinv[0])
-    outer = call(
+        in_specs=[SMEM] + [VMEM] * 4,
+        scratch_shapes=[pltpu.VMEM((columns, local, entries), jnp.float32)],
+    )(me, low, background, diffusion, advection)
+    inner = exchange(inner)
+    outer, obs = call(
         outer_kernel,
-        jax.ShapeDtypeStruct((groups, *block), jnp.float32),
+        [whole, jax.ShapeDtypeStruct((2 * half, 8, entries), jnp.float32)],
         20 * size,
         8 * size,
-        in_specs=[VMEM] * 6,
-    )(obs, rest, before, after, diffusion[None], advection[None])
+        in_specs=[SMEM] + [VMEM] * 9,
+    )(me, rest, before, after, diffusion, advection, obs_count, obs_where[0], obs_value[0], obs_rinv[0])
     outer = lax.all_to_all(outer, "mem", split_axis=0, concat_axis=0, tiled=True)
 
     inner, done = analyse(inner, obs, 0, me, obs[0], False)

time: 55.2 us -> 54.3 us (0.984)
  starting transfers between devices: 22.8 us -> 25.6 us
  waiting for transfers between devices: 6.87 us -> 4.81 us
  Pallas kernels: 23.5 us -> 22 us
    ppermute x7 -> x14, starting transfers between devices: 6.51 us -> 12.8 us  [exchange(): out.append(lax.ppermute(block, 'mem', pairs) if k else block)]
    all_to_all x2 -> x1, starting transfers between devices: 8.99 us -> 3.67 us  [body(): lax.all_to_all(inner, 'mem', split_axis=0, concat_axis=0, tiled=True)]
    pallas_call x5, Pallas kernels: 21.8 us -> 20.3 us  [the longest x2 16.6 us: analyse(): call(kernel, [block] * groups + [token] if back else [whole, token], colu...]
    ppermute x1, starting transfers between devices: 1.58 us -> 3.08 us  [body(): lax.ppermute(high, 'tile', [(i, (i + 1) % tiles) for i in range(tiles)])]
    ppermute x1, waiting for transfers between devices: 1.08 us -> 0.01 us  [body(): lax.ppermute(high, 'tile', [(i, (i + 1) % tiles) for i in range(tiles)])]
    all_to_all x2 -> x1, waiting for transfers between devices: 0.71 us -> 0.01 us  [body(): lax.all_to_all(inner, 'mem', split_axis=0, concat_axis=0, tiled=True)]
    ppermute x1, waiting for transfers between devices: 0.69 us -> 0.01 us  [body(): lax.ppermute(low, 'tile', [((i + 1) % tiles, i) for i in range(tiles)])]
    ppermute x7 -> x14, waiting for transfers between devices: 3.6 us -> 3.64 us  [exchange(): out.append(lax.ppermute(block, 'mem', pairs) if k else block)]
  transfers between devices with their start and end apart: 12 -> 18, of which waited for: 10 -> 7; matrix products, arithmetic and copies ran while one was open for 0% -> 0% of each run, Pallas kernels for 37% -> 37%
where the time goes in v6:
time: 54.3 us; the launch traced here: 54 us
  starting transfers between devices  25.6 us (47%)
  Pallas kernels  22 us (41%)
  waiting for transfers between devices  4.81 us (9%)
  local copies, waits for them, and re-layouts  1.35 us (2%)
    pallas_call x2, Pallas kernels, analyse(): call(kernel, [block] * groups + [token] if back else [whole, token], colu...  16.6 us
    ppermute x14, starting transfers between devices, exchange(): out.append(lax.ppermute(block, 'mem', pairs) if k else block)  12.8 us
    all_to_all x1, starting transfers between devices, body(): lax.all_to_all(outer, 'mem', split_axis=0, concat_axis=0, tiled=True)  3.88 us
    all_to_all x1, starting transfers between devices, body(): lax.all_to_all(inner, 'mem', split_axis=0, concat_axis=0, tiled=True)  3.67 us
    ppermute x14, waiting for transfers between devices, exchange(): out.append(lax.ppermute(block, 'mem', pairs) if k else block)  3.64 us
    ppermute x1, starting transfers between devices, body(): lax.ppermute(high, 'tile', [(i, (i + 1) % tiles) for i in range(tiles)])  3.08 us
    ppermute x1, starting transfers between devices, body(): lax.ppermute(low, 'tile', [((i + 1) % tiles, i) for i in range(tiles)])  2.09 us
    pallas_call x1, Pallas kernels, body(): call(outer_kernel, [whole, jax.ShapeDtypeStruct((2 * half, 8, entries), j...  1.76 us
  transfers between devices with their start and end apart: 18, of which 7 were waited for; matrix products, arithmetic and copies ran while one was open for 0% of the time, Pallas kernels for 37%

profile of v6, /device:TPU:0, one launch (start us, length us, event | category | flops | bytes accessed | tf_op | source)
XLA Modules:
  0.0 54.0 jit_solution(6527357179778166438)
XLA Ops:
  0.0 1.2 %shard_map.73 = (f32[2,32,256]{2,1,0:T(8,128)S(1)}, f32[2,32,256]{2,1,0:T(8,128)S(1)}) custom-call(f32[32,32,256]{2,1,0:T(8,128)} %state_ref.3), custom_call_target="tpu_custom_call" | custom-call | bytes 1048576 | tf_op jit(solution)/shard_map/pallas_call | solution.py:333
  1.2 3.1 %collective-permute-start = (f32[2,32,256]{2,1,0:T(8,128)S(1)}, f32[2,32,256]{2,1,0:T(8,128)S(1)}, u32[]{:S(2)}, u32[]{:S(2)}) collective-permute-start(f32[2,32,256]{2,1,0:T(8,128)S(1)} %get-tuple-element.30), channel_id=1, source_target_pairs={{0,1},{1,2},{2,3},{3,0},{4,5},{5,6},{6,7},{7,4},{8,9},{9,10},{10,1... | collective-permute-start | bytes 196616 | tf_op jit(solution)/shard_map/ppermute | solution.py:344
  4.2 2.1 %collective-permute-start.1 = (f32[2,32,256]{2,1,0:T(8,128)S(1)}, f32[2,32,256]{2,1,0:T(8,128)S(1)}, u32[]{:S(2)}, u32[]{:S(2)}) collective-permute-start(f32[2,32,256]{2,1,0:T(8,128)S(1)} %get-tuple-element.28.after_ref), channel_id=1, source_target_pairs={{1,0},{2,1},{3,2},{0,3},{5,4},{6,5},{7,6},{4,7},{9,8},{10,9},{11,1... | collective-permute-start | bytes 196616 | tf_op jit(solution)/shard_map/ppermute | solution.py:345
  6.3 0.0 copy-done
  6.3 0.7 %copy-done.5 = f32[256]{0:T(256)S(1)} copy-done((f32[256]{0:T(256)S(1)}, f32[256]{0:T(256)}, u32[]{:S(2)}) %copy-start.5) | copy-done | bytes 1048
  7.0 0.0 copy-done.4
  7.0 0.7 %shard_map.74 = (f32[2,32,256]{2,1,0:T(8,128)S(1)}, f32[2,32,256]{2,1,0:T(8,128)S(1)}, f32[2,32,256]{2,1,0:T(8,128)S(1)}, f32[2,32,256]{2,1,0:T(8,128)S(1)}, f32...) custom-call(s32[1]{0:T(128)} %bitcast.me_ref, ...), custom_call_target="tpu_custom_call" | custom-call | flops 5242880 | bytes 2097152 | tf_op jit(solution)/shard_map/pallas_call | solution.py:346
  7.8 0.1 collective-permute-start.2
  7.9 2.7 %collective-permute-start.3 = (f32[2,32,256]{2,1,0:T(8,128)S(1)}, f32[2,32,256]{2,1,0:T(8,128)S(1)}, u32[]{:S(2)}, u32[]{:S(2)}) collective-permute-start(f32[2,32,256]{2,1,0:T(8,128)S(1)} %get-tuple-element.33), channel_id=1, source_target_pairs={{0,24},{4,28},{8,16},{12,20},{16,8},{20,12},{24,0},{28,4},{1,25},{... | collective-permute-start | bytes 196616 | tf_op jit(solution)/shard_map/ppermute | solution.py:51
  10.5 0.1 collective-permute-start.4
  10.6 0.0 collective-permute-done.before_ref
  10.6 1.6 %collective-permute-start.5 = (f32[2,32,256]{2,1,0:T(8,128)S(1)}, f32[2,32,256]{2,1,0:T(8,128)S(1)}, u32[]{:S(2)}, u32[]{:S(2)}) collective-permute-start(f32[2,32,256]{2,1,0:T(8,128)S(1)} %get-tuple-element.35), channel_id=1, source_target_pairs={{0,8},{4,12},{8,0},{12,4},{16,24},{20,28},{24,16},{28,20},{1,9},{5... | collective-permute-start | bytes 196616 | tf_op jit(solution)/shard_map/ppermute | solution.py:51
  12.3 0.0 collective-permute-done.1.after_ref
  12.3 0.0 collective-permute-start.6
  12.3 0.0 copy-done.1
  12.3 0.6 %copy-done.6 = s32[1,32]{1,0:T(1,128)S(1)} copy-done((s32[1,32]{1,0:T(1,128)S(1)}, s32[1,32]{1,0:T(1,128)}, u32[]{:S(2)}) %copy-start.6) | copy-done | bytes 152
  13.0 1.8 %shard_map.75 = (f32[8,2,32,256]{3,2,1,0:T(8,128)}, f32[4,8,256]{2,1,0:T(8,128)S(1)}) custom-call(s32[1]{0:T(128)} %bitcast.me_ref, f32[2,10,32,256]{3,2,1,0:T(8,128)S(1)} %get-tuple-element.29.rest_ref, f32[2,32,256]{2,1,0:T(8,128)S(1)} %collective-permute-done.before_ref, f32[2,32,256]{2,1,0:T(8,128)S(1)} %collective-permute-done.1.after_ref, ...), custom_call_target="tpu_custom_call" | custom-call | flops 5242880 | bytes 2097152 | tf_op jit(solution)/shard_map/pallas_call | solution.py:355
  14.7 0.0 collective-permute-done.2.refs_0_
  14.7 1.7 %collective-permute-start.7 = (f32[2,32,256]{2,1,0:T(8,128)S(1)}, f32[2,32,256]{2,1,0:T(8,128)S(1)}, u32[]{:S(2)}, u32[]{:S(2)}) collective-permute-start(f32[2,32,256]{2,1,0:T(8,128)S(1)} %get-tuple-element.37), channel_id=1, source_target_pairs={{0,16},{4,20},{8,24},{12,28},{16,0},{20,4},{24,8},{28,12},{1,17},{... | collective-permute-start | bytes 196616 | tf_op jit(solution)/shard_map/ppermute | solution.py:51
  16.4 0.0 collective-permute-done.3.refs_1_
  16.4 0.1 collective-permute-start.8
  16.6 3.9 %all-to-all-start = ((f32[8,2,32,256]{3,2,1,0:T(8,128)}), f32[8,2,32,256]{3,2,1,0:T(8,128)S(1)}, u32[]{:S(2)}, u32[]{:S(2)}) async-start(f32[8,2,32,256]{3,2,1,0:T(8,128)} %get-tuple-element.41), calls=%async_computation | async-start | bytes 1048576 | tf_op jit(solution)/shard_map/all_to_all | solution.py:362
  20.4 0.0 collective-permute-done.4.refs_2_
  20.4 0.0 collective-permute-done.5.refs_3_
  20.4 0.0 collective-permute-done.6.refs_4_
  20.5 0.0 collective-permute-done.7.refs_5_
  20.5 0.0 collective-permute-done.8.refs_6_
  20.5 8.5 %shard_map.76 = (f32[8,2,32,256]{3,2,1,0:T(8,128)}, f32[8,256]{1,0:T(8,128)S(1)}) custom-call(s32[1]{0:T(128)} %bitcast.me_ref, f32[8,256]{1,0:T(8,128)S(1)} %slice_bitcast_fusion.after_ref, f32[4,8,256]{2,1,0:T(8,128)S(1)} %get-tuple-element.31.obs_ref, f32[2,32,256]{2,1,0:T(8,128)S(1)} %collective-permute-done.2.refs_0_, ...), custom_call_target="tpu_custom_call" | custom-call | flops 6039797760 | bytes 1048576 | tf_op jit(solution)/shard_map/pallas_call | solution.py:308
  29.0 1.2 %all-to-all-done.refs_0_ = f32[8,2,32,256]{3,2,1,0:T(8,128)S(1)} async-done(((f32[8,2,32,256]{3,2,1,0:T(8,128)}), f32[8,2,32,256]{3,2,1,0:T(8,128)S(1)}, u32[]{:S(2)}, u32[]{:S(2)}) %all-to-all-start) | async-done | bytes 524320 | tf_op jit(solution)/shard_map/all_to_all | solution.py:362
  30.2 3.7 %all-to-all-start.1 = ((f32[8,2,32,256]{3,2,1,0:T(8,128)}), f32[8,2,32,256]{3,2,1,0:T(8,128)S(1)}, u32[]{:S(2)}, u32[]{:S(2)}) async-start(f32[8,2,32,256]{3,2,1,0:T(8,128)} %get-tuple-element.43), calls=%async_computation.1 | async-start | bytes 1048576 | tf_op jit(solution)/shard_map/all_to_all | solution.py:365
  33.9 8.1 %shard_map.77 = (f32[2,32,256]{2,1,0:T(8,128)S(1)}, f32[2,32,256]{2,1,0:T(8,128)S(1)}, f32[2,32,256]{2,1,0:T(8,128)S(1)}, f32[2,32,256]{2,1,0:T(8,128)S(1)}, f32...) custom-call(s32[1]{0:T(128)} %bitcast.me_ref, ...), custom_call_target="tpu_custom_call" | custom-call | flops 6039797760 | bytes 1048576 | tf_op jit(solution)/shard_map/pallas_call | solution.py:308
  41.9 2.4 %collective-permute-start.9 = (f32[2,32,256]{2,1,0:T(8,128)S(1)}, f32[2,32,256]{2,1,0:T(8,128)S(1)}, u32[]{:S(2)}, u32[]{:S(2)}) collective-permute-start(f32[2,32,256]{2,1,0:T(8,128)S(1)} %get-tuple-element.42), channel_id=1, source_target_pairs={{0,28},{4,24},{8,20},{12,16},{16,12},{20,8},{24,4},{28,0},{1,29},{... | collective-permute-start | bytes 196616 | tf_op jit(solution)/shard_map/ppermute | solution.py:51
  44.3 0.4 collective-permute-start.10
  44.7 0.3 collective-permute-start.11
  45.0 1.7 %collective-permute-start.12 = (f32[2,32,256]{2,1,0:T(8,128)S(1)}, f32[2,32,256]{2,1,0:T(8,128)S(1)}, u32[]{:S(2)}, u32[]{:S(2)}) collective-permute-start(f32[2,32,256]{2,1,0:T(8,128)S(1)} %get-tuple-element.46), channel_id=1, source_target_pairs={{0,8},{4,12},{8,0},{12,4},{16,24},{20,28},{24,16},{28,20},{1,9},{5... | collective-permute-start | bytes 196616 | tf_op jit(solution)/shard_map/ppermute | solution.py:51
  46.7 0.0 collective-permute-start.13
  46.7 0.2 collective-permute-done.9.after_ref.refs_2_
  46.9 1.7 %collective-permute-start.14 = (f32[2,32,256]{2,1,0:T(8,128)S(1)}, f32[2,32,256]{2,1,0:T(8,128)S(1)}, u32[]{:S(2)}, u32[]{:S(2)}) collective-permute-start(f32[2,32,256]{2,1,0:T(8,128)S(1)} %get-tuple-element.48), channel_id=1, source_target_pairs={{0,16},{4,20},{8,24},{12,28},{16,0},{20,4},{24,8},{28,12},{1,17},{... | collective-permute-start | bytes 196616 | tf_op jit(solution)/shard_map/ppermute | solution.py:51
  48.7 0.0 collective-permute-done.10.refs_0_
  48.7 0.0 collective-permute-start.15
  48.7 0.0 all-to-all-done.1.inner_ref
  48.7 0.8 %shard_map.78.held_ref = f32[32,32,256]{2,1,0:T(8,128)} custom-call(f32[2,32,256]{2,1,0:T(8,128)S(1)} %collective-permute-done.9.after_ref.refs_2_, f32[8,2,32,256]{3,2,1,0:T(8,128)S(1)} %all-to-all-done.1.inner_ref), custom_call_target="tpu_custom_call" | custom-call | flops 262144 | bytes 1048576 | tf_op jit(solution)/shard_map/pallas_call | solution.py:369
  49.5 1.0 %collective-permute-done.11.refs_1_ = f32[2,32,256]{2,1,0:T(8,128)S(1)} collective-permute-done((f32[2,32,256]{2,1,0:T(8,128)S(1)}, f32[2,32,256]{2,1,0:T(8,128)S(1)}, u32[]{:S(2)}, u32[]{:S(2)}) %collective-permute-start.11) | collective-permute-done | bytes 65568 | tf_op jit(solution)/shard_map/ppermute | solution.py:51
  50.6 0.3 collective-permute-done.12.refs_3_
  50.9 0.2 collective-permute-done.13.refs_4_
  51.1 0.4 collective-permute-done.14.refs_5_
  51.5 1.4 %collective-permute-done.15.refs_6_ = f32[2,32,256]{2,1,0:T(8,128)S(1)} collective-permute-done((f32[2,32,256]{2,1,0:T(8,128)S(1)}, f32[2,32,256]{2,1,0:T(8,128)S(1)}, u32[]{:S(2)}, u32[]{:S(2)}) %collective-permute-start.15) | collective-permute-done | bytes 65568 | tf_op jit(solution)/shard_map/ppermute | solution.py:51
  52.9 0.9 %shard_map.79 = f32[32,32,256]{2,1,0:T(8,128)} custom-call(s32[1]{0:T(128)} %bitcast.me_ref, f32[32,32,256]{2,1,0:T(8,128)} %shard_map.78.held_ref, f32[2,32,256]{2,1,0:T(8,128)S(1)} %collective-permute-done.10.refs_0_, f32[2,32,256]{2,1,0:T(8,128)S(1)} %collective-permute-done.11.refs_1_, ...), custom_call_target="tpu_custom_call", output_to_operand_aliasing={{}: (1, {})} | custom-call | flops 262144 | bytes 1048576 | tf_op jit(solution)/shard_map/pallas_call | solution.py:381
  (10 shorter events, 0.0 us)
Async XLA Ops:
  0.0 6.3 %copy-start = (f32[32,32,256]{2,1,0:T(8,128)S(1)}, f32[32,32,256]{2,1,0:T(8,128)}, u32[]{:S(2)}) copy-start(f32[32,32,256]{2,1,0:T(8,128)} %state_ref.3) | copy-start | bytes 3145732
  1.2 9.5 %collective-permute-start = (f32[2,32,256]{2,1,0:T(8,128)S(1)}, f32[2,32,256]{2,1,0:T(8,128)S(1)}, u32[]{:S(2)}, u32[]{:S(2)}) collective-permute-start(f32[2,32,256]{2,1,0:T(8,128)S(1)} %get-tuple-element.30), channel_id=1, source_target_pairs={{0,1},{1,2},{2,3},{3,0},{4,5},{5,6},{6,7},{7,4},{8,9},{9,10},{10,1... | collective-permute-start | bytes 196616 | tf_op jit(solution)/shard_map/ppermute | solution.py:344
  4.2 8.0 %collective-permute-start.1 = (f32[2,32,256]{2,1,0:T(8,128)S(1)}, f32[2,32,256]{2,1,0:T(8,128)S(1)}, u32[]{:S(2)}, u32[]{:S(2)}) collective-permute-start(f32[2,32,256]{2,1,0:T(8,128)S(1)} %get-tuple-element.28.after_ref), channel_id=1, source_target_pairs={{1,0},{2,1},{3,2},{0,3},{5,4},{6,5},{7,6},{4,7},{9,8},{10,9},{11,1... | collective-permute-start | bytes 196616 | tf_op jit(solution)/shard_map/ppermute | solution.py:345
  6.3 0.7 %copy-start.5 = (f32[256]{0:T(256)S(1)}, f32[256]{0:T(256)}, u32[]{:S(2)}) copy-start(f32[256]{0:T(256)} %param.9) | copy-start | bytes 3076
  6.3 0.7 %copy-start.4 = (f32[256]{0:T(256)S(1)}, f32[256]{0:T(256)}, u32[]{:S(2)}) copy-start(f32[256]{0:T(256)} %param.8) | copy-start | bytes 3076
  7.0 5.3 %copy-start.1 = (s32[1,32,512]{2,1,0:T(8,128)S(1)}, s32[1,32,512]{2,1,0:T(8,128)}, u32[]{:S(2)}) copy-start(s32[1,32,512]{2,1,0:T(8,128)} %param.10) | copy-start | bytes 196612
  7.0 5.3 %copy-start.2 = (f32[1,32,512]{2,1,0:T(8,128)S(1)}, f32[1,32,512]{2,1,0:T(8,128)}, u32[]{:S(2)}) copy-start(f32[1,32,512]{2,1,0:T(8,128)} %param.12) | copy-start | bytes 196612
  7.0 5.3 %copy-start.3 = (f32[1,32,512]{2,1,0:T(8,128)S(1)}, f32[1,32,512]{2,1,0:T(8,128)}, u32[]{:S(2)}) copy-start(f32[1,32,512]{2,1,0:T(8,128)} %param.13) | copy-start | bytes 196612
  7.8 7.0 %collective-permute-start.2 = (f32[2,32,256]{2,1,0:T(8,128)S(1)}, f32[2,32,256]{2,1,0:T(8,128)S(1)}, u32[]{:S(2)}, u32[]{:S(2)}) collective-permute-start(f32[2,32,256]{2,1,0:T(8,128)S(1)} %get-tuple-element.32), channel_id=1, source_target_pairs={{0,4},{4,0},{8,12},{12,8},{16,20},{20,16},{24,28},{28,24},{1,5},{5... | collective-permute-start | bytes 196616 | tf_op jit(solution)/shard_map/ppermute | solution.py:51
  7.9 8.6 %collective-permute-start.3 = (f32[2,32,256]{2,1,0:T(8,128)S(1)}, f32[2,32,256]{2,1,0:T(8,128)S(1)}, u32[]{:S(2)}, u32[]{:S(2)}) collective-permute-start(f32[2,32,256]{2,1,0:T(8,128)S(1)} %get-tuple-element.33), channel_id=1, source_target_pairs={{0,24},{4,28},{8,16},{12,20},{16,8},{20,12},{24,0},{28,4},{1,25},{... | collective-permute-start | bytes 196616 | tf_op jit(solution)/shard_map/ppermute | solution.py:51
  10.5 9.9 %collective-permute-start.4 = (f32[2,32,256]{2,1,0:T(8,128)S(1)}, f32[2,32,256]{2,1,0:T(8,128)S(1)}, u32[]{:S(2)}, u32[]{:S(2)}) collective-permute-start(f32[2,32,256]{2,1,0:T(8,128)S(1)} %get-tuple-element.34), channel_id=1, source_target_pairs={{0,28},{4,24},{8,20},{12,16},{16,12},{20,8},{24,4},{28,0},{1,29},{... | collective-permute-start | bytes 196616 | tf_op jit(solution)/shard_map/ppermute | solution.py:51
  10.6 9.8 %collective-permute-start.5 = (f32[2,32,256]{2,1,0:T(8,128)S(1)}, f32[2,32,256]{2,1,0:T(8,128)S(1)}, u32[]{:S(2)}, u32[]{:S(2)}) collective-permute-start(f32[2,32,256]{2,1,0:T(8,128)S(1)} %get-tuple-element.35), channel_id=1, source_target_pairs={{0,8},{4,12},{8,0},{12,4},{16,24},{20,28},{24,16},{28,20},{1,9},{5... | collective-permute-start | bytes 196616 | tf_op jit(solution)/shard_map/ppermute | solution.py:51
  12.3 8.2 %collective-permute-start.6 = (f32[2,32,256]{2,1,0:T(8,128)S(1)}, f32[2,32,256]{2,1,0:T(8,128)S(1)}, u32[]{:S(2)}, u32[]{:S(2)}) collective-permute-start(f32[2,32,256]{2,1,0:T(8,128)S(1)} %get-tuple-element.36), channel_id=1, source_target_pairs={{0,12},{4,8},{8,4},{12,0},{16,28},{20,24},{24,20},{28,16},{1,13},{... | collective-permute-start | bytes 196616 | tf_op jit(solution)/shard_map/ppermute | solution.py:51
  12.3 0.7 %copy-start.6 = (s32[1,32]{1,0:T(1,128)S(1)}, s32[1,32]{1,0:T(1,128)}, u32[]{:S(2)}) copy-start(s32[1,32]{1,0:T(1,128)} %count_ref.1) | copy-start | bytes 388
  14.7 5.7 %collective-permute-start.7 = (f32[2,32,256]{2,1,0:T(8,128)S(1)}, f32[2,32,256]{2,1,0:T(8,128)S(1)}, u32[]{:S(2)}, u32[]{:S(2)}) collective-permute-start(f32[2,32,256]{2,1,0:T(8,128)S(1)} %get-tuple-element.37), channel_id=1, source_target_pairs={{0,16},{4,20},{8,24},{12,28},{16,0},{20,4},{24,8},{28,12},{1,17},{... | collective-permute-start | bytes 196616 | tf_op jit(solution)/shard_map/ppermute | solution.py:51
  16.4 4.0 %collective-permute-start.8 = (f32[2,32,256]{2,1,0:T(8,128)S(1)}, f32[2,32,256]{2,1,0:T(8,128)S(1)}, u32[]{:S(2)}, u32[]{:S(2)}) collective-permute-start(f32[2,32,256]{2,1,0:T(8,128)S(1)} %get-tuple-element.38), channel_id=1, source_target_pairs={{0,20},{4,16},{8,28},{12,24},{16,4},{20,0},{24,12},{28,8},{1,21},{... | collective-permute-start | bytes 196616 | tf_op jit(solution)/shard_map/ppermute | solution.py:51
  16.6 13.6 %all-to-all-start = ((f32[8,2,32,256]{3,2,1,0:T(8,128)}), f32[8,2,32,256]{3,2,1,0:T(8,128)S(1)}, u32[]{:S(2)}, u32[]{:S(2)}) async-start(f32[8,2,32,256]{3,2,1,0:T(8,128)} %get-tuple-element.41), calls=%async_computation | async-start | bytes 1048576 | tf_op jit(solution)/shard_map/all_to_all | solution.py:362
  30.2 18.5 %all-to-all-start.1 = ((f32[8,2,32,256]{3,2,1,0:T(8,128)}), f32[8,2,32,256]{3,2,1,0:T(8,128)S(1)}, u32[]{:S(2)}, u32[]{:S(2)}) async-start(f32[8,2,32,256]{3,2,1,0:T(8,128)} %get-tuple-element.43), calls=%async_computation.1 | async-start | bytes 1048576 | tf_op jit(solution)/shard_map/all_to_all | solution.py:365
  41.9 5.0 %collective-permute-start.9 = (f32[2,32,256]{2,1,0:T(8,128)S(1)}, f32[2,32,256]{2,1,0:T(8,128)S(1)}, u32[]{:S(2)}, u32[]{:S(2)}) collective-permute-start(f32[2,32,256]{2,1,0:T(8,128)S(1)} %get-tuple-element.42), channel_id=1, source_target_pairs={{0,28},{4,24},{8,20},{12,16},{16,12},{20,8},{24,4},{28,0},{1,29},{... | collective-permute-start | bytes 196616 | tf_op jit(solution)/shard_map/ppermute | solution.py:51
  44.3 4.3 %collective-permute-start.10 = (f32[2,32,256]{2,1,0:T(8,128)S(1)}, f32[2,32,256]{2,1,0:T(8,128)S(1)}, u32[]{:S(2)}, u32[]{:S(2)}) collective-permute-start(f32[2,32,256]{2,1,0:T(8,128)S(1)} %get-tuple-element.44), channel_id=1, source_target_pairs={{0,4},{4,0},{8,12},{12,8},{16,20},{20,16},{24,28},{28,24},{1,5},{5... | collective-permute-start | bytes 196616 | tf_op jit(solution)/shard_map/ppermute | solution.py:51
  44.7 5.9 %collective-permute-start.11 = (f32[2,32,256]{2,1,0:T(8,128)S(1)}, f32[2,32,256]{2,1,0:T(8,128)S(1)}, u32[]{:S(2)}, u32[]{:S(2)}) collective-permute-start(f32[2,32,256]{2,1,0:T(8,128)S(1)} %get-tuple-element.45), channel_id=1, source_target_pairs={{0,24},{4,28},{8,16},{12,20},{16,8},{20,12},{24,0},{28,4},{1,25},{... | collective-permute-start | bytes 196616 | tf_op jit(solution)/shard_map/ppermute | solution.py:51
  45.0 5.9 %collective-permute-start.12 = (f32[2,32,256]{2,1,0:T(8,128)S(1)}, f32[2,32,256]{2,1,0:T(8,128)S(1)}, u32[]{:S(2)}, u32[]{:S(2)}) collective-permute-start(f32[2,32,256]{2,1,0:T(8,128)S(1)} %get-tuple-element.46), channel_id=1, source_target_pairs={{0,8},{4,12},{8,0},{12,4},{16,24},{20,28},{24,16},{28,20},{1,9},{5... | collective-permute-start | bytes 196616 | tf_op jit(solution)/shard_map/ppermute | solution.py:51
  46.7 4.5 %collective-permute-start.13 = (f32[2,32,256]{2,1,0:T(8,128)S(1)}, f32[2,32,256]{2,1,0:T(8,128)S(1)}, u32[]{:S(2)}, u32[]{:S(2)}) collective-permute-start(f32[2,32,256]{2,1,0:T(8,128)S(1)} %get-tuple-element.47), channel_id=1, source_target_pairs={{0,12},{4,8},{8,4},{12,0},{16,28},{20,24},{24,20},{28,16},{1,13},{... | collective-permute-start | bytes 196616 | tf_op jit(solution)/shard_map/ppermute | solution.py:51
  46.9 4.6 %collective-permute-start.14 = (f32[2,32,256]{2,1,0:T(8,128)S(1)}, f32[2,32,256]{2,1,0:T(8,128)S(1)}, u32[]{:S(2)}, u32[]{:S(2)}) collective-permute-start(f32[2,32,256]{2,1,0:T(8,128)S(1)} %get-tuple-element.48), channel_id=1, source_target_pairs={{0,16},{4,20},{8,24},{12,28},{16,0},{20,4},{24,8},{28,12},{1,17},{... | collective-permute-start | bytes 196616 | tf_op jit(solution)/shard_map/ppermute | solution.py:51
  48.7 4.3 %collective-permute-start.15 = (f32[2,32,256]{2,1,0:T(8,128)S(1)}, f32[2,32,256]{2,1,0:T(8,128)S(1)}, u32[]{:S(2)}, u32[]{:S(2)}) collective-permute-start(f32[2,32,256]{2,1,0:T(8,128)S(1)} %get-tuple-element.49), channel_id=1, source_target_pairs={{0,20},{4,16},{8,28},{12,24},{16,4},{20,0},{24,12},{28,8},{1,21},{... | collective-permute-start | bytes 196616 | tf_op jit(solution)/shard_map/ppermute | solution.py:51

commit v7 on v6

--- a/solution.py
+++ b/solution.py
@@ -99,13 +99,16 @@
     return [pl.ds(first, rows) for first in range(0, members, rows)]
 
 
-def edge_kernel(state_ref, low_ref, high_ref, held_ref, sems):
+def edge_kernel(state_ref, diff_ref, adv_ref, count_ref, low_ref, high_ref, num_ref, counts_ref, held_ref, sems):
     columns = state_ref.shape[1]
     width = held_ref.shape[2]
     reads = [
         pltpu.make_async_copy(state_ref.at[:, pl.ds(first, width)], held_ref.at[i], sems.at[i])
         for i, first in enumerate((0, columns - width))
     ]
+    reads.append(pltpu.make_async_copy(diff_ref, num_ref.at[0], sems.at[2]))
+    reads.append(pltpu.make_async_copy(adv_ref, num_ref.at[1], sems.at[3]))
+    reads.append(pltpu.make_async_copy(count_ref, counts_ref, sems.at[4]))
     for copy in reads:
         copy.start()
     reads[0].wait()
@@ -114,18 +117,19 @@
     reads[1].wait()
     for i in range(2):
         high_ref[i] = held_ref[1, :, width - 2 + i]
-
-
-def inner_kernel(me_ref, after_ref, state_ref, diff_ref, adv_ref, *refs):
-    del after_ref
+    for copy in reads[2:]:
+        copy.wait()
+
+
+def inner_kernel(me_ref, state_ref, num_ref, *refs):
     *outs, rest_ref, turned_ref = refs
     groups = len(outs)
     half = outs[0].shape[0]
     columns = state_ref.shape[1]
     quarter = columns // 4
     turned_ref[...] = jnp.swapaxes(state_ref[...], 0, 1)
-    diffusion = diff_ref[...][None]
-    advection = adv_ref[...][None]
+    diffusion = num_ref[0:1][None]
+    advection = num_ref[1:2][None]
     for k, out_ref in zip(issue_order(groups), outs):
         x = turned_ref[pl.ds(target(me_ref[0], k, groups) * half + (quarter - 2), half + 4)]
         out_ref[...] = stencil(stencil(x, diffusion, advection), diffusion, advection)
@@ -134,16 +138,18 @@
 
 
 def outer_kernel(
-    me_ref, rest_ref, before_ref, after_ref, diff_ref, adv_ref, count_ref, where_ref, value_ref, rinv_ref, out_ref, obs_ref
+    me_ref, rest_ref, before_ref, after_ref, num_ref, count_ref, where_ref, value_ref, rinv_ref, out_ref, obs_ref
 ):
-    diffusion = diff_ref[...][None]
-    advection = adv_ref[...][None]
+    diffusion = num_ref[0:1][None]
+    advection = num_ref[1:2][None]
     low = jnp.concatenate([before_ref[...], rest_ref[0]], axis=0)
     high = jnp.concatenate([rest_ref[1], after_ref[...]], axis=0)
     low = stencil(stencil(low, diffusion, advection), diffusion, advection)
     high = stencil(stencil(high, diffusion, advection), diffusion, advection)
     out_ref[...] = jnp.concatenate([low, high], axis=0).reshape(out_ref.shape)
-    observe(me_ref[0], count_ref, where_ref, value_ref, rinv_ref, obs_ref)
+    half = obs_ref.shape[0]
+    first = inner_start(me_ref[0] * half, where_ref.shape[0] // 4)
+    observe(first, count_ref, where_ref, value_ref, rinv_ref, obs_ref)
 
 
 def inner_join_kernel(after_ref, inner_ref, out_ref, made_ref, sems):
@@ -188,24 +194,28 @@
         copy.wait()
 
 
-def observe(me, count_ref, where_ref, value_ref, rinv_ref, out_ref):
+def observe_kernel(me_ref, after_ref, count_ref, where_ref, value_ref, rinv_ref, out_ref):
+    del after_ref
+    half = out_ref.shape[0]
+    first = outer_start(me_ref[0] * half, where_ref.shape[0] // 4)
+    observe(first, count_ref, where_ref, value_ref, rinv_ref, out_ref)
+
+
+def observe(first, count_ref, where_ref, value_ref, rinv_ref, out_ref):
     columns, _, entries = out_ref.shape
-    half = columns // 2
-    quarter = where_ref.shape[0] // 4
     slots = where_ref.shape[1]
-    place = me * half
     column = lax.broadcasted_iota(jnp.int32, count_ref.shape, 1)
     slot = lax.broadcasted_iota(jnp.int32, (1, slots), 1)
     row = lax.broadcasted_iota(jnp.int32, (16, slots), 0)
     entry = lax.broadcasted_iota(jnp.int32, (entries, slots), 0)
     for c in range(columns):
-        at = inner_start(place, quarter) + c if c < half else outer_start(place, quarter) + c - half
+        at = first + c
         count = jnp.sum(jnp.where(column == at, count_ref[...], 0), axis=1, keepdims=True)
         weight = jnp.where(slot < count, rinv_ref[pl.ds(at, 1), :], 0.0)
         lhs = jnp.zeros((16, slots), jnp.float32)
-        for first, source in ((0, weight), (3, weight * value_ref[pl.ds(at, 1), :])):
-            for k, part in enumerate(split(source, 3)):
-                lhs = jnp.where(row == first + k, part.astype(jnp.float32), lhs)
+        for line, values in ((0, weight), (3, weight * value_ref[pl.ds(at, 1), :])):
+            for k, part in enumerate(split(values, 3)):
+                lhs = jnp.where(row == line + k, part.astype(jnp.float32), lhs)
         onehot = (entry == where_ref[pl.ds(at, 1), :]).astype(jnp.float32).astype(jnp.bfloat16)
         sums = lax.dot_general(
             lhs.astype(jnp.bfloat16), onehot, (((1,), (1,)), ((), ())), preferred_element_type=jnp.float32
@@ -214,7 +224,7 @@
         out_ref[c, 1:2] = sums[3:4] + (sums[4:5] + sums[5:6])
 
 
-def analyse_kernel(first, after_ref, obs_ref, states, outs, done_ref, root, mixed, ahead, s, p, u, t, r, w):
+def analyse_kernel(after_ref, obs_ref, states, outs, done_ref, root, mixed, ahead, s, p, u, t, r, w):
     del after_ref
     done_ref[...] = jnp.zeros_like(done_ref)
     groups = len(outs)
@@ -230,8 +240,8 @@
         x = jnp.concatenate([ref[c] for ref in states], axis=0)
         mean = jnp.sum(x, axis=0, keepdims=True) * (1.0 / members)
         anomaly = x - mean
-        total = obs_ref[first + c, 0:1]
-        forces.append(obs_ref[first + c, 1:2] - total * mean)
+        total = obs_ref[c, 0:1]
+        forces.append(obs_ref[c, 1:2] - total * mean)
         means.append(mean)
         grams.append(square_by_rows(split(anomaly * jnp.sqrt(total), 3)))
         ahead[c] = anomaly
@@ -281,7 +291,7 @@
             outs[k][c] = result[k * local : (k + 1) * local]
 
 
-def analyse(states, obs, first, me, after, back):
+def analyse(states, obs, me, after, back):
     groups = len(states)
     columns, local, entries = states[0].shape
     members = groups * local
@@ -302,7 +312,7 @@
         else:
             *ins, whole_ref = blocks
             outs = [whole_ref.at[source(me_ref[0], k, groups)] for k in issue_order(groups)]
-        analyse_kernel(first, after_ref, obs_ref, ins, outs, done_ref, *refs[-SCRATCH:])
+        analyse_kernel(after_ref, obs_ref, ins, outs, done_ref, *refs[-SCRATCH:])
 
     operands = [states] if back else states
     return call(
@@ -328,19 +338,20 @@
     me = lax.axis_index("mem")[None].astype(jnp.int32)
     pieces = len(pieces_of(local))
     width = min(columns, 8)
-    diffusion, advection = diffusion[None], advection[None]
-
-    low, high = call(
+    seen = jax.ShapeDtypeStruct((half, 8, entries), jnp.float32)
+    numbers = jax.ShapeDtypeStruct((8, entries), jnp.float32)
+
+    low, high, numbers, counts = call(
         edge_kernel,
-        [edge, edge],
+        [edge, edge, numbers, jax.ShapeDtypeStruct(obs_count.shape, jnp.int32)],
         0,
         16 * local * width * entries,
-        in_specs=[HBM],
+        in_specs=[HBM] * 4,
         scratch_shapes=[
             pltpu.VMEM((2, local, width, entries), jnp.float32),
-            pltpu.SemaphoreType.DMA((2,)),
+            pltpu.SemaphoreType.DMA((5,)),
         ],
-    )(in_hbm(background))
+    )(*(in_hbm(x) for x in (background, diffusion, advection, obs_count)))
     before = lax.ppermute(high, "tile", [(i, (i + 1) % tiles) for i in range(tiles)])
     after = lax.ppermute(low, "tile", [((i + 1) % tiles, i) for i in range(tiles)])
     *inner, rest = call(
@@ -348,22 +359,30 @@
         [block] * groups + [rest],
         20 * size,
         8 * size,
-        in_specs=[SMEM] + [VMEM] * 4,
+        in_specs=[SMEM] + [VMEM] * 2,
         scratch_shapes=[pltpu.VMEM((columns, local, entries), jnp.float32)],
-    )(me, low, background, diffusion, advection)
+    )(me, background, numbers)
     inner = exchange(inner)
+    slots = (counts, obs_where[0], obs_value[0], obs_rinv[0])
     outer, obs = call(
         outer_kernel,
-        [whole, jax.ShapeDtypeStruct((2 * half, 8, entries), jnp.float32)],
+        [whole, seen],
         20 * size,
         8 * size,
-        in_specs=[SMEM] + [VMEM] * 9,
-    )(me, rest, before, after, diffusion, advection, obs_count, obs_where[0], obs_value[0], obs_rinv[0])
+        in_specs=[SMEM] + [VMEM] * 8,
+    )(me, rest, before, after, numbers, *slots)
     outer = lax.all_to_all(outer, "mem", split_axis=0, concat_axis=0, tiled=True)
 
-    inner, done = analyse(inner, obs, 0, me, obs[0], False)
+    inner, done = analyse(inner, obs, me, obs[0], False)
     inner = lax.all_to_all(inner, "mem", split_axis=0, concat_axis=0, tiled=True)
-    *outer, _ = analyse(outer, obs, half, me, done, True)
+    obs = call(
+        observe_kernel,
+        seen,
+        half * 2 * 16 * obs_where.shape[2] * entries,
+        12 * obs_where.size,
+        in_specs=[SMEM] + [VMEM] * 5,
+    )(me, done, *slots)
+    *outer, _ = analyse(outer, obs, me, done, True)
     outer = exchange(outer)
     result = jax.ShapeDtypeStruct(background.shape, jnp.float32)
     made = call(

time: 54.3 us -> 52.8 us (0.972)
  local copies, waits for them, and re-layouts: 1.35 us -> 0.02 us
    unnamed x14 -> x8, local copies, waits for them, and re-layouts: 1.35 us -> 0.01 us
    pallas_call x2 -> x3, Pallas kernels: 2.92 us -> 3.11 us  [the longest x1 1.62 us: body(): call(outer_kernel, [whole, seen], 20 * size, 8 * size, in_specs=[SMEM] +...]
  transfers between devices with their start and end apart: 18 -> 18, of which waited for: 7 -> 7; matrix products, arithmetic and copies ran while one was open for 0% -> 0% of each run, Pallas kernels for 37% -> 38%
where the time goes in v7:
time: 52.8 us; the launch traced here: 52.5 us
  starting transfers between devices  25.6 us (48%)
  Pallas kernels  22.2 us (42%)
  waiting for transfers between devices  4.46 us (8%)
    pallas_call x2, Pallas kernels, analyse(): call(kernel, [block] * groups + [token] if back else [whole, token], colu...  16.6 us
    ppermute x14, starting transfers between devices, exchange(): out.append(lax.ppermute(block, 'mem', pairs) if k else block)  12.8 us
    all_to_all x1, starting transfers between devices, body(): lax.all_to_all(outer, 'mem', split_axis=0, concat_axis=0, tiled=True)  3.88 us
    all_to_all x1, starting transfers between devices, body(): lax.all_to_all(inner, 'mem', split_axis=0, concat_axis=0, tiled=True)  3.67 us
    ppermute x14, waiting for transfers between devices, exchange(): out.append(lax.ppermute(block, 'mem', pairs) if k else block)  3.61 us
    ppermute x1, starting transfers between devices, body(): lax.ppermute(high, 'tile', [(i, (i + 1) % tiles) for i in range(tiles)])  3.08 us
    ppermute x1, starting transfers between devices, body(): lax.ppermute(low, 'tile', [((i + 1) % tiles, i) for i in range(tiles)])  2.09 us
    pallas_call x1, Pallas kernels, body(): call(outer_kernel, [whole, seen], 20 * size, 8 * size, in_specs=[SMEM] +...  1.62 us
  transfers between devices with their start and end apart: 18, of which 7 were waited for; matrix products, arithmetic and copies ran while one was open for 0% of the time, Pallas kernels for 38%

profile of v7, /device:TPU:0, one launch (start us, length us, event | category | flops | bytes accessed | tf_op | source)
XLA Modules:
  0.0 52.5 jit_solution(660201435953131389)
XLA Ops:
  0.0 1.2 %shard_map.73 = (f32[2,32,256]{2,1,0:T(8,128)S(1)}, f32[2,32,256]{2,1,0:T(8,128)S(1)}, f32[8,256]{1,0:T(8,128)S(1)}, s32[1,32]{1,0:T(1,128)S(1)}) custom-call(f32[32,32,256]{2,1,0:T(8,128)} %state_ref.3, f32[256]{0:T(256)} %diff_ref.1, f32[256]{0:T(256)} %adv_ref.1, s32[1,32]{1,0:T(1,128)} %count_ref.1), custom_call_target="tpu_custom_call" | custom-call | bytes 1048576 | tf_op jit(solution)/shard_map/pallas_call | solution.py:344
  1.2 3.1 %collective-permute-start = (f32[2,32,256]{2,1,0:T(8,128)S(1)}, f32[2,32,256]{2,1,0:T(8,128)S(1)}, u32[]{:S(2)}, u32[]{:S(2)}) collective-permute-start(f32[2,32,256]{2,1,0:T(8,128)S(1)} %get-tuple-element.32), channel_id=1, source_target_pairs={{0,1},{1,2},{2,3},{3,0},{4,5},{5,6},{6,7},{7,4},{8,9},{9,10},{10,1... | collective-permute-start | bytes 196616 | tf_op jit(solution)/shard_map/ppermute | solution.py:355
  4.3 2.1 %collective-permute-start.1 = (f32[2,32,256]{2,1,0:T(8,128)S(1)}, f32[2,32,256]{2,1,0:T(8,128)S(1)}, u32[]{:S(2)}, u32[]{:S(2)}) collective-permute-start(f32[2,32,256]{2,1,0:T(8,128)S(1)} %get-tuple-element.33), channel_id=1, source_target_pairs={{1,0},{2,1},{3,2},{0,3},{5,4},{6,5},{7,6},{4,7},{9,8},{10,9},{11,1... | collective-permute-start | bytes 196616 | tf_op jit(solution)/shard_map/ppermute | solution.py:356
  6.4 0.0 copy-done
  6.4 0.7 %shard_map.74 = (f32[2,32,256]{2,1,0:T(8,128)S(1)}, f32[2,32,256]{2,1,0:T(8,128)S(1)}, f32[2,32,256]{2,1,0:T(8,128)S(1)}, f32[2,32,256]{2,1,0:T(8,128)S(1)}, f32...) custom-call(s32[1]{0:T(128)} %bitcast.me_ref, ...), custom_call_target="tpu_custom_call" | custom-call | flops 5242880 | bytes 2097152 | tf_op jit(solution)/shard_map/pallas_call | solution.py:357
  7.1 0.1 collective-permute-start.2
  7.2 2.7 %collective-permute-start.3 = (f32[2,32,256]{2,1,0:T(8,128)S(1)}, f32[2,32,256]{2,1,0:T(8,128)S(1)}, u32[]{:S(2)}, u32[]{:S(2)}) collective-permute-start(f32[2,32,256]{2,1,0:T(8,128)S(1)} %get-tuple-element.37), channel_id=1, source_target_pairs={{0,24},{4,28},{8,16},{12,20},{16,8},{20,12},{24,0},{28,4},{1,25},{... | collective-permute-start | bytes 196616 | tf_op jit(solution)/shard_map/ppermute | solution.py:51
  9.9 0.1 collective-permute-start.4
  10.0 0.0 collective-permute-done.before_ref
  10.0 1.6 %collective-permute-start.5 = (f32[2,32,256]{2,1,0:T(8,128)S(1)}, f32[2,32,256]{2,1,0:T(8,128)S(1)}, u32[]{:S(2)}, u32[]{:S(2)}) collective-permute-start(f32[2,32,256]{2,1,0:T(8,128)S(1)} %get-tuple-element.39), channel_id=1, source_target_pairs={{0,8},{4,12},{8,0},{12,4},{16,24},{20,28},{24,16},{28,20},{1,9},{5... | collective-permute-start | bytes 196616 | tf_op jit(solution)/shard_map/ppermute | solution.py:51
  11.6 0.0 collective-permute-done.1.after_ref
  11.6 0.0 collective-permute-start.6
  11.7 0.0 copy-done.1
  11.7 0.0 copy-done.2
  11.7 0.0 copy-done.3
  11.7 1.6 %shard_map.75 = (f32[8,2,32,256]{3,2,1,0:T(8,128)}, f32[2,8,256]{2,1,0:T(8,128)S(1)}) custom-call(s32[1]{0:T(128)} %bitcast.me_ref, f32[2,10,32,256]{3,2,1,0:T(8,128)S(1)} %get-tuple-element.31.rest_ref, f32[2,32,256]{2,1,0:T(8,128)S(1)} %collective-permute-done.before_ref, f32[2,32,256]{2,1,0:T(8,128)S(1)} %collective-permute-done.1.after_ref, ...), custom_call_target="tpu_custom_call" | custom-call | flops 5242880 | bytes 2097152 | tf_op jit(solution)/shard_map/pallas_call | solution.py:367
  13.3 0.0 collective-permute-done.2.refs_0_
  13.3 1.7 %collective-permute-start.7 = (f32[2,32,256]{2,1,0:T(8,128)S(1)}, f32[2,32,256]{2,1,0:T(8,128)S(1)}, u32[]{:S(2)}, u32[]{:S(2)}) collective-permute-start(f32[2,32,256]{2,1,0:T(8,128)S(1)} %get-tuple-element.41), channel_id=1, source_target_pairs={{0,16},{4,20},{8,24},{12,28},{16,0},{20,4},{24,8},{28,12},{1,17},{... | collective-permute-start | bytes 196616 | tf_op jit(solution)/shard_map/ppermute | solution.py:51
  15.0 0.0 collective-permute-done.3.refs_1_
  15.0 0.1 collective-permute-start.8
  15.1 3.9 %all-to-all-start = ((f32[8,2,32,256]{3,2,1,0:T(8,128)}), f32[8,2,32,256]{3,2,1,0:T(8,128)S(1)}, u32[]{:S(2)}, u32[]{:S(2)}) async-start(f32[8,2,32,256]{3,2,1,0:T(8,128)} %get-tuple-element.45), calls=%async_computation | async-start | bytes 1048576 | tf_op jit(solution)/shard_map/all_to_all | solution.py:374
  19.0 0.0 collective-permute-done.4.refs_2_
  19.0 0.0 collective-permute-done.5.refs_3_
  19.0 0.0 collective-permute-done.6.refs_4_
  19.0 0.0 collective-permute-done.7.refs_5_
  19.0 0.0 collective-permute-done.8.refs_6_
  19.0 8.5 %shard_map.76 = (f32[8,2,32,256]{3,2,1,0:T(8,128)}, f32[8,256]{1,0:T(8,128)S(1)}) custom-call(s32[1]{0:T(128)} %bitcast.me_ref, f32[8,256]{1,0:T(8,128)S(1)} %slice_bitcast_fusion.after_ref, f32[2,8,256]{2,1,0:T(8,128)S(1)} %get-tuple-element.35.obs_ref, f32[2,32,256]{2,1,0:T(8,128)S(1)} %collective-permute-done.2.refs_0_, ...), custom_call_target="tpu_custom_call" | custom-call | flops 6039797760 | bytes 1048576 | tf_op jit(solution)/shard_map/pallas_call | solution.py:318
  27.6 0.3 shard_map.77.obs_ref
  27.9 0.8 %all-to-all-done.refs_0_ = f32[8,2,32,256]{3,2,1,0:T(8,128)S(1)} async-done(((f32[8,2,32,256]{3,2,1,0:T(8,128)}), f32[8,2,32,256]{3,2,1,0:T(8,128)S(1)}, u32[]{:S(2)}, u32[]{:S(2)}) %all-to-all-start) | async-done | bytes 524320 | tf_op jit(solution)/shard_map/all_to_all | solution.py:374
  28.7 3.7 %all-to-all-start.1 = ((f32[8,2,32,256]{3,2,1,0:T(8,128)}), f32[8,2,32,256]{3,2,1,0:T(8,128)S(1)}, u32[]{:S(2)}, u32[]{:S(2)}) async-start(f32[8,2,32,256]{3,2,1,0:T(8,128)} %get-tuple-element.47), calls=%async_computation.1 | async-start | bytes 1048576 | tf_op jit(solution)/shard_map/all_to_all | solution.py:377
  32.4 8.1 %shard_map.78 = (f32[2,32,256]{2,1,0:T(8,128)S(1)}, f32[2,32,256]{2,1,0:T(8,128)S(1)}, f32[2,32,256]{2,1,0:T(8,128)S(1)}, f32[2,32,256]{2,1,0:T(8,128)S(1)}, f32...) custom-call(s32[1]{0:T(128)} %bitcast.me_ref, ...), custom_call_target="tpu_custom_call" | custom-call | flops 6039797760 | bytes 1048576 | tf_op jit(solution)/shard_map/pallas_call | solution.py:318
  40.5 2.4 %collective-permute-start.9 = (f32[2,32,256]{2,1,0:T(8,128)S(1)}, f32[2,32,256]{2,1,0:T(8,128)S(1)}, u32[]{:S(2)}, u32[]{:S(2)}) collective-permute-start(f32[2,32,256]{2,1,0:T(8,128)S(1)} %get-tuple-element.46), channel_id=1, source_target_pairs={{0,28},{4,24},{8,20},{12,16},{16,12},{20,8},{24,4},{28,0},{1,29},{... | collective-permute-start | bytes 196616 | tf_op jit(solution)/shard_map/ppermute | solution.py:51
  42.9 0.4 collective-permute-start.10
  43.3 0.3 collective-permute-start.11
  43.5 1.7 %collective-permute-start.12 = (f32[2,32,256]{2,1,0:T(8,128)S(1)}, f32[2,32,256]{2,1,0:T(8,128)S(1)}, u32[]{:S(2)}, u32[]{:S(2)}) collective-permute-start(f32[2,32,256]{2,1,0:T(8,128)S(1)} %get-tuple-element.50), channel_id=1, source_target_pairs={{0,8},{4,12},{8,0},{12,4},{16,24},{20,28},{24,16},{28,20},{1,9},{5... | collective-permute-start | bytes 196616 | tf_op jit(solution)/shard_map/ppermute | solution.py:51
  45.3 0.0 collective-permute-start.13
  45.3 0.2 collective-permute-done.9.after_ref.refs_2_
  45.5 1.7 %collective-permute-start.14 = (f32[2,32,256]{2,1,0:T(8,128)S(1)}, f32[2,32,256]{2,1,0:T(8,128)S(1)}, u32[]{:S(2)}, u32[]{:S(2)}) collective-permute-start(f32[2,32,256]{2,1,0:T(8,128)S(1)} %get-tuple-element.52), channel_id=1, source_target_pairs={{0,16},{4,20},{8,24},{12,28},{16,0},{20,4},{24,8},{28,12},{1,17},{... | collective-permute-start | bytes 196616 | tf_op jit(solution)/shard_map/ppermute | solution.py:51
  47.2 0.0 collective-permute-done.10.refs_0_
  47.2 0.0 collective-permute-start.15
  47.2 0.0 all-to-all-done.1.inner_ref
  47.2 0.8 %shard_map.79.held_ref = f32[32,32,256]{2,1,0:T(8,128)} custom-call(f32[2,32,256]{2,1,0:T(8,128)S(1)} %collective-permute-done.9.after_ref.refs_2_, f32[8,2,32,256]{3,2,1,0:T(8,128)S(1)} %all-to-all-done.1.inner_ref), custom_call_target="tpu_custom_call" | custom-call | flops 262144 | bytes 1048576 | tf_op jit(solution)/shard_map/pallas_call | solution.py:388
  48.1 1.1 %collective-permute-done.11.refs_1_ = f32[2,32,256]{2,1,0:T(8,128)S(1)} collective-permute-done((f32[2,32,256]{2,1,0:T(8,128)S(1)}, f32[2,32,256]{2,1,0:T(8,128)S(1)}, u32[]{:S(2)}, u32[]{:S(2)}) %collective-permute-start.11) | collective-permute-done | bytes 65568 | tf_op jit(solution)/shard_map/ppermute | solution.py:51
  49.1 0.3 collective-permute-done.12.refs_3_
  49.4 0.3 collective-permute-done.13.refs_4_
  49.7 0.4 collective-permute-done.14.refs_5_
  50.1 1.4 %collective-permute-done.15.refs_6_ = f32[2,32,256]{2,1,0:T(8,128)S(1)} collective-permute-done((f32[2,32,256]{2,1,0:T(8,128)S(1)}, f32[2,32,256]{2,1,0:T(8,128)S(1)}, u32[]{:S(2)}, u32[]{:S(2)}) %collective-permute-start.15) | collective-permute-done | bytes 65568 | tf_op jit(solution)/shard_map/ppermute | solution.py:51
  51.5 0.9 %shard_map.80 = f32[32,32,256]{2,1,0:T(8,128)} custom-call(s32[1]{0:T(128)} %bitcast.me_ref, f32[32,32,256]{2,1,0:T(8,128)} %shard_map.79.held_ref, f32[2,32,256]{2,1,0:T(8,128)S(1)} %collective-permute-done.10.refs_0_, f32[2,32,256]{2,1,0:T(8,128)S(1)} %collective-permute-done.11.refs_1_, ...), custom_call_target="tpu_custom_call", output_to_operand_aliasing={{}: (1, {})} | custom-call | flops 262144 | bytes 1048576 | tf_op jit(solution)/shard_map/pallas_call | solution.py:400
  (5 shorter events, 0.0 us)
Async XLA Ops:
  0.0 6.4 %copy-start = (f32[32,32,256]{2,1,0:T(8,128)S(1)}, f32[32,32,256]{2,1,0:T(8,128)}, u32[]{:S(2)}) copy-start(f32[32,32,256]{2,1,0:T(8,128)} %state_ref.3) | copy-start | bytes 3145732
  1.2 8.8 %collective-permute-start = (f32[2,32,256]{2,1,0:T(8,128)S(1)}, f32[2,32,256]{2,1,0:T(8,128)S(1)}, u32[]{:S(2)}, u32[]{:S(2)}) collective-permute-start(f32[2,32,256]{2,1,0:T(8,128)S(1)} %get-tuple-element.32), channel_id=1, source_target_pairs={{0,1},{1,2},{2,3},{3,0},{4,5},{5,6},{6,7},{7,4},{8,9},{9,10},{10,1... | collective-permute-start | bytes 196616 | tf_op jit(solution)/shard_map/ppermute | solution.py:355
  4.3 7.3 %collective-permute-start.1 = (f32[2,32,256]{2,1,0:T(8,128)S(1)}, f32[2,32,256]{2,1,0:T(8,128)S(1)}, u32[]{:S(2)}, u32[]{:S(2)}) collective-permute-start(f32[2,32,256]{2,1,0:T(8,128)S(1)} %get-tuple-element.33), channel_id=1, source_target_pairs={{1,0},{2,1},{3,2},{0,3},{5,4},{6,5},{7,6},{4,7},{9,8},{10,9},{11,1... | collective-permute-start | bytes 196616 | tf_op jit(solution)/shard_map/ppermute | solution.py:356
  6.4 5.3 %copy-start.1 = (s32[1,32,512]{2,1,0:T(8,128)S(1)}, s32[1,32,512]{2,1,0:T(8,128)}, u32[]{:S(2)}) copy-start(s32[1,32,512]{2,1,0:T(8,128)} %param.10) | copy-start | bytes 196612
  6.4 5.3 %copy-start.2 = (f32[1,32,512]{2,1,0:T(8,128)S(1)}, f32[1,32,512]{2,1,0:T(8,128)}, u32[]{:S(2)}) copy-start(f32[1,32,512]{2,1,0:T(8,128)} %param.12) | copy-start | bytes 196612
  6.4 5.3 %copy-start.3 = (f32[1,32,512]{2,1,0:T(8,128)S(1)}, f32[1,32,512]{2,1,0:T(8,128)}, u32[]{:S(2)}) copy-start(f32[1,32,512]{2,1,0:T(8,128)} %param.13) | copy-start | bytes 196612
  7.1 6.2 %collective-permute-start.2 = (f32[2,32,256]{2,1,0:T(8,128)S(1)}, f32[2,32,256]{2,1,0:T(8,128)S(1)}, u32[]{:S(2)}, u32[]{:S(2)}) collective-permute-start(f32[2,32,256]{2,1,0:T(8,128)S(1)} %get-tuple-element.36), channel_id=1, source_target_pairs={{0,4},{4,0},{8,12},{12,8},{16,20},{20,16},{24,28},{28,24},{1,5},{5... | collective-permute-start | bytes 196616 | tf_op jit(solution)/shard_map/ppermute | solution.py:51
  7.2 7.8 %collective-permute-start.3 = (f32[2,32,256]{2,1,0:T(8,128)S(1)}, f32[2,32,256]{2,1,0:T(8,128)S(1)}, u32[]{:S(2)}, u32[]{:S(2)}) collective-permute-start(f32[2,32,256]{2,1,0:T(8,128)S(1)} %get-tuple-element.37), channel_id=1, source_target_pairs={{0,24},{4,28},{8,16},{12,20},{16,8},{20,12},{24,0},{28,4},{1,25},{... | collective-permute-start | bytes 196616 | tf_op jit(solution)/shard_map/ppermute | solution.py:51
  9.9 9.1 %collective-permute-start.4 = (f32[2,32,256]{2,1,0:T(8,128)S(1)}, f32[2,32,256]{2,1,0:T(8,128)S(1)}, u32[]{:S(2)}, u32[]{:S(2)}) collective-permute-start(f32[2,32,256]{2,1,0:T(8,128)S(1)} %get-tuple-element.38), channel_id=1, source_target_pairs={{0,28},{4,24},{8,20},{12,16},{16,12},{20,8},{24,4},{28,0},{1,29},{... | collective-permute-start | bytes 196616 | tf_op jit(solution)/shard_map/ppermute | solution.py:51
  10.0 9.0 %collective-permute-start.5 = (f32[2,32,256]{2,1,0:T(8,128)S(1)}, f32[2,32,256]{2,1,0:T(8,128)S(1)}, u32[]{:S(2)}, u32[]{:S(2)}) collective-permute-start(f32[2,32,256]{2,1,0:T(8,128)S(1)} %get-tuple-element.39), channel_id=1, source_target_pairs={{0,8},{4,12},{8,0},{12,4},{16,24},{20,28},{24,16},{28,20},{1,9},{5... | collective-permute-start | bytes 196616 | tf_op jit(solution)/shard_map/ppermute | solution.py:51
  11.6 7.4 %collective-permute-start.6 = (f32[2,32,256]{2,1,0:T(8,128)S(1)}, f32[2,32,256]{2,1,0:T(8,128)S(1)}, u32[]{:S(2)}, u32[]{:S(2)}) collective-permute-start(f32[2,32,256]{2,1,0:T(8,128)S(1)} %get-tuple-element.40), channel_id=1, source_target_pairs={{0,12},{4,8},{8,4},{12,0},{16,28},{20,24},{24,20},{28,16},{1,13},{... | collective-permute-start | bytes 196616 | tf_op jit(solution)/shard_map/ppermute | solution.py:51
  13.3 5.7 %collective-permute-start.7 = (f32[2,32,256]{2,1,0:T(8,128)S(1)}, f32[2,32,256]{2,1,0:T(8,128)S(1)}, u32[]{:S(2)}, u32[]{:S(2)}) collective-permute-start(f32[2,32,256]{2,1,0:T(8,128)S(1)} %get-tuple-element.41), channel_id=1, source_target_pairs={{0,16},{4,20},{8,24},{12,28},{16,0},{20,4},{24,8},{28,12},{1,17},{... | collective-permute-start | bytes 196616 | tf_op jit(solution)/shard_map/ppermute | solution.py:51
  15.0 4.0 %collective-permute-start.8 = (f32[2,32,256]{2,1,0:T(8,128)S(1)}, f32[2,32,256]{2,1,0:T(8,128)S(1)}, u32[]{:S(2)}, u32[]{:S(2)}) collective-permute-start(f32[2,32,256]{2,1,0:T(8,128)S(1)} %get-tuple-element.42), channel_id=1, source_target_pairs={{0,20},{4,16},{8,28},{12,24},{16,4},{20,0},{24,12},{28,8},{1,21},{... | collective-permute-start | bytes 196616 | tf_op jit(solution)/shard_map/ppermute | solution.py:51
  15.1 13.6 %all-to-all-start = ((f32[8,2,32,256]{3,2,1,0:T(8,128)}), f32[8,2,32,256]{3,2,1,0:T(8,128)S(1)}, u32[]{:S(2)}, u32[]{:S(2)}) async-start(f32[8,2,32,256]{3,2,1,0:T(8,128)} %get-tuple-element.45), calls=%async_computation | async-start | bytes 1048576 | tf_op jit(solution)/shard_map/all_to_all | solution.py:374
  28.7 18.5 %all-to-all-start.1 = ((f32[8,2,32,256]{3,2,1,0:T(8,128)}), f32[8,2,32,256]{3,2,1,0:T(8,128)S(1)}, u32[]{:S(2)}, u32[]{:S(2)}) async-start(f32[8,2,32,256]{3,2,1,0:T(8,128)} %get-tuple-element.47), calls=%async_computation.1 | async-start | bytes 1048576 | tf_op jit(solution)/shard_map/all_to_all | solution.py:377
  40.5 5.0 %collective-permute-start.9 = (f32[2,32,256]{2,1,0:T(8,128)S(1)}, f32[2,32,256]{2,1,0:T(8,128)S(1)}, u32[]{:S(2)}, u32[]{:S(2)}) collective-permute-start(f32[2,32,256]{2,1,0:T(8,128)S(1)} %get-tuple-element.46), channel_id=1, source_target_pairs={{0,28},{4,24},{8,20},{12,16},{16,12},{20,8},{24,4},{28,0},{1,29},{... | collective-permute-start | bytes 196616 | tf_op jit(solution)/shard_map/ppermute | solution.py:51
  42.9 4.3 %collective-permute-start.10 = (f32[2,32,256]{2,1,0:T(8,128)S(1)}, f32[2,32,256]{2,1,0:T(8,128)S(1)}, u32[]{:S(2)}, u32[]{:S(2)}) collective-permute-start(f32[2,32,256]{2,1,0:T(8,128)S(1)} %get-tuple-element.48), channel_id=1, source_target_pairs={{0,4},{4,0},{8,12},{12,8},{16,20},{20,16},{24,28},{28,24},{1,5},{5... | collective-permute-start | bytes 196616 | tf_op jit(solution)/shard_map/ppermute | solution.py:51
  43.3 5.9 %collective-permute-start.11 = (f32[2,32,256]{2,1,0:T(8,128)S(1)}, f32[2,32,256]{2,1,0:T(8,128)S(1)}, u32[]{:S(2)}, u32[]{:S(2)}) collective-permute-start(f32[2,32,256]{2,1,0:T(8,128)S(1)} %get-tuple-element.49), channel_id=1, source_target_pairs={{0,24},{4,28},{8,16},{12,20},{16,8},{20,12},{24,0},{28,4},{1,25},{... | collective-permute-start | bytes 196616 | tf_op jit(solution)/shard_map/ppermute | solution.py:51
  43.5 5.9 %collective-permute-start.12 = (f32[2,32,256]{2,1,0:T(8,128)S(1)}, f32[2,32,256]{2,1,0:T(8,128)S(1)}, u32[]{:S(2)}, u32[]{:S(2)}) collective-permute-start(f32[2,32,256]{2,1,0:T(8,128)S(1)} %get-tuple-element.50), channel_id=1, source_target_pairs={{0,8},{4,12},{8,0},{12,4},{16,24},{20,28},{24,16},{28,20},{1,9},{5... | collective-permute-start | bytes 196616 | tf_op jit(solution)/shard_map/ppermute | solution.py:51
  45.3 4.4 %collective-permute-start.13 = (f32[2,32,256]{2,1,0:T(8,128)S(1)}, f32[2,32,256]{2,1,0:T(8,128)S(1)}, u32[]{:S(2)}, u32[]{:S(2)}) collective-permute-start(f32[2,32,256]{2,1,0:T(8,128)S(1)} %get-tuple-element.51), channel_id=1, source_target_pairs={{0,12},{4,8},{8,4},{12,0},{16,28},{20,24},{24,20},{28,16},{1,13},{... | collective-permute-start | bytes 196616 | tf_op jit(solution)/shard_map/ppermute | solution.py:51
  45.5 4.6 %collective-permute-start.14 = (f32[2,32,256]{2,1,0:T(8,128)S(1)}, f32[2,32,256]{2,1,0:T(8,128)S(1)}, u32[]{:S(2)}, u32[]{:S(2)}) collective-permute-start(f32[2,32,256]{2,1,0:T(8,128)S(1)} %get-tuple-element.52), channel_id=1, source_target_pairs={{0,16},{4,20},{8,24},{12,28},{16,0},{20,4},{24,8},{28,12},{1,17},{... | collective-permute-start | bytes 196616 | tf_op jit(solution)/shard_map/ppermute | solution.py:51
  47.2 4.3 %collective-permute-start.15 = (f32[2,32,256]{2,1,0:T(8,128)S(1)}, f32[2,32,256]{2,1,0:T(8,128)S(1)}, u32[]{:S(2)}, u32[]{:S(2)}) collective-permute-start(f32[2,32,256]{2,1,0:T(8,128)S(1)} %get-tuple-element.53), channel_id=1, source_target_pairs={{0,20},{4,16},{8,28},{12,24},{16,4},{20,0},{24,12},{28,8},{1,21},{... | collective-permute-start | bytes 196616 | tf_op jit(solution)/shard_map/ppermute | solution.py:51

commit v8 on v7

--- a/solution.py
+++ b/solution.py
@@ -137,9 +137,8 @@
     rest_ref[1] = turned_ref[columns - quarter - 2 :]
 
 
-def outer_kernel(
-    me_ref, rest_ref, before_ref, after_ref, num_ref, count_ref, where_ref, value_ref, rinv_ref, out_ref, obs_ref
-):
+def outer_kernel(rest_ref, before_ref, after_ref, num_ref, out_ref, done_ref):
+    done_ref[...] = jnp.zeros_like(done_ref)
     diffusion = num_ref[0:1][None]
     advection = num_ref[1:2][None]
     low = jnp.concatenate([before_ref[...], rest_ref[0]], axis=0)
@@ -147,9 +146,6 @@
     low = stencil(stencil(low, diffusion, advection), diffusion, advection)
     high = stencil(stencil(high, diffusion, advection), diffusion, advection)
     out_ref[...] = jnp.concatenate([low, high], axis=0).reshape(out_ref.shape)
-    half = obs_ref.shape[0]
-    first = inner_start(me_ref[0] * half, where_ref.shape[0] // 4)
-    observe(first, count_ref, where_ref, value_ref, rinv_ref, obs_ref)
 
 
 def inner_join_kernel(after_ref, inner_ref, out_ref, made_ref, sems):
@@ -194,13 +190,6 @@
         copy.wait()
 
 
-def observe_kernel(me_ref, after_ref, count_ref, where_ref, value_ref, rinv_ref, out_ref):
-    del after_ref
-    half = out_ref.shape[0]
-    first = outer_start(me_ref[0] * half, where_ref.shape[0] // 4)
-    observe(first, count_ref, where_ref, value_ref, rinv_ref, out_ref)
-
-
 def observe(first, count_ref, where_ref, value_ref, rinv_ref, out_ref):
     columns, _, entries = out_ref.shape
     slots = where_ref.shape[1]
@@ -224,9 +213,7 @@
         out_ref[c, 1:2] = sums[3:4] + (sums[4:5] + sums[5:6])
 
 
-def analyse_kernel(after_ref, obs_ref, states, outs, done_ref, root, mixed, ahead, s, p, u, t, r, w):
-    del after_ref
-    done_ref[...] = jnp.zeros_like(done_ref)
+def analyse_kernel(obs_ref, states, outs, root, mixed, ahead, s, p, u, t, r, w):
     groups = len(outs)
     columns, local, entries = outs[0].shape
     members = groups * local
@@ -254,13 +241,14 @@
         root[c] = gram
         store(s, c, slice(None), gram)
 
-    def advance(step):
-        for c, rows in parts:
+    def advance(step, some):
+        for c, rows in some:
             x = 2.25 * ahead[c, rows] + multiply(r.at[step % 2], w.at[step % 2], c, rows)
             ahead[c, rows] = x
             if step < PAIRS - 1:
                 store(w.at[(step + 1) % 2], c, rows, x)
 
+    gaps = [parts[i::4] for i in range(4)]
     for step in range(PAIRS):
         for c, rows in parts:
             x = multiply(s, s, c, rows)
@@ -269,19 +257,26 @@
             store(u, c, rows, 0.0625 * x - 0.5625 * y)
             mixed[c, rows] = 1.6875 * x - 2.4375 * y
         if step > 0:
-            advance(step - 1)
+            advance(step - 1, gaps[0])
         for c, rows in parts:
             store(r.at[step % 2], c, rows, mixed[c, rows] + multiply(u, p, c, rows))
+        if step > 0:
+            advance(step - 1, gaps[1])
         if step < PAIRS - 1:
             for c, rows in parts:
                 x = 2.25 * root[c, rows] + multiply(r.at[step % 2], s, c, rows)
                 store(t, c, rows, x)
                 mixed[c, rows] = 2.25 * x
+        if step > 0:
+            advance(step - 1, gaps[2])
+        if step < PAIRS - 1:
             for c, rows in parts:
                 x = mixed[c, rows] + multiply(t, r.at[step % 2], c, rows)
                 root[c, rows] = x
                 store(s, c, rows, x)
-    advance(PAIRS - 1)
+        if step > 0:
+            advance(step - 1, gaps[3])
+    advance(PAIRS - 1, parts)
     for c in every:
         x = ahead[c]
         inner = jnp.sum(x * forces[c], axis=1, keepdims=True)
@@ -291,38 +286,36 @@
             outs[k][c] = result[k * local : (k + 1) * local]
 
 
-def analyse(states, obs, me, after, back):
-    groups = len(states)
-    columns, local, entries = states[0].shape
-    members = groups * local
-    block = jax.ShapeDtypeStruct((columns, local, entries), jnp.float32)
-    whole = jax.ShapeDtypeStruct((groups, columns, local, entries), jnp.float32)
-    token = jax.ShapeDtypeStruct(after.shape, jnp.float32)
+def sizes_of(columns, local, entries, members):
     full = pltpu.VMEM((columns, members, members), jnp.float32)
     pair = pltpu.VMEM((2, columns, members, members), jnp.bfloat16)
     two = pltpu.VMEM((2, 2, columns, members, members), jnp.bfloat16)
     ahead = pltpu.VMEM((columns, members, entries), jnp.float32)
     factor = pltpu.VMEM((2, 2, columns, members, entries), jnp.bfloat16)
-
-    def kernel(me_ref, after_ref, obs_ref, *refs):
-        *blocks, done_ref = refs[:-SCRATCH]
-        if back:
-            whole_ref, *outs = blocks
-            ins = [whole_ref.at[target(me_ref[0], k, groups)] for k in issue_order(groups)]
-        else:
-            *ins, whole_ref = blocks
-            outs = [whole_ref.at[source(me_ref[0], k, groups)] for k in issue_order(groups)]
-        analyse_kernel(after_ref, obs_ref, ins, outs, done_ref, *refs[-SCRATCH:])
-
-    operands = [states] if back else states
-    return call(
-        kernel,
-        [block] * groups + [token] if back else [whole, token],
-        columns * 90 * 2 * members * members * entries,
-        8 * columns * members * entries,
-        in_specs=[SMEM] + [VMEM] * (len(operands) + 2),
-        scratch_shapes=[full, full, ahead, pair, pair, pair, pair, two, factor],
-    )(me, after, obs, *operands)
+    return [full, full, ahead, pair, pair, pair, pair, two, factor]
+
+
+def inner_analysis(me_ref, after_ref, count_ref, where_ref, value_ref, rinv_ref, *refs):
+    del after_ref
+    *ins, whole_ref, done_ref, obs_ref = refs[:-SCRATCH]
+    groups = len(ins)
+    half = ins[0].shape[0]
+    done_ref[...] = jnp.zeros_like(done_ref)
+    outs = [whole_ref.at[source(me_ref[0], k, groups)] for k in issue_order(groups)]
+    first = inner_start(me_ref[0] * half, where_ref.shape[0] // 4)
+    observe(first, count_ref, where_ref, value_ref, rinv_ref, obs_ref)
+    analyse_kernel(obs_ref, ins, outs, *refs[-SCRATCH:])
+
+
+def outer_analysis(me_ref, after_ref, count_ref, where_ref, value_ref, rinv_ref, whole_ref, *refs):
+    del after_ref
+    *outs, obs_ref = refs[:-SCRATCH]
+    groups = len(outs)
+    half = outs[0].shape[0]
+    ins = [whole_ref.at[target(me_ref[0], k, groups)] for k in issue_order(groups)]
+    first = outer_start(me_ref[0] * half, where_ref.shape[0] // 4)
+    observe(first, count_ref, where_ref, value_ref, rinv_ref, obs_ref)
+    analyse_kernel(obs_ref, ins, outs, *refs[-SCRATCH:])
 
 
 def body(background, diffusion, advection, obs_where, obs_count, obs_value, obs_rinv):
@@ -338,7 +331,9 @@
     me = lax.axis_index("mem")[None].astype(jnp.int32)
     pieces = len(pieces_of(local))
     width = min(columns, 8)
-    seen = jax.ShapeDtypeStruct((half, 8, entries), jnp.float32)
+    token = jax.ShapeDtypeStruct((8, entries), jnp.float32)
+    scratch = [pltpu.VMEM((half, 8, entries), jnp.float32)] + sizes_of(half, local, entries, groups * local)
+    flops = half * 180 * (groups * local) ** 2 * entries
     numbers = jax.ShapeDtypeStruct((8, entries), jnp.float32)
 
     low, high, numbers, counts = call(
@@ -364,25 +359,32 @@
     )(me, background, numbers)
     inner = exchange(inner)
     slots = (counts, obs_where[0], obs_value[0], obs_rinv[0])
-    outer, obs = call(
+    outer, done = call(
         outer_kernel,
-        [whole, seen],
+        [whole, token],
         20 * size,
         8 * size,
-        in_specs=[SMEM] + [VMEM] * 8,
-    )(me, rest, before, after, numbers, *slots)
+        in_specs=[VMEM] * 4,
+    )(rest, before, after, numbers)
     outer = lax.all_to_all(outer, "mem", split_axis=0, concat_axis=0, tiled=True)
 
-    inner, done = analyse(inner, obs, me, obs[0], False)
+    inner, done = call(
+        inner_analysis,
+        [whole, token],
+        flops,
+        4 * size,
+        in_specs=[SMEM] + [VMEM] * (groups + 5),
+        scratch_shapes=scratch,
+    )(me, done, *slots, *inner)
     inner = lax.all_to_all(inner, "mem", split_axis=0, concat_axis=0, tiled=True)
-    obs = call(
-        observe_kernel,
-        seen,
-        half * 2 * 16 * obs_where.shape[2] * entries,
-        12 * obs_where.size,
-        in_specs=[SMEM] + [VMEM] * 5,
-    )(me, done, *slots)
-    *outer, _ = analyse(outer, obs, me, done, True)
+    outer = call(
+        outer_analysis,
+        [block] * groups,
+        flops,
+        4 * size,
+        in_specs=[SMEM] + [VMEM] * 6,
+        scratch_shapes=scratch,
+    )(me, done, *slots, outer)
     outer = exchange(outer)
     result = jax.ShapeDtypeStruct(background.shape, jnp.float32)
     made = call(

time: 52.8 us -> 52.1 us (0.987)
  Pallas kernels: 22.2 us -> 20.8 us
    pallas_call x4 -> x3, Pallas kernels: 18.5 us -> 17.1 us  [the longest x1 8.37 us: body(): call(inner_analysis, [whole, token], flops, 4 * size, in_specs=[SMEM] + [...]
  transfers between devices with their start and end apart: 18 -> 18, of which waited for: 7 -> 7; matrix products, arithmetic and copies ran while one was open for 0% -> 0% of each run, Pallas kernels for 38% -> 36%
where the time goes in v8:
time: 52.1 us; the launch traced here: 51.7 us
  starting transfers between devices  25.8 us (50%)
  Pallas kernels  20.8 us (40%)
  waiting for transfers between devices  4.89 us (9%)
    ppermute x14, starting transfers between devices, exchange(): out.append(lax.ppermute(block, 'mem', pairs) if k else block)  13 us
    pallas_call x1, Pallas kernels, body(): call(inner_analysis, [whole, token], flops, 4 * size, in_specs=[SMEM] + [...  8.37 us
    pallas_call x1, Pallas kernels, body(): call(outer_analysis, [block] * groups, flops, 4 * size, in_specs=[SMEM] +...  7.57 us
    all_to_all x1, starting transfers between devices, body(): lax.all_to_all(outer, 'mem', split_axis=0, concat_axis=0, tiled=True)  3.93 us
    all_to_all x1, starting transfers between devices, body(): lax.all_to_all(inner, 'mem', split_axis=0, concat_axis=0, tiled=True)  3.67 us
    ppermute x14, waiting for transfers between devices, exchange(): out.append(lax.ppermute(block, 'mem', pairs) if k else block)  3.59 us
    ppermute x1, starting transfers between devices, body(): lax.ppermute(high, 'tile', [(i, (i + 1) % tiles) for i in range(tiles)])  3.08 us
    ppermute x1, starting transfers between devices, body(): lax.ppermute(low, 'tile', [((i + 1) % tiles, i) for i in range(tiles)])  2.09 us
  transfers between devices with their start and end apart: 18, of which 7 were waited for; matrix products, arithmetic and copies ran while one was open for 0% of the time, Pallas kernels for 36%

profile of v8, /device:TPU:0, one launch (start us, length us, event | category | flops | bytes accessed | tf_op | source)
XLA Modules:
  0.0 51.7 jit_solution(12793966742412843574)
XLA Ops:
  0.0 0.0 copy-start
  0.0 1.2 %shard_map.73 = (f32[2,32,256]{2,1,0:T(8,128)S(1)}, f32[2,32,256]{2,1,0:T(8,128)S(1)}, f32[8,256]{1,0:T(8,128)S(1)}, s32[1,32]{1,0:T(1,128)S(1)}) custom-call(f32[32,32,256]{2,1,0:T(8,128)} %state_ref.3, f32[256]{0:T(256)} %diff_ref.1, f32[256]{0:T(256)} %adv_ref.1, s32[1,32]{1,0:T(1,128)} %count_ref.1), custom_call_target="tpu_custom_call" | custom-call | bytes 1048576 | tf_op jit(solution)/shard_map/pallas_call | solution.py:339
  1.2 3.1 %collective-permute-start = (f32[2,32,256]{2,1,0:T(8,128)S(1)}, f32[2,32,256]{2,1,0:T(8,128)S(1)}, u32[]{:S(2)}, u32[]{:S(2)}) collective-permute-start(f32[2,32,256]{2,1,0:T(8,128)S(1)} %get-tuple-element.32), channel_id=1, source_target_pairs={{0,1},{1,2},{2,3},{3,0},{4,5},{5,6},{6,7},{7,4},{8,9},{9,10},{10,1... | collective-permute-start | bytes 196616 | tf_op jit(solution)/shard_map/ppermute | solution.py:350
  4.3 2.1 %collective-permute-start.1 = (f32[2,32,256]{2,1,0:T(8,128)S(1)}, f32[2,32,256]{2,1,0:T(8,128)S(1)}, u32[]{:S(2)}, u32[]{:S(2)}) collective-permute-start(f32[2,32,256]{2,1,0:T(8,128)S(1)} %get-tuple-element.33), channel_id=1, source_target_pairs={{1,0},{2,1},{3,2},{0,3},{5,4},{6,5},{7,6},{4,7},{9,8},{10,9},{11,1... | collective-permute-start | bytes 196616 | tf_op jit(solution)/shard_map/ppermute | solution.py:351
  6.4 0.0 copy-done
  6.4 0.7 %shard_map.74 = (f32[2,32,256]{2,1,0:T(8,128)S(1)}, f32[2,32,256]{2,1,0:T(8,128)S(1)}, f32[2,32,256]{2,1,0:T(8,128)S(1)}, f32[2,32,256]{2,1,0:T(8,128)S(1)}, f32...) custom-call(s32[1]{0:T(128)} %bitcast.me_ref, ...), custom_call_target="tpu_custom_call" | custom-call | flops 5242880 | bytes 2097152 | tf_op jit(solution)/shard_map/pallas_call | solution.py:352
  7.1 0.1 collective-permute-start.2
  7.2 2.7 %collective-permute-start.3 = (f32[2,32,256]{2,1,0:T(8,128)S(1)}, f32[2,32,256]{2,1,0:T(8,128)S(1)}, u32[]{:S(2)}, u32[]{:S(2)}) collective-permute-start(f32[2,32,256]{2,1,0:T(8,128)S(1)} %get-tuple-element.37), channel_id=1, source_target_pairs={{0,24},{4,28},{8,16},{12,20},{16,8},{20,12},{24,0},{28,4},{1,25},{... | collective-permute-start | bytes 196616 | tf_op jit(solution)/shard_map/ppermute | solution.py:51
  9.9 0.1 collective-permute-start.4
  10.0 0.0 collective-permute-done.before_ref
  10.0 1.6 %collective-permute-start.5 = (f32[2,32,256]{2,1,0:T(8,128)S(1)}, f32[2,32,256]{2,1,0:T(8,128)S(1)}, u32[]{:S(2)}, u32[]{:S(2)}) collective-permute-start(f32[2,32,256]{2,1,0:T(8,128)S(1)} %get-tuple-element.39), channel_id=1, source_target_pairs={{0,8},{4,12},{8,0},{12,4},{16,24},{20,28},{24,16},{28,20},{1,9},{5... | collective-permute-start | bytes 196616 | tf_op jit(solution)/shard_map/ppermute | solution.py:51
  11.6 0.0 collective-permute-done.1.after_ref
  11.6 0.0 collective-permute-start.6
  11.7 0.0 collective-permute-done.2.refs_0_
  11.7 1.7 %collective-permute-start.7 = (f32[2,32,256]{2,1,0:T(8,128)S(1)}, f32[2,32,256]{2,1,0:T(8,128)S(1)}, u32[]{:S(2)}, u32[]{:S(2)}) collective-permute-start(f32[2,32,256]{2,1,0:T(8,128)S(1)} %get-tuple-element.41), channel_id=1, source_target_pairs={{0,16},{4,20},{8,24},{12,28},{16,0},{20,4},{24,8},{28,12},{1,17},{... | collective-permute-start | bytes 196616 | tf_op jit(solution)/shard_map/ppermute | solution.py:51
  13.3 0.0 collective-permute-done.3.refs_1_
  13.3 0.2 collective-permute-start.8
  13.5 1.1 %shard_map.75 = (f32[8,2,32,256]{3,2,1,0:T(8,128)}, f32[8,256]{1,0:T(8,128)S(1)}) custom-call(f32[2,10,32,256]{3,2,1,0:T(8,128)S(1)} %get-tuple-element.31.rest_ref, f32[2,32,256]{2,1,0:T(8,128)S(1)} %collective-permute-done.before_ref, f32[2,32,256]{2,1,0:T(8,128)S(1)} %collective-permute-done.1.after_ref, f32[8,256]{1,0:T(8,128)S(1)} %get-tuple-element.30.num_ref), custom_call_target="tpu_custom_call" | custom-call | flops 5242880 | bytes 2097152 | tf_op jit(solution)/shard_map/pallas_call | solution.py:362
  14.7 3.9 %all-to-all-start = ((f32[8,2,32,256]{3,2,1,0:T(8,128)}), f32[8,2,32,256]{3,2,1,0:T(8,128)S(1)}, u32[]{:S(2)}, u32[]{:S(2)}) async-start(f32[8,2,32,256]{3,2,1,0:T(8,128)} %get-tuple-element.45), calls=%async_computation | async-start | bytes 1048576 | tf_op jit(solution)/shard_map/all_to_all | solution.py:369
  18.6 0.0 collective-permute-done.4.refs_2_
  18.6 0.0 collective-permute-done.5.refs_3_
  18.6 0.0 collective-permute-done.6.refs_4_
  18.6 0.0 collective-permute-done.7.refs_5_
  18.7 0.0 collective-permute-done.8.refs_6_
  18.7 0.0 copy-done.1
  18.7 0.0 copy-done.2
  18.7 0.0 copy-done.3
  18.7 8.4 %shard_map.76 = (f32[8,2,32,256]{3,2,1,0:T(8,128)}, f32[8,256]{1,0:T(8,128)S(1)}) custom-call(s32[1]{0:T(128)} %bitcast.me_ref, f32[8,256]{1,0:T(8,128)S(1)} %get-tuple-element.34.after_ref, s32[1,32]{1,0:T(1,128)S(1)} %get-tuple-element.35.count_ref, s32[32,512]{1,0:T(8,128)S(1)} %bitcast.4, f32[32,512]{1,0:T(8,128)S(1)} %bitcast.6, f32[32,512]{1,0:T(8,128)S(1)} %bitcast.8, ...), custom_call_target="tpu_custom_call" | custom-call | flops 6039797760 | bytes 1048576 | tf_op jit(solution)/shard_map/pallas_call | solution.py:371
  27.1 1.3 %all-to-all-done.whole_ref = f32[8,2,32,256]{3,2,1,0:T(8,128)S(1)} async-done(((f32[8,2,32,256]{3,2,1,0:T(8,128)}), f32[8,2,32,256]{3,2,1,0:T(8,128)S(1)}, u32[]{:S(2)}, u32[]{:S(2)}) %all-to-all-start) | async-done | bytes 524320 | tf_op jit(solution)/shard_map/all_to_all | solution.py:369
  28.4 3.7 %all-to-all-start.1 = ((f32[8,2,32,256]{3,2,1,0:T(8,128)}), f32[8,2,32,256]{3,2,1,0:T(8,128)S(1)}, u32[]{:S(2)}, u32[]{:S(2)}) async-start(f32[8,2,32,256]{3,2,1,0:T(8,128)} %get-tuple-element.47), calls=%async_computation.1 | async-start | bytes 1048576 | tf_op jit(solution)/shard_map/all_to_all | solution.py:379
  32.0 7.6 %shard_map.77 = (f32[2,32,256]{2,1,0:T(8,128)S(1)}, f32[2,32,256]{2,1,0:T(8,128)S(1)}, f32[2,32,256]{2,1,0:T(8,128)S(1)}, f32[2,32,256]{2,1,0:T(8,128)S(1)}, f32...) custom-call(s32[1]{0:T(128)} %bitcast.me_ref, ...), custom_call_target="tpu_custom_call" | custom-call | flops 6039797760 | bytes 1048576 | tf_op jit(solution)/shard_map/pallas_call | solution.py:380
  39.6 2.5 %collective-permute-start.9 = (f32[2,32,256]{2,1,0:T(8,128)S(1)}, f32[2,32,256]{2,1,0:T(8,128)S(1)}, u32[]{:S(2)}, u32[]{:S(2)}) collective-permute-start(f32[2,32,256]{2,1,0:T(8,128)S(1)} %get-tuple-element.46), channel_id=1, source_target_pairs={{0,28},{4,24},{8,20},{12,16},{16,12},{20,8},{24,4},{28,0},{1,29},{... | collective-permute-start | bytes 196616 | tf_op jit(solution)/shard_map/ppermute | solution.py:51
  42.1 0.4 collective-permute-start.10
  42.5 0.3 collective-permute-start.11
  42.7 1.7 %collective-permute-start.12 = (f32[2,32,256]{2,1,0:T(8,128)S(1)}, f32[2,32,256]{2,1,0:T(8,128)S(1)}, u32[]{:S(2)}, u32[]{:S(2)}) collective-permute-start(f32[2,32,256]{2,1,0:T(8,128)S(1)} %get-tuple-element.50), channel_id=1, source_target_pairs={{0,8},{4,12},{8,0},{12,4},{16,24},{20,28},{24,16},{28,20},{1,9},{5... | collective-permute-start | bytes 196616 | tf_op jit(solution)/shard_map/ppermute | solution.py:51
  44.5 0.0 collective-permute-start.13
  44.5 0.2 collective-permute-done.9.after_ref.refs_2_
  44.7 1.7 %collective-permute-start.14 = (f32[2,32,256]{2,1,0:T(8,128)S(1)}, f32[2,32,256]{2,1,0:T(8,128)S(1)}, u32[]{:S(2)}, u32[]{:S(2)}) collective-permute-start(f32[2,32,256]{2,1,0:T(8,128)S(1)} %get-tuple-element.52), channel_id=1, source_target_pairs={{0,16},{4,20},{8,24},{12,28},{16,0},{20,4},{24,8},{28,12},{1,17},{... | collective-permute-start | bytes 196616 | tf_op jit(solution)/shard_map/ppermute | solution.py:51
  46.4 0.0 collective-permute-done.10.refs_0_
  46.4 0.0 collective-permute-start.15
  46.4 0.0 all-to-all-done.1.inner_ref
  46.4 0.8 %shard_map.78.held_ref = f32[32,32,256]{2,1,0:T(8,128)} custom-call(f32[2,32,256]{2,1,0:T(8,128)S(1)} %collective-permute-done.9.after_ref.refs_2_, f32[8,2,32,256]{3,2,1,0:T(8,128)S(1)} %all-to-all-done.1.inner_ref), custom_call_target="tpu_custom_call" | custom-call | flops 262144 | bytes 1048576 | tf_op jit(solution)/shard_map/pallas_call | solution.py:390
  47.3 1.1 %collective-permute-done.11.refs_1_ = f32[2,32,256]{2,1,0:T(8,128)S(1)} collective-permute-done((f32[2,32,256]{2,1,0:T(8,128)S(1)}, f32[2,32,256]{2,1,0:T(8,128)S(1)}, u32[]{:S(2)}, u32[]{:S(2)}) %collective-permute-start.11) | collective-permute-done | bytes 65568 | tf_op jit(solution)/shard_map/ppermute | solution.py:51
  48.3 0.3 collective-permute-done.12.refs_3_
  48.6 0.3 collective-permute-done.13.refs_4_
  48.9 0.4 collective-permute-done.14.refs_5_
  49.3 1.4 %collective-permute-done.15.refs_6_ = f32[2,32,256]{2,1,0:T(8,128)S(1)} collective-permute-done((f32[2,32,256]{2,1,0:T(8,128)S(1)}, f32[2,32,256]{2,1,0:T(8,128)S(1)}, u32[]{:S(2)}, u32[]{:S(2)}) %collective-permute-start.15) | collective-permute-done | bytes 65568 | tf_op jit(solution)/shard_map/ppermute | solution.py:51
  50.7 0.9 %shard_map.79 = f32[32,32,256]{2,1,0:T(8,128)} custom-call(s32[1]{0:T(128)} %bitcast.me_ref, f32[32,32,256]{2,1,0:T(8,128)} %shard_map.78.held_ref, f32[2,32,256]{2,1,0:T(8,128)S(1)} %collective-permute-done.10.refs_0_, f32[2,32,256]{2,1,0:T(8,128)S(1)} %collective-permute-done.11.refs_1_, ...), custom_call_target="tpu_custom_call", output_to_operand_aliasing={{}: (1, {})} | custom-call | flops 262144 | bytes 1048576 | tf_op jit(solution)/shard_map/pallas_call | solution.py:402
  (3 shorter events, 0.0 us)
Async XLA Ops:
  0.0 6.4 %copy-start = (f32[32,32,256]{2,1,0:T(8,128)S(1)}, f32[32,32,256]{2,1,0:T(8,128)}, u32[]{:S(2)}) copy-start(f32[32,32,256]{2,1,0:T(8,128)} %state_ref.3) | copy-start | bytes 3145732
  1.2 8.8 %collective-permute-start = (f32[2,32,256]{2,1,0:T(8,128)S(1)}, f32[2,32,256]{2,1,0:T(8,128)S(1)}, u32[]{:S(2)}, u32[]{:S(2)}) collective-permute-start(f32[2,32,256]{2,1,0:T(8,128)S(1)} %get-tuple-element.32), channel_id=1, source_target_pairs={{0,1},{1,2},{2,3},{3,0},{4,5},{5,6},{6,7},{7,4},{8,9},{9,10},{10,1... | collective-permute-start | bytes 196616 | tf_op jit(solution)/shard_map/ppermute | solution.py:350
  4.3 7.3 %collective-permute-start.1 = (f32[2,32,256]{2,1,0:T(8,128)S(1)}, f32[2,32,256]{2,1,0:T(8,128)S(1)}, u32[]{:S(2)}, u32[]{:S(2)}) collective-permute-start(f32[2,32,256]{2,1,0:T(8,128)S(1)} %get-tuple-element.33), channel_id=1, source_target_pairs={{1,0},{2,1},{3,2},{0,3},{5,4},{6,5},{7,6},{4,7},{9,8},{10,9},{11,1... | collective-permute-start | bytes 196616 | tf_op jit(solution)/shard_map/ppermute | solution.py:351
  7.1 4.5 %collective-permute-start.2 = (f32[2,32,256]{2,1,0:T(8,128)S(1)}, f32[2,32,256]{2,1,0:T(8,128)S(1)}, u32[]{:S(2)}, u32[]{:S(2)}) collective-permute-start(f32[2,32,256]{2,1,0:T(8,128)S(1)} %get-tuple-element.36), channel_id=1, source_target_pairs={{0,4},{4,0},{8,12},{12,8},{16,20},{20,16},{24,28},{28,24},{1,5},{5... | collective-permute-start | bytes 196616 | tf_op jit(solution)/shard_map/ppermute | solution.py:51
  7.2 6.1 %collective-permute-start.3 = (f32[2,32,256]{2,1,0:T(8,128)S(1)}, f32[2,32,256]{2,1,0:T(8,128)S(1)}, u32[]{:S(2)}, u32[]{:S(2)}) collective-permute-start(f32[2,32,256]{2,1,0:T(8,128)S(1)} %get-tuple-element.37), channel_id=1, source_target_pairs={{0,24},{4,28},{8,16},{12,20},{16,8},{20,12},{24,0},{28,4},{1,25},{... | collective-permute-start | bytes 196616 | tf_op jit(solution)/shard_map/ppermute | solution.py:51
  9.9 8.8 %collective-permute-start.4 = (f32[2,32,256]{2,1,0:T(8,128)S(1)}, f32[2,32,256]{2,1,0:T(8,128)S(1)}, u32[]{:S(2)}, u32[]{:S(2)}) collective-permute-start(f32[2,32,256]{2,1,0:T(8,128)S(1)} %get-tuple-element.38), channel_id=1, source_target_pairs={{0,28},{4,24},{8,20},{12,16},{16,12},{20,8},{24,4},{28,0},{1,29},{... | collective-permute-start | bytes 196616 | tf_op jit(solution)/shard_map/ppermute | solution.py:51
  10.0 8.7 %collective-permute-start.5 = (f32[2,32,256]{2,1,0:T(8,128)S(1)}, f32[2,32,256]{2,1,0:T(8,128)S(1)}, u32[]{:S(2)}, u32[]{:S(2)}) collective-permute-start(f32[2,32,256]{2,1,0:T(8,128)S(1)} %get-tuple-element.39), channel_id=1, source_target_pairs={{0,8},{4,12},{8,0},{12,4},{16,24},{20,28},{24,16},{28,20},{1,9},{5... | collective-permute-start | bytes 196616 | tf_op jit(solution)/shard_map/ppermute | solution.py:51
  11.6 7.0 %collective-permute-start.6 = (f32[2,32,256]{2,1,0:T(8,128)S(1)}, f32[2,32,256]{2,1,0:T(8,128)S(1)}, u32[]{:S(2)}, u32[]{:S(2)}) collective-permute-start(f32[2,32,256]{2,1,0:T(8,128)S(1)} %get-tuple-element.40), channel_id=1, source_target_pairs={{0,12},{4,8},{8,4},{12,0},{16,28},{20,24},{24,20},{28,16},{1,13},{... | collective-permute-start | bytes 196616 | tf_op jit(solution)/shard_map/ppermute | solution.py:51
  11.7 7.0 %collective-permute-start.7 = (f32[2,32,256]{2,1,0:T(8,128)S(1)}, f32[2,32,256]{2,1,0:T(8,128)S(1)}, u32[]{:S(2)}, u32[]{:S(2)}) collective-permute-start(f32[2,32,256]{2,1,0:T(8,128)S(1)} %get-tuple-element.41), channel_id=1, source_target_pairs={{0,16},{4,20},{8,24},{12,28},{16,0},{20,4},{24,8},{28,12},{1,17},{... | collective-permute-start | bytes 196616 | tf_op jit(solution)/shard_map/ppermute | solution.py:51
  13.3 5.3 %collective-permute-start.8 = (f32[2,32,256]{2,1,0:T(8,128)S(1)}, f32[2,32,256]{2,1,0:T(8,128)S(1)}, u32[]{:S(2)}, u32[]{:S(2)}) collective-permute-start(f32[2,32,256]{2,1,0:T(8,128)S(1)} %get-tuple-element.42), channel_id=1, source_target_pairs={{0,20},{4,16},{8,28},{12,24},{16,4},{20,0},{24,12},{28,8},{1,21},{... | collective-permute-start | bytes 196616 | tf_op jit(solution)/shard_map/ppermute | solution.py:51
  14.7 4.0 %copy-start.1 = (s32[1,32,512]{2,1,0:T(8,128)S(1)}, s32[1,32,512]{2,1,0:T(8,128)}, u32[]{:S(2)}) copy-start(s32[1,32,512]{2,1,0:T(8,128)} %param.10) | copy-start | bytes 196612
  14.7 4.0 %copy-start.2 = (f32[1,32,512]{2,1,0:T(8,128)S(1)}, f32[1,32,512]{2,1,0:T(8,128)}, u32[]{:S(2)}) copy-start(f32[1,32,512]{2,1,0:T(8,128)} %param.12) | copy-start | bytes 196612
  14.7 4.0 %copy-start.3 = (f32[1,32,512]{2,1,0:T(8,128)S(1)}, f32[1,32,512]{2,1,0:T(8,128)}, u32[]{:S(2)}) copy-start(f32[1,32,512]{2,1,0:T(8,128)} %param.13) | copy-start | bytes 196612
  14.7 13.7 %all-to-all-start = ((f32[8,2,32,256]{3,2,1,0:T(8,128)}), f32[8,2,32,256]{3,2,1,0:T(8,128)S(1)}, u32[]{:S(2)}, u32[]{:S(2)}) async-start(f32[8,2,32,256]{3,2,1,0:T(8,128)} %get-tuple-element.45), calls=%async_computation | async-start | bytes 1048576 | tf_op jit(solution)/shard_map/all_to_all | solution.py:369
  28.4 18.0 %all-to-all-start.1 = ((f32[8,2,32,256]{3,2,1,0:T(8,128)}), f32[8,2,32,256]{3,2,1,0:T(8,128)S(1)}, u32[]{:S(2)}, u32[]{:S(2)}) async-start(f32[8,2,32,256]{3,2,1,0:T(8,128)} %get-tuple-element.47), calls=%async_computation.1 | async-start | bytes 1048576 | tf_op jit(solution)/shard_map/all_to_all | solution.py:379
  39.6 5.0 %collective-permute-start.9 = (f32[2,32,256]{2,1,0:T(8,128)S(1)}, f32[2,32,256]{2,1,0:T(8,128)S(1)}, u32[]{:S(2)}, u32[]{:S(2)}) collective-permute-start(f32[2,32,256]{2,1,0:T(8,128)S(1)} %get-tuple-element.46), channel_id=1, source_target_pairs={{0,28},{4,24},{8,20},{12,16},{16,12},{20,8},{24,4},{28,0},{1,29},{... | collective-permute-start | bytes 196616 | tf_op jit(solution)/shard_map/ppermute | solution.py:51
  42.1 4.3 %collective-permute-start.10 = (f32[2,32,256]{2,1,0:T(8,128)S(1)}, f32[2,32,256]{2,1,0:T(8,128)S(1)}, u32[]{:S(2)}, u32[]{:S(2)}) collective-permute-start(f32[2,32,256]{2,1,0:T(8,128)S(1)} %get-tuple-element.48), channel_id=1, source_target_pairs={{0,4},{4,0},{8,12},{12,8},{16,20},{20,16},{24,28},{28,24},{1,5},{5... | collective-permute-start | bytes 196616 | tf_op jit(solution)/shard_map/ppermute | solution.py:51
  42.5 5.9 %collective-permute-start.11 = (f32[2,32,256]{2,1,0:T(8,128)S(1)}, f32[2,32,256]{2,1,0:T(8,128)S(1)}, u32[]{:S(2)}, u32[]{:S(2)}) collective-permute-start(f32[2,32,256]{2,1,0:T(8,128)S(1)} %get-tuple-element.49), channel_id=1, source_target_pairs={{0,24},{4,28},{8,16},{12,20},{16,8},{20,12},{24,0},{28,4},{1,25},{... | collective-permute-start | bytes 196616 | tf_op jit(solution)/shard_map/ppermute | solution.py:51
  42.7 5.9 %collective-permute-start.12 = (f32[2,32,256]{2,1,0:T(8,128)S(1)}, f32[2,32,256]{2,1,0:T(8,128)S(1)}, u32[]{:S(2)}, u32[]{:S(2)}) collective-permute-start(f32[2,32,256]{2,1,0:T(8,128)S(1)} %get-tuple-element.50), channel_id=1, source_target_pairs={{0,8},{4,12},{8,0},{12,4},{16,24},{20,28},{24,16},{28,20},{1,9},{5... | collective-permute-start | bytes 196616 | tf_op jit(solution)/shard_map/ppermute | solution.py:51
  44.5 4.4 %collective-permute-start.13 = (f32[2,32,256]{2,1,0:T(8,128)S(1)}, f32[2,32,256]{2,1,0:T(8,128)S(1)}, u32[]{:S(2)}, u32[]{:S(2)}) collective-permute-start(f32[2,32,256]{2,1,0:T(8,128)S(1)} %get-tuple-element.51), channel_id=1, source_target_pairs={{0,12},{4,8},{8,4},{12,0},{16,28},{20,24},{24,20},{28,16},{1,13},{... | collective-permute-start | bytes 196616 | tf_op jit(solution)/shard_map/ppermute | solution.py:51
  44.7 4.6 %collective-permute-start.14 = (f32[2,32,256]{2,1,0:T(8,128)S(1)}, f32[2,32,256]{2,1,0:T(8,128)S(1)}, u32[]{:S(2)}, u32[]{:S(2)}) collective-permute-start(f32[2,32,256]{2,1,0:T(8,128)S(1)} %get-tuple-element.52), channel_id=1, source_target_pairs={{0,16},{4,20},{8,24},{12,28},{16,0},{20,4},{24,8},{28,12},{1,17},{... | collective-permute-start | bytes 196616 | tf_op jit(solution)/shard_map/ppermute | solution.py:51
  46.4 4.3 %collective-permute-start.15 = (f32[2,32,256]{2,1,0:T(8,128)S(1)}, f32[2,32,256]{2,1,0:T(8,128)S(1)}, u32[]{:S(2)}, u32[]{:S(2)}) collective-permute-start(f32[2,32,256]{2,1,0:T(8,128)S(1)} %get-tuple-element.53), channel_id=1, source_target_pairs={{0,20},{4,16},{8,28},{12,24},{16,4},{20,0},{24,12},{28,8},{1,21},{... | collective-permute-start | bytes 196616 | tf_op jit(solution)/shard_map/ppermute | solution.py:51

commit v9 on v8

--- a/solution.py
+++ b/solution.py
@@ -27,28 +27,46 @@
     return pltpu.with_memory_space_constraint(x, pltpu.HBM)
 
 
-def target(me, k, groups):
-    if groups & (groups - 1) == 0:
-        return me ^ k
-    return lax.rem(me + k, groups)
-
-
-def source(me, k, groups):
-    if groups & (groups - 1) == 0:
-        return me ^ k
-    return lax.rem(me + groups - k, groups)
+def chips_from(chip, step, chips):
+    if chips & (chips - 1) == 0:
+        return chip ^ step
+    return (chip + step) % chips if isinstance(chip, int) else lax.rem(chip + step, chips)
+
+
+def step_of(core, round, chips):
+    steps = sorted(range(1, chips), key=lambda step: (-step.bit_count(), step))
+    near, far = steps[round - 1], steps[round % len(steps)]
+    if isinstance(core, int):
+        return far if core else near
+    return jnp.where(core == 1, far, near)
+
+
+def target(me, block, groups):
+    round, other = block
+    chip = chips_from(me // 2, step_of(me & 1, round, groups // 2), groups // 2) if round else me // 2
+    return 2 * chip + (me & 1 ^ other)
+
+
+def source(me, block, groups):
+    round, other = block
+    chips = groups // 2
+    core = me & 1 ^ other
+    if not round:
+        return 2 * (me // 2) + core
+    step = step_of(core, round, chips)
+    return 2 * chips_from(me // 2, step if chips & (chips - 1) == 0 else chips - step, chips) + core
 
 
 def issue_order(groups):
-    return sorted(range(1, groups), key=lambda k: (k != 1, -(k // 2).bit_count(), k)) + [0]
+    return [(0, 1)] + [(round, other) for round in range(1, groups // 2) for other in range(2)] + [(0, 0)]
 
 
 def exchange(blocks):
     groups = len(blocks)
     out = []
     for k, block in zip(issue_order(groups), blocks):
-        pairs = [(i, i ^ k if groups & (groups - 1) == 0 else (i + k) % groups) for i in range(groups)]
-        out.append(lax.ppermute(block, "mem", pairs) if k else block)
+        pairs = [(i, target(i, k, groups)) for i in range(groups)]
+        out.append(lax.ppermute(block, "mem", pairs) if k != (0, 0) else block)
     return out
 
 

time: 52.1 us -> 52.1 us (level)
  waiting for transfers between devices: 4.89 us -> 3.39 us
  starting transfers between devices: 25.8 us -> 27.2 us
    ppermute x14, starting transfers between devices: 13 us -> 14.5 us  [exchange(): out.append(lax.ppermute(block, 'mem', pairs) if k != (0, 0) else block)]
    ppermute x14, waiting for transfers between devices: 3.59 us -> 2.1 us  [exchange(): out.append(lax.ppermute(block, 'mem', pairs) if k != (0, 0) else block)]
  transfers between devices with their start and end apart: 18 -> 18, of which waited for: 7 -> 3; matrix products, arithmetic and copies ran while one was open for 0% -> 0% of each run, Pallas kernels for 36% -> 36%
where the time goes in v9:
time: 52.1 us; the launch traced here: 51.7 us
  starting transfers between devices  27.2 us (52%)
  Pallas kernels  20.8 us (40%)
  waiting for transfers between devices  3.39 us (7%)
    ppermute x14, starting transfers between devices, exchange(): out.append(lax.ppermute(block, 'mem', pairs) if k != (0, 0) else block)  14.5 us
    pallas_call x1, Pallas kernels, body(): call(inner_analysis, [whole, token], flops, 4 * size, in_specs=[SMEM] + [...  8.38 us
    pallas_call x1, Pallas kernels, body(): call(outer_analysis, [block] * groups, flops, 4 * size, in_specs=[SMEM] +...  7.57 us
    all_to_all x1, starting transfers between devices, body(): lax.all_to_all(outer, 'mem', split_axis=0, concat_axis=0, tiled=True)  3.84 us
    all_to_all x1, starting transfers between devices, body(): lax.all_to_all(inner, 'mem', split_axis=0, concat_axis=0, tiled=True)  3.67 us
    ppermute x1, starting transfers between devices, body(): lax.ppermute(high, 'tile', [(i, (i + 1) % tiles) for i in range(tiles)])  3.08 us
    ppermute x14, waiting for transfers between devices, exchange(): out.append(lax.ppermute(block, 'mem', pairs) if k != (0, 0) else block)  2.1 us
    ppermute x1, starting transfers between devices, body(): lax.ppermute(low, 'tile', [((i + 1) % tiles, i) for i in range(tiles)])  2.09 us
  transfers between devices with their start and end apart: 18, of which 3 were waited for; matrix products, arithmetic and copies ran while one was open for 0% of the time, Pallas kernels for 36%

profile of v9, /device:TPU:0, one launch (start us, length us, event | category | flops | bytes accessed | tf_op | source)
XLA Modules:
  0.0 51.7 jit_solution(11300199089237077584)
XLA Ops:
  0.0 0.0 copy-start
  0.0 1.2 %shard_map.73 = (f32[2,32,256]{2,1,0:T(8,128)S(1)}, f32[2,32,256]{2,1,0:T(8,128)S(1)}, f32[8,256]{1,0:T(8,128)S(1)}, s32[1,32]{1,0:T(1,128)S(1)}) custom-call(f32[32,32,256]{2,1,0:T(8,128)} %state_ref.3, f32[256]{0:T(256)} %diff_ref.1, f32[256]{0:T(256)} %adv_ref.1, s32[1,32]{1,0:T(1,128)} %count_ref.1), custom_call_target="tpu_custom_call" | custom-call | bytes 1048576 | tf_op jit(solution)/shard_map/pallas_call | solution.py:357
  1.2 3.1 %collective-permute-start = (f32[2,32,256]{2,1,0:T(8,128)S(1)}, f32[2,32,256]{2,1,0:T(8,128)S(1)}, u32[]{:S(2)}, u32[]{:S(2)}) collective-permute-start(f32[2,32,256]{2,1,0:T(8,128)S(1)} %get-tuple-element.32), channel_id=1, source_target_pairs={{0,1},{1,2},{2,3},{3,0},{4,5},{5,6},{6,7},{7,4},{8,9},{9,10},{10,1... | collective-permute-start | bytes 196616 | tf_op jit(solution)/shard_map/ppermute | solution.py:368
  4.3 2.1 %collective-permute-start.1 = (f32[2,32,256]{2,1,0:T(8,128)S(1)}, f32[2,32,256]{2,1,0:T(8,128)S(1)}, u32[]{:S(2)}, u32[]{:S(2)}) collective-permute-start(f32[2,32,256]{2,1,0:T(8,128)S(1)} %get-tuple-element.33), channel_id=1, source_target_pairs={{1,0},{2,1},{3,2},{0,3},{5,4},{6,5},{7,6},{4,7},{9,8},{10,9},{11,1... | collective-permute-start | bytes 196616 | tf_op jit(solution)/shard_map/ppermute | solution.py:369
  6.4 0.0 copy-done
  6.4 0.7 %shard_map.74 = (f32[2,32,256]{2,1,0:T(8,128)S(1)}, f32[2,32,256]{2,1,0:T(8,128)S(1)}, f32[2,32,256]{2,1,0:T(8,128)S(1)}, f32[2,32,256]{2,1,0:T(8,128)S(1)}, f32...) custom-call(s32[1]{0:T(128)} %bitcast.me_ref, ...), custom_call_target="tpu_custom_call" | custom-call | flops 5242880 | bytes 2097152 | tf_op jit(solution)/shard_map/pallas_call | solution.py:370
  7.1 0.1 collective-permute-start.2
  7.2 2.7 %collective-permute-start.3 = (f32[2,32,256]{2,1,0:T(8,128)S(1)}, f32[2,32,256]{2,1,0:T(8,128)S(1)}, u32[]{:S(2)}, u32[]{:S(2)}) collective-permute-start(f32[2,32,256]{2,1,0:T(8,128)S(1)} %get-tuple-element.37), channel_id=1, source_target_pairs={{0,24},{4,12},{8,16},{12,4},{16,8},{20,28},{24,0},{28,20},{1,25},{... | collective-permute-start | bytes 196616 | tf_op jit(solution)/shard_map/ppermute | solution.py:69
  9.9 0.3 collective-permute-start.4
  10.2 0.0 collective-permute-done.before_ref
  10.2 1.5 %collective-permute-start.5 = (f32[2,32,256]{2,1,0:T(8,128)S(1)}, f32[2,32,256]{2,1,0:T(8,128)S(1)}, u32[]{:S(2)}, u32[]{:S(2)}) collective-permute-start(f32[2,32,256]{2,1,0:T(8,128)S(1)} %get-tuple-element.39), channel_id=1, source_target_pairs={{0,8},{4,20},{8,0},{12,28},{16,24},{20,4},{24,16},{28,12},{1,9},{5... | collective-permute-start | bytes 196616 | tf_op jit(solution)/shard_map/ppermute | solution.py:69
  11.6 0.0 collective-permute-done.1.after_ref
  11.7 0.2 collective-permute-start.6
  11.8 0.0 collective-permute-done.2.refs_0_
  11.8 1.5 %collective-permute-start.7 = (f32[2,32,256]{2,1,0:T(8,128)S(1)}, f32[2,32,256]{2,1,0:T(8,128)S(1)}, u32[]{:S(2)}, u32[]{:S(2)}) collective-permute-start(f32[2,32,256]{2,1,0:T(8,128)S(1)} %get-tuple-element.41), channel_id=1, source_target_pairs={{0,16},{4,28},{8,24},{12,20},{16,0},{20,12},{24,8},{28,4},{1,17},{... | collective-permute-start | bytes 196616 | tf_op jit(solution)/shard_map/ppermute | solution.py:69
  13.4 0.0 collective-permute-done.3.refs_1_
  13.4 0.3 collective-permute-start.8
  13.6 1.1 %shard_map.75 = (f32[8,2,32,256]{3,2,1,0:T(8,128)}, f32[8,256]{1,0:T(8,128)S(1)}) custom-call(f32[2,10,32,256]{3,2,1,0:T(8,128)S(1)} %get-tuple-element.31.rest_ref, f32[2,32,256]{2,1,0:T(8,128)S(1)} %collective-permute-done.before_ref, f32[2,32,256]{2,1,0:T(8,128)S(1)} %collective-permute-done.1.after_ref, f32[8,256]{1,0:T(8,128)S(1)} %get-tuple-element.30.num_ref), custom_call_target="tpu_custom_call" | custom-call | flops 5242880 | bytes 2097152 | tf_op jit(solution)/shard_map/pallas_call | solution.py:380
  14.8 3.8 %all-to-all-start = ((f32[8,2,32,256]{3,2,1,0:T(8,128)}), f32[8,2,32,256]{3,2,1,0:T(8,128)S(1)}, u32[]{:S(2)}, u32[]{:S(2)}) async-start(f32[8,2,32,256]{3,2,1,0:T(8,128)} %get-tuple-element.45), calls=%async_computation | async-start | bytes 1048576 | tf_op jit(solution)/shard_map/all_to_all | solution.py:387
  18.6 0.0 collective-permute-done.4.refs_2_
  18.6 0.0 collective-permute-done.5.refs_3_
  18.6 0.0 collective-permute-done.6.refs_4_
  18.6 0.0 collective-permute-done.7.refs_5_
  18.7 0.0 collective-permute-done.8.refs_6_
  18.7 0.0 copy-done.1
  18.7 0.0 copy-done.2
  18.7 0.0 copy-done.3
  18.7 8.4 %shard_map.76 = (f32[8,2,32,256]{3,2,1,0:T(8,128)}, f32[8,256]{1,0:T(8,128)S(1)}) custom-call(s32[1]{0:T(128)} %bitcast.me_ref, f32[8,256]{1,0:T(8,128)S(1)} %get-tuple-element.34.after_ref, s32[1,32]{1,0:T(1,128)S(1)} %get-tuple-element.35.count_ref, s32[32,512]{1,0:T(8,128)S(1)} %bitcast.4, f32[32,512]{1,0:T(8,128)S(1)} %bitcast.6, f32[32,512]{1,0:T(8,128)S(1)} %bitcast.8, ...), custom_call_target="tpu_custom_call" | custom-call | flops 6039797760 | bytes 1048576 | tf_op jit(solution)/shard_map/pallas_call | solution.py:389
  27.1 1.3 %all-to-all-done.whole_ref = f32[8,2,32,256]{3,2,1,0:T(8,128)S(1)} async-done(((f32[8,2,32,256]{3,2,1,0:T(8,128)}), f32[8,2,32,256]{3,2,1,0:T(8,128)S(1)}, u32[]{:S(2)}, u32[]{:S(2)}) %all-to-all-start) | async-done | bytes 524320 | tf_op jit(solution)/shard_map/all_to_all | solution.py:387
  28.4 3.7 %all-to-all-start.1 = ((f32[8,2,32,256]{3,2,1,0:T(8,128)}), f32[8,2,32,256]{3,2,1,0:T(8,128)S(1)}, u32[]{:S(2)}, u32[]{:S(2)}) async-start(f32[8,2,32,256]{3,2,1,0:T(8,128)} %get-tuple-element.47), calls=%async_computation.1 | async-start | bytes 1048576 | tf_op jit(solution)/shard_map/all_to_all | solution.py:397
  32.0 7.6 %shard_map.77 = (f32[2,32,256]{2,1,0:T(8,128)S(1)}, f32[2,32,256]{2,1,0:T(8,128)S(1)}, f32[2,32,256]{2,1,0:T(8,128)S(1)}, f32[2,32,256]{2,1,0:T(8,128)S(1)}, f32...) custom-call(s32[1]{0:T(128)} %bitcast.me_ref, ...), custom_call_target="tpu_custom_call" | custom-call | flops 6039797760 | bytes 1048576 | tf_op jit(solution)/shard_map/pallas_call | solution.py:398
  39.6 2.5 %collective-permute-start.9 = (f32[2,32,256]{2,1,0:T(8,128)S(1)}, f32[2,32,256]{2,1,0:T(8,128)S(1)}, u32[]{:S(2)}, u32[]{:S(2)}) collective-permute-start(f32[2,32,256]{2,1,0:T(8,128)S(1)} %get-tuple-element.46), channel_id=1, source_target_pairs={{0,28},{4,8},{8,20},{12,0},{16,12},{20,24},{24,4},{28,16},{1,29},{... | collective-permute-start | bytes 196616 | tf_op jit(solution)/shard_map/ppermute | solution.py:69
  42.1 0.0 collective-permute-start.10
  42.1 0.9 %collective-permute-start.11 = (f32[2,32,256]{2,1,0:T(8,128)S(1)}, f32[2,32,256]{2,1,0:T(8,128)S(1)}, u32[]{:S(2)}, u32[]{:S(2)}) collective-permute-start(f32[2,32,256]{2,1,0:T(8,128)S(1)} %get-tuple-element.49), channel_id=1, source_target_pairs={{0,24},{4,12},{8,16},{12,4},{16,8},{20,28},{24,0},{28,20},{1,25},{... | collective-permute-start | bytes 196616 | tf_op jit(solution)/shard_map/ppermute | solution.py:69
  43.0 1.5 %collective-permute-start.12 = (f32[2,32,256]{2,1,0:T(8,128)S(1)}, f32[2,32,256]{2,1,0:T(8,128)S(1)}, u32[]{:S(2)}, u32[]{:S(2)}) collective-permute-start(f32[2,32,256]{2,1,0:T(8,128)S(1)} %get-tuple-element.50), channel_id=1, source_target_pairs={{0,8},{4,20},{8,0},{12,28},{16,24},{20,4},{24,16},{28,12},{1,9},{5... | collective-permute-start | bytes 196616 | tf_op jit(solution)/shard_map/ppermute | solution.py:69
  44.5 0.0 collective-permute-start.13
  44.5 0.0 collective-permute-done.9.after_ref.refs_2_
  44.5 1.2 %collective-permute-start.14 = (f32[2,32,256]{2,1,0:T(8,128)S(1)}, f32[2,32,256]{2,1,0:T(8,128)S(1)}, u32[]{:S(2)}, u32[]{:S(2)}) collective-permute-start(f32[2,32,256]{2,1,0:T(8,128)S(1)} %get-tuple-element.52), channel_id=1, source_target_pairs={{0,16},{4,28},{8,24},{12,20},{16,0},{20,12},{24,8},{28,4},{1,17},{... | collective-permute-start | bytes 196616 | tf_op jit(solution)/shard_map/ppermute | solution.py:69
  45.7 0.0 collective-permute-done.10.refs_0_
  45.7 1.9 %collective-permute-start.15 = (f32[2,32,256]{2,1,0:T(8,128)S(1)}, f32[2,32,256]{2,1,0:T(8,128)S(1)}, u32[]{:S(2)}, u32[]{:S(2)}) collective-permute-start(f32[2,32,256]{2,1,0:T(8,128)S(1)} %get-tuple-element.53), channel_id=1, source_target_pairs={{0,20},{4,24},{8,28},{12,16},{16,4},{20,8},{24,12},{28,0},{1,21},{... | collective-permute-start | bytes 196616 | tf_op jit(solution)/shard_map/ppermute | solution.py:69
  47.6 0.0 all-to-all-done.1.inner_ref
  47.6 0.8 %shard_map.78.held_ref = f32[32,32,256]{2,1,0:T(8,128)} custom-call(f32[2,32,256]{2,1,0:T(8,128)S(1)} %collective-permute-done.9.after_ref.refs_2_, f32[8,2,32,256]{3,2,1,0:T(8,128)S(1)} %all-to-all-done.1.inner_ref), custom_call_target="tpu_custom_call" | custom-call | flops 262144 | bytes 1048576 | tf_op jit(solution)/shard_map/pallas_call | solution.py:408
  48.5 0.0 collective-permute-done.11.refs_1_
  48.5 0.0 collective-permute-done.12.refs_3_
  48.5 0.0 collective-permute-done.13.refs_4_
  48.5 0.4 collective-permute-done.14.refs_5_
  48.9 1.7 %collective-permute-done.15.refs_6_ = f32[2,32,256]{2,1,0:T(8,128)S(1)} collective-permute-done((f32[2,32,256]{2,1,0:T(8,128)S(1)}, f32[2,32,256]{2,1,0:T(8,128)S(1)}, u32[]{:S(2)}, u32[]{:S(2)}) %collective-permute-start.15) | collective-permute-done | bytes 65568 | tf_op jit(solution)/shard_map/ppermute | solution.py:69
  50.6 0.9 %shard_map.79 = f32[32,32,256]{2,1,0:T(8,128)} custom-call(s32[1]{0:T(128)} %bitcast.me_ref, f32[32,32,256]{2,1,0:T(8,128)} %shard_map.78.held_ref, f32[2,32,256]{2,1,0:T(8,128)S(1)} %collective-permute-done.10.refs_0_, f32[2,32,256]{2,1,0:T(8,128)S(1)} %collective-permute-done.11.refs_1_, ...), custom_call_target="tpu_custom_call", output_to_operand_aliasing={{}: (1, {})} | custom-call | flops 262144 | bytes 1048576 | tf_op jit(solution)/shard_map/pallas_call | solution.py:420
  (3 shorter events, 0.0 us)
Async XLA Ops:
  0.0 6.4 %copy-start = (f32[32,32,256]{2,1,0:T(8,128)S(1)}, f32[32,32,256]{2,1,0:T(8,128)}, u32[]{:S(2)}) copy-start(f32[32,32,256]{2,1,0:T(8,128)} %state_ref.3) | copy-start | bytes 3145732
  1.2 9.0 %collective-permute-start = (f32[2,32,256]{2,1,0:T(8,128)S(1)}, f32[2,32,256]{2,1,0:T(8,128)S(1)}, u32[]{:S(2)}, u32[]{:S(2)}) collective-permute-start(f32[2,32,256]{2,1,0:T(8,128)S(1)} %get-tuple-element.32), channel_id=1, source_target_pairs={{0,1},{1,2},{2,3},{3,0},{4,5},{5,6},{6,7},{7,4},{8,9},{9,10},{10,1... | collective-permute-start | bytes 196616 | tf_op jit(solution)/shard_map/ppermute | solution.py:368
  4.3 7.4 %collective-permute-start.1 = (f32[2,32,256]{2,1,0:T(8,128)S(1)}, f32[2,32,256]{2,1,0:T(8,128)S(1)}, u32[]{:S(2)}, u32[]{:S(2)}) collective-permute-start(f32[2,32,256]{2,1,0:T(8,128)S(1)} %get-tuple-element.33), channel_id=1, source_target_pairs={{1,0},{2,1},{3,2},{0,3},{5,4},{6,5},{7,6},{4,7},{9,8},{10,9},{11,1... | collective-permute-start | bytes 196616 | tf_op jit(solution)/shard_map/ppermute | solution.py:369
  7.1 4.7 %collective-permute-start.2 = (f32[2,32,256]{2,1,0:T(8,128)S(1)}, f32[2,32,256]{2,1,0:T(8,128)S(1)}, u32[]{:S(2)}, u32[]{:S(2)}) collective-permute-start(f32[2,32,256]{2,1,0:T(8,128)S(1)} %get-tuple-element.36), channel_id=1, source_target_pairs={{0,4},{4,0},{8,12},{12,8},{16,20},{20,16},{24,28},{28,24},{1,5},{5... | collective-permute-start | bytes 196616 | tf_op jit(solution)/shard_map/ppermute | solution.py:69
  7.2 6.2 %collective-permute-start.3 = (f32[2,32,256]{2,1,0:T(8,128)S(1)}, f32[2,32,256]{2,1,0:T(8,128)S(1)}, u32[]{:S(2)}, u32[]{:S(2)}) collective-permute-start(f32[2,32,256]{2,1,0:T(8,128)S(1)} %get-tuple-element.37), channel_id=1, source_target_pairs={{0,24},{4,12},{8,16},{12,4},{16,8},{20,28},{24,0},{28,20},{1,25},{... | collective-permute-start | bytes 196616 | tf_op jit(solution)/shard_map/ppermute | solution.py:69
  9.9 8.8 %collective-permute-start.4 = (f32[2,32,256]{2,1,0:T(8,128)S(1)}, f32[2,32,256]{2,1,0:T(8,128)S(1)}, u32[]{:S(2)}, u32[]{:S(2)}) collective-permute-start(f32[2,32,256]{2,1,0:T(8,128)S(1)} %get-tuple-element.38), channel_id=1, source_target_pairs={{0,28},{4,8},{8,20},{12,0},{16,12},{20,24},{24,4},{28,16},{1,29},{... | collective-permute-start | bytes 196616 | tf_op jit(solution)/shard_map/ppermute | solution.py:69
  10.2 8.5 %collective-permute-start.5 = (f32[2,32,256]{2,1,0:T(8,128)S(1)}, f32[2,32,256]{2,1,0:T(8,128)S(1)}, u32[]{:S(2)}, u32[]{:S(2)}) collective-permute-start(f32[2,32,256]{2,1,0:T(8,128)S(1)} %get-tuple-element.39), channel_id=1, source_target_pairs={{0,8},{4,20},{8,0},{12,28},{16,24},{20,4},{24,16},{28,12},{1,9},{5... | collective-permute-start | bytes 196616 | tf_op jit(solution)/shard_map/ppermute | solution.py:69
  11.7 7.0 %collective-permute-start.6 = (f32[2,32,256]{2,1,0:T(8,128)S(1)}, f32[2,32,256]{2,1,0:T(8,128)S(1)}, u32[]{:S(2)}, u32[]{:S(2)}) collective-permute-start(f32[2,32,256]{2,1,0:T(8,128)S(1)} %get-tuple-element.40), channel_id=1, source_target_pairs={{0,12},{4,16},{8,4},{12,24},{16,28},{20,0},{24,20},{28,8},{1,13},{... | collective-permute-start | bytes 196616 | tf_op jit(solution)/shard_map/ppermute | solution.py:69
  11.8 6.8 %collective-permute-start.7 = (f32[2,32,256]{2,1,0:T(8,128)S(1)}, f32[2,32,256]{2,1,0:T(8,128)S(1)}, u32[]{:S(2)}, u32[]{:S(2)}) collective-permute-start(f32[2,32,256]{2,1,0:T(8,128)S(1)} %get-tuple-element.41), channel_id=1, source_target_pairs={{0,16},{4,28},{8,24},{12,20},{16,0},{20,12},{24,8},{28,4},{1,17},{... | collective-permute-start | bytes 196616 | tf_op jit(solution)/shard_map/ppermute | solution.py:69
  13.4 5.3 %collective-permute-start.8 = (f32[2,32,256]{2,1,0:T(8,128)S(1)}, f32[2,32,256]{2,1,0:T(8,128)S(1)}, u32[]{:S(2)}, u32[]{:S(2)}) collective-permute-start(f32[2,32,256]{2,1,0:T(8,128)S(1)} %get-tuple-element.42), channel_id=1, source_target_pairs={{0,20},{4,24},{8,28},{12,16},{16,4},{20,8},{24,12},{28,0},{1,21},{... | collective-permute-start | bytes 196616 | tf_op jit(solution)/shard_map/ppermute | solution.py:69
  14.8 3.9 %copy-start.1 = (s32[1,32,512]{2,1,0:T(8,128)S(1)}, s32[1,32,512]{2,1,0:T(8,128)}, u32[]{:S(2)}) copy-start(s32[1,32,512]{2,1,0:T(8,128)} %param.10) | copy-start | bytes 196612
  14.8 3.9 %copy-start.2 = (f32[1,32,512]{2,1,0:T(8,128)S(1)}, f32[1,32,512]{2,1,0:T(8,128)}, u32[]{:S(2)}) copy-start(f32[1,32,512]{2,1,0:T(8,128)} %param.12) | copy-start | bytes 196612
  14.8 3.9 %copy-start.3 = (f32[1,32,512]{2,1,0:T(8,128)S(1)}, f32[1,32,512]{2,1,0:T(8,128)}, u32[]{:S(2)}) copy-start(f32[1,32,512]{2,1,0:T(8,128)} %param.13) | copy-start | bytes 196612
  14.8 13.6 %all-to-all-start = ((f32[8,2,32,256]{3,2,1,0:T(8,128)}), f32[8,2,32,256]{3,2,1,0:T(8,128)S(1)}, u32[]{:S(2)}, u32[]{:S(2)}) async-start(f32[8,2,32,256]{3,2,1,0:T(8,128)} %get-tuple-element.45), calls=%async_computation | async-start | bytes 1048576 | tf_op jit(solution)/shard_map/all_to_all | solution.py:387
  28.4 19.3 %all-to-all-start.1 = ((f32[8,2,32,256]{3,2,1,0:T(8,128)}), f32[8,2,32,256]{3,2,1,0:T(8,128)S(1)}, u32[]{:S(2)}, u32[]{:S(2)}) async-start(f32[8,2,32,256]{3,2,1,0:T(8,128)} %get-tuple-element.47), calls=%async_computation.1 | async-start | bytes 1048576 | tf_op jit(solution)/shard_map/all_to_all | solution.py:397
  39.6 4.9 %collective-permute-start.9 = (f32[2,32,256]{2,1,0:T(8,128)S(1)}, f32[2,32,256]{2,1,0:T(8,128)S(1)}, u32[]{:S(2)}, u32[]{:S(2)}) collective-permute-start(f32[2,32,256]{2,1,0:T(8,128)S(1)} %get-tuple-element.46), channel_id=1, source_target_pairs={{0,28},{4,8},{8,20},{12,0},{16,12},{20,24},{24,4},{28,16},{1,29},{... | collective-permute-start | bytes 196616 | tf_op jit(solution)/shard_map/ppermute | solution.py:69
  42.1 3.6 %collective-permute-start.10 = (f32[2,32,256]{2,1,0:T(8,128)S(1)}, f32[2,32,256]{2,1,0:T(8,128)S(1)}, u32[]{:S(2)}, u32[]{:S(2)}) collective-permute-start(f32[2,32,256]{2,1,0:T(8,128)S(1)} %get-tuple-element.48), channel_id=1, source_target_pairs={{0,4},{4,0},{8,12},{12,8},{16,20},{20,16},{24,28},{28,24},{1,5},{5... | collective-permute-start | bytes 196616 | tf_op jit(solution)/shard_map/ppermute | solution.py:69
  42.1 6.4 %collective-permute-start.11 = (f32[2,32,256]{2,1,0:T(8,128)S(1)}, f32[2,32,256]{2,1,0:T(8,128)S(1)}, u32[]{:S(2)}, u32[]{:S(2)}) collective-permute-start(f32[2,32,256]{2,1,0:T(8,128)S(1)} %get-tuple-element.49), channel_id=1, source_target_pairs={{0,24},{4,12},{8,16},{12,4},{16,8},{20,28},{24,0},{28,20},{1,25},{... | collective-permute-start | bytes 196616 | tf_op jit(solution)/shard_map/ppermute | solution.py:69
  43.0 5.5 %collective-permute-start.12 = (f32[2,32,256]{2,1,0:T(8,128)S(1)}, f32[2,32,256]{2,1,0:T(8,128)S(1)}, u32[]{:S(2)}, u32[]{:S(2)}) collective-permute-start(f32[2,32,256]{2,1,0:T(8,128)S(1)} %get-tuple-element.50), channel_id=1, source_target_pairs={{0,8},{4,20},{8,0},{12,28},{16,24},{20,4},{24,16},{28,12},{1,9},{5... | collective-permute-start | bytes 196616 | tf_op jit(solution)/shard_map/ppermute | solution.py:69
  44.5 4.0 %collective-permute-start.13 = (f32[2,32,256]{2,1,0:T(8,128)S(1)}, f32[2,32,256]{2,1,0:T(8,128)S(1)}, u32[]{:S(2)}, u32[]{:S(2)}) collective-permute-start(f32[2,32,256]{2,1,0:T(8,128)S(1)} %get-tuple-element.51), channel_id=1, source_target_pairs={{0,12},{4,16},{8,4},{12,24},{16,28},{20,0},{24,20},{28,8},{1,13},{... | collective-permute-start | bytes 196616 | tf_op jit(solution)/shard_map/ppermute | solution.py:69
  44.5 4.4 %collective-permute-start.14 = (f32[2,32,256]{2,1,0:T(8,128)S(1)}, f32[2,32,256]{2,1,0:T(8,128)S(1)}, u32[]{:S(2)}, u32[]{:S(2)}) collective-permute-start(f32[2,32,256]{2,1,0:T(8,128)S(1)} %get-tuple-element.52), channel_id=1, source_target_pairs={{0,16},{4,28},{8,24},{12,20},{16,0},{20,12},{24,8},{28,4},{1,17},{... | collective-permute-start | bytes 196616 | tf_op jit(solution)/shard_map/ppermute | solution.py:69
  45.7 4.9 %collective-permute-start.15 = (f32[2,32,256]{2,1,0:T(8,128)S(1)}, f32[2,32,256]{2,1,0:T(8,128)S(1)}, u32[]{:S(2)}, u32[]{:S(2)}) collective-permute-start(f32[2,32,256]{2,1,0:T(8,128)S(1)} %get-tuple-element.53), channel_id=1, source_target_pairs={{0,20},{4,24},{8,28},{12,16},{16,4},{20,8},{24,12},{28,0},{1,21},{... | collective-permute-start | bytes 196616 | tf_op jit(solution)/shard_map/ppermute | solution.py:69

commit v10 on v8

--- a/solution.py
+++ b/solution.py
@@ -137,15 +137,28 @@
     rest_ref[1] = turned_ref[columns - quarter - 2 :]
 
 
-def outer_kernel(rest_ref, before_ref, after_ref, num_ref, out_ref, done_ref):
+def outer_kernel(rest_ref, before_ref, after_ref, num_ref, out_ref, done_ref, made_ref, sems):
     done_ref[...] = jnp.zeros_like(done_ref)
+    groups, half, members, entries = out_ref.shape
+    quarter = groups * half // 2
+    owners = groups // sems.shape[0]
     diffusion = num_ref[0:1][None]
     advection = num_ref[1:2][None]
     low = jnp.concatenate([before_ref[...], rest_ref[0]], axis=0)
     high = jnp.concatenate([rest_ref[1], after_ref[...]], axis=0)
-    low = stencil(stencil(low, diffusion, advection), diffusion, advection)
-    high = stencil(stencil(high, diffusion, advection), diffusion, advection)
-    out_ref[...] = jnp.concatenate([low, high], axis=0).reshape(out_ref.shape)
+    writes = []
+    for i in range(sems.shape[0]):
+        first = i * owners * half
+        padded, first = (low, first) if first < quarter else (high, first - quarter)
+        x = padded[first : first + owners * half + 4]
+        x = stencil(stencil(x, diffusion, advection), diffusion, advection)
+        part = pl.ds(i * owners, owners)
+        made_ref[part] = x.reshape(owners, half, members, entries)
+        copy = pltpu.make_async_copy(made_ref.at[part], out_ref.at[part], sems.at[i])
+        copy.start()
+        writes.append(copy)
+    for copy in writes:
+        copy.wait()
 
 
 def inner_join_kernel(after_ref, inner_ref, out_ref, made_ref, sems):
@@ -365,6 +378,11 @@
         20 * size,
         8 * size,
         in_specs=[VMEM] * 4,
+        out_specs=[HBM, VMEM],
+        scratch_shapes=[
+            pltpu.VMEM(whole.shape, jnp.float32),
+            pltpu.SemaphoreType.DMA((4 if groups % 4 == 0 else 2,)),
+        ],
     )(rest, before, after, numbers)
     outer = lax.all_to_all(outer, "mem", split_axis=0, concat_axis=0, tiled=True)
 

time: 52.1 us -> 52 us (level)
  no operation moved by 1% of the time
where the time goes in v10:
time: 52 us; the launch traced here: 51.7 us
  starting transfers between devices  25.8 us (50%)
  Pallas kernels  20.7 us (40%)
  waiting for transfers between devices  4.9 us (9%)
    ppermute x14, starting transfers between devices, exchange(): out.append(lax.ppermute(block, 'mem', pairs) if k else block)  13 us
    pallas_call x1, Pallas kernels, body(): call(inner_analysis, [whole, token], flops, 4 * size, in_specs=[SMEM] + [...  8.38 us
    pallas_call x1, Pallas kernels, body(): call(outer_analysis, [block] * groups, flops, 4 * size, in_specs=[SMEM] +...  7.57 us
    all_to_all x1, starting transfers between devices, body(): lax.all_to_all(outer, 'mem', split_axis=0, concat_axis=0, tiled=True)  3.94 us
    all_to_all x1, starting transfers between devices, body(): lax.all_to_all(inner, 'mem', split_axis=0, concat_axis=0, tiled=True)  3.67 us
    ppermute x14, waiting for transfers between devices, exchange(): out.append(lax.ppermute(block, 'mem', pairs) if k else block)  3.6 us
    ppermute x1, starting transfers between devices, body(): lax.ppermute(high, 'tile', [(i, (i + 1) % tiles) for i in range(tiles)])  3.08 us
    ppermute x1, starting transfers between devices, body(): lax.ppermute(low, 'tile', [((i + 1) % tiles, i) for i in range(tiles)])  2.09 us
  transfers between devices with their start and end apart: 18, of which 7 were waited for; matrix products, arithmetic and copies ran while one was open for 0% of the time, Pallas kernels for 36%

profile of v10, /device:TPU:0, one launch (start us, length us, event | category | flops | bytes accessed | tf_op | source)
XLA Modules:
  0.0 51.7 jit_solution(13068563121900977118)
XLA Ops:
  0.0 1.2 %shard_map.73 = (f32[2,32,256]{2,1,0:T(8,128)S(1)}, f32[2,32,256]{2,1,0:T(8,128)S(1)}, f32[8,256]{1,0:T(8,128)S(1)}, s32[1,32]{1,0:T(1,128)S(1)}) custom-call(f32[32,32,256]{2,1,0:T(8,128)} %state_ref.3, f32[256]{0:T(256)} %diff_ref.1, f32[256]{0:T(256)} %adv_ref.1, s32[1,32]{1,0:T(1,128)} %count_ref.1), custom_call_target="tpu_custom_call" | custom-call | bytes 1048576 | tf_op jit(solution)/shard_map/pallas_call | solution.py:352
  1.2 3.1 %collective-permute-start = (f32[2,32,256]{2,1,0:T(8,128)S(1)}, f32[2,32,256]{2,1,0:T(8,128)S(1)}, u32[]{:S(2)}, u32[]{:S(2)}) collective-permute-start(f32[2,32,256]{2,1,0:T(8,128)S(1)} %get-tuple-element.32), channel_id=1, source_target_pairs={{0,1},{1,2},{2,3},{3,0},{4,5},{5,6},{6,7},{7,4},{8,9},{9,10},{10,1... | collective-permute-start | bytes 196616 | tf_op jit(solution)/shard_map/ppermute | solution.py:363
  4.3 2.1 %collective-permute-start.1 = (f32[2,32,256]{2,1,0:T(8,128)S(1)}, f32[2,32,256]{2,1,0:T(8,128)S(1)}, u32[]{:S(2)}, u32[]{:S(2)}) collective-permute-start(f32[2,32,256]{2,1,0:T(8,128)S(1)} %get-tuple-element.33), channel_id=1, source_target_pairs={{1,0},{2,1},{3,2},{0,3},{5,4},{6,5},{7,6},{4,7},{9,8},{10,9},{11,1... | collective-permute-start | bytes 196616 | tf_op jit(solution)/shard_map/ppermute | solution.py:364
  6.4 0.0 copy-done
  6.4 0.7 %shard_map.74 = (f32[2,32,256]{2,1,0:T(8,128)S(1)}, f32[2,32,256]{2,1,0:T(8,128)S(1)}, f32[2,32,256]{2,1,0:T(8,128)S(1)}, f32[2,32,256]{2,1,0:T(8,128)S(1)}, f32...) custom-call(s32[1]{0:T(128)} %bitcast.me_ref, ...), custom_call_target="tpu_custom_call" | custom-call | flops 5242880 | bytes 2097152 | tf_op jit(solution)/shard_map/pallas_call | solution.py:365
  7.1 0.1 collective-permute-start.2
  7.2 2.7 %collective-permute-start.3 = (f32[2,32,256]{2,1,0:T(8,128)S(1)}, f32[2,32,256]{2,1,0:T(8,128)S(1)}, u32[]{:S(2)}, u32[]{:S(2)}) collective-permute-start(f32[2,32,256]{2,1,0:T(8,128)S(1)} %get-tuple-element.37), channel_id=1, source_target_pairs={{0,24},{4,28},{8,16},{12,20},{16,8},{20,12},{24,0},{28,4},{1,25},{... | collective-permute-start | bytes 196616 | tf_op jit(solution)/shard_map/ppermute | solution.py:51
  9.9 0.1 collective-permute-start.4
  10.0 0.0 collective-permute-done.before_ref
  10.0 1.6 %collective-permute-start.5 = (f32[2,32,256]{2,1,0:T(8,128)S(1)}, f32[2,32,256]{2,1,0:T(8,128)S(1)}, u32[]{:S(2)}, u32[]{:S(2)}) collective-permute-start(f32[2,32,256]{2,1,0:T(8,128)S(1)} %get-tuple-element.39), channel_id=1, source_target_pairs={{0,8},{4,12},{8,0},{12,4},{16,24},{20,28},{24,16},{28,20},{1,9},{5... | collective-permute-start | bytes 196616 | tf_op jit(solution)/shard_map/ppermute | solution.py:51
  11.6 0.0 collective-permute-done.1.after_ref
  11.6 0.0 collective-permute-start.6
  11.7 0.0 collective-permute-done.2.refs_0_
  11.7 1.7 %collective-permute-start.7 = (f32[2,32,256]{2,1,0:T(8,128)S(1)}, f32[2,32,256]{2,1,0:T(8,128)S(1)}, u32[]{:S(2)}, u32[]{:S(2)}) collective-permute-start(f32[2,32,256]{2,1,0:T(8,128)S(1)} %get-tuple-element.41), channel_id=1, source_target_pairs={{0,16},{4,20},{8,24},{12,28},{16,0},{20,4},{24,8},{28,12},{1,17},{... | collective-permute-start | bytes 196616 | tf_op jit(solution)/shard_map/ppermute | solution.py:51
  13.3 0.0 collective-permute-done.3.refs_1_
  13.3 0.2 collective-permute-start.8
  13.5 1.0 %shard_map.75 = (f32[8,2,32,256]{3,2,1,0:T(8,128)}, f32[8,256]{1,0:T(8,128)S(1)}) custom-call(f32[2,10,32,256]{3,2,1,0:T(8,128)S(1)} %get-tuple-element.31.rest_ref, f32[2,32,256]{2,1,0:T(8,128)S(1)} %collective-permute-done.before_ref, f32[2,32,256]{2,1,0:T(8,128)S(1)} %collective-permute-done.1.after_ref, f32[8,256]{1,0:T(8,128)S(1)} %get-tuple-element.30.num_ref), custom_call_target="tpu_custom_call" | custom-call | flops 5242880 | bytes 2097152 | tf_op jit(solution)/shard_map/pallas_call | solution.py:375
  14.6 0.0 copy-start.1
  14.6 0.0 copy-start.2
  14.6 0.0 copy-start.3
  14.6 3.9 %all-to-all-start = ((f32[8,2,32,256]{3,2,1,0:T(8,128)}), f32[8,2,32,256]{3,2,1,0:T(8,128)S(1)}, u32[]{:S(2)}, u32[]{:S(2)}) async-start(f32[8,2,32,256]{3,2,1,0:T(8,128)} %get-tuple-element.45), calls=%async_computation | async-start | bytes 1048576 | tf_op jit(solution)/shard_map/all_to_all | solution.py:387
  18.6 0.0 collective-permute-done.4.refs_2_
  18.6 0.0 collective-permute-done.5.refs_3_
  18.6 0.0 collective-permute-done.6.refs_4_
  18.6 0.0 collective-permute-done.7.refs_5_
  18.6 0.0 collective-permute-done.8.refs_6_
  18.6 0.0 copy-done.1
  18.6 8.4 %shard_map.76 = (f32[8,2,32,256]{3,2,1,0:T(8,128)}, f32[8,256]{1,0:T(8,128)S(1)}) custom-call(s32[1]{0:T(128)} %bitcast.me_ref, f32[8,256]{1,0:T(8,128)S(1)} %get-tuple-element.34.after_ref, s32[1,32]{1,0:T(1,128)S(1)} %get-tuple-element.35.count_ref, s32[32,512]{1,0:T(8,128)S(1)} %bitcast.4, f32[32,512]{1,0:T(8,128)S(1)} %bitcast.6, f32[32,512]{1,0:T(8,128)S(1)} %bitcast.8, ...), custom_call_target="tpu_custom_call" | custom-call | flops 6039797760 | bytes 1048576 | tf_op jit(solution)/shard_map/pallas_call | solution.py:389
  27.0 1.3 %all-to-all-done.whole_ref = f32[8,2,32,256]{3,2,1,0:T(8,128)S(1)} async-done(((f32[8,2,32,256]{3,2,1,0:T(8,128)}), f32[8,2,32,256]{3,2,1,0:T(8,128)S(1)}, u32[]{:S(2)}, u32[]{:S(2)}) %all-to-all-start) | async-done | bytes 524320 | tf_op jit(solution)/shard_map/all_to_all | solution.py:387
  28.3 3.7 %all-to-all-start.1 = ((f32[8,2,32,256]{3,2,1,0:T(8,128)}), f32[8,2,32,256]{3,2,1,0:T(8,128)S(1)}, u32[]{:S(2)}, u32[]{:S(2)}) async-start(f32[8,2,32,256]{3,2,1,0:T(8,128)} %get-tuple-element.47), calls=%async_computation.1 | async-start | bytes 1048576 | tf_op jit(solution)/shard_map/all_to_all | solution.py:397
  32.0 7.6 %shard_map.77 = (f32[2,32,256]{2,1,0:T(8,128)S(1)}, f32[2,32,256]{2,1,0:T(8,128)S(1)}, f32[2,32,256]{2,1,0:T(8,128)S(1)}, f32[2,32,256]{2,1,0:T(8,128)S(1)}, f32...) custom-call(s32[1]{0:T(128)} %bitcast.me_ref, ...), custom_call_target="tpu_custom_call" | custom-call | flops 6039797760 | bytes 1048576 | tf_op jit(solution)/shard_map/pallas_call | solution.py:398
  39.6 2.5 %collective-permute-start.9 = (f32[2,32,256]{2,1,0:T(8,128)S(1)}, f32[2,32,256]{2,1,0:T(8,128)S(1)}, u32[]{:S(2)}, u32[]{:S(2)}) collective-permute-start(f32[2,32,256]{2,1,0:T(8,128)S(1)} %get-tuple-element.46), channel_id=1, source_target_pairs={{0,28},{4,24},{8,20},{12,16},{16,12},{20,8},{24,4},{28,0},{1,29},{... | collective-permute-start | bytes 196616 | tf_op jit(solution)/shard_map/ppermute | solution.py:51
  42.0 0.4 collective-permute-start.10
  42.4 0.3 collective-permute-start.11
  42.7 1.7 %collective-permute-start.12 = (f32[2,32,256]{2,1,0:T(8,128)S(1)}, f32[2,32,256]{2,1,0:T(8,128)S(1)}, u32[]{:S(2)}, u32[]{:S(2)}) collective-permute-start(f32[2,32,256]{2,1,0:T(8,128)S(1)} %get-tuple-element.50), channel_id=1, source_target_pairs={{0,8},{4,12},{8,0},{12,4},{16,24},{20,28},{24,16},{28,20},{1,9},{5... | collective-permute-start | bytes 196616 | tf_op jit(solution)/shard_map/ppermute | solution.py:51
  44.4 0.0 collective-permute-start.13
  44.4 0.2 collective-permute-done.9.after_ref.refs_2_
  44.6 1.7 %collective-permute-start.14 = (f32[2,32,256]{2,1,0:T(8,128)S(1)}, f32[2,32,256]{2,1,0:T(8,128)S(1)}, u32[]{:S(2)}, u32[]{:S(2)}) collective-permute-start(f32[2,32,256]{2,1,0:T(8,128)S(1)} %get-tuple-element.52), channel_id=1, source_target_pairs={{0,16},{4,20},{8,24},{12,28},{16,0},{20,4},{24,8},{28,12},{1,17},{... | collective-permute-start | bytes 196616 | tf_op jit(solution)/shard_map/ppermute | solution.py:51
  46.3 0.0 collective-permute-done.10.refs_0_
  46.4 0.0 collective-permute-start.15
  46.4 0.0 all-to-all-done.1.inner_ref
  46.4 0.8 %shard_map.78.held_ref = f32[32,32,256]{2,1,0:T(8,128)} custom-call(f32[2,32,256]{2,1,0:T(8,128)S(1)} %collective-permute-done.9.after_ref.refs_2_, f32[8,2,32,256]{3,2,1,0:T(8,128)S(1)} %all-to-all-done.1.inner_ref), custom_call_target="tpu_custom_call" | custom-call | flops 262144 | bytes 1048576 | tf_op jit(solution)/shard_map/pallas_call | solution.py:408
  47.2 1.1 %collective-permute-done.11.refs_1_ = f32[2,32,256]{2,1,0:T(8,128)S(1)} collective-permute-done((f32[2,32,256]{2,1,0:T(8,128)S(1)}, f32[2,32,256]{2,1,0:T(8,128)S(1)}, u32[]{:S(2)}, u32[]{:S(2)}) %collective-permute-start.11) | collective-permute-done | bytes 65568 | tf_op jit(solution)/shard_map/ppermute | solution.py:51
  48.3 0.3 collective-permute-done.12.refs_3_
  48.6 0.3 collective-permute-done.13.refs_4_
  48.9 0.4 collective-permute-done.14.refs_5_
  49.3 1.4 %collective-permute-done.15.refs_6_ = f32[2,32,256]{2,1,0:T(8,128)S(1)} collective-permute-done((f32[2,32,256]{2,1,0:T(8,128)S(1)}, f32[2,32,256]{2,1,0:T(8,128)S(1)}, u32[]{:S(2)}, u32[]{:S(2)}) %collective-permute-start.15) | collective-permute-done | bytes 65568 | tf_op jit(solution)/shard_map/ppermute | solution.py:51
  50.6 0.9 %shard_map.79 = f32[32,32,256]{2,1,0:T(8,128)} custom-call(s32[1]{0:T(128)} %bitcast.me_ref, f32[32,32,256]{2,1,0:T(8,128)} %shard_map.78.held_ref, f32[2,32,256]{2,1,0:T(8,128)S(1)} %collective-permute-done.10.refs_0_, f32[2,32,256]{2,1,0:T(8,128)S(1)} %collective-permute-done.11.refs_1_, ...), custom_call_target="tpu_custom_call", output_to_operand_aliasing={{}: (1, {})} | custom-call | flops 262144 | bytes 1048576 | tf_op jit(solution)/shard_map/pallas_call | solution.py:420
  (3 shorter events, 0.0 us)
Async XLA Ops:
  0.0 6.4 %copy-start = (f32[32,32,256]{2,1,0:T(8,128)S(1)}, f32[32,32,256]{2,1,0:T(8,128)}, u32[]{:S(2)}) copy-start(f32[32,32,256]{2,1,0:T(8,128)} %state_ref.3) | copy-start | bytes 3145732
  1.2 8.8 %collective-permute-start = (f32[2,32,256]{2,1,0:T(8,128)S(1)}, f32[2,32,256]{2,1,0:T(8,128)S(1)}, u32[]{:S(2)}, u32[]{:S(2)}) collective-permute-start(f32[2,32,256]{2,1,0:T(8,128)S(1)} %get-tuple-element.32), channel_id=1, source_target_pairs={{0,1},{1,2},{2,3},{3,0},{4,5},{5,6},{6,7},{7,4},{8,9},{9,10},{10,1... | collective-permute-start | bytes 196616 | tf_op jit(solution)/shard_map/ppermute | solution.py:363
  4.3 7.3 %collective-permute-start.1 = (f32[2,32,256]{2,1,0:T(8,128)S(1)}, f32[2,32,256]{2,1,0:T(8,128)S(1)}, u32[]{:S(2)}, u32[]{:S(2)}) collective-permute-start(f32[2,32,256]{2,1,0:T(8,128)S(1)} %get-tuple-element.33), channel_id=1, source_target_pairs={{1,0},{2,1},{3,2},{0,3},{5,4},{6,5},{7,6},{4,7},{9,8},{10,9},{11,1... | collective-permute-start | bytes 196616 | tf_op jit(solution)/shard_map/ppermute | solution.py:364
  7.1 4.5 %collective-permute-start.2 = (f32[2,32,256]{2,1,0:T(8,128)S(1)}, f32[2,32,256]{2,1,0:T(8,128)S(1)}, u32[]{:S(2)}, u32[]{:S(2)}) collective-permute-start(f32[2,32,256]{2,1,0:T(8,128)S(1)} %get-tuple-element.36), channel_id=1, source_target_pairs={{0,4},{4,0},{8,12},{12,8},{16,20},{20,16},{24,28},{28,24},{1,5},{5... | collective-permute-start | bytes 196616 | tf_op jit(solution)/shard_map/ppermute | solution.py:51
  7.2 6.1 %collective-permute-start.3 = (f32[2,32,256]{2,1,0:T(8,128)S(1)}, f32[2,32,256]{2,1,0:T(8,128)S(1)}, u32[]{:S(2)}, u32[]{:S(2)}) collective-permute-start(f32[2,32,256]{2,1,0:T(8,128)S(1)} %get-tuple-element.37), channel_id=1, source_target_pairs={{0,24},{4,28},{8,16},{12,20},{16,8},{20,12},{24,0},{28,4},{1,25},{... | collective-permute-start | bytes 196616 | tf_op jit(solution)/shard_map/ppermute | solution.py:51
  9.9 8.7 %collective-permute-start.4 = (f32[2,32,256]{2,1,0:T(8,128)S(1)}, f32[2,32,256]{2,1,0:T(8,128)S(1)}, u32[]{:S(2)}, u32[]{:S(2)}) collective-permute-start(f32[2,32,256]{2,1,0:T(8,128)S(1)} %get-tuple-element.38), channel_id=1, source_target_pairs={{0,28},{4,24},{8,20},{12,16},{16,12},{20,8},{24,4},{28,0},{1,29},{... | collective-permute-start | bytes 196616 | tf_op jit(solution)/shard_map/ppermute | solution.py:51
  10.0 8.6 %collective-permute-start.5 = (f32[2,32,256]{2,1,0:T(8,128)S(1)}, f32[2,32,256]{2,1,0:T(8,128)S(1)}, u32[]{:S(2)}, u32[]{:S(2)}) collective-permute-start(f32[2,32,256]{2,1,0:T(8,128)S(1)} %get-tuple-element.39), channel_id=1, source_target_pairs={{0,8},{4,12},{8,0},{12,4},{16,24},{20,28},{24,16},{28,20},{1,9},{5... | collective-permute-start | bytes 196616 | tf_op jit(solution)/shard_map/ppermute | solution.py:51
  11.6 7.0 %collective-permute-start.6 = (f32[2,32,256]{2,1,0:T(8,128)S(1)}, f32[2,32,256]{2,1,0:T(8,128)S(1)}, u32[]{:S(2)}, u32[]{:S(2)}) collective-permute-start(f32[2,32,256]{2,1,0:T(8,128)S(1)} %get-tuple-element.40), channel_id=1, source_target_pairs={{0,12},{4,8},{8,4},{12,0},{16,28},{20,24},{24,20},{28,16},{1,13},{... | collective-permute-start | bytes 196616 | tf_op jit(solution)/shard_map/ppermute | solution.py:51
  11.7 6.9 %collective-permute-start.7 = (f32[2,32,256]{2,1,0:T(8,128)S(1)}, f32[2,32,256]{2,1,0:T(8,128)S(1)}, u32[]{:S(2)}, u32[]{:S(2)}) collective-permute-start(f32[2,32,256]{2,1,0:T(8,128)S(1)} %get-tuple-element.41), channel_id=1, source_target_pairs={{0,16},{4,20},{8,24},{12,28},{16,0},{20,4},{24,8},{28,12},{1,17},{... | collective-permute-start | bytes 196616 | tf_op jit(solution)/shard_map/ppermute | solution.py:51
  13.3 5.3 %collective-permute-start.8 = (f32[2,32,256]{2,1,0:T(8,128)S(1)}, f32[2,32,256]{2,1,0:T(8,128)S(1)}, u32[]{:S(2)}, u32[]{:S(2)}) collective-permute-start(f32[2,32,256]{2,1,0:T(8,128)S(1)} %get-tuple-element.42), channel_id=1, source_target_pairs={{0,20},{4,16},{8,28},{12,24},{16,4},{20,0},{24,12},{28,8},{1,21},{... | collective-permute-start | bytes 196616 | tf_op jit(solution)/shard_map/ppermute | solution.py:51
  14.6 4.0 %copy-start.1 = (s32[1,32,512]{2,1,0:T(8,128)S(1)}, s32[1,32,512]{2,1,0:T(8,128)}, u32[]{:S(2)}) copy-start(s32[1,32,512]{2,1,0:T(8,128)} %param.10) | copy-start | bytes 196612
  14.6 4.0 %copy-start.2 = (f32[1,32,512]{2,1,0:T(8,128)S(1)}, f32[1,32,512]{2,1,0:T(8,128)}, u32[]{:S(2)}) copy-start(f32[1,32,512]{2,1,0:T(8,128)} %param.12) | copy-start | bytes 196612
  14.6 4.0 %copy-start.3 = (f32[1,32,512]{2,1,0:T(8,128)S(1)}, f32[1,32,512]{2,1,0:T(8,128)}, u32[]{:S(2)}) copy-start(f32[1,32,512]{2,1,0:T(8,128)} %param.13) | copy-start | bytes 196612
  14.6 13.7 %all-to-all-start = ((f32[8,2,32,256]{3,2,1,0:T(8,128)}), f32[8,2,32,256]{3,2,1,0:T(8,128)S(1)}, u32[]{:S(2)}, u32[]{:S(2)}) async-start(f32[8,2,32,256]{3,2,1,0:T(8,128)} %get-tuple-element.45), calls=%async_computation | async-start | bytes 1048576 | tf_op jit(solution)/shard_map/all_to_all | solution.py:387
  28.3 18.0 %all-to-all-start.1 = ((f32[8,2,32,256]{3,2,1,0:T(8,128)}), f32[8,2,32,256]{3,2,1,0:T(8,128)S(1)}, u32[]{:S(2)}, u32[]{:S(2)}) async-start(f32[8,2,32,256]{3,2,1,0:T(8,128)} %get-tuple-element.47), calls=%async_computation.1 | async-start | bytes 1048576 | tf_op jit(solution)/shard_map/all_to_all | solution.py:397
  39.6 5.0 %collective-permute-start.9 = (f32[2,32,256]{2,1,0:T(8,128)S(1)}, f32[2,32,256]{2,1,0:T(8,128)S(1)}, u32[]{:S(2)}, u32[]{:S(2)}) collective-permute-start(f32[2,32,256]{2,1,0:T(8,128)S(1)} %get-tuple-element.46), channel_id=1, source_target_pairs={{0,28},{4,24},{8,20},{12,16},{16,12},{20,8},{24,4},{28,0},{1,29},{... | collective-permute-start | bytes 196616 | tf_op jit(solution)/shard_map/ppermute | solution.py:51
  42.0 4.3 %collective-permute-start.10 = (f32[2,32,256]{2,1,0:T(8,128)S(1)}, f32[2,32,256]{2,1,0:T(8,128)S(1)}, u32[]{:S(2)}, u32[]{:S(2)}) collective-permute-start(f32[2,32,256]{2,1,0:T(8,128)S(1)} %get-tuple-element.48), channel_id=1, source_target_pairs={{0,4},{4,0},{8,12},{12,8},{16,20},{20,16},{24,28},{28,24},{1,5},{5... | collective-permute-start | bytes 196616 | tf_op jit(solution)/shard_map/ppermute | solution.py:51
  42.4 5.9 %collective-permute-start.11 = (f32[2,32,256]{2,1,0:T(8,128)S(1)}, f32[2,32,256]{2,1,0:T(8,128)S(1)}, u32[]{:S(2)}, u32[]{:S(2)}) collective-permute-start(f32[2,32,256]{2,1,0:T(8,128)S(1)} %get-tuple-element.49), channel_id=1, source_target_pairs={{0,24},{4,28},{8,16},{12,20},{16,8},{20,12},{24,0},{28,4},{1,25},{... | collective-permute-start | bytes 196616 | tf_op jit(solution)/shard_map/ppermute | solution.py:51
  42.7 5.9 %collective-permute-start.12 = (f32[2,32,256]{2,1,0:T(8,128)S(1)}, f32[2,32,256]{2,1,0:T(8,128)S(1)}, u32[]{:S(2)}, u32[]{:S(2)}) collective-permute-start(f32[2,32,256]{2,1,0:T(8,128)S(1)} %get-tuple-element.50), channel_id=1, source_target_pairs={{0,8},{4,12},{8,0},{12,4},{16,24},{20,28},{24,16},{28,20},{1,9},{5... | collective-permute-start | bytes 196616 | tf_op jit(solution)/shard_map/ppermute | solution.py:51
  44.4 4.4 %collective-permute-start.13 = (f32[2,32,256]{2,1,0:T(8,128)S(1)}, f32[2,32,256]{2,1,0:T(8,128)S(1)}, u32[]{:S(2)}, u32[]{:S(2)}) collective-permute-start(f32[2,32,256]{2,1,0:T(8,128)S(1)} %get-tuple-element.51), channel_id=1, source_target_pairs={{0,12},{4,8},{8,4},{12,0},{16,28},{20,24},{24,20},{28,16},{1,13},{... | collective-permute-start | bytes 196616 | tf_op jit(solution)/shard_map/ppermute | solution.py:51
  44.6 4.6 %collective-permute-start.14 = (f32[2,32,256]{2,1,0:T(8,128)S(1)}, f32[2,32,256]{2,1,0:T(8,128)S(1)}, u32[]{:S(2)}, u32[]{:S(2)}) collective-permute-start(f32[2,32,256]{2,1,0:T(8,128)S(1)} %get-tuple-element.52), channel_id=1, source_target_pairs={{0,16},{4,20},{8,24},{12,28},{16,0},{20,4},{24,8},{28,12},{1,17},{... | collective-permute-start | bytes 196616 | tf_op jit(solution)/shard_map/ppermute | solution.py:51
  46.4 4.3 %collective-permute-start.15 = (f32[2,32,256]{2,1,0:T(8,128)S(1)}, f32[2,32,256]{2,1,0:T(8,128)S(1)}, u32[]{:S(2)}, u32[]{:S(2)}) collective-permute-start(f32[2,32,256]{2,1,0:T(8,128)S(1)} %get-tuple-element.53), channel_id=1, source_target_pairs={{0,20},{4,16},{8,28},{12,24},{16,4},{20,0},{24,12},{28,8},{1,21},{... | collective-permute-start | bytes 196616 | tf_op jit(solution)/shard_map/ppermute | solution.py:51

commit v11 on v10

--- a/solution.py
+++ b/solution.py
@@ -320,14 +320,16 @@
     analyse_kernel(obs_ref, ins, outs, *refs[-SCRATCH:])
 
 
-def outer_analysis(me_ref, after_ref, count_ref, where_ref, value_ref, rinv_ref, whole_ref, *refs):
+def outer_observations(me_ref, after_ref, count_ref, where_ref, value_ref, rinv_ref, out_ref):
     del after_ref
-    *outs, obs_ref = refs[:-SCRATCH]
+    first = outer_start(me_ref[0] * out_ref.shape[0], where_ref.shape[0] // 4)
+    observe(first, count_ref, where_ref, value_ref, rinv_ref, out_ref)
+
+
+def outer_analysis(me_ref, obs_ref, whole_ref, *refs):
+    outs = refs[:-SCRATCH]
     groups = len(outs)
-    half = outs[0].shape[0]
     ins = [whole_ref.at[target(me_ref[0], k, groups)] for k in issue_order(groups)]
-    first = outer_start(me_ref[0] * half, where_ref.shape[0] // 4)
-    observe(first, count_ref, where_ref, value_ref, rinv_ref, obs_ref)
     analyse_kernel(obs_ref, ins, outs, *refs[-SCRATCH:])
 
 
@@ -395,14 +397,21 @@
         scratch_shapes=scratch,
     )(me, done, *slots, *inner)
     inner = lax.all_to_all(inner, "mem", split_axis=0, concat_axis=0, tiled=True)
+    obs = call(
+        outer_observations,
+        jax.ShapeDtypeStruct((half, 8, entries), jnp.float32),
+        half * 32 * obs_where.shape[2] * entries,
+        12 * obs_where.size,
+        in_specs=[SMEM] + [VMEM] * 5,
+    )(me, done, *slots)
     outer = call(
         outer_analysis,
         [block] * groups,
         flops,
         4 * size,
-        in_specs=[SMEM] + [VMEM] * 6,
-        scratch_shapes=scratch,
-    )(me, done, *slots, outer)
+        in_specs=[SMEM] + [VMEM] * 2,
+        scratch_shapes=scratch[1:],
+    )(me, obs, outer)
     outer = exchange(outer)
     result = jax.ShapeDtypeStruct(background.shape, jnp.float32)
     made = call(

time: 52 us -> 51.7 us (level)
  no operation moved by 1% of the time
where the time goes in v11:
time: 51.7 us; the launch traced here: 51.4 us
  starting transfers between devices  25.8 us (50%)
  Pallas kernels  20.7 us (40%)
  waiting for transfers between devices  4.59 us (9%)
    ppermute x14, starting transfers between devices, exchange(): out.append(lax.ppermute(block, 'mem', pairs) if k else block)  13 us
    pallas_call x1, Pallas kernels, body(): call(inner_analysis, [whole, token], flops, 4 * size, in_specs=[SMEM] + [...  8.38 us
    pallas_call x1, Pallas kernels, body(): call(outer_analysis, [block] * groups, flops, 4 * size, in_specs=[SMEM] +...  7.31 us
    all_to_all x1, starting transfers between devices, body(): lax.all_to_all(outer, 'mem', split_axis=0, concat_axis=0, tiled=True)  3.94 us
    all_to_all x1, starting transfers between devices, body(): lax.all_to_all(inner, 'mem', split_axis=0, concat_axis=0, tiled=True)  3.67 us
    ppermute x14, waiting for transfers between devices, exchange(): out.append(lax.ppermute(block, 'mem', pairs) if k else block)  3.59 us
    ppermute x1, starting transfers between devices, body(): lax.ppermute(high, 'tile', [(i, (i + 1) % tiles) for i in range(tiles)])  3.08 us
    ppermute x1, starting transfers between devices, body(): lax.ppermute(low, 'tile', [((i + 1) % tiles, i) for i in range(tiles)])  2.09 us
  transfers between devices with their start and end apart: 18, of which 7 were waited for; matrix products, arithmetic and copies ran while one was open for 0% of the time, Pallas kernels for 36%

profile of v11, /device:TPU:0, one launch (start us, length us, event | category | flops | bytes accessed | tf_op | source)
XLA Modules:
  0.0 51.4 jit_solution(17427298778030345633)
XLA Ops:
  0.0 1.2 %shard_map.73 = (f32[2,32,256]{2,1,0:T(8,128)S(1)}, f32[2,32,256]{2,1,0:T(8,128)S(1)}, f32[8,256]{1,0:T(8,128)S(1)}, s32[1,32]{1,0:T(1,128)S(1)}) custom-call(f32[32,32,256]{2,1,0:T(8,128)} %state_ref.3, f32[256]{0:T(256)} %diff_ref.1, f32[256]{0:T(256)} %adv_ref.1, s32[1,32]{1,0:T(1,128)} %count_ref.1), custom_call_target="tpu_custom_call" | custom-call | bytes 1048576 | tf_op jit(solution)/shard_map/pallas_call | solution.py:354
  1.2 3.1 %collective-permute-start = (f32[2,32,256]{2,1,0:T(8,128)S(1)}, f32[2,32,256]{2,1,0:T(8,128)S(1)}, u32[]{:S(2)}, u32[]{:S(2)}) collective-permute-start(f32[2,32,256]{2,1,0:T(8,128)S(1)} %get-tuple-element.32), channel_id=1, source_target_pairs={{0,1},{1,2},{2,3},{3,0},{4,5},{5,6},{6,7},{7,4},{8,9},{9,10},{10,1... | collective-permute-start | bytes 196616 | tf_op jit(solution)/shard_map/ppermute | solution.py:365
  4.3 2.1 %collective-permute-start.1 = (f32[2,32,256]{2,1,0:T(8,128)S(1)}, f32[2,32,256]{2,1,0:T(8,128)S(1)}, u32[]{:S(2)}, u32[]{:S(2)}) collective-permute-start(f32[2,32,256]{2,1,0:T(8,128)S(1)} %get-tuple-element.33), channel_id=1, source_target_pairs={{1,0},{2,1},{3,2},{0,3},{5,4},{6,5},{7,6},{4,7},{9,8},{10,9},{11,1... | collective-permute-start | bytes 196616 | tf_op jit(solution)/shard_map/ppermute | solution.py:366
  6.4 0.0 copy-done
  6.4 0.7 %shard_map.74 = (f32[2,32,256]{2,1,0:T(8,128)S(1)}, f32[2,32,256]{2,1,0:T(8,128)S(1)}, f32[2,32,256]{2,1,0:T(8,128)S(1)}, f32[2,32,256]{2,1,0:T(8,128)S(1)}, f32...) custom-call(s32[1]{0:T(128)} %bitcast.me_ref, ...), custom_call_target="tpu_custom_call" | custom-call | flops 5242880 | bytes 2097152 | tf_op jit(solution)/shard_map/pallas_call | solution.py:367
  7.1 0.1 collective-permute-start.2
  7.2 2.7 %collective-permute-start.3 = (f32[2,32,256]{2,1,0:T(8,128)S(1)}, f32[2,32,256]{2,1,0:T(8,128)S(1)}, u32[]{:S(2)}, u32[]{:S(2)}) collective-permute-start(f32[2,32,256]{2,1,0:T(8,128)S(1)} %get-tuple-element.37), channel_id=1, source_target_pairs={{0,24},{4,28},{8,16},{12,20},{16,8},{20,12},{24,0},{28,4},{1,25},{... | collective-permute-start | bytes 196616 | tf_op jit(solution)/shard_map/ppermute | solution.py:51
  9.9 0.1 collective-permute-start.4
  10.0 0.0 collective-permute-done.before_ref
  10.0 1.6 %collective-permute-start.5 = (f32[2,32,256]{2,1,0:T(8,128)S(1)}, f32[2,32,256]{2,1,0:T(8,128)S(1)}, u32[]{:S(2)}, u32[]{:S(2)}) collective-permute-start(f32[2,32,256]{2,1,0:T(8,128)S(1)} %get-tuple-element.39), channel_id=1, source_target_pairs={{0,8},{4,12},{8,0},{12,4},{16,24},{20,28},{24,16},{28,20},{1,9},{5... | collective-permute-start | bytes 196616 | tf_op jit(solution)/shard_map/ppermute | solution.py:51
  11.6 0.0 collective-permute-done.1.after_ref
  11.6 0.0 collective-permute-start.6
  11.7 0.0 collective-permute-done.2.refs_0_
  11.7 1.7 %collective-permute-start.7 = (f32[2,32,256]{2,1,0:T(8,128)S(1)}, f32[2,32,256]{2,1,0:T(8,128)S(1)}, u32[]{:S(2)}, u32[]{:S(2)}) collective-permute-start(f32[2,32,256]{2,1,0:T(8,128)S(1)} %get-tuple-element.41), channel_id=1, source_target_pairs={{0,16},{4,20},{8,24},{12,28},{16,0},{20,4},{24,8},{28,12},{1,17},{... | collective-permute-start | bytes 196616 | tf_op jit(solution)/shard_map/ppermute | solution.py:51
  13.3 0.0 collective-permute-done.3.refs_1_
  13.3 0.2 collective-permute-start.8
  13.5 1.0 %shard_map.75 = (f32[8,2,32,256]{3,2,1,0:T(8,128)}, f32[8,256]{1,0:T(8,128)S(1)}) custom-call(f32[2,10,32,256]{3,2,1,0:T(8,128)S(1)} %get-tuple-element.31.rest_ref, f32[2,32,256]{2,1,0:T(8,128)S(1)} %collective-permute-done.before_ref, f32[2,32,256]{2,1,0:T(8,128)S(1)} %collective-permute-done.1.after_ref, f32[8,256]{1,0:T(8,128)S(1)} %get-tuple-element.30.num_ref), custom_call_target="tpu_custom_call" | custom-call | flops 5242880 | bytes 2097152 | tf_op jit(solution)/shard_map/pallas_call | solution.py:377
  14.6 0.0 copy-start.1
  14.6 0.0 copy-start.2
  14.6 0.0 copy-start.3
  14.6 3.9 %all-to-all-start = ((f32[8,2,32,256]{3,2,1,0:T(8,128)}), f32[8,2,32,256]{3,2,1,0:T(8,128)S(1)}, u32[]{:S(2)}, u32[]{:S(2)}) async-start(f32[8,2,32,256]{3,2,1,0:T(8,128)} %get-tuple-element.45), calls=%async_computation | async-start | bytes 1048576 | tf_op jit(solution)/shard_map/all_to_all | solution.py:389
  18.6 0.0 collective-permute-done.4.refs_2_
  18.6 0.0 collective-permute-done.5.refs_3_
  18.6 0.0 collective-permute-done.6.refs_4_
  18.6 0.0 collective-permute-done.7.refs_5_
  18.6 0.0 collective-permute-done.8.refs_6_
  18.6 8.4 %shard_map.76 = (f32[8,2,32,256]{3,2,1,0:T(8,128)}, f32[8,256]{1,0:T(8,128)S(1)}) custom-call(s32[1]{0:T(128)} %bitcast.me_ref, f32[8,256]{1,0:T(8,128)S(1)} %get-tuple-element.34.after_ref, s32[1,32]{1,0:T(1,128)S(1)} %get-tuple-element.35.count_ref, s32[32,512]{1,0:T(8,128)S(1)} %bitcast.4, f32[32,512]{1,0:T(8,128)S(1)} %bitcast.6, f32[32,512]{1,0:T(8,128)S(1)} %bitcast.8, ...), custom_call_target="tpu_custom_call" | custom-call | flops 6039797760 | bytes 1048576 | tf_op jit(solution)/shard_map/pallas_call | solution.py:391
  27.0 0.3 shard_map.77.obs_ref
  27.3 1.0 %all-to-all-done.whole_ref = f32[8,2,32,256]{3,2,1,0:T(8,128)S(1)} async-done(((f32[8,2,32,256]{3,2,1,0:T(8,128)}), f32[8,2,32,256]{3,2,1,0:T(8,128)S(1)}, u32[]{:S(2)}, u32[]{:S(2)}) %all-to-all-start) | async-done | bytes 524320 | tf_op jit(solution)/shard_map/all_to_all | solution.py:389
  28.3 3.7 %all-to-all-start.1 = ((f32[8,2,32,256]{3,2,1,0:T(8,128)}), f32[8,2,32,256]{3,2,1,0:T(8,128)S(1)}, u32[]{:S(2)}, u32[]{:S(2)}) async-start(f32[8,2,32,256]{3,2,1,0:T(8,128)} %get-tuple-element.47), calls=%async_computation.1 | async-start | bytes 1048576 | tf_op jit(solution)/shard_map/all_to_all | solution.py:399
  32.0 7.3 %shard_map.78 = (f32[2,32,256]{2,1,0:T(8,128)S(1)}, f32[2,32,256]{2,1,0:T(8,128)S(1)}, f32[2,32,256]{2,1,0:T(8,128)S(1)}, f32[2,32,256]{2,1,0:T(8,128)S(1)}, f32...) custom-call(s32[1]{0:T(128)} %bitcast.me_ref, ...), custom_call_target="tpu_custom_call" | custom-call | flops 6039797760 | bytes 1048576 | tf_op jit(solution)/shard_map/pallas_call | solution.py:407
  39.3 2.5 %collective-permute-start.9 = (f32[2,32,256]{2,1,0:T(8,128)S(1)}, f32[2,32,256]{2,1,0:T(8,128)S(1)}, u32[]{:S(2)}, u32[]{:S(2)}) collective-permute-start(f32[2,32,256]{2,1,0:T(8,128)S(1)} %get-tuple-element.46), channel_id=1, source_target_pairs={{0,28},{4,24},{8,20},{12,16},{16,12},{20,8},{24,4},{28,0},{1,29},{... | collective-permute-start | bytes 196616 | tf_op jit(solution)/shard_map/ppermute | solution.py:51
  41.8 0.4 collective-permute-start.10
  42.2 0.3 collective-permute-start.11
  42.4 1.7 %collective-permute-start.12 = (f32[2,32,256]{2,1,0:T(8,128)S(1)}, f32[2,32,256]{2,1,0:T(8,128)S(1)}, u32[]{:S(2)}, u32[]{:S(2)}) collective-permute-start(f32[2,32,256]{2,1,0:T(8,128)S(1)} %get-tuple-element.50), channel_id=1, source_target_pairs={{0,8},{4,12},{8,0},{12,4},{16,24},{20,28},{24,16},{28,20},{1,9},{5... | collective-permute-start | bytes 196616 | tf_op jit(solution)/shard_map/ppermute | solution.py:51
  44.2 0.0 collective-permute-start.13
  44.2 0.2 collective-permute-done.9.after_ref.refs_2_
  44.4 1.7 %collective-permute-start.14 = (f32[2,32,256]{2,1,0:T(8,128)S(1)}, f32[2,32,256]{2,1,0:T(8,128)S(1)}, u32[]{:S(2)}, u32[]{:S(2)}) collective-permute-start(f32[2,32,256]{2,1,0:T(8,128)S(1)} %get-tuple-element.52), channel_id=1, source_target_pairs={{0,16},{4,20},{8,24},{12,28},{16,0},{20,4},{24,8},{28,12},{1,17},{... | collective-permute-start | bytes 196616 | tf_op jit(solution)/shard_map/ppermute | solution.py:51
  46.1 0.0 collective-permute-done.10.refs_0_
  46.1 0.0 collective-permute-start.15
  46.1 0.0 all-to-all-done.1.inner_ref
  46.1 0.8 %shard_map.79.held_ref = f32[32,32,256]{2,1,0:T(8,128)} custom-call(f32[2,32,256]{2,1,0:T(8,128)S(1)} %collective-permute-done.9.after_ref.refs_2_, f32[8,2,32,256]{3,2,1,0:T(8,128)S(1)} %all-to-all-done.1.inner_ref), custom_call_target="tpu_custom_call" | custom-call | flops 262144 | bytes 1048576 | tf_op jit(solution)/shard_map/pallas_call | solution.py:417
  47.0 1.1 %collective-permute-done.11.refs_1_ = f32[2,32,256]{2,1,0:T(8,128)S(1)} collective-permute-done((f32[2,32,256]{2,1,0:T(8,128)S(1)}, f32[2,32,256]{2,1,0:T(8,128)S(1)}, u32[]{:S(2)}, u32[]{:S(2)}) %collective-permute-start.11) | collective-permute-done | bytes 65568 | tf_op jit(solution)/shard_map/ppermute | solution.py:51
  48.0 0.3 collective-permute-done.12.refs_3_
  48.3 0.3 collective-permute-done.13.refs_4_
  48.6 0.4 collective-permute-done.14.refs_5_
  49.0 1.3 %collective-permute-done.15.refs_6_ = f32[2,32,256]{2,1,0:T(8,128)S(1)} collective-permute-done((f32[2,32,256]{2,1,0:T(8,128)S(1)}, f32[2,32,256]{2,1,0:T(8,128)S(1)}, u32[]{:S(2)}, u32[]{:S(2)}) %collective-permute-start.15) | collective-permute-done | bytes 65568 | tf_op jit(solution)/shard_map/ppermute | solution.py:51
  50.3 0.9 %shard_map.80 = f32[32,32,256]{2,1,0:T(8,128)} custom-call(s32[1]{0:T(128)} %bitcast.me_ref, f32[32,32,256]{2,1,0:T(8,128)} %shard_map.79.held_ref, f32[2,32,256]{2,1,0:T(8,128)S(1)} %collective-permute-done.10.refs_0_, f32[2,32,256]{2,1,0:T(8,128)S(1)} %collective-permute-done.11.refs_1_, ...), custom_call_target="tpu_custom_call", output_to_operand_aliasing={{}: (1, {})} | custom-call | flops 262144 | bytes 1048576 | tf_op jit(solution)/shard_map/pallas_call | solution.py:429
  (4 shorter events, 0.0 us)
Async XLA Ops:
  0.0 6.4 %copy-start = (f32[32,32,256]{2,1,0:T(8,128)S(1)}, f32[32,32,256]{2,1,0:T(8,128)}, u32[]{:S(2)}) copy-start(f32[32,32,256]{2,1,0:T(8,128)} %state_ref.3) | copy-start | bytes 3145732
  1.2 8.8 %collective-permute-start = (f32[2,32,256]{2,1,0:T(8,128)S(1)}, f32[2,32,256]{2,1,0:T(8,128)S(1)}, u32[]{:S(2)}, u32[]{:S(2)}) collective-permute-start(f32[2,32,256]{2,1,0:T(8,128)S(1)} %get-tuple-element.32), channel_id=1, source_target_pairs={{0,1},{1,2},{2,3},{3,0},{4,5},{5,6},{6,7},{7,4},{8,9},{9,10},{10,1... | collective-permute-start | bytes 196616 | tf_op jit(solution)/shard_map/ppermute | solution.py:365
  4.3 7.3 %collective-permute-start.1 = (f32[2,32,256]{2,1,0:T(8,128)S(1)}, f32[2,32,256]{2,1,0:T(8,128)S(1)}, u32[]{:S(2)}, u32[]{:S(2)}) collective-permute-start(f32[2,32,256]{2,1,0:T(8,128)S(1)} %get-tuple-element.33), channel_id=1, source_target_pairs={{1,0},{2,1},{3,2},{0,3},{5,4},{6,5},{7,6},{4,7},{9,8},{10,9},{11,1... | collective-permute-start | bytes 196616 | tf_op jit(solution)/shard_map/ppermute | solution.py:366
  7.1 4.5 %collective-permute-start.2 = (f32[2,32,256]{2,1,0:T(8,128)S(1)}, f32[2,32,256]{2,1,0:T(8,128)S(1)}, u32[]{:S(2)}, u32[]{:S(2)}) collective-permute-start(f32[2,32,256]{2,1,0:T(8,128)S(1)} %get-tuple-element.36), channel_id=1, source_target_pairs={{0,4},{4,0},{8,12},{12,8},{16,20},{20,16},{24,28},{28,24},{1,5},{5... | collective-permute-start | bytes 196616 | tf_op jit(solution)/shard_map/ppermute | solution.py:51
  7.2 6.1 %collective-permute-start.3 = (f32[2,32,256]{2,1,0:T(8,128)S(1)}, f32[2,32,256]{2,1,0:T(8,128)S(1)}, u32[]{:S(2)}, u32[]{:S(2)}) collective-permute-start(f32[2,32,256]{2,1,0:T(8,128)S(1)} %get-tuple-element.37), channel_id=1, source_target_pairs={{0,24},{4,28},{8,16},{12,20},{16,8},{20,12},{24,0},{28,4},{1,25},{... | collective-permute-start | bytes 196616 | tf_op jit(solution)/shard_map/ppermute | solution.py:51
  9.9 8.7 %collective-permute-start.4 = (f32[2,32,256]{2,1,0:T(8,128)S(1)}, f32[2,32,256]{2,1,0:T(8,128)S(1)}, u32[]{:S(2)}, u32[]{:S(2)}) collective-permute-start(f32[2,32,256]{2,1,0:T(8,128)S(1)} %get-tuple-element.38), channel_id=1, source_target_pairs={{0,28},{4,24},{8,20},{12,16},{16,12},{20,8},{24,4},{28,0},{1,29},{... | collective-permute-start | bytes 196616 | tf_op jit(solution)/shard_map/ppermute | solution.py:51
  10.0 8.6 %collective-permute-start.5 = (f32[2,32,256]{2,1,0:T(8,128)S(1)}, f32[2,32,256]{2,1,0:T(8,128)S(1)}, u32[]{:S(2)}, u32[]{:S(2)}) collective-permute-start(f32[2,32,256]{2,1,0:T(8,128)S(1)} %get-tuple-element.39), channel_id=1, source_target_pairs={{0,8},{4,12},{8,0},{12,4},{16,24},{20,28},{24,16},{28,20},{1,9},{5... | collective-permute-start | bytes 196616 | tf_op jit(solution)/shard_map/ppermute | solution.py:51
  11.6 7.0 %collective-permute-start.6 = (f32[2,32,256]{2,1,0:T(8,128)S(1)}, f32[2,32,256]{2,1,0:T(8,128)S(1)}, u32[]{:S(2)}, u32[]{:S(2)}) collective-permute-start(f32[2,32,256]{2,1,0:T(8,128)S(1)} %get-tuple-element.40), channel_id=1, source_target_pairs={{0,12},{4,8},{8,4},{12,0},{16,28},{20,24},{24,20},{28,16},{1,13},{... | collective-permute-start | bytes 196616 | tf_op jit(solution)/shard_map/ppermute | solution.py:51
  11.7 6.9 %collective-permute-start.7 = (f32[2,32,256]{2,1,0:T(8,128)S(1)}, f32[2,32,256]{2,1,0:T(8,128)S(1)}, u32[]{:S(2)}, u32[]{:S(2)}) collective-permute-start(f32[2,32,256]{2,1,0:T(8,128)S(1)} %get-tuple-element.41), channel_id=1, source_target_pairs={{0,16},{4,20},{8,24},{12,28},{16,0},{20,4},{24,8},{28,12},{1,17},{... | collective-permute-start | bytes 196616 | tf_op jit(solution)/shard_map/ppermute | solution.py:51
  13.3 5.3 %collective-permute-start.8 = (f32[2,32,256]{2,1,0:T(8,128)S(1)}, f32[2,32,256]{2,1,0:T(8,128)S(1)}, u32[]{:S(2)}, u32[]{:S(2)}) collective-permute-start(f32[2,32,256]{2,1,0:T(8,128)S(1)} %get-tuple-element.42), channel_id=1, source_target_pairs={{0,20},{4,16},{8,28},{12,24},{16,4},{20,0},{24,12},{28,8},{1,21},{... | collective-permute-start | bytes 196616 | tf_op jit(solution)/shard_map/ppermute | solution.py:51
  14.6 4.0 %copy-start.1 = (s32[1,32,512]{2,1,0:T(8,128)S(1)}, s32[1,32,512]{2,1,0:T(8,128)}, u32[]{:S(2)}) copy-start(s32[1,32,512]{2,1,0:T(8,128)} %param.10) | copy-start | bytes 196612
  14.6 4.0 %copy-start.2 = (f32[1,32,512]{2,1,0:T(8,128)S(1)}, f32[1,32,512]{2,1,0:T(8,128)}, u32[]{:S(2)}) copy-start(f32[1,32,512]{2,1,0:T(8,128)} %param.12) | copy-start | bytes 196612
  14.6 4.0 %copy-start.3 = (f32[1,32,512]{2,1,0:T(8,128)S(1)}, f32[1,32,512]{2,1,0:T(8,128)}, u32[]{:S(2)}) copy-start(f32[1,32,512]{2,1,0:T(8,128)} %param.13) | copy-start | bytes 196612
  14.6 13.7 %all-to-all-start = ((f32[8,2,32,256]{3,2,1,0:T(8,128)}), f32[8,2,32,256]{3,2,1,0:T(8,128)S(1)}, u32[]{:S(2)}, u32[]{:S(2)}) async-start(f32[8,2,32,256]{3,2,1,0:T(8,128)} %get-tuple-element.45), calls=%async_computation | async-start | bytes 1048576 | tf_op jit(solution)/shard_map/all_to_all | solution.py:389
  28.3 17.8 %all-to-all-start.1 = ((f32[8,2,32,256]{3,2,1,0:T(8,128)}), f32[8,2,32,256]{3,2,1,0:T(8,128)S(1)}, u32[]{:S(2)}, u32[]{:S(2)}) async-start(f32[8,2,32,256]{3,2,1,0:T(8,128)} %get-tuple-element.47), calls=%async_computation.1 | async-start | bytes 1048576 | tf_op jit(solution)/shard_map/all_to_all | solution.py:399
  39.3 5.0 %collective-permute-start.9 = (f32[2,32,256]{2,1,0:T(8,128)S(1)}, f32[2,32,256]{2,1,0:T(8,128)S(1)}, u32[]{:S(2)}, u32[]{:S(2)}) collective-permute-start(f32[2,32,256]{2,1,0:T(8,128)S(1)} %get-tuple-element.46), channel_id=1, source_target_pairs={{0,28},{4,24},{8,20},{12,16},{16,12},{20,8},{24,4},{28,0},{1,29},{... | collective-permute-start | bytes 196616 | tf_op jit(solution)/shard_map/ppermute | solution.py:51
  41.8 4.3 %collective-permute-start.10 = (f32[2,32,256]{2,1,0:T(8,128)S(1)}, f32[2,32,256]{2,1,0:T(8,128)S(1)}, u32[]{:S(2)}, u32[]{:S(2)}) collective-permute-start(f32[2,32,256]{2,1,0:T(8,128)S(1)} %get-tuple-element.48), channel_id=1, source_target_pairs={{0,4},{4,0},{8,12},{12,8},{16,20},{20,16},{24,28},{28,24},{1,5},{5... | collective-permute-start | bytes 196616 | tf_op jit(solution)/shard_map/ppermute | solution.py:51
  42.2 5.9 %collective-permute-start.11 = (f32[2,32,256]{2,1,0:T(8,128)S(1)}, f32[2,32,256]{2,1,0:T(8,128)S(1)}, u32[]{:S(2)}, u32[]{:S(2)}) collective-permute-start(f32[2,32,256]{2,1,0:T(8,128)S(1)} %get-tuple-element.49), channel_id=1, source_target_pairs={{0,24},{4,28},{8,16},{12,20},{16,8},{20,12},{24,0},{28,4},{1,25},{... | collective-permute-start | bytes 196616 | tf_op jit(solution)/shard_map/ppermute | solution.py:51
  42.4 5.9 %collective-permute-start.12 = (f32[2,32,256]{2,1,0:T(8,128)S(1)}, f32[2,32,256]{2,1,0:T(8,128)S(1)}, u32[]{:S(2)}, u32[]{:S(2)}) collective-permute-start(f32[2,32,256]{2,1,0:T(8,128)S(1)} %get-tuple-element.50), channel_id=1, source_target_pairs={{0,8},{4,12},{8,0},{12,4},{16,24},{20,28},{24,16},{28,20},{1,9},{5... | collective-permute-start | bytes 196616 | tf_op jit(solution)/shard_map/ppermute | solution.py:51
  44.2 4.4 %collective-permute-start.13 = (f32[2,32,256]{2,1,0:T(8,128)S(1)}, f32[2,32,256]{2,1,0:T(8,128)S(1)}, u32[]{:S(2)}, u32[]{:S(2)}) collective-permute-start(f32[2,32,256]{2,1,0:T(8,128)S(1)} %get-tuple-element.51), channel_id=1, source_target_pairs={{0,12},{4,8},{8,4},{12,0},{16,28},{20,24},{24,20},{28,16},{1,13},{... | collective-permute-start | bytes 196616 | tf_op jit(solution)/shard_map/ppermute | solution.py:51
  44.4 4.6 %collective-permute-start.14 = (f32[2,32,256]{2,1,0:T(8,128)S(1)}, f32[2,32,256]{2,1,0:T(8,128)S(1)}, u32[]{:S(2)}, u32[]{:S(2)}) collective-permute-start(f32[2,32,256]{2,1,0:T(8,128)S(1)} %get-tuple-element.52), channel_id=1, source_target_pairs={{0,16},{4,20},{8,24},{12,28},{16,0},{20,4},{24,8},{28,12},{1,17},{... | collective-permute-start | bytes 196616 | tf_op jit(solution)/shard_map/ppermute | solution.py:51
  46.1 4.2 %collective-permute-start.15 = (f32[2,32,256]{2,1,0:T(8,128)S(1)}, f32[2,32,256]{2,1,0:T(8,128)S(1)}, u32[]{:S(2)}, u32[]{:S(2)}) collective-permute-start(f32[2,32,256]{2,1,0:T(8,128)S(1)} %get-tuple-element.53), channel_id=1, source_target_pairs={{0,20},{4,16},{8,28},{12,24},{16,4},{20,0},{24,12},{28,8},{1,21},{... | collective-permute-start | bytes 196616 | tf_op jit(solution)/shard_map/ppermute | solution.py:51

commit v12 on v11

--- a/solution.py
+++ b/solution.py
@@ -261,7 +261,7 @@
             if step < PAIRS - 1:
                 store(w.at[(step + 1) % 2], c, rows, x)
 
-    gaps = [parts[i::4] for i in range(4)]
+    gaps = [parts[::2], [], [], parts[1::2]]
     for step in range(PAIRS):
         for c, rows in parts:
             x = multiply(s, s, c, rows)

time: 51.7 us -> 52.3 us (1.012)
  Pallas kernels: 20.7 us -> 21.4 us
  transfers between devices with their start and end apart: 18 -> 18, of which waited for: 7 -> 7; matrix products, arithmetic and copies ran while one was open for 0% -> 0% of each run, Pallas kernels for 36% -> 37%
where the time goes in v12:
time: 52.3 us; the launch traced here: 52 us
  starting transfers between devices  26.1 us (50%)
  Pallas kernels  21.4 us (41%)
  waiting for transfers between devices  4.14 us (8%)
    ppermute x14, starting transfers between devices, exchange(): out.append(lax.ppermute(block, 'mem', pairs) if k else block)  13.3 us
    pallas_call x1, Pallas kernels, body(): call(inner_analysis, [whole, token], flops, 4 * size, in_specs=[SMEM] + [...  8.74 us
    pallas_call x1, Pallas kernels, body(): call(outer_analysis, [block] * groups, flops, 4 * size, in_specs=[SMEM] +...  7.66 us
    all_to_all x1, starting transfers between devices, body(): lax.all_to_all(outer, 'mem', split_axis=0, concat_axis=0, tiled=True)  3.94 us
    all_to_all x1, starting transfers between devices, body(): lax.all_to_all(inner, 'mem', split_axis=0, concat_axis=0, tiled=True)  3.67 us
    ppermute x14, waiting for transfers between devices, exchange(): out.append(lax.ppermute(block, 'mem', pairs) if k else block)  3.51 us
    ppermute x1, starting transfers between devices, body(): lax.ppermute(high, 'tile', [(i, (i + 1) % tiles) for i in range(tiles)])  3.08 us
    ppermute x1, starting transfers between devices, body(): lax.ppermute(low, 'tile', [((i + 1) % tiles, i) for i in range(tiles)])  2.09 us
  transfers between devices with their start and end apart: 18, of which 7 were waited for; matrix products, arithmetic and copies ran while one was open for 0% of the time, Pallas kernels for 37%

profile of v12, /device:TPU:0, one launch (start us, length us, event | category | flops | bytes accessed | tf_op | source)
XLA Modules:
  0.0 52.0 jit_solution(12126474960572064375)
XLA Ops:
  0.0 1.2 %shard_map.73 = (f32[2,32,256]{2,1,0:T(8,128)S(1)}, f32[2,32,256]{2,1,0:T(8,128)S(1)}, f32[8,256]{1,0:T(8,128)S(1)}, s32[1,32]{1,0:T(1,128)S(1)}) custom-call(f32[32,32,256]{2,1,0:T(8,128)} %state_ref.3, f32[256]{0:T(256)} %diff_ref.1, f32[256]{0:T(256)} %adv_ref.1, s32[1,32]{1,0:T(1,128)} %count_ref.1), custom_call_target="tpu_custom_call" | custom-call | bytes 1048576 | tf_op jit(solution)/shard_map/pallas_call | solution.py:354
  1.2 3.1 %collective-permute-start = (f32[2,32,256]{2,1,0:T(8,128)S(1)}, f32[2,32,256]{2,1,0:T(8,128)S(1)}, u32[]{:S(2)}, u32[]{:S(2)}) collective-permute-start(f32[2,32,256]{2,1,0:T(8,128)S(1)} %get-tuple-element.32), channel_id=1, source_target_pairs={{0,1},{1,2},{2,3},{3,0},{4,5},{5,6},{6,7},{7,4},{8,9},{9,10},{10,1... | collective-permute-start | bytes 196616 | tf_op jit(solution)/shard_map/ppermute | solution.py:365
  4.3 2.1 %collective-permute-start.1 = (f32[2,32,256]{2,1,0:T(8,128)S(1)}, f32[2,32,256]{2,1,0:T(8,128)S(1)}, u32[]{:S(2)}, u32[]{:S(2)}) collective-permute-start(f32[2,32,256]{2,1,0:T(8,128)S(1)} %get-tuple-element.33), channel_id=1, source_target_pairs={{1,0},{2,1},{3,2},{0,3},{5,4},{6,5},{7,6},{4,7},{9,8},{10,9},{11,1... | collective-permute-start | bytes 196616 | tf_op jit(solution)/shard_map/ppermute | solution.py:366
  6.4 0.7 %shard_map.74 = (f32[2,32,256]{2,1,0:T(8,128)S(1)}, f32[2,32,256]{2,1,0:T(8,128)S(1)}, f32[2,32,256]{2,1,0:T(8,128)S(1)}, f32[2,32,256]{2,1,0:T(8,128)S(1)}, f32...) custom-call(s32[1]{0:T(128)} %bitcast.me_ref, ...), custom_call_target="tpu_custom_call" | custom-call | flops 5242880 | bytes 2097152 | tf_op jit(solution)/shard_map/pallas_call | solution.py:367
  7.1 0.1 collective-permute-start.2
  7.2 2.7 %collective-permute-start.3 = (f32[2,32,256]{2,1,0:T(8,128)S(1)}, f32[2,32,256]{2,1,0:T(8,128)S(1)}, u32[]{:S(2)}, u32[]{:S(2)}) collective-permute-start(f32[2,32,256]{2,1,0:T(8,128)S(1)} %get-tuple-element.37), channel_id=1, source_target_pairs={{0,24},{4,28},{8,16},{12,20},{16,8},{20,12},{24,0},{28,4},{1,25},{... | collective-permute-start | bytes 196616 | tf_op jit(solution)/shard_map/ppermute | solution.py:51
  9.9 0.1 collective-permute-start.4
  10.0 0.0 collective-permute-done.before_ref
  10.0 1.6 %collective-permute-start.5 = (f32[2,32,256]{2,1,0:T(8,128)S(1)}, f32[2,32,256]{2,1,0:T(8,128)S(1)}, u32[]{:S(2)}, u32[]{:S(2)}) collective-permute-start(f32[2,32,256]{2,1,0:T(8,128)S(1)} %get-tuple-element.39), channel_id=1, source_target_pairs={{0,8},{4,12},{8,0},{12,4},{16,24},{20,28},{24,16},{28,20},{1,9},{5... | collective-permute-start | bytes 196616 | tf_op jit(solution)/shard_map/ppermute | solution.py:51
  11.6 0.0 collective-permute-done.1.after_ref
  11.6 0.0 collective-permute-start.6
  11.7 0.0 collective-permute-done.2.refs_0_
  11.7 1.7 %collective-permute-start.7 = (f32[2,32,256]{2,1,0:T(8,128)S(1)}, f32[2,32,256]{2,1,0:T(8,128)S(1)}, u32[]{:S(2)}, u32[]{:S(2)}) collective-permute-start(f32[2,32,256]{2,1,0:T(8,128)S(1)} %get-tuple-element.41), channel_id=1, source_target_pairs={{0,16},{4,20},{8,24},{12,28},{16,0},{20,4},{24,8},{28,12},{1,17},{... | collective-permute-start | bytes 196616 | tf_op jit(solution)/shard_map/ppermute | solution.py:51
  13.3 0.0 collective-permute-done.3.refs_1_
  13.3 0.2 collective-permute-start.8
  13.5 1.0 %shard_map.75 = (f32[8,2,32,256]{3,2,1,0:T(8,128)}, f32[8,256]{1,0:T(8,128)S(1)}) custom-call(f32[2,10,32,256]{3,2,1,0:T(8,128)S(1)} %get-tuple-element.31.rest_ref, f32[2,32,256]{2,1,0:T(8,128)S(1)} %collective-permute-done.before_ref, f32[2,32,256]{2,1,0:T(8,128)S(1)} %collective-permute-done.1.after_ref, f32[8,256]{1,0:T(8,128)S(1)} %get-tuple-element.30.num_ref), custom_call_target="tpu_custom_call" | custom-call | flops 5242880 | bytes 2097152 | tf_op jit(solution)/shard_map/pallas_call | solution.py:377
  14.6 0.0 copy-start.1
  14.6 0.0 copy-start.2
  14.6 0.0 copy-start.3
  14.6 3.9 %all-to-all-start = ((f32[8,2,32,256]{3,2,1,0:T(8,128)}), f32[8,2,32,256]{3,2,1,0:T(8,128)S(1)}, u32[]{:S(2)}, u32[]{:S(2)}) async-start(f32[8,2,32,256]{3,2,1,0:T(8,128)} %get-tuple-element.45), calls=%async_computation | async-start | bytes 1048576 | tf_op jit(solution)/shard_map/all_to_all | solution.py:389
  18.6 0.0 collective-permute-done.4.refs_2_
  18.6 0.0 collective-permute-done.5.refs_3_
  18.6 0.0 collective-permute-done.6.refs_4_
  18.6 0.0 collective-permute-done.7.refs_5_
  18.6 0.0 collective-permute-done.8.refs_6_
  18.6 0.0 copy-done.1
  18.6 8.7 %shard_map.76 = (f32[8,2,32,256]{3,2,1,0:T(8,128)}, f32[8,256]{1,0:T(8,128)S(1)}) custom-call(s32[1]{0:T(128)} %bitcast.me_ref, f32[8,256]{1,0:T(8,128)S(1)} %get-tuple-element.34.after_ref, s32[1,32]{1,0:T(1,128)S(1)} %get-tuple-element.35.count_ref, s32[32,512]{1,0:T(8,128)S(1)} %bitcast.4, f32[32,512]{1,0:T(8,128)S(1)} %bitcast.6, f32[32,512]{1,0:T(8,128)S(1)} %bitcast.8, ...), custom_call_target="tpu_custom_call" | custom-call | flops 6039797760 | bytes 1048576 | tf_op jit(solution)/shard_map/pallas_call | solution.py:391
  27.4 0.3 shard_map.77.obs_ref
  27.7 0.6 %all-to-all-done.whole_ref = f32[8,2,32,256]{3,2,1,0:T(8,128)S(1)} async-done(((f32[8,2,32,256]{3,2,1,0:T(8,128)}), f32[8,2,32,256]{3,2,1,0:T(8,128)S(1)}, u32[]{:S(2)}, u32[]{:S(2)}) %all-to-all-start) | async-done | bytes 524320 | tf_op jit(solution)/shard_map/all_to_all | solution.py:389
  28.3 3.7 %all-to-all-start.1 = ((f32[8,2,32,256]{3,2,1,0:T(8,128)}), f32[8,2,32,256]{3,2,1,0:T(8,128)S(1)}, u32[]{:S(2)}, u32[]{:S(2)}) async-start(f32[8,2,32,256]{3,2,1,0:T(8,128)} %get-tuple-element.47), calls=%async_computation.1 | async-start | bytes 1048576 | tf_op jit(solution)/shard_map/all_to_all | solution.py:399
  32.0 7.7 %shard_map.78 = (f32[2,32,256]{2,1,0:T(8,128)S(1)}, f32[2,32,256]{2,1,0:T(8,128)S(1)}, f32[2,32,256]{2,1,0:T(8,128)S(1)}, f32[2,32,256]{2,1,0:T(8,128)S(1)}, f32...) custom-call(s32[1]{0:T(128)} %bitcast.me_ref, ...), custom_call_target="tpu_custom_call" | custom-call | flops 6039797760 | bytes 1048576 | tf_op jit(solution)/shard_map/pallas_call | solution.py:407
  39.7 2.7 %collective-permute-start.9 = (f32[2,32,256]{2,1,0:T(8,128)S(1)}, f32[2,32,256]{2,1,0:T(8,128)S(1)}, u32[]{:S(2)}, u32[]{:S(2)}) collective-permute-start(f32[2,32,256]{2,1,0:T(8,128)S(1)} %get-tuple-element.46), channel_id=1, source_target_pairs={{0,28},{4,24},{8,20},{12,16},{16,12},{20,8},{24,4},{28,0},{1,29},{... | collective-permute-start | bytes 196616 | tf_op jit(solution)/shard_map/ppermute | solution.py:51
  42.3 0.4 collective-permute-start.10
  42.7 0.1 collective-permute-start.11
  42.8 1.9 %collective-permute-start.12 = (f32[2,32,256]{2,1,0:T(8,128)S(1)}, f32[2,32,256]{2,1,0:T(8,128)S(1)}, u32[]{:S(2)}, u32[]{:S(2)}) collective-permute-start(f32[2,32,256]{2,1,0:T(8,128)S(1)} %get-tuple-element.50), channel_id=1, source_target_pairs={{0,8},{4,12},{8,0},{12,4},{16,24},{20,28},{24,16},{28,20},{1,9},{5... | collective-permute-start | bytes 196616 | tf_op jit(solution)/shard_map/ppermute | solution.py:51
  44.7 0.0 collective-permute-start.13
  44.7 0.1 collective-permute-done.9.after_ref.refs_2_
  44.8 1.8 %collective-permute-start.14 = (f32[2,32,256]{2,1,0:T(8,128)S(1)}, f32[2,32,256]{2,1,0:T(8,128)S(1)}, u32[]{:S(2)}, u32[]{:S(2)}) collective-permute-start(f32[2,32,256]{2,1,0:T(8,128)S(1)} %get-tuple-element.52), channel_id=1, source_target_pairs={{0,16},{4,20},{8,24},{12,28},{16,0},{20,4},{24,8},{28,12},{1,17},{... | collective-permute-start | bytes 196616 | tf_op jit(solution)/shard_map/ppermute | solution.py:51
  46.6 0.0 collective-permute-done.10.refs_0_
  46.6 0.0 collective-permute-start.15
  46.6 0.0 all-to-all-done.1.inner_ref
  46.6 0.8 %shard_map.79.held_ref = f32[32,32,256]{2,1,0:T(8,128)} custom-call(f32[2,32,256]{2,1,0:T(8,128)S(1)} %collective-permute-done.9.after_ref.refs_2_, f32[8,2,32,256]{3,2,1,0:T(8,128)S(1)} %all-to-all-done.1.inner_ref), custom_call_target="tpu_custom_call" | custom-call | flops 262144 | bytes 1048576 | tf_op jit(solution)/shard_map/pallas_call | solution.py:417
  47.5 1.0 %collective-permute-done.11.refs_1_ = f32[2,32,256]{2,1,0:T(8,128)S(1)} collective-permute-done((f32[2,32,256]{2,1,0:T(8,128)S(1)}, f32[2,32,256]{2,1,0:T(8,128)S(1)}, u32[]{:S(2)}, u32[]{:S(2)}) %collective-permute-start.11) | collective-permute-done | bytes 65568 | tf_op jit(solution)/shard_map/ppermute | solution.py:51
  48.5 0.3 collective-permute-done.12.refs_3_
  48.9 0.3 collective-permute-done.13.refs_4_
  49.1 0.4 collective-permute-done.14.refs_5_
  49.5 1.4 %collective-permute-done.15.refs_6_ = f32[2,32,256]{2,1,0:T(8,128)S(1)} collective-permute-done((f32[2,32,256]{2,1,0:T(8,128)S(1)}, f32[2,32,256]{2,1,0:T(8,128)S(1)}, u32[]{:S(2)}, u32[]{:S(2)}) %collective-permute-start.15) | collective-permute-done | bytes 65568 | tf_op jit(solution)/shard_map/ppermute | solution.py:51
  50.9 0.9 %shard_map.80 = f32[32,32,256]{2,1,0:T(8,128)} custom-call(s32[1]{0:T(128)} %bitcast.me_ref, f32[32,32,256]{2,1,0:T(8,128)} %shard_map.79.held_ref, f32[2,32,256]{2,1,0:T(8,128)S(1)} %collective-permute-done.10.refs_0_, f32[2,32,256]{2,1,0:T(8,128)S(1)} %collective-permute-done.11.refs_1_, ...), custom_call_target="tpu_custom_call", output_to_operand_aliasing={{}: (1, {})} | custom-call | flops 262144 | bytes 1048576 | tf_op jit(solution)/shard_map/pallas_call | solution.py:429
  (4 shorter events, 0.0 us)
Async XLA Ops:
  0.0 6.4 %copy-start = (f32[32,32,256]{2,1,0:T(8,128)S(1)}, f32[32,32,256]{2,1,0:T(8,128)}, u32[]{:S(2)}) copy-start(f32[32,32,256]{2,1,0:T(8,128)} %state_ref.3) | copy-start | bytes 3145732
  1.2 8.8 %collective-permute-start = (f32[2,32,256]{2,1,0:T(8,128)S(1)}, f32[2,32,256]{2,1,0:T(8,128)S(1)}, u32[]{:S(2)}, u32[]{:S(2)}) collective-permute-start(f32[2,32,256]{2,1,0:T(8,128)S(1)} %get-tuple-element.32), channel_id=1, source_target_pairs={{0,1},{1,2},{2,3},{3,0},{4,5},{5,6},{6,7},{7,4},{8,9},{9,10},{10,1... | collective-permute-start | bytes 196616 | tf_op jit(solution)/shard_map/ppermute | solution.py:365
  4.3 7.3 %collective-permute-start.1 = (f32[2,32,256]{2,1,0:T(8,128)S(1)}, f32[2,32,256]{2,1,0:T(8,128)S(1)}, u32[]{:S(2)}, u32[]{:S(2)}) collective-permute-start(f32[2,32,256]{2,1,0:T(8,128)S(1)} %get-tuple-element.33), channel_id=1, source_target_pairs={{1,0},{2,1},{3,2},{0,3},{5,4},{6,5},{7,6},{4,7},{9,8},{10,9},{11,1... | collective-permute-start | bytes 196616 | tf_op jit(solution)/shard_map/ppermute | solution.py:366
  7.1 4.5 %collective-permute-start.2 = (f32[2,32,256]{2,1,0:T(8,128)S(1)}, f32[2,32,256]{2,1,0:T(8,128)S(1)}, u32[]{:S(2)}, u32[]{:S(2)}) collective-permute-start(f32[2,32,256]{2,1,0:T(8,128)S(1)} %get-tuple-element.36), channel_id=1, source_target_pairs={{0,4},{4,0},{8,12},{12,8},{16,20},{20,16},{24,28},{28,24},{1,5},{5... | collective-permute-start | bytes 196616 | tf_op jit(solution)/shard_map/ppermute | solution.py:51
  7.2 6.1 %collective-permute-start.3 = (f32[2,32,256]{2,1,0:T(8,128)S(1)}, f32[2,32,256]{2,1,0:T(8,128)S(1)}, u32[]{:S(2)}, u32[]{:S(2)}) collective-permute-start(f32[2,32,256]{2,1,0:T(8,128)S(1)} %get-tuple-element.37), channel_id=1, source_target_pairs={{0,24},{4,28},{8,16},{12,20},{16,8},{20,12},{24,0},{28,4},{1,25},{... | collective-permute-start | bytes 196616 | tf_op jit(solution)/shard_map/ppermute | solution.py:51
  9.9 8.7 %collective-permute-start.4 = (f32[2,32,256]{2,1,0:T(8,128)S(1)}, f32[2,32,256]{2,1,0:T(8,128)S(1)}, u32[]{:S(2)}, u32[]{:S(2)}) collective-permute-start(f32[2,32,256]{2,1,0:T(8,128)S(1)} %get-tuple-element.38), channel_id=1, source_target_pairs={{0,28},{4,24},{8,20},{12,16},{16,12},{20,8},{24,4},{28,0},{1,29},{... | collective-permute-start | bytes 196616 | tf_op jit(solution)/shard_map/ppermute | solution.py:51
  10.0 8.6 %collective-permute-start.5 = (f32[2,32,256]{2,1,0:T(8,128)S(1)}, f32[2,32,256]{2,1,0:T(8,128)S(1)}, u32[]{:S(2)}, u32[]{:S(2)}) collective-permute-start(f32[2,32,256]{2,1,0:T(8,128)S(1)} %get-tuple-element.39), channel_id=1, source_target_pairs={{0,8},{4,12},{8,0},{12,4},{16,24},{20,28},{24,16},{28,20},{1,9},{5... | collective-permute-start | bytes 196616 | tf_op jit(solution)/shard_map/ppermute | solution.py:51
  11.6 7.0 %collective-permute-start.6 = (f32[2,32,256]{2,1,0:T(8,128)S(1)}, f32[2,32,256]{2,1,0:T(8,128)S(1)}, u32[]{:S(2)}, u32[]{:S(2)}) collective-permute-start(f32[2,32,256]{2,1,0:T(8,128)S(1)} %get-tuple-element.40), channel_id=1, source_target_pairs={{0,12},{4,8},{8,4},{12,0},{16,28},{20,24},{24,20},{28,16},{1,13},{... | collective-permute-start | bytes 196616 | tf_op jit(solution)/shard_map/ppermute | solution.py:51
  11.7 6.9 %collective-permute-start.7 = (f32[2,32,256]{2,1,0:T(8,128)S(1)}, f32[2,32,256]{2,1,0:T(8,128)S(1)}, u32[]{:S(2)}, u32[]{:S(2)}) collective-permute-start(f32[2,32,256]{2,1,0:T(8,128)S(1)} %get-tuple-element.41), channel_id=1, source_target_pairs={{0,16},{4,20},{8,24},{12,28},{16,0},{20,4},{24,8},{28,12},{1,17},{... | collective-permute-start | bytes 196616 | tf_op jit(solution)/shard_map/ppermute | solution.py:51
  13.3 5.3 %collective-permute-start.8 = (f32[2,32,256]{2,1,0:T(8,128)S(1)}, f32[2,32,256]{2,1,0:T(8,128)S(1)}, u32[]{:S(2)}, u32[]{:S(2)}) collective-permute-start(f32[2,32,256]{2,1,0:T(8,128)S(1)} %get-tuple-element.42), channel_id=1, source_target_pairs={{0,20},{4,16},{8,28},{12,24},{16,4},{20,0},{24,12},{28,8},{1,21},{... | collective-permute-start | bytes 196616 | tf_op jit(solution)/shard_map/ppermute | solution.py:51
  14.6 4.0 %copy-start.1 = (s32[1,32,512]{2,1,0:T(8,128)S(1)}, s32[1,32,512]{2,1,0:T(8,128)}, u32[]{:S(2)}) copy-start(s32[1,32,512]{2,1,0:T(8,128)} %param.10) | copy-start | bytes 196612
  14.6 4.0 %copy-start.2 = (f32[1,32,512]{2,1,0:T(8,128)S(1)}, f32[1,32,512]{2,1,0:T(8,128)}, u32[]{:S(2)}) copy-start(f32[1,32,512]{2,1,0:T(8,128)} %param.12) | copy-start | bytes 196612
  14.6 4.0 %copy-start.3 = (f32[1,32,512]{2,1,0:T(8,128)S(1)}, f32[1,32,512]{2,1,0:T(8,128)}, u32[]{:S(2)}) copy-start(f32[1,32,512]{2,1,0:T(8,128)} %param.13) | copy-start | bytes 196612
  14.6 13.7 %all-to-all-start = ((f32[8,2,32,256]{3,2,1,0:T(8,128)}), f32[8,2,32,256]{3,2,1,0:T(8,128)S(1)}, u32[]{:S(2)}, u32[]{:S(2)}) async-start(f32[8,2,32,256]{3,2,1,0:T(8,128)} %get-tuple-element.45), calls=%async_computation | async-start | bytes 1048576 | tf_op jit(solution)/shard_map/all_to_all | solution.py:389
  28.3 18.3 %all-to-all-start.1 = ((f32[8,2,32,256]{3,2,1,0:T(8,128)}), f32[8,2,32,256]{3,2,1,0:T(8,128)S(1)}, u32[]{:S(2)}, u32[]{:S(2)}) async-start(f32[8,2,32,256]{3,2,1,0:T(8,128)} %get-tuple-element.47), calls=%async_computation.1 | async-start | bytes 1048576 | tf_op jit(solution)/shard_map/all_to_all | solution.py:399
  39.7 5.1 %collective-permute-start.9 = (f32[2,32,256]{2,1,0:T(8,128)S(1)}, f32[2,32,256]{2,1,0:T(8,128)S(1)}, u32[]{:S(2)}, u32[]{:S(2)}) collective-permute-start(f32[2,32,256]{2,1,0:T(8,128)S(1)} %get-tuple-element.46), channel_id=1, source_target_pairs={{0,28},{4,24},{8,20},{12,16},{16,12},{20,8},{24,4},{28,0},{1,29},{... | collective-permute-start | bytes 196616 | tf_op jit(solution)/shard_map/ppermute | solution.py:51
  42.3 4.3 %collective-permute-start.10 = (f32[2,32,256]{2,1,0:T(8,128)S(1)}, f32[2,32,256]{2,1,0:T(8,128)S(1)}, u32[]{:S(2)}, u32[]{:S(2)}) collective-permute-start(f32[2,32,256]{2,1,0:T(8,128)S(1)} %get-tuple-element.48), channel_id=1, source_target_pairs={{0,4},{4,0},{8,12},{12,8},{16,20},{20,16},{24,28},{28,24},{1,5},{5... | collective-permute-start | bytes 196616 | tf_op jit(solution)/shard_map/ppermute | solution.py:51
  42.7 5.8 %collective-permute-start.11 = (f32[2,32,256]{2,1,0:T(8,128)S(1)}, f32[2,32,256]{2,1,0:T(8,128)S(1)}, u32[]{:S(2)}, u32[]{:S(2)}) collective-permute-start(f32[2,32,256]{2,1,0:T(8,128)S(1)} %get-tuple-element.49), channel_id=1, source_target_pairs={{0,24},{4,28},{8,16},{12,20},{16,8},{20,12},{24,0},{28,4},{1,25},{... | collective-permute-start | bytes 196616 | tf_op jit(solution)/shard_map/ppermute | solution.py:51
  42.8 6.1 %collective-permute-start.12 = (f32[2,32,256]{2,1,0:T(8,128)S(1)}, f32[2,32,256]{2,1,0:T(8,128)S(1)}, u32[]{:S(2)}, u32[]{:S(2)}) collective-permute-start(f32[2,32,256]{2,1,0:T(8,128)S(1)} %get-tuple-element.50), channel_id=1, source_target_pairs={{0,8},{4,12},{8,0},{12,4},{16,24},{20,28},{24,16},{28,20},{1,9},{5... | collective-permute-start | bytes 196616 | tf_op jit(solution)/shard_map/ppermute | solution.py:51
  44.7 4.4 %collective-permute-start.13 = (f32[2,32,256]{2,1,0:T(8,128)S(1)}, f32[2,32,256]{2,1,0:T(8,128)S(1)}, u32[]{:S(2)}, u32[]{:S(2)}) collective-permute-start(f32[2,32,256]{2,1,0:T(8,128)S(1)} %get-tuple-element.51), channel_id=1, source_target_pairs={{0,12},{4,8},{8,4},{12,0},{16,28},{20,24},{24,20},{28,16},{1,13},{... | collective-permute-start | bytes 196616 | tf_op jit(solution)/shard_map/ppermute | solution.py:51
  44.8 4.7 %collective-permute-start.14 = (f32[2,32,256]{2,1,0:T(8,128)S(1)}, f32[2,32,256]{2,1,0:T(8,128)S(1)}, u32[]{:S(2)}, u32[]{:S(2)}) collective-permute-start(f32[2,32,256]{2,1,0:T(8,128)S(1)} %get-tuple-element.52), channel_id=1, source_target_pairs={{0,16},{4,20},{8,24},{12,28},{16,0},{20,4},{24,8},{28,12},{1,17},{... | collective-permute-start | bytes 196616 | tf_op jit(solution)/shard_map/ppermute | solution.py:51
  46.6 4.3 %collective-permute-start.15 = (f32[2,32,256]{2,1,0:T(8,128)S(1)}, f32[2,32,256]{2,1,0:T(8,128)S(1)}, u32[]{:S(2)}, u32[]{:S(2)}) collective-permute-start(f32[2,32,256]{2,1,0:T(8,128)S(1)} %get-tuple-element.53), channel_id=1, source_target_pairs={{0,20},{4,16},{8,28},{12,24},{16,4},{20,0},{24,12},{28,8},{1,21},{... | collective-permute-start | bytes 196616 | tf_op jit(solution)/shard_map/ppermute | solution.py:51
